TPU v7x, 512 devices: a whole 4x4x16 slice. The times are simulated.
512 devices in a mesh: centres: 128 (over x, z, core), rep: 4 (over y).
Axes of the slice: x: 4, y: 4, z: 16, core: 2. Of those that a mesh axis runs over, the one named last changes fastest.
Arguments:
- embeddings: bfloat16 [4096, 512], P(('centres', 'rep'))
- bn_gain: float32 [512], replicated, may hold values from 0.5 to 2
- bn_bias: float32 [512], replicated, may hold values from -3 to 3
- centres: bfloat16 [262144, 512], P('centres'), may hold values from -6 to 6
- sample_rows: int32 [128, 768], P('centres'), may hold values from 0 to 2047, as said below
- label_shard: int32 [128, 4, 8], P(None, 'rep'), may hold values from 0 to 127
- label_slot: int32 [128, 4, 8], P(None, 'rep'), may hold values from 0 to 767
Outputs:
- row_loss: float32 [4096], P(('centres', 'rep'))
- emb_grad: float32 [4096, 512], P(('centres', 'rep'))
- centre_grad: bfloat16 [98304, 512], P('centres')
- gain_grad: float32 [512], replicated
- bias_grad: float32 [512], replicated
Inputs may be any that keep to these rules, and one draw needn't show every extreme that they name: `sample_rows`: within each shard's row the entries are distinct.
All inputs are finite; a program needn't handle non-finite values.
Results may differ from a plain program's by a relative error of at most 0.0059.
Values may be sent and summed in bfloat16 or wider, within the bound.
No kernel may reach another device: no remote copies, remote signals or barrier semaphores. Data moves between devices by JAX's collectives and lax.ppermute only.
A program may use at most 64 MiB of HBM per device.

v0:
```python
import jax
import jax.numpy as jnp
from jax import lax
from jax.sharding import PartitionSpec as P

LOGIT_SCALE = 64.0
MARGIN = 0.4
EPSILON = 1e-05


def project(raw_grad, w_unit, inv_norm):
    radial = jnp.sum(w_unit * raw_grad, 1, keepdims=True)
    return (raw_grad - w_unit * radial) * inv_norm


def body(embeddings, bn_gain, bn_bias, centres, sample_rows, label_shard, label_slot):
    rows_dev = embeddings.shape[0]
    shards = lax.axis_size("centres")
    replicas = lax.axis_size("rep")
    batch_total = rows_dev * shards * replicas
    inputs = embeddings.astype(jnp.float32)
    col_sum, col_sq = lax.psum(
        (jnp.sum(inputs, 0), jnp.sum(inputs * inputs, 0)), ("centres", "rep")
    )
    col_mean = col_sum / batch_total
    col_var = col_sq / batch_total - col_mean * col_mean
    inv_std = lax.rsqrt(col_var + EPSILON)
    normed = (inputs - col_mean) * inv_std
    shifted = normed * bn_gain + bn_bias
    row_scale = lax.rsqrt(jnp.sum(shifted * shifted, 1, keepdims=True) + EPSILON)
    unit_f = shifted * row_scale
    unit = unit_f.astype(jnp.bfloat16)
    gathered = lax.all_gather(unit, "centres", axis=0, tiled=True)
    picked = jnp.take(centres, sample_rows[0], axis=0).astype(jnp.float32)
    inv_norm = lax.rsqrt(jnp.sum(picked * picked, 1, keepdims=True) + EPSILON)
    w_unit = picked * inv_norm
    w_hat = w_unit.astype(jnp.bfloat16)
    shard_id = lax.axis_index("centres")
    owners = label_shard[:, 0, :].reshape(-1)
    slot_ids = label_slot[:, 0, :].reshape(-1)
    columns = jnp.arange(w_hat.shape[0], dtype=jnp.int32)
    targets = (owners[:, None] == shard_id) & (slot_ids[:, None] == columns[None, :])
    cosine = jnp.dot(gathered, w_hat.T, preferred_element_type=jnp.float32)
    logits = LOGIT_SCALE * cosine - jnp.where(targets, LOGIT_SCALE * MARGIN, 0.0)
    target_part = jnp.sum(jnp.where(targets, logits, 0.0), 1)
    exp_logits = jnp.exp(logits)
    row_total, target_logit = lax.psum((jnp.sum(exp_logits, 1), target_part), "centres")
    loss_all = jnp.log(row_total) - target_logit
    row_loss = lax.dynamic_slice_in_dim(loss_all, shard_id * rows_dev, rows_dev, 0)
    probability = exp_logits / row_total[:, None]
    grad_cos = (probability - targets.astype(jnp.float32)).astype(jnp.bfloat16)
    grad_unit = lax.psum_scatter(
        jnp.dot(grad_cos, w_hat, preferred_element_type=jnp.float32),
        "centres",
        scatter_dimension=0,
        tiled=True,
    )
    local_grad = lax.dot_general(
        grad_cos, gathered, (((0,), (0,)), ((), ())), preferred_element_type=jnp.float32
    )
    summed = lax.psum(local_grad, "rep")
    centre_grad = project(summed, w_unit, inv_norm).astype(jnp.bfloat16)
    radial = jnp.sum(unit_f * grad_unit, 1, keepdims=True)
    grad_shift = (grad_unit - unit_f * radial) * row_scale
    bias_grad, gain_grad = lax.psum(
        (jnp.sum(grad_shift, 0), jnp.sum(grad_shift * normed, 0)), ("centres", "rep")
    )
    emb_grad = inv_std * (
        grad_shift * bn_gain
        - bn_gain * bias_grad / batch_total
        - normed * (bn_gain * gain_grad / batch_total)
    )
    return (row_loss, emb_grad, centre_grad, gain_grad, bias_grad)


def solution(mesh):
    return jax.shard_map(
        body,
        mesh=mesh,
        in_specs=(
            P(("centres", "rep"), None),
            P(),
            P(),
            P("centres", None),
            P("centres", None),
            P(None, "rep", None),
            P(None, "rep", None),
        ),
        out_specs=(
            P(("centres", "rep")),
            P(("centres", "rep"), None),
            P("centres", None),
            P(),
            P(),
        ),
        check_vma=False,
    )
```

profile of v0, /device:TPU:1, one launch (start us, length us, event | category | flops | bytes accessed | tf_op | source)
XLA Modules:
  0.0 943.3 jit_solution(14115677009855710179)
XLA Ops:
  7.2 0.9 convert_reduce_fusion
  8.1 111.0 %all-reduce.1 = (f32[512]{0:T(512)S(1)}, f32[512]{0:T(512)S(1)}) all-reduce(f32[512]{0:T(512)S(1)} %get-tuple-element.10, f32[512]{0:T(512)S(1)} %get-tuple-element.9), channel_id=1, replica_groups=mesh['centres'=128,'rep'=4] {'centres','rep'}, use_global_device_ids=true, to_apply=%region_3.0 | all-reduce | flops 1024 | bytes 8192 | tf_op jit(solution)/shard_map/psum | solution.py:22
  119.1 0.8 fusion.19
  120.0 1.4 fusion.24
  121.4 0.8 copy.13
  122.3 0.7 broadcast_compare_fusion
  123.3 0.7 reduce
  124.0 0.7 fusion.25
  124.7 2.7 gather_fusion
  127.8 118.0 %all-gather.2.cloned.1.call-done = bf16[1024,512]{1,0:T(8,128)(2,1)} async-done(((bf16[8,512]{1,0:T(8,128)(2,1)}), bf16[1024,512]{1,0:T(8,128)(2,1)}) %all-gather.2.cloned.1.call-update) | async-done | bytes 1048592 | tf_op jit(solution)/shard_map/all_gather | solution.py:33
  245.8 4.7 exponential_reduce_fusion
  250.4 250.4 %all-reduce.2 = (f32[1024]{0:T(1024)S(1)}, f32[1024]{0:T(1024)S(1)}) all-reduce(f32[1024]{0:T(1024)S(1)} %get-tuple-element.6, f32[1024]{0:T(1024)S(1)} %get-tuple-element.5), channel_id=1, replica_groups=mesh['centres'=128,'rep'=4] {'centres'}, use_global_device_ids=true, to_apply=%region_9.10 | all-reduce | flops 2048 | bytes 16384 | tf_op jit(solution)/shard_map/psum | solution.py:47
  500.9 2.9 subtract_convert_fusion
  503.9 1.2 copy-done.2
  505.0 2.2 fusion.27
  507.3 3.9 fusion.9
  511.8 53.8 %all-reduce.5.cloned.1.call-done = f32[768,512]{1,0:T(8,128)} async-done(((f32[768,512]{1,0:T(8,128)}), f32[768,512]{1,0:T(8,128)}) %all-reduce.5.cloned.1.call-update) | async-done | bytes 1572880 | tf_op jit(solution)/shard_map/psum | solution.py:61
  565.6 2.0 fusion.4
  567.7 1.3 fusion.7
  569.0 251.9 %reduce-scatter.2.cloned.1.call-done = f32[8,512]{1,0:T(8,128)} async-done(((f32[1024,512]{1,0:T(8,128)}), f32[8,512]{1,0:T(8,128)}) %reduce-scatter.2.cloned.1.call-update) | async-done | bytes 16400 | tf_op jit(solution)/shard_map/reduce_scatter | solution.py:52
  820.9 0.9 multiply_reduce_fusion
  821.8 0.8 fusion.26
  822.7 112.7 %all-reduce = (f32[512]{0:T(512)S(1)}, f32[512]{0:T(512)S(1)}) all-reduce(f32[512]{0:T(512)S(1)} %get-tuple-element.8, f32[512]{0:T(512)S(1)} %get-tuple-element.7), channel_id=1, replica_groups=mesh['centres'=128,'rep'=4] {'centres','rep'}, use_global_device_ids=true, to_apply=%region_15.16 | all-reduce | flops 1024 | bytes 8192 | tf_op jit(solution)/shard_map/psum | solution.py:65
  935.4 1.4 fusion.22
  (35 shorter events, 1.6 us)
Async XLA Ops:
  7.2 117.5 %copy-start = (bf16[2048,512]{1,0:T(8,128)(2,1)S(1)}, bf16[2048,512]{1,0:T(8,128)(2,1)}, u32[]{:S(2)}) copy-start(bf16[2048,512]{1,0:T(8,128)(2,1)} %param.10) | copy-start | bytes 6291460
  7.2 238.6 %all-gather.2.cloned.1.call-start = ((), (), s32[]{:S(2)}) async-start(), calls=%async_computation.1 | async-start | bytes 1056768 | tf_op jit(solution)/shard_map/all_gather | solution.py:33
  121.4 444.2 %all-reduce.5.cloned.1.call-start = ((), (), s32[]{:S(2)}) async-start(), calls=%async_computation.3 | async-start | bytes 3145728 | tf_op jit(solution)/shard_map/psum | solution.py:61
  500.9 4.1 copy-start.8
  503.9 1.2 copy-start.2
  507.2 313.7 %reduce-scatter.2.cloned.1.call-start = ((), (), s32[]{:S(2)}) async-start(), calls=%async_computation.2 | async-start | bytes 2113536 | tf_op jit(solution)/shard_map/reduce_scatter | solution.py:52
  565.6 2.1 copy-start.1
  567.6 253.3 %copy-start.3 = (bf16[8,512]{1,0:T(8,128)(2,1)S(1)}, bf16[8,512]{1,0:T(8,128)(2,1)}, u32[]{:S(2)}) copy-start(bf16[8,512]{1,0:T(8,128)(2,1)} %param.7) | copy-start | bytes 24580
  567.7 253.3 %copy-start.4 = (f32[512]{0:T(512)S(1)}, f32[512]{0:T(512)}, u32[]{:S(2)}) copy-start(f32[512]{0:T(512)} %param.8) | copy-start | bytes 6148
  567.7 253.3 %copy-start.5 = (f32[512]{0:T(512)S(1)}, f32[512]{0:T(512)}, u32[]{:S(2)}) copy-start(f32[512]{0:T(512)} %param.9) | copy-start | bytes 6148
  935.4 1.4 copy-start.6
  935.4 1.4 copy-start.7
Sparse Core Ops, SparseCore 0:
  121.5 124.2 all-gather.1
  507.4 58.1 all-reduce.4
  570.2 250.6 reduce-scatter.1
where the time goes:
time: 944 us; the launch traced here: 943 us
  blocking collectives  474 us (50%)
  waiting for transfers between devices  424 us (45%)
  other arithmetic  15 us (2%)
  between operations  13.9 us (1%)
  matrix products  10.7 us (1%)
    reduce_scatter x1, waiting for transfers between devices, body(): lax.psum_scatter(jnp.dot(grad_cos, w_hat, preferred_element_type=jnp.floa...  252 us
    psum x1, blocking collectives, body(): lax.psum((jnp.sum(exp_logits, 1), target_part), 'centres')  250 us
    all_gather x1, waiting for transfers between devices, body(): gathered = lax.all_gather(unit, 'centres', axis=0, tiled=True)  118 us
    psum x1, blocking collectives, body(): lax.psum((jnp.sum(grad_shift, 0), jnp.sum(grad_shift * normed, 0)), ('cen...  113 us
    psum x1, blocking collectives, body(): lax.psum((jnp.sum(inputs, 0), jnp.sum(inputs * inputs, 0)), ('centres', '...  111 us
    psum x1, waiting for transfers between devices, body(): summed = lax.psum(local_grad, 'rep')  53.8 us
  transfers between devices with their start and end apart: 3, of which 3 were waited for; matrix products, arithmetic and copies ran while one was open for 1% of the time, Pallas kernels for 0%

commit v1 on v0

v1 whole, which is shorter than its diff:
```python
import jax
import jax.numpy as jnp
from jax import lax
from jax.sharding import Mesh, PartitionSpec as P

LOGIT_SCALE = 64.0
MARGIN = 0.4
EPSILON = 1e-05
F32 = jnp.float32
BF16 = jnp.bfloat16


def spread(block, axes):
    copies = jnp.broadcast_to(block[None], (lax.axis_size(axes),) + block.shape)
    return lax.all_to_all(copies, axes, 0, 0)


def swap_cores(block):
    return lax.ppermute(block, "core", [(0, 1), (1, 0)])


def body(embeddings, bn_gain, bn_bias, centres, sample_rows, label_shard, label_slot):
    nx, nz, nc, nr = (lax.axis_size(a) for a in ("x", "z", "core", "rep"))
    ix, iz, ic, ir = (lax.axis_index(a) for a in ("x", "z", "core", "rep"))
    rows_dev, width = embeddings.shape
    slots = sample_rows.shape[1]
    batch_total = rows_dev * nx * nz * nc * nr
    group = nx * nz * rows_dev

    line = spread(embeddings, "z").reshape(nz * rows_dev, width)
    line_f = line.astype(F32)
    line_sums = jnp.stack([jnp.sum(line_f, 0), jnp.sum(line_f * line_f, 0)])
    sums = jnp.sum(spread(line_sums, ("x", "core", "rep")), 0)
    rows = spread(line, "x").reshape(group, width)

    picked = jnp.take(centres, sample_rows[0], axis=0).astype(F32)
    inv_norm = lax.rsqrt(jnp.sum(picked * picked, 1, keepdims=True) + EPSILON)
    w_unit = picked * inv_norm
    w_own = w_unit.astype(BF16)
    w_hat = jnp.concatenate([w_own, swap_cores(w_own)], 0)

    def mine(labels):
        return jnp.take(labels.reshape(nx * nz, nc, rows_dev), ic, axis=1).reshape(group)

    owner = mine(label_shard)
    slot = mine(label_slot)
    chip = (ix * nz + iz) * nc
    place = jnp.where(
        owner == chip + ic, slot, jnp.where(owner == chip + 1 - ic, slot + slots, -1)
    )
    columns = jnp.arange(nc * slots, dtype=jnp.int32)
    targets = place[:, None] == columns[None, :]

    hit = jnp.dot(targets.astype(BF16), w_hat, preferred_element_type=F32).astype(BF16)
    hit = lax.all_to_all(hit.reshape(nx, nz * rows_dev, width), "x", 0, 0)
    hit = jnp.sum(hit.astype(F32), 0).astype(BF16)
    hit = lax.all_to_all(hit.reshape(nz, rows_dev, width), "z", 0, 0)
    w_target = jnp.sum(hit.astype(F32), 0)

    col_mean = sums[0] / batch_total
    col_var = sums[1] / batch_total - col_mean * col_mean
    inv_std = lax.rsqrt(col_var + EPSILON)

    def head(inputs):
        normed = (inputs.astype(F32) - col_mean) * inv_std
        shifted = normed * bn_gain + bn_bias
        row_scale = lax.rsqrt(jnp.sum(shifted * shifted, 1, keepdims=True) + EPSILON)
        return normed, shifted * row_scale, row_scale

    unit = head(rows)[1].astype(BF16)
    cosine = jnp.dot(unit, w_hat.T, preferred_element_type=F32)
    exp_logits = jnp.exp(
        LOGIT_SCALE * cosine - jnp.where(targets, LOGIT_SCALE * MARGIN, 0.0)
    )
    part = jnp.sum(exp_logits, 1)
    part = jnp.sum(spread(part, "x"), 0)
    row_total = jnp.sum(spread(part, "z"), 0)

    others = jnp.where(targets, 0.0, exp_logits).astype(BF16)
    pull = jnp.dot(others, w_hat, preferred_element_type=F32).astype(BF16)
    pull = lax.all_to_all(pull.reshape(nx, nz * rows_dev, width), "x", 0, 0)
    pull = jnp.sum(pull.astype(F32), 0).astype(BF16)
    pull = lax.all_to_all(pull.reshape(nz, rows_dev, width), "z", 0, 0)
    pull = jnp.sum(pull.astype(F32), 0)

    normed, unit_f, row_scale = head(embeddings)
    own_total = lax.dynamic_slice_in_dim(
        row_total, (ix * nz + iz) * rows_dev, rows_dev, 0
    )[:, None]
    own_unit = unit_f.astype(BF16).astype(F32)
    target_logit = LOGIT_SCALE * jnp.sum(own_unit * w_target, 1, keepdims=True) - (
        LOGIT_SCALE * MARGIN
    )
    row_loss = (jnp.log(own_total) - target_logit)[:, 0]
    weight = (jnp.exp(target_logit) / own_total - 1.0).astype(BF16).astype(F32)
    grad_unit = pull / own_total + weight * w_target
    radial = jnp.sum(unit_f * grad_unit, 1, keepdims=True)
    grad_shift = (grad_unit - unit_f * radial) * row_scale
    ends = jnp.stack([jnp.sum(grad_shift, 0), jnp.sum(grad_shift * normed, 0)])
    ends = jnp.sum(spread(ends, "z"), 0)
    ends = jnp.sum(spread(ends, ("x", "core", "rep")), 0)
    bias_grad, gain_grad = ends[0], ends[1]
    emb_grad = inv_std * (
        grad_shift * bn_gain
        - bn_gain * bias_grad / batch_total
        - normed * (bn_gain * gain_grad / batch_total)
    )

    grad_cos = (exp_logits / row_total[:, None] - targets.astype(F32)).astype(BF16)
    raw = lax.dot_general(
        grad_cos, unit, (((0,), (0,)), ((), ())), preferred_element_type=F32
    )
    raw = raw[:slots] + swap_cores(raw[slots:].astype(BF16)).astype(F32)
    quarter = slots // nr
    raw = lax.all_to_all(raw.astype(BF16).reshape(nr, quarter, width), "rep", 0, 0)
    raw = jnp.sum(raw.astype(F32), 0)
    w_part = lax.dynamic_slice_in_dim(w_unit, ir * quarter, quarter, 0)
    n_part = lax.dynamic_slice_in_dim(inv_norm, ir * quarter, quarter, 0)
    along = jnp.sum(w_part * raw, 1, keepdims=True)
    grad = ((raw - w_part * along) * n_part).astype(BF16)
    centre_grad = spread(grad, "rep").reshape(slots, width)
    return (row_loss, emb_grad, centre_grad, gain_grad, bias_grad)


def solution(mesh):
    shards, replicas = mesh.devices.shape
    split = (4, shards // 8, 2, replicas)
    fine = Mesh(mesh.devices.reshape(split), ("x", "z", "core", "rep"))
    cen = ("x", "z", "core")
    every = cen + ("rep",)
    return jax.shard_map(
        body,
        mesh=fine,
        in_specs=(
            P(every, None),
            P(),
            P(),
            P(cen, None),
            P(cen, None),
            P(None, "rep", None),
            P(None, "rep", None),
        ),
        out_specs=(P(every), P(every, None), P(cen, None), P(), P()),
        check_vma=False,
    )
```

time: 944 us -> 219 us (0.23)
  blocking collectives: 474 us -> 29.7 us
  waiting for transfers between devices: 424 us -> 73.1 us
  starting transfers between devices: 0.12 us -> 74.7 us
  between operations: 13.9 us -> 1.06 us
    psum x3 -> x0, blocking collectives: 474 us -> none  [the longest x1 250 us: body(): lax.psum((jnp.sum(exp_logits, 1), target_part), 'centres')]
    reduce_scatter x1 -> x0, waiting for transfers between devices: 252 us -> none  [body(): lax.psum_scatter(jnp.dot(grad_cos, w_hat, preferred_element_type=jnp.floa...]
    all_gather x1 -> x0, waiting for transfers between devices: 118 us -> none  [body(): gathered = lax.all_gather(unit, 'centres', axis=0, tiled=True)]
    all_to_all x0 -> x11, waiting for transfers between devices: none -> 73.1 us  [the longest x6 42 us: spread(): return lax.all_to_all(copies, axes, 0, 0)]
    all_to_all x0 -> x11, starting transfers between devices: none -> 62.6 us  [the longest x6 44.7 us: spread(): return lax.all_to_all(copies, axes, 0, 0)]
    psum x1 -> x0, waiting for transfers between devices: 53.8 us -> none  [body(): summed = lax.psum(local_grad, 'rep')]
    all_to_all x0 -> x2, blocking collectives: none -> 29.7 us  [spread(): return lax.all_to_all(copies, axes, 0, 0)]
    ppermute x0 -> x2, starting transfers between devices: none -> 12.1 us  [swap_cores(): return lax.ppermute(block, 'core', [(0, 1), (1, 0)])]
  transfers between devices with their start and end apart: 3 -> 13, of which waited for: 3 -> 10; matrix products, arithmetic and copies ran while one was open for 1% -> 12% of each run, Pallas kernels for 0% -> 0%
where the time goes in v1:
time: 219 us; the launch traced here: 218 us
  starting transfers between devices  74.7 us (34%)
  waiting for transfers between devices  73.1 us (33%)
  blocking collectives  29.7 us (14%)
  matrix products  15 us (7%)
  other arithmetic  12.9 us (6%)
  local copies, waits for them, and re-layouts  11.5 us (5%)
    all_to_all x6, starting transfers between devices, spread(): return lax.all_to_all(copies, axes, 0, 0)  44.7 us
    all_to_all x6, waiting for transfers between devices, spread(): return lax.all_to_all(copies, axes, 0, 0)  42 us
    all_to_all x2, blocking collectives, spread(): return lax.all_to_all(copies, axes, 0, 0)  29.7 us
    ppermute x2, starting transfers between devices, swap_cores(): return lax.ppermute(block, 'core', [(0, 1), (1, 0)])  12.1 us
    all_to_all x1, waiting for transfers between devices, body(): lax.all_to_all(raw.astype(BF16).reshape(nr, quarter, width), 'rep', 0, 0)  11.2 us
    all_to_all x1, waiting for transfers between devices, body(): hit = lax.all_to_all(hit.reshape(nz, rows_dev, width), 'z', 0, 0)  11.1 us
    all_to_all x1, waiting for transfers between devices, body(): pull = lax.all_to_all(pull.reshape(nx, nz * rows_dev, width), 'x', 0, 0)  6.15 us
    broadcast_in_dim x8, local copies, waits for them, and re-layouts, spread(): copies = jnp.broadcast_to(block[None], (lax.axis_size(axes),) + block.shape)  5.29 us
  transfers between devices with their start and end apart: 13, of which 10 were waited for; matrix products, arithmetic and copies ran while one was open for 12% of the time, Pallas kernels for 0%

profile of v1, /device:TPU:1, one launch (start us, length us, event | category | flops | bytes accessed | tf_op | source)
XLA Modules:
  0.0 218.1 jit_solution(12130391744294393805)
XLA Ops:
  2.1 15.7 %all-to-all-start = ((bf16[16,8,512]{2,1,0:T(8,128)(2,1)}), bf16[16,8,512]{2,1,0:T(8,128)(2,1)S(1)}, u32[]{:S(2)}, u32[]{:S(2)}) async-start(bf16[16,8,512]{2,1,0:T(8,128)(2,1)} %broadcast_in_dim.51), calls=%async_computation | async-start | bytes 262144 | tf_op jit(solution)/shard_map/all_to_all | solution.py:15
  30.6 10.7 %all-to-all-start.2 = ((f32[32,2,512]{2,1,0:T(2,128)}), f32[32,2,512]{2,1,0:T(2,128)S(1)}, u32[]{:S(2)}, u32[]{:S(2)}) async-start(f32[32,2,512]{2,1,0:T(2,128)} %broadcast_in_dim.54), calls=%async_computation.2 | async-start | bytes 262144 | tf_op jit(solution)/shard_map/all_to_all | solution.py:15
  41.9 7.1 %all-to-all-done.2 = f32[32,2,512]{2,1,0:T(2,128)S(1)} async-done(((f32[32,2,512]{2,1,0:T(2,128)}), f32[32,2,512]{2,1,0:T(2,128)S(1)}, u32[]{:S(2)}, u32[]{:S(2)}) %all-to-all-start.2) | async-done | bytes 131104 | tf_op jit(solution)/shard_map/all_to_all | solution.py:15
  49.8 3.5 %all-to-all-start.1 = ((bf16[4,128,512]{2,1,0:T(8,128)(2,1)}), bf16[4,128,512]{2,1,0:T(8,128)(2,1)S(1)}, u32[]{:S(2)}, u32[]{:S(2)}) async-start(bf16[4,128,512]{2,1,0:T(8,128)(2,1)} %broadcast_in_dim.53), calls=%async_computation.1 | async-start | bytes 1048576 | tf_op jit(solution)/shard_map/all_to_all | solution.py:15
  53.4 9.0 %all-to-all-done.1 = bf16[4,128,512]{2,1,0:T(8,128)(2,1)S(1)} async-done(((bf16[4,128,512]{2,1,0:T(8,128)(2,1)}), bf16[4,128,512]{2,1,0:T(8,128)(2,1)S(1)}, u32[]{:S(2)}, u32[]{:S(2)}) %all-to-all-start.1) | async-done | bytes 524320 | tf_op jit(solution)/shard_map/all_to_all | solution.py:15
  62.9 4.5 %fusion.29 = (f32[512]{0:T(512)S(1)}, f32[512,1536]{1,0:T(8,128)}) fusion(s32[512]{0:T(512)S(1)} %select_select_fusion, bf16[512,512]{1,0:T(8,128)(2,1)S(1)} %fusion.16, bf16[768,512]{1,0:T(8,128)(2,1)} %collective-permute-done, bf16[768,512]{1,0:T(8,128)(2,1)} %get-tuple-element.25), kind=kOutput, calls=%fused_computation.81 | convolution fusion | flops 812383744 | bytes 5246976 | tf_op jit(solution)/shard_map/dot_general | solution.py:71
  67.4 6.5 %all_to_all.67 = f32[4,1,512]{2,1,0:T(1,128)S(1)} all-to-all(f32[4,1,512]{2,1,0:T(1,128)S(1)} %broadcast_in_dim.60), channel_id=1, replica_groups=mesh['x'=4,'z'=16,'core'=2,'rep'=4] {'x'}, dimensions={0} | all-to-all | bytes 16384 | tf_op jit(solution)/shard_map/all_to_all | solution.py:15
  74.6 5.7 %all-to-all-start.4 = ((f32[16,1,512]{2,1,0:T(1,128)}), f32[16,1,512]{2,1,0:T(1,128)S(1)}, u32[]{:S(2)}, u32[]{:S(2)}) async-start(f32[16,1,512]{2,1,0:T(1,128)} %broadcast_in_dim.61), calls=%async_computation.4 | async-start | bytes 65536 | tf_op jit(solution)/shard_map/all_to_all | solution.py:15
  83.5 8.3 %all-to-all-done.4 = f32[16,1,512]{2,1,0:T(1,128)S(1)} async-done(((f32[16,1,512]{2,1,0:T(1,128)}), f32[16,1,512]{2,1,0:T(1,128)S(1)}, u32[]{:S(2)}, u32[]{:S(2)}) %all-to-all-start.4) | async-done | bytes 32800 | tf_op jit(solution)/shard_map/all_to_all | solution.py:15
  91.8 3.5 %all-to-all-start.5 = ((bf16[4,128,512]{2,1,0:T(8,128)(2,1)}), bf16[4,128,512]{2,1,0:T(8,128)(2,1)S(1)}, u32[]{:S(2)}, u32[]{:S(2)}) async-start(bf16[4,128,512]{2,1,0:T(8,128)(2,1)} %bitcast.12), calls=%async_computation.5 | async-start | bytes 1048576 | tf_op jit(solution)/shard_map/all_to_all | solution.py:55
  95.3 4.1 %fusion.11 = bf16[512,512]{1,0:T(8,128)(2,1)} fusion(f32[512,1536]{1,0:T(8,128)} %get-tuple-element.35, s32[512]{0:T(512)S(1)} %select_select_fusion, bf16[768,512]{1,0:T(8,128)(2,1)} %collective-permute-done, bf16[768,512]{1,0:T(8,128)(2,1)} %get-tuple-element.25), kind=kOutput, calls=%fused_computation.22 | convolution fusion | flops 810287104 | bytes 5244928 | tf_op jit(solution)/shard_map/dot_general | solution.py:80
  102.2 3.5 %all-to-all-start.7 = ((bf16[4,128,512]{2,1,0:T(8,128)(2,1)}), bf16[4,128,512]{2,1,0:T(8,128)(2,1)S(1)}, u32[]{:S(2)}, u32[]{:S(2)}) async-start(bf16[4,128,512]{2,1,0:T(8,128)(2,1)} %bitcast.42), calls=%async_computation.7 | async-start | bytes 1048576 | tf_op jit(solution)/shard_map/all_to_all | solution.py:81
  106.4 6.1 %all-to-all-done.7 = bf16[4,128,512]{2,1,0:T(8,128)(2,1)S(1)} async-done(((bf16[4,128,512]{2,1,0:T(8,128)(2,1)}), bf16[4,128,512]{2,1,0:T(8,128)(2,1)S(1)}, u32[]{:S(2)}, u32[]{:S(2)}) %all-to-all-start.7) | async-done | bytes 524320 | tf_op jit(solution)/shard_map/all_to_all | solution.py:81
  112.5 3.5 %all-to-all-start.6 = ((bf16[16,8,512]{2,1,0:T(8,128)(2,1)}), bf16[16,8,512]{2,1,0:T(8,128)(2,1)S(1)}, u32[]{:S(2)}, u32[]{:S(2)}) async-start(bf16[16,8,512]{2,1,0:T(8,128)(2,1)} %bitcast.13), calls=%async_computation.6 | async-start | bytes 262144 | tf_op jit(solution)/shard_map/all_to_all | solution.py:57
  117.0 11.1 %all-to-all-done.6 = bf16[16,8,512]{2,1,0:T(8,128)(2,1)S(1)} async-done(((bf16[16,8,512]{2,1,0:T(8,128)(2,1)}), bf16[16,8,512]{2,1,0:T(8,128)(2,1)S(1)}, u32[]{:S(2)}, u32[]{:S(2)}) %all-to-all-start.6) | async-done | bytes 131104 | tf_op jit(solution)/shard_map/all_to_all | solution.py:57
  128.0 3.9 %all-to-all-start.8 = ((bf16[16,8,512]{2,1,0:T(8,128)(2,1)}), bf16[16,8,512]{2,1,0:T(8,128)(2,1)S(1)}, u32[]{:S(2)}, u32[]{:S(2)}) async-start(bf16[16,8,512]{2,1,0:T(8,128)(2,1)} %bitcast.15), calls=%async_computation.8 | async-start | bytes 262144 | tf_op jit(solution)/shard_map/all_to_all | solution.py:83
  137.0 9.2 %collective-permute-start.1 = (bf16[768,512]{1,0:T(8,128)(2,1)S(1)}, bf16[768,512]{1,0:T(8,128)(2,1)}, u32[]{:S(2)}, u32[]{:S(2)}) collective-permute-start(bf16[768,512]{1,0:T(8,128)(2,1)S(1)} %slice.54), channel_id=1, source_target_pairs={{0,4},{4,0},{1,5},{5,1},{2,6},{6,2},{3,7},{7,3},{8,12},{12,8},{9,1... | collective-permute-start | bytes 2359304 | tf_op jit(solution)/shard_map/ppermute | solution.py:19
  146.9 23.2 %all_to_all.68 = f32[16,2,512]{2,1,0:T(2,128)S(1)} all-to-all(f32[16,2,512]{2,1,0:T(2,128)S(1)} %broadcast_in_dim.62), channel_id=1, replica_groups=mesh['x'=4,'z'=16,'core'=2,'rep'=4] {'z'}, dimensions={0} | all-to-all | bytes 131072 | tf_op jit(solution)/shard_map/all_to_all | solution.py:15
  170.8 5.6 %all-to-all-start.10 = ((f32[32,2,512]{2,1,0:T(2,128)}), f32[32,2,512]{2,1,0:T(2,128)S(1)}, u32[]{:S(2)}, u32[]{:S(2)}) async-start(f32[32,2,512]{2,1,0:T(2,128)} %broadcast_in_dim.63), calls=%async_computation.10 | async-start | bytes 262144 | tf_op jit(solution)/shard_map/all_to_all | solution.py:15
  179.1 4.9 %all-to-all-done.10 = f32[32,2,512]{2,1,0:T(2,128)S(1)} async-done(((f32[32,2,512]{2,1,0:T(2,128)}), f32[32,2,512]{2,1,0:T(2,128)S(1)}, u32[]{:S(2)}, u32[]{:S(2)}) %all-to-all-start.10) | async-done | bytes 131104 | tf_op jit(solution)/shard_map/all_to_all | solution.py:15
  184.1 3.5 %all-to-all-start.11 = ((bf16[4,192,512]{2,1,0:T(8,128)(2,1)}), bf16[4,192,512]{2,1,0:T(8,128)(2,1)S(1)}, u32[]{:S(2)}, u32[]{:S(2)}) async-start(bf16[4,192,512]{2,1,0:T(8,128)(2,1)} %bitcast.40), calls=%async_computation.11 | async-start | bytes 1572864 | tf_op jit(solution)/shard_map/all_to_all | solution.py:115
  188.2 11.2 %all-to-all-done.11 = bf16[4,192,512]{2,1,0:T(8,128)(2,1)S(1)} async-done(((bf16[4,192,512]{2,1,0:T(8,128)(2,1)}), bf16[4,192,512]{2,1,0:T(8,128)(2,1)S(1)}, u32[]{:S(2)}, u32[]{:S(2)}) %all-to-all-start.11) | async-done | bytes 786464 | tf_op jit(solution)/shard_map/all_to_all | solution.py:115
  202.7 3.5 %all-to-all-start.12 = ((bf16[4,192,512]{2,1,0:T(8,128)(2,1)}), bf16[4,192,512]{2,1,0:T(8,128)(2,1)S(1)}, u32[]{:S(2)}, u32[]{:S(2)}) async-start(bf16[4,192,512]{2,1,0:T(8,128)(2,1)} %broadcast_in_dim.64), calls=%async_computation.12 | async-start | bytes 1572864 | tf_op jit(solution)/shard_map/all_to_all | solution.py:15
  206.9 10.3 %all-to-all-done.12 = bf16[4,192,512]{2,1,0:T(8,128)(2,1)S(1)} async-done(((bf16[4,192,512]{2,1,0:T(8,128)(2,1)}), bf16[4,192,512]{2,1,0:T(8,128)(2,1)S(1)}, u32[]{:S(2)}, u32[]{:S(2)}) %all-to-all-start.12) | async-done | bytes 786464 | tf_op jit(solution)/shard_map/all_to_all | solution.py:15
  (88 shorter events, 39.0 us)
Async XLA Ops:
  0.6 18.7 %copy-start = (bf16[2048,512]{1,0:T(8,128)(2,1)S(1)}, bf16[2048,512]{1,0:T(8,128)(2,1)}, u32[]{:S(2)}) copy-start(bf16[2048,512]{1,0:T(8,128)(2,1)} %param.12) | copy-start | bytes 6291460
  2.1 27.8 %all-to-all-start = ((bf16[16,8,512]{2,1,0:T(8,128)(2,1)}), bf16[16,8,512]{2,1,0:T(8,128)(2,1)S(1)}, u32[]{:S(2)}, u32[]{:S(2)}) async-start(bf16[16,8,512]{2,1,0:T(8,128)(2,1)} %broadcast_in_dim.51), calls=%async_computation | async-start | bytes 262144 | tf_op jit(solution)/shard_map/all_to_all | solution.py:15
  22.0 5.0 %copy-start.8 = (s32[128,1,8]{0,2,1:T(8,128)S(1)}, s32[128,1,8]{0,2,1:T(8,128)}, u32[]{:S(2)}) copy-start(s32[128,1,8]{0,2,1:T(8,128)} %param.15) | copy-start | bytes 12292
  22.0 5.1 %copy-start.9 = (s32[128,1,8]{0,2,1:T(8,128)S(1)}, s32[128,1,8]{0,2,1:T(8,128)}, u32[]{:S(2)}) copy-start(s32[128,1,8]{0,2,1:T(8,128)} %param.14) | copy-start | bytes 12292
  22.5 39.9 %copy-start.4 = (f32[512]{0:T(512)S(1)}, f32[512]{0:T(512)}, u32[]{:S(2)}) copy-start(f32[512]{0:T(512)} %param.10) | copy-start | bytes 6148
  22.5 39.9 %copy-start.5 = (f32[512]{0:T(512)S(1)}, f32[512]{0:T(512)}, u32[]{:S(2)}) copy-start(f32[512]{0:T(512)} %param.11) | copy-start | bytes 6148
  24.2 38.7 %collective-permute-start = (bf16[768,512]{1,0:T(8,128)(2,1)}, bf16[768,512]{1,0:T(8,128)(2,1)}, u32[]{:S(2)}, u32[]{:S(2)}) collective-permute-start(bf16[768,512]{1,0:T(8,128)(2,1)} %get-tuple-element.25), channel_id=1, source_target_pairs={{0,4},{4,0},{1,5},{5,1},{2,6},{6,2},{3,7},{7,3},{8,12},{12,8},{9,1... | collective-permute-start | bytes 2359304 | tf_op jit(solution)/shard_map/ppermute | solution.py:19
  30.6 18.3 %all-to-all-start.2 = ((f32[32,2,512]{2,1,0:T(2,128)}), f32[32,2,512]{2,1,0:T(2,128)S(1)}, u32[]{:S(2)}, u32[]{:S(2)}) async-start(f32[32,2,512]{2,1,0:T(2,128)} %broadcast_in_dim.54), calls=%async_computation.2 | async-start | bytes 262144 | tf_op jit(solution)/shard_map/all_to_all | solution.py:15
  49.8 12.5 %all-to-all-start.1 = ((bf16[4,128,512]{2,1,0:T(8,128)(2,1)}), bf16[4,128,512]{2,1,0:T(8,128)(2,1)S(1)}, u32[]{:S(2)}, u32[]{:S(2)}) async-start(bf16[4,128,512]{2,1,0:T(8,128)(2,1)} %broadcast_in_dim.53), calls=%async_computation.1 | async-start | bytes 1048576 | tf_op jit(solution)/shard_map/all_to_all | solution.py:15
  62.9 4.5 %copy-start.2 = (bf16[512,512]{1,0:T(8,128)(2,1)}, bf16[512,512]{1,0:T(8,128)(2,1)S(1)}, u32[]{:S(2)}) copy-start(bf16[512,512]{1,0:T(8,128)(2,1)S(1)} %fusion.16) | copy-start | bytes 1572868
  74.6 17.2 %all-to-all-start.4 = ((f32[16,1,512]{2,1,0:T(1,128)}), f32[16,1,512]{2,1,0:T(1,128)S(1)}, u32[]{:S(2)}, u32[]{:S(2)}) async-start(f32[16,1,512]{2,1,0:T(1,128)} %broadcast_in_dim.61), calls=%async_computation.4 | async-start | bytes 65536 | tf_op jit(solution)/shard_map/all_to_all | solution.py:15
  91.8 10.4 %all-to-all-start.5 = ((bf16[4,128,512]{2,1,0:T(8,128)(2,1)}), bf16[4,128,512]{2,1,0:T(8,128)(2,1)S(1)}, u32[]{:S(2)}, u32[]{:S(2)}) async-start(bf16[4,128,512]{2,1,0:T(8,128)(2,1)} %bitcast.12), calls=%async_computation.5 | async-start | bytes 1048576 | tf_op jit(solution)/shard_map/all_to_all | solution.py:55
  95.3 20.8 %copy-start.3 = (bf16[8,512]{1,0:T(8,128)(2,1)S(1)}, bf16[8,512]{1,0:T(8,128)(2,1)}, u32[]{:S(2)}) copy-start(bf16[8,512]{1,0:T(8,128)(2,1)} %param.9) | copy-start | bytes 24580
  102.2 10.4 %all-to-all-start.7 = ((bf16[4,128,512]{2,1,0:T(8,128)(2,1)}), bf16[4,128,512]{2,1,0:T(8,128)(2,1)S(1)}, u32[]{:S(2)}, u32[]{:S(2)}) async-start(bf16[4,128,512]{2,1,0:T(8,128)(2,1)} %bitcast.42), calls=%async_computation.7 | async-start | bytes 1048576 | tf_op jit(solution)/shard_map/all_to_all | solution.py:81
  112.5 15.5 %all-to-all-start.6 = ((bf16[16,8,512]{2,1,0:T(8,128)(2,1)}), bf16[16,8,512]{2,1,0:T(8,128)(2,1)S(1)}, u32[]{:S(2)}, u32[]{:S(2)}) async-start(bf16[16,8,512]{2,1,0:T(8,128)(2,1)} %bitcast.13), calls=%async_computation.6 | async-start | bytes 262144 | tf_op jit(solution)/shard_map/all_to_all | solution.py:57
  128.0 18.5 %all-to-all-start.8 = ((bf16[16,8,512]{2,1,0:T(8,128)(2,1)}), bf16[16,8,512]{2,1,0:T(8,128)(2,1)S(1)}, u32[]{:S(2)}, u32[]{:S(2)}) async-start(bf16[16,8,512]{2,1,0:T(8,128)(2,1)} %bitcast.15), calls=%async_computation.8 | async-start | bytes 262144 | tf_op jit(solution)/shard_map/all_to_all | solution.py:83
  135.2 1.7 copy-start.1
  137.0 39.4 %collective-permute-start.1 = (bf16[768,512]{1,0:T(8,128)(2,1)S(1)}, bf16[768,512]{1,0:T(8,128)(2,1)}, u32[]{:S(2)}, u32[]{:S(2)}) collective-permute-start(bf16[768,512]{1,0:T(8,128)(2,1)S(1)} %slice.54), channel_id=1, source_target_pairs={{0,4},{4,0},{1,5},{5,1},{2,6},{6,2},{3,7},{7,3},{8,12},{12,8},{9,1... | collective-permute-start | bytes 2359304 | tf_op jit(solution)/shard_map/ppermute | solution.py:19
  170.8 13.2 %all-to-all-start.10 = ((f32[32,2,512]{2,1,0:T(2,128)}), f32[32,2,512]{2,1,0:T(2,128)S(1)}, u32[]{:S(2)}, u32[]{:S(2)}) async-start(f32[32,2,512]{2,1,0:T(2,128)} %broadcast_in_dim.63), calls=%async_computation.10 | async-start | bytes 262144 | tf_op jit(solution)/shard_map/all_to_all | solution.py:15
  184.1 15.4 %all-to-all-start.11 = ((bf16[4,192,512]{2,1,0:T(8,128)(2,1)}), bf16[4,192,512]{2,1,0:T(8,128)(2,1)S(1)}, u32[]{:S(2)}, u32[]{:S(2)}) async-start(bf16[4,192,512]{2,1,0:T(8,128)(2,1)} %bitcast.40), calls=%async_computation.11 | async-start | bytes 1572864 | tf_op jit(solution)/shard_map/all_to_all | solution.py:115
  202.7 14.4 %all-to-all-start.12 = ((bf16[4,192,512]{2,1,0:T(8,128)(2,1)}), bf16[4,192,512]{2,1,0:T(8,128)(2,1)S(1)}, u32[]{:S(2)}, u32[]{:S(2)}) async-start(bf16[4,192,512]{2,1,0:T(8,128)(2,1)} %broadcast_in_dim.64), calls=%async_computation.12 | async-start | bytes 1572864 | tf_op jit(solution)/shard_map/all_to_all | solution.py:15
  206.3 11.8 %copy-start.6 = (f32[1,512]{1,0:T(1,128)}, f32[1,512]{1,0:T(1,128)S(1)}, u32[]{:S(2)}) copy-start(f32[1,512]{1,0:T(1,128)S(1)} %get-tuple-element.26) | copy-start | bytes 6148
  206.3 11.8 %copy-start.7 = (f32[1,512]{1,0:T(1,128)}, f32[1,512]{1,0:T(1,128)S(1)}, u32[]{:S(2)}) copy-start(f32[1,512]{1,0:T(1,128)S(1)} %get-tuple-element.27) | copy-start | bytes 6148

commit v2 on v1

v2 whole, which is shorter than its diff:
```python
import jax
import jax.numpy as jnp
from jax import lax
from jax.experimental import pallas as pl
from jax.experimental.pallas import tpu as pltpu
from jax.sharding import Mesh, PartitionSpec as P

LOGIT_SCALE = 64.0
MARGIN = 0.4
EPSILON = 1e-05
F32 = jnp.float32
BF16 = jnp.bfloat16
VMEM = 48 * 1024 * 1024
PAD = 16


def spread(block, axes):
    copies = jnp.broadcast_to(block[None], (lax.axis_size(axes),) + block.shape)
    return lax.all_to_all(copies, axes, 0, 0)


def shift(block, axis, by):
    n = lax.axis_size(axis)
    return lax.ppermute(block, axis, [(i, (i + by) % n) for i in range(n)])


def head(inputs, sums, gain, bias, batch_total):
    mean = sums[0:1] / batch_total
    inv_std = lax.rsqrt(sums[1:2] / batch_total - mean * mean + EPSILON)
    normed = (inputs.astype(F32) - mean) * inv_std
    shifted = normed * gain + bias
    scale = lax.rsqrt(jnp.sum(shifted * shifted, 1, keepdims=True) + EPSILON)
    return normed, shifted * scale, scale, inv_std


def call(kernel, grid, ins, outs, shapes, scratch, flops, size, exps=0):
    return pl.pallas_call(
        kernel,
        grid=(grid,),
        in_specs=ins,
        out_specs=outs,
        out_shape=shapes,
        scratch_shapes=scratch,
        compiler_params=pltpu.CompilerParams(vmem_limit_bytes=VMEM),
        cost_estimate=pl.CostEstimate(
            flops=flops, bytes_accessed=size, transcendentals=exps
        ),
    )


def whole(*shape):
    return pl.BlockSpec(shape, lambda i: (0,) * len(shape))


def rows_of(block, width):
    return pl.BlockSpec((block, width), lambda i: (i, 0))


def hits(place, block, count, first):
    return place == lax.broadcasted_iota(jnp.int32, (block, count), 0) + first


def exp_kernel(batch, rows, sums, gain, bias, place, w_hat, unit, expo, stats):
    i = pl.program_id(0)
    block, count = expo.shape

    @pl.when(i == 0)
    def _():
        total = jnp.sum(sums[...], 0)
        unit[...] = head(rows[...], total, gain[...], bias[...], batch)[1].astype(BF16)
        stats[...] = jnp.zeros_like(stats)

    cosine = lax.dot_general(
        w_hat[...], unit[...], (((1,), (1,)), ((), ())), preferred_element_type=F32
    )
    target = hits(place[...], block, count, i * block)
    logits = LOGIT_SCALE * cosine - jnp.where(target, LOGIT_SCALE * MARGIN, 0.0)
    exps = jnp.exp(logits)
    expo[...] = exps
    stats[0:1] += jnp.sum(exps, 0, keepdims=True)
    stats[1:2] += jnp.sum(jnp.where(target, logits, 0.0), 0, keepdims=True)


def grad_of(expo, total, place, first):
    block, count = expo.shape
    target = hits(place, block, count, first)
    return (expo / total - target.astype(F32)).astype(BF16)


def pull_kernel(
    batch, parts, rows, sums, gain, bias, place, totals, w_hat, expo, packed, acc
):
    i = pl.program_id(0)
    block = expo.shape[0]
    grad = grad_of(expo[...], totals[0:1], place[...], i * block)
    term = lax.dot_general(
        grad, w_hat[...], (((0,), (0,)), ((), ())), preferred_element_type=F32
    )

    @pl.when(i == 0)
    def _():
        acc[...] = term

    @pl.when(i > 0)
    def _():
        acc[...] += term

    @pl.when(i == pl.num_programs(0) - 1)
    def _():
        total = jnp.sum(sums[...], 0)
        normed, unit_f, scale, _ = head(rows[...], total, gain[...], bias[...], batch)
        pull = acc[...]
        radial = jnp.sum(unit_f * pull, 1, keepdims=True)
        shifts = (pull - unit_f * radial) * scale
        bias_part = jnp.sum(shifts, 0, keepdims=True)
        gain_part = jnp.sum(shifts * normed, 0, keepdims=True)
        tail = pack_ends(bias_part, gain_part)
        n = pull.shape[0] // parts
        for p in range(parts):
            packed[p, :n] = pull[p * n : (p + 1) * n].astype(BF16)
            packed[p, n:] = tail


def pack_ends(bias_part, gain_part):
    pieces = []
    for value in (bias_part, gain_part):
        for _ in range(3):
            piece = value.astype(BF16)
            value = value - piece.astype(F32)
            pieces.append(piece.astype(F32))
    fill = jnp.zeros((PAD - 6, bias_part.shape[1]), F32)
    return jnp.concatenate(pieces + [fill], 0).astype(BF16)


def unpack_ends(tail):
    tail = tail.astype(F32)
    return jnp.concatenate(
        [
            jnp.sum(tail[0:3], 0, keepdims=True),
            jnp.sum(tail[3:6], 0, keepdims=True),
        ],
        0,
    )


def mid_kernel(lines, rows_dev, arrived, packed):
    total = jnp.sum(arrived[...].astype(F32), 0)
    n = lines * rows_dev
    ends = unpack_ends(total[n:])
    tail = pack_ends(ends[0:1], ends[1:2]).astype(F32)
    both = PAD // rows_dev
    for p in range(lines):
        piece = total[p * rows_dev : (p + 1) * rows_dev]
        fill = [tail[: PAD - rows_dev]]
        packed[p] = jnp.concatenate([piece] + fill, 0).astype(BF16)


def raw_kernel(place, totals, unit, expo, own, other):
    i = pl.program_id(0)
    block = expo.shape[0]
    half = pl.num_programs(0) // 2
    grad = grad_of(expo[...], totals[0:1], place[...], i * block)
    term = jnp.dot(grad, unit[...], preferred_element_type=F32)

    @pl.when(i < half)
    def _():
        own[...] = term

    @pl.when(i >= half)
    def _():
        other[...] = term.astype(BF16)


def body(embeddings, bn_gain, bn_bias, centres, sample_rows, label_shard, label_slot):
    nx, nz, nc, nr = (lax.axis_size(a) for a in ("x", "z", "core", "rep"))
    ix, iz, ic, ir = (lax.axis_index(a) for a in ("x", "z", "core", "rep"))
    rows_dev, width = embeddings.shape
    slots = sample_rows.shape[1]
    batch = rows_dev * nx * nz * nc * nr
    line_rows = nz * rows_dev
    group = nx * line_rows
    held = nc * slots
    gain, bias = bn_gain[None], bn_bias[None]

    line = spread(embeddings, "z").reshape(line_rows, width)
    rows = spread(line, "x").reshape(group, width)
    rows_f = rows.astype(F32)
    sums = spread(
        jnp.stack([jnp.sum(rows_f, 0), jnp.sum(rows_f * rows_f, 0)]), ("core", "rep")
    )
    peers = nc * nr

    picked = jnp.take(centres, sample_rows[0], axis=0).astype(F32)
    inv_norm = lax.rsqrt(jnp.sum(picked * picked, 1, keepdims=True) + EPSILON)
    w_unit = picked * inv_norm
    w_own = w_unit.astype(BF16)
    w_hat = jnp.concatenate([w_own, shift(w_own, "core", 1)], 0)

    def mine(labels):
        return jnp.take(labels.reshape(nx * nz, nc, rows_dev), ic, axis=1).reshape(
            1, group
        )

    owner = mine(label_shard)
    slot = mine(label_slot)
    chip = (ix * nz + iz) * nc
    place = jnp.where(
        owner == chip + ic, slot, jnp.where(owner == chip + 1 - ic, slot + slots, -1)
    )

    def exp_call():
        block = held // 3
        return call(
            lambda *refs: exp_kernel(batch, *refs),
            3,
            [
                whole(group, width),
                whole(peers, 2, width),
                whole(1, width),
                whole(1, width),
                whole(1, group),
                rows_of(block, width),
            ],
            [whole(group, width), rows_of(block, group), whole(2, group)],
            [
                jax.ShapeDtypeStruct((group, width), BF16),
                jax.ShapeDtypeStruct((held, group), F32),
                jax.ShapeDtypeStruct((2, group), F32),
            ],
            [],
            2 * held * group * width,
            4 * held * group + 2 * held * width,
            held * group,
        )(rows, sums, gain, bias, place, w_hat)

    unit, expo, stats = exp_call()
    stats = jnp.sum(spread(stats, "x"), 0)
    stats = jnp.sum(spread(stats, "z"), 0)

    pull = call(
        lambda *refs: pull_kernel(batch, nx, *refs),
        3,
        [
            whole(group, width),
            whole(peers, 2, width),
            whole(1, width),
            whole(1, width),
            whole(1, group),
            whole(2, group),
            rows_of(held // 3, width),
            rows_of(held // 3, group),
        ],
        whole(nx, line_rows + PAD, width),
        jax.ShapeDtypeStruct((nx, line_rows + PAD, width), BF16),
        [pltpu.VMEM((group, width), F32)],
        2 * held * group * width,
        4 * held * group + 2 * held * width,
    )(rows, sums, gain, bias, place, stats, w_hat, expo)
    pull = lax.all_to_all(pull, "x", 0, 0)
    pull = call(
        lambda *refs: mid_kernel(nz, rows_dev, *refs),
        1,
        [whole(nx, line_rows + PAD, width)],
        whole(nz, PAD, width),
        jax.ShapeDtypeStruct((nz, PAD, width), BF16),
        [],
        nx * line_rows * width,
        2 * nx * line_rows * width,
    )(pull)
    pull = jnp.sum(lax.all_to_all(pull, "z", 0, 0).astype(F32), 0)
    grad_unit = pull[:rows_dev]
    ends = jnp.sum(spread(unpack_ends(pull[rows_dev:]), ("core", "rep")), 0)

    own_stats = lax.dynamic_slice_in_dim(
        stats, (ix * nz + iz) * rows_dev, rows_dev, 1
    )
    row_loss = jnp.log(own_stats[0]) - own_stats[1]
    normed, unit_f, row_scale, inv_std = head(
        embeddings, jnp.sum(sums, 0), gain, bias, batch
    )
    radial = jnp.sum(unit_f * grad_unit, 1, keepdims=True)
    grad_shift = (grad_unit - unit_f * radial) * row_scale
    bias_grad, gain_grad = ends[0], ends[1]
    emb_grad = inv_std * (
        grad_shift * bn_gain
        - bn_gain * bias_grad / batch
        - normed * (bn_gain * gain_grad / batch)
    )

    raw_block = slots // 2
    own, other = call(
        raw_kernel,
        4,
        [
            whole(1, group),
            whole(2, group),
            whole(group, width),
            rows_of(raw_block, group),
        ],
        [
            pl.BlockSpec((raw_block, width), lambda i: (jnp.minimum(i, 1), 0)),
            pl.BlockSpec((raw_block, width), lambda i: (jnp.maximum(i - 2, 0), 0)),
        ],
        [
            jax.ShapeDtypeStruct((slots, width), F32),
            jax.ShapeDtypeStruct((slots, width), BF16),
        ],
        [],
        2 * held * group * width,
        4 * held * group + 6 * slots * width,
    )(place, stats, unit, expo)
    raw = own + shift(other, "core", 1).astype(F32)
    quarter = slots // nr
    sent = raw.astype(BF16).reshape(nr, quarter, width)

    def piece(whole_array, at):
        return lax.dynamic_index_in_dim(whole_array, at, 0, keepdims=False)

    mine_raw = piece(raw.reshape(nr, quarter, width), ir)
    for by in range(1, nr):
        mine_raw = mine_raw + shift(
            piece(sent, lax.rem(ir + by, nr)), "rep", by
        ).astype(F32)
    w_part = piece(w_unit.reshape(nr, quarter, width), ir)
    n_part = piece(inv_norm.reshape(nr, quarter, 1), ir)
    along = jnp.sum(w_part * mine_raw, 1, keepdims=True)
    grad = ((mine_raw - w_part * along) * n_part).astype(BF16)
    found = jnp.stack([grad] + [shift(grad, "rep", by) for by in range(1, nr)])
    order = lax.rem(ir - jnp.arange(nr, dtype=jnp.int32) + nr, nr)
    centre_grad = jnp.take(found, order, axis=0).reshape(slots, width)
    return (row_loss, emb_grad, centre_grad, ends[1], ends[0])


def solution(mesh):
    shards, replicas = mesh.devices.shape
    split = (4, shards // 8, 2, replicas)
    fine = Mesh(mesh.devices.reshape(split), ("x", "z", "core", "rep"))
    cen = ("x", "z", "core")
    every = cen + ("rep",)
    return jax.shard_map(
        body,
        mesh=fine,
        in_specs=(
            P(every, None),
            P(),
            P(),
            P(cen, None),
            P(cen, None),
            P(None, "rep", None),
            P(None, "rep", None),
        ),
        out_specs=(P(every), P(every, None), P(cen, None), P(), P()),
        check_vma=False,
    )
```

time: 219 us -> 166 us (0.76)
  blocking collectives: 29.7 us -> 0 us
  waiting for transfers between devices: 73.1 us -> 44.7 us
  matrix products: 15 us -> 0 us
  local copies, waits for them, and re-layouts: 11.5 us -> 20.3 us
  Pallas kernels: 0 us -> 8.73 us
  other arithmetic: 12.9 us -> 15.7 us
    all_to_all x5 -> x2, waiting for transfers between devices: 31.2 us -> 0.01 us  [the longest x1 0.01 us: body(): pull = lax.all_to_all(pull, 'x', 0, 0)]
    all_to_all x2 -> x0, blocking collectives: 29.7 us -> none  [spread(): return lax.all_to_all(copies, axes, 0, 0)]
    dot_general x4 -> x0, matrix products: 15 us -> none  [the longest x1 4.47 us: body(): cosine = jnp.dot(unit, w_hat.T, preferred_element_type=F32)]
    ppermute x2 -> x8, waiting for transfers between devices: 0.01 us -> 12.5 us  [shift(): return lax.ppermute(block, axis, [(i, (i + by) % n) for i in range(n)])]
    ppermute x2 -> x8, starting transfers between devices: 12.1 us -> 23.7 us  [shift(): return lax.ppermute(block, axis, [(i, (i + by) % n) for i in range(n)])]
    all_to_all x5 -> x2, starting transfers between devices: 17.9 us -> 7.01 us  [the longest x1 3.53 us: body(): pull = jnp.sum(lax.all_to_all(pull, 'z', 0, 0).astype(F32), 0)]
    all_to_all x6, waiting for transfers between devices: 42 us -> 32.2 us  [spread(): return lax.all_to_all(copies, axes, 0, 0)]
    pallas_call x0 -> x4, Pallas kernels: none -> 8.73 us  [the longest x1 3.15 us: body(): call(lambda *refs: pull_kernel(batch, nx, *refs), 3, [whole(group, width)...]
  transfers between devices with their start and end apart: 13 -> 16, of which waited for: 10 -> 10; matrix products, arithmetic and copies ran while one was open for 12% -> 14% of each run, Pallas kernels for 0% -> 2%
where the time goes in v2:
time: 166 us; the launch traced here: 165 us
  starting transfers between devices  74.7 us (45%)
  waiting for transfers between devices  44.7 us (27%)
  local copies, waits for them, and re-layouts  20.3 us (12%)
  other arithmetic  15.7 us (9%)
  Pallas kernels  8.73 us (5%)
    all_to_all x6, starting transfers between devices, spread(): return lax.all_to_all(copies, axes, 0, 0)  44 us
    all_to_all x6, waiting for transfers between devices, spread(): return lax.all_to_all(copies, axes, 0, 0)  32.2 us
    ppermute x8, starting transfers between devices, shift(): return lax.ppermute(block, axis, [(i, (i + by) % n) for i in range(n)])  23.7 us
    ppermute x8, waiting for transfers between devices, shift(): return lax.ppermute(block, axis, [(i, (i + by) % n) for i in range(n)])  12.5 us
    unnamed x32, local copies, waits for them, and re-layouts  9.66 us
    broadcast_in_dim x6, local copies, waits for them, and re-layouts, spread(): copies = jnp.broadcast_to(block[None], (lax.axis_size(axes),) + block.shape)  4.85 us
    all_to_all x1, starting transfers between devices, body(): pull = jnp.sum(lax.all_to_all(pull, 'z', 0, 0).astype(F32), 0)  3.53 us
    all_to_all x1, starting transfers between devices, body(): pull = lax.all_to_all(pull, 'x', 0, 0)  3.48 us
  transfers between devices with their start and end apart: 16, of which 10 were waited for; matrix products, arithmetic and copies ran while one was open for 14% of the time, Pallas kernels for 2%

profile of v2, /device:TPU:1, one launch (start us, length us, event | category | flops | bytes accessed | tf_op | source)
XLA Modules:
  0.0 165.1 jit_solution(4804726283667879074)
XLA Ops:
  2.2 15.7 %all-to-all-start = ((bf16[16,8,512]{2,1,0:T(8,128)(2,1)}), bf16[16,8,512]{2,1,0:T(8,128)(2,1)S(1)}, u32[]{:S(2)}, u32[]{:S(2)}) async-start(bf16[16,8,512]{2,1,0:T(8,128)(2,1)} %broadcast_in_dim.95), calls=%async_computation | async-start | bytes 262144 | tf_op jit(solution)/shard_map/all_to_all | solution.py:19
  19.3 2.7 %gather_fusion = bf16[768,512]{1,0:T(8,128)(2,1)S(1)} fusion(bf16[2048,512]{1,0:T(8,128)(2,1)S(1)} %copy-done, s32[1024]{0:T(1024)S(1)} %pad_clamp_fusion.1), kind=kCustom, calls=%fused_computation | custom fusion | bytes 1575936 | tf_op jit(solution)/shard_map/jit(_take)/gather | solution.py:193
  23.7 2.9 %collective-permute-start = (bf16[768,512]{1,0:T(8,128)(2,1)}, bf16[768,512]{1,0:T(8,128)(2,1)}, u32[]{:S(2)}, u32[]{:S(2)}) collective-permute-start(bf16[768,512]{1,0:T(8,128)(2,1)} %fusion.1), channel_id=1, source_target_pairs={{0,4},{4,0},{1,5},{5,1},{2,6},{6,2},{3,7},{7,3},{8,12},{12,8},{9,1... | collective-permute-start | bytes 2359304 | tf_op jit(solution)/shard_map/ppermute | solution.py:24
  26.9 3.0 %all-to-all-done = bf16[16,8,512]{2,1,0:T(8,128)(2,1)S(1)} async-done(((bf16[16,8,512]{2,1,0:T(8,128)(2,1)}), bf16[16,8,512]{2,1,0:T(8,128)(2,1)S(1)}, u32[]{:S(2)}, u32[]{:S(2)}) %all-to-all-start) | async-done | bytes 131104 | tf_op jit(solution)/shard_map/all_to_all | solution.py:19
  30.8 4.0 %all-to-all-start.1 = ((bf16[4,128,512]{2,1,0:T(8,128)(2,1)}), bf16[4,128,512]{2,1,0:T(8,128)(2,1)S(1)}, u32[]{:S(2)}, u32[]{:S(2)}) async-start(bf16[4,128,512]{2,1,0:T(8,128)(2,1)} %broadcast_in_dim.97), calls=%async_computation.1 | async-start | bytes 1048576 | tf_op jit(solution)/shard_map/all_to_all | solution.py:19
  35.1 6.6 %all-to-all-done.1 = bf16[4,128,512]{2,1,0:T(8,128)(2,1)S(1)} async-done(((bf16[4,128,512]{2,1,0:T(8,128)(2,1)}), bf16[4,128,512]{2,1,0:T(8,128)(2,1)S(1)}, u32[]{:S(2)}, u32[]{:S(2)}) %all-to-all-start.1) | async-done | bytes 524320 | tf_op jit(solution)/shard_map/all_to_all | solution.py:19
  42.5 9.6 %all-to-all-start.2 = ((f32[8,2,512]{2,1,0:T(2,128)}), f32[8,2,512]{2,1,0:T(2,128)S(1)}, u32[]{:S(2)}, u32[]{:S(2)}) async-start(f32[8,2,512]{2,1,0:T(2,128)} %broadcast_in_dim.98), calls=%async_computation.2 | async-start | bytes 65536 | tf_op jit(solution)/shard_map/all_to_all | solution.py:19
  63.0 3.3 %all-to-all-start.3 = ((f32[4,2,512]{2,1,0:T(2,128)}), f32[4,2,512]{2,1,0:T(2,128)S(1)}, u32[]{:S(2)}, u32[]{:S(2)}) async-start(f32[4,2,512]{2,1,0:T(2,128)} %broadcast_in_dim.104), calls=%async_computation.3 | async-start | bytes 32768 | tf_op jit(solution)/shard_map/all_to_all | solution.py:19
  66.3 4.2 %all-to-all-done.3 = f32[4,2,512]{2,1,0:T(2,128)S(1)} async-done(((f32[4,2,512]{2,1,0:T(2,128)}), f32[4,2,512]{2,1,0:T(2,128)S(1)}, u32[]{:S(2)}, u32[]{:S(2)}) %all-to-all-start.3) | async-done | bytes 16416 | tf_op jit(solution)/shard_map/all_to_all | solution.py:19
  71.1 7.2 %all-to-all-start.4 = ((f32[16,2,512]{2,1,0:T(2,128)}), f32[16,2,512]{2,1,0:T(2,128)S(1)}, u32[]{:S(2)}, u32[]{:S(2)}) async-start(f32[16,2,512]{2,1,0:T(2,128)} %broadcast_in_dim.105), calls=%async_computation.4 | async-start | bytes 131072 | tf_op jit(solution)/shard_map/all_to_all | solution.py:19
  78.4 11.5 %all-to-all-done.4 = f32[16,2,512]{2,1,0:T(2,128)S(1)} async-done(((f32[16,2,512]{2,1,0:T(2,128)}), f32[16,2,512]{2,1,0:T(2,128)S(1)}, u32[]{:S(2)}, u32[]{:S(2)}) %all-to-all-start.4) | async-done | bytes 65568 | tf_op jit(solution)/shard_map/all_to_all | solution.py:19
  95.4 5.0 %collective-permute-start.1 = (bf16[768,512]{1,0:T(8,128)(2,1)}, bf16[768,512]{1,0:T(8,128)(2,1)}, u32[]{:S(2)}, u32[]{:S(2)}) collective-permute-start(bf16[768,512]{1,0:T(8,128)(2,1)} %get-tuple-element.15), channel_id=1, source_target_pairs={{0,4},{4,0},{1,5},{5,1},{2,6},{6,2},{3,7},{7,3},{8,12},{12,8},{9,1... | collective-permute-start | bytes 2359304 | tf_op jit(solution)/shard_map/ppermute | solution.py:24
  104.2 3.1 %shard_map.111 = bf16[4,144,512]{2,1,0:T(8,128)(2,1)} custom-call(bf16[512,512]{1,0:T(8,128)(2,1)S(1)} %bitcast.60, f32[8,2,512]{2,1,0:T(2,128)S(1)} %all-to-all-done.2.refs_1_, f32[1,512]{1,0:T(1,128)S(1)} %bitcast.62, f32[1,512]{1,0:T(1,128)S(1)} %bitcast.64, s32[1,512]{1,0:T(1,128)S(1)} %select_select_fusion.refs_4_.place, ...), custom_call_target="tpu_custom_call" | custom-call | flops 805306368 | bytes 4718592 | tf_op jit(solution)/shard_map/pallas_call | solution.py:240
  107.4 3.5 %all-to-all-start.5 = ((bf16[4,144,512]{2,1,0:T(8,128)(2,1)}), bf16[4,144,512]{2,1,0:T(8,128)(2,1)S(1)}, u32[]{:S(2)}, u32[]{:S(2)}) async-start(bf16[4,144,512]{2,1,0:T(8,128)(2,1)} %shard_map.111), calls=%async_computation.5 | async-start | bytes 1179648 | tf_op jit(solution)/shard_map/all_to_all | solution.py:259
  110.9 3.1 %fusion.15 = (bf16[768,512]{1,0:T(8,128)(2,1)S(1)}, f32[768,512]{1,0:T(8,128)}) fusion(f32[768,512]{1,0:T(8,128)} %copy-done.6, bf16[768,512]{1,0:T(8,128)(2,1)} %collective-permute-done.1), kind=kLoop, calls=%fused_computation.75 | loop fusion | flops 1179648 | bytes 4718592 | tf_op jit(solution)/shard_map/convert_element_type | solution.py:314
  114.8 2.8 %collective-permute-start.4 = (bf16[192,512]{1,0:T(8,128)(2,1)}, bf16[192,512]{1,0:T(8,128)(2,1)S(1)}, u32[]{:S(2)}, u32[]{:S(2)}) collective-permute-start(bf16[192,512]{1,0:T(8,128)(2,1)} %get-tuple-element.34), channel_id=1, source_target_pairs={{0,3},{1,0},{2,1},{3,2},{4,7},{5,4},{6,5},{7,6},{8,11},{9,8},{10,9... | collective-permute-start | bytes 589832 | tf_op jit(solution)/shard_map/ppermute | solution.py:24
  117.6 3.1 %collective-permute-start.3 = (bf16[192,512]{1,0:T(8,128)(2,1)}, bf16[192,512]{1,0:T(8,128)(2,1)S(1)}, u32[]{:S(2)}, u32[]{:S(2)}) collective-permute-start(bf16[192,512]{1,0:T(8,128)(2,1)} %get-tuple-element.35), channel_id=1, source_target_pairs={{0,2},{1,3},{2,0},{3,1},{4,6},{5,7},{6,4},{7,5},{8,10},{9,11},{10,... | collective-permute-start | bytes 589832 | tf_op jit(solution)/shard_map/ppermute | solution.py:24
  123.6 3.5 %all-to-all-start.6 = ((bf16[16,16,512]{2,1,0:T(8,128)(2,1)}), bf16[16,16,512]{2,1,0:T(8,128)(2,1)S(1)}, u32[]{:S(2)}, u32[]{:S(2)}) async-start(bf16[16,16,512]{2,1,0:T(8,128)(2,1)} %shard_map.112), calls=%async_computation.6 | async-start | bytes 524288 | tf_op jit(solution)/shard_map/all_to_all | solution.py:270
  127.4 4.7 %collective-permute-done.2 = bf16[192,512]{1,0:T(8,128)(2,1)S(1)} collective-permute-done((bf16[192,512]{1,0:T(8,128)(2,1)}, bf16[192,512]{1,0:T(8,128)(2,1)S(1)}, u32[]{:S(2)}, u32[]{:S(2)}) %collective-permute-start.2) | collective-permute-done | bytes 196640 | tf_op jit(solution)/shard_map/ppermute | solution.py:24
  136.8 3.2 %collective-permute-start.6 = (bf16[192,512]{1,0:T(8,128)(2,1)S(1)}, bf16[192,512]{1,0:T(8,128)(2,1)S(1)}, u32[]{:S(2)}, u32[]{:S(2)}) collective-permute-start(bf16[192,512]{1,0:T(8,128)(2,1)S(1)} %fusion.6), channel_id=1, source_target_pairs={{0,2},{1,3},{2,0},{3,1},{4,6},{5,7},{6,4},{7,5},{8,10},{9,11},{10,... | collective-permute-start | bytes 589832 | tf_op jit(solution)/shard_map/ppermute | solution.py:24
  140.0 2.8 %collective-permute-start.5 = (bf16[192,512]{1,0:T(8,128)(2,1)S(1)}, bf16[192,512]{1,0:T(8,128)(2,1)S(1)}, u32[]{:S(2)}, u32[]{:S(2)}) collective-permute-start(bf16[192,512]{1,0:T(8,128)(2,1)S(1)} %fusion.6), channel_id=1, source_target_pairs={{0,1},{1,2},{2,3},{3,0},{4,5},{5,6},{6,7},{7,4},{8,9},{9,10},{10,1... | collective-permute-start | bytes 589832 | tf_op jit(solution)/shard_map/ppermute | solution.py:24
  145.4 5.3 %collective-permute-done.5 = bf16[192,512]{1,0:T(8,128)(2,1)S(1)} collective-permute-done((bf16[192,512]{1,0:T(8,128)(2,1)S(1)}, bf16[192,512]{1,0:T(8,128)(2,1)S(1)}, u32[]{:S(2)}, u32[]{:S(2)}) %collective-permute-start.5) | collective-permute-done | bytes 196640 | tf_op jit(solution)/shard_map/ppermute | solution.py:24
  155.2 4.2 %all-to-all-start.7 = ((f32[8,2,512]{2,1,0:T(2,128)}), f32[8,2,512]{2,1,0:T(2,128)S(1)}, u32[]{:S(2)}, u32[]{:S(2)}) async-start(f32[8,2,512]{2,1,0:T(2,128)} %broadcast_in_dim.108), calls=%async_computation.7 | async-start | bytes 65536 | tf_op jit(solution)/shard_map/all_to_all | solution.py:19
  159.6 4.7 %all-to-all-done.7 = f32[8,2,512]{2,1,0:T(2,128)S(1)} async-done(((f32[8,2,512]{2,1,0:T(2,128)}), f32[8,2,512]{2,1,0:T(2,128)S(1)}, u32[]{:S(2)}, u32[]{:S(2)}) %all-to-all-start.7) | async-done | bytes 32800 | tf_op jit(solution)/shard_map/all_to_all | solution.py:19
  (102 shorter events, 44.4 us)
Async XLA Ops:
  0.6 18.7 %copy-start = (bf16[2048,512]{1,0:T(8,128)(2,1)S(1)}, bf16[2048,512]{1,0:T(8,128)(2,1)}, u32[]{:S(2)}) copy-start(bf16[2048,512]{1,0:T(8,128)(2,1)} %param.12) | copy-start | bytes 6291460
  2.2 27.8 %all-to-all-start = ((bf16[16,8,512]{2,1,0:T(8,128)(2,1)}), bf16[16,8,512]{2,1,0:T(8,128)(2,1)S(1)}, u32[]{:S(2)}, u32[]{:S(2)}) async-start(bf16[16,8,512]{2,1,0:T(8,128)(2,1)} %broadcast_in_dim.95), calls=%async_computation | async-start | bytes 262144 | tf_op jit(solution)/shard_map/all_to_all | solution.py:19
  22.0 8.7 %copy-start.9 = (bf16[768,512]{1,0:T(8,128)(2,1)}, bf16[768,512]{1,0:T(8,128)(2,1)S(1)}, u32[]{:S(2)}) copy-start(bf16[768,512]{1,0:T(8,128)(2,1)S(1)} %gather_fusion) | copy-start | bytes 2359300
  22.0 4.6 %copy-start.13 = (s32[128,1,8]{0,2,1:T(8,128)S(1)}, s32[128,1,8]{0,2,1:T(8,128)}, u32[]{:S(2)}) copy-start(s32[128,1,8]{0,2,1:T(8,128)} %param.15) | copy-start | bytes 12292
  22.1 4.7 %copy-start.14 = (s32[128,1,8]{0,2,1:T(8,128)S(1)}, s32[128,1,8]{0,2,1:T(8,128)}, u32[]{:S(2)}) copy-start(s32[128,1,8]{0,2,1:T(8,128)} %param.14) | copy-start | bytes 12292
  23.7 28.4 %collective-permute-start = (bf16[768,512]{1,0:T(8,128)(2,1)}, bf16[768,512]{1,0:T(8,128)(2,1)}, u32[]{:S(2)}, u32[]{:S(2)}) collective-permute-start(bf16[768,512]{1,0:T(8,128)(2,1)} %fusion.1), channel_id=1, source_target_pairs={{0,4},{4,0},{1,5},{5,1},{2,6},{6,2},{3,7},{7,3},{8,12},{12,8},{9,1... | collective-permute-start | bytes 2359304 | tf_op jit(solution)/shard_map/ppermute | solution.py:24
  30.8 10.9 %all-to-all-start.1 = ((bf16[4,128,512]{2,1,0:T(8,128)(2,1)}), bf16[4,128,512]{2,1,0:T(8,128)(2,1)S(1)}, u32[]{:S(2)}, u32[]{:S(2)}) async-start(bf16[4,128,512]{2,1,0:T(8,128)(2,1)} %broadcast_in_dim.97), calls=%async_computation.1 | async-start | bytes 1048576 | tf_op jit(solution)/shard_map/all_to_all | solution.py:19
  42.5 14.5 %all-to-all-start.2 = ((f32[8,2,512]{2,1,0:T(2,128)}), f32[8,2,512]{2,1,0:T(2,128)S(1)}, u32[]{:S(2)}, u32[]{:S(2)}) async-start(f32[8,2,512]{2,1,0:T(2,128)} %broadcast_in_dim.98), calls=%async_computation.2 | async-start | bytes 65536 | tf_op jit(solution)/shard_map/all_to_all | solution.py:19
  52.1 4.9 %copy-start.7 = (f32[512]{0:T(512)S(1)}, f32[512]{0:T(512)}, u32[]{:S(2)}) copy-start(f32[512]{0:T(512)} %param.10) | copy-start | bytes 6148
  52.1 4.9 %copy-start.8 = (f32[512]{0:T(512)S(1)}, f32[512]{0:T(512)}, u32[]{:S(2)}) copy-start(f32[512]{0:T(512)} %param.11) | copy-start | bytes 6148
  63.0 7.4 %all-to-all-start.3 = ((f32[4,2,512]{2,1,0:T(2,128)}), f32[4,2,512]{2,1,0:T(2,128)S(1)}, u32[]{:S(2)}, u32[]{:S(2)}) async-start(f32[4,2,512]{2,1,0:T(2,128)} %broadcast_in_dim.104), calls=%async_computation.3 | async-start | bytes 32768 | tf_op jit(solution)/shard_map/all_to_all | solution.py:19
  71.1 18.7 %all-to-all-start.4 = ((f32[16,2,512]{2,1,0:T(2,128)}), f32[16,2,512]{2,1,0:T(2,128)S(1)}, u32[]{:S(2)}, u32[]{:S(2)}) async-start(f32[16,2,512]{2,1,0:T(2,128)} %broadcast_in_dim.105), calls=%async_computation.4 | async-start | bytes 131072 | tf_op jit(solution)/shard_map/all_to_all | solution.py:19
  91.8 9.0 %copy-start.10 = (bf16[8,512]{1,0:T(8,128)(2,1)S(1)}, bf16[8,512]{1,0:T(8,128)(2,1)}, u32[]{:S(2)}) copy-start(bf16[8,512]{1,0:T(8,128)(2,1)} %param.9) | copy-start | bytes 24580
  95.4 15.5 %collective-permute-start.1 = (bf16[768,512]{1,0:T(8,128)(2,1)}, bf16[768,512]{1,0:T(8,128)(2,1)}, u32[]{:S(2)}, u32[]{:S(2)}) collective-permute-start(bf16[768,512]{1,0:T(8,128)(2,1)} %get-tuple-element.15), channel_id=1, source_target_pairs={{0,4},{4,0},{1,5},{5,1},{2,6},{6,2},{3,7},{7,3},{8,12},{12,8},{9,1... | collective-permute-start | bytes 2359304 | tf_op jit(solution)/shard_map/ppermute | solution.py:24
  100.9 1.9 %copy-start.3 = (f32[1536,512]{1,0:T(8,128)S(1)}, f32[1536,512]{1,0:T(8,128)}, u32[]{:S(2)}) copy-start(f32[1536,512]{1,0:T(8,128)} %copy-done.1) | copy-start | bytes 9437188
  107.4 15.4 %all-to-all-start.5 = ((bf16[4,144,512]{2,1,0:T(8,128)(2,1)}), bf16[4,144,512]{2,1,0:T(8,128)(2,1)S(1)}, u32[]{:S(2)}, u32[]{:S(2)}) async-start(bf16[4,144,512]{2,1,0:T(8,128)(2,1)} %shard_map.111), calls=%async_computation.5 | async-start | bytes 1179648 | tf_op jit(solution)/shard_map/all_to_all | solution.py:259
  114.8 12.3 %collective-permute-start.4 = (bf16[192,512]{1,0:T(8,128)(2,1)}, bf16[192,512]{1,0:T(8,128)(2,1)S(1)}, u32[]{:S(2)}, u32[]{:S(2)}) collective-permute-start(bf16[192,512]{1,0:T(8,128)(2,1)} %get-tuple-element.34), channel_id=1, source_target_pairs={{0,3},{1,0},{2,1},{3,2},{4,7},{5,4},{6,5},{7,6},{8,11},{9,8},{10,9... | collective-permute-start | bytes 589832 | tf_op jit(solution)/shard_map/ppermute | solution.py:24
  117.6 9.8 %collective-permute-start.3 = (bf16[192,512]{1,0:T(8,128)(2,1)}, bf16[192,512]{1,0:T(8,128)(2,1)S(1)}, u32[]{:S(2)}, u32[]{:S(2)}) collective-permute-start(bf16[192,512]{1,0:T(8,128)(2,1)} %get-tuple-element.35), channel_id=1, source_target_pairs={{0,2},{1,3},{2,0},{3,1},{4,6},{5,7},{6,4},{7,5},{8,10},{9,11},{10,... | collective-permute-start | bytes 589832 | tf_op jit(solution)/shard_map/ppermute | solution.py:24
  120.7 11.4 %collective-permute-start.2 = (bf16[192,512]{1,0:T(8,128)(2,1)}, bf16[192,512]{1,0:T(8,128)(2,1)S(1)}, u32[]{:S(2)}, u32[]{:S(2)}) collective-permute-start(bf16[192,512]{1,0:T(8,128)(2,1)} %get-tuple-element.33), channel_id=1, source_target_pairs={{0,1},{1,2},{2,3},{3,0},{4,5},{5,6},{6,7},{7,4},{8,9},{9,10},{10,1... | collective-permute-start | bytes 589832 | tf_op jit(solution)/shard_map/ppermute | solution.py:24
  123.6 30.9 %all-to-all-start.6 = ((bf16[16,16,512]{2,1,0:T(8,128)(2,1)}), bf16[16,16,512]{2,1,0:T(8,128)(2,1)S(1)}, u32[]{:S(2)}, u32[]{:S(2)}) async-start(bf16[16,16,512]{2,1,0:T(8,128)(2,1)} %shard_map.112), calls=%async_computation.6 | async-start | bytes 524288 | tf_op jit(solution)/shard_map/all_to_all | solution.py:270
  134.8 8.5 %collective-permute-start.7 = (bf16[192,512]{1,0:T(8,128)(2,1)S(1)}, bf16[192,512]{1,0:T(8,128)(2,1)S(1)}, u32[]{:S(2)}, u32[]{:S(2)}) collective-permute-start(bf16[192,512]{1,0:T(8,128)(2,1)S(1)} %fusion.6), channel_id=1, source_target_pairs={{0,3},{1,0},{2,1},{3,2},{4,7},{5,4},{6,5},{7,6},{8,11},{9,8},{10,9... | collective-permute-start | bytes 589832 | tf_op jit(solution)/shard_map/ppermute | solution.py:24
  136.8 8.7 %collective-permute-start.6 = (bf16[192,512]{1,0:T(8,128)(2,1)S(1)}, bf16[192,512]{1,0:T(8,128)(2,1)S(1)}, u32[]{:S(2)}, u32[]{:S(2)}) collective-permute-start(bf16[192,512]{1,0:T(8,128)(2,1)S(1)} %fusion.6), channel_id=1, source_target_pairs={{0,2},{1,3},{2,0},{3,1},{4,6},{5,7},{6,4},{7,5},{8,10},{9,11},{10,... | collective-permute-start | bytes 589832 | tf_op jit(solution)/shard_map/ppermute | solution.py:24
  140.0 10.7 %collective-permute-start.5 = (bf16[192,512]{1,0:T(8,128)(2,1)S(1)}, bf16[192,512]{1,0:T(8,128)(2,1)S(1)}, u32[]{:S(2)}, u32[]{:S(2)}) collective-permute-start(bf16[192,512]{1,0:T(8,128)(2,1)S(1)} %fusion.6), channel_id=1, source_target_pairs={{0,1},{1,2},{2,3},{3,0},{4,5},{5,6},{6,7},{7,4},{8,9},{9,10},{10,1... | collective-permute-start | bytes 589832 | tf_op jit(solution)/shard_map/ppermute | solution.py:24
  155.2 9.2 %all-to-all-start.7 = ((f32[8,2,512]{2,1,0:T(2,128)}), f32[8,2,512]{2,1,0:T(2,128)S(1)}, u32[]{:S(2)}, u32[]{:S(2)}) async-start(f32[8,2,512]{2,1,0:T(2,128)} %broadcast_in_dim.108), calls=%async_computation.7 | async-start | bytes 65536 | tf_op jit(solution)/shard_map/all_to_all | solution.py:19
  (7 other events, 9.0 us)

commit v3 on v2

v3 whole, which is shorter than its diff:
```python
import jax
import jax.numpy as jnp
from jax import lax
from jax.experimental import pallas as pl
from jax.experimental.pallas import tpu as pltpu
from jax.sharding import Mesh, PartitionSpec as P

LOGIT_SCALE = 64.0
MARGIN = 0.4
EPSILON = 1e-05
F32 = jnp.float32
BF16 = jnp.bfloat16
VMEM = 60 * 1024 * 1024
PAD = 16


def spread(block, axes):
    copies = jnp.broadcast_to(block[None], (lax.axis_size(axes),) + block.shape)
    return lax.all_to_all(copies, axes, 0, 0)


def shift(block, axis, by):
    n = lax.axis_size(axis)
    return lax.ppermute(block, axis, [(i, (i + by) % n) for i in range(n)])


def head(inputs, sums, gain, bias, batch_total):
    mean = sums[0:1] / batch_total
    inv_std = lax.rsqrt(sums[1:2] / batch_total - mean * mean + EPSILON)
    normed = (inputs.astype(F32) - mean) * inv_std
    shifted = normed * gain + bias
    scale = lax.rsqrt(jnp.sum(shifted * shifted, 1, keepdims=True) + EPSILON)
    return normed, shifted * scale, scale, inv_std


def call(kernel, grid, ins, outs, shapes, scratch, flops, size, exps=0):
    return pl.pallas_call(
        kernel,
        grid=(grid,),
        in_specs=ins,
        out_specs=outs,
        out_shape=shapes,
        scratch_shapes=scratch,
        compiler_params=pltpu.CompilerParams(vmem_limit_bytes=VMEM),
        cost_estimate=pl.CostEstimate(
            flops=flops, bytes_accessed=size, transcendentals=exps
        ),
    )


def whole(*shape):
    return pl.BlockSpec(shape, lambda i: (0,) * len(shape))


def rows_of(block, width):
    return pl.BlockSpec((block, width), lambda i: (i, 0))


def hits(place, block, count, first):
    return place == lax.broadcasted_iota(jnp.int32, (block, count), 0) + first


def exp_kernel(
    batch, rows, sums, gain, bias, place, w_own, w_other, unit, expo, stats, acc
):
    i = pl.program_id(0)
    half = pl.num_programs(0) // 2
    block, count = expo.shape

    @pl.when(i == 0)
    def _():
        total = jnp.sum(sums[...], 0)
        unit[...] = head(rows[...], total, gain[...], bias[...], batch)[1].astype(BF16)
        acc[...] = jnp.zeros_like(acc)

    w_hat = jnp.where(i < half, w_own[...], w_other[...])
    cosine = lax.dot_general(
        w_hat, unit[...], (((1,), (1,)), ((), ())), preferred_element_type=F32
    )
    target = hits(place[...], block, count, i * block)
    logits = LOGIT_SCALE * cosine - jnp.where(target, LOGIT_SCALE * MARGIN, 0.0)
    exps = jnp.exp(logits)
    expo[...] = exps
    acc[0:1] += jnp.sum(exps, 0, keepdims=True)
    acc[1:2] += jnp.sum(jnp.where(target, logits, 0.0), 0, keepdims=True)

    @pl.when(i == pl.num_programs(0) - 1)
    def _():
        for p in range(stats.shape[0]):
            stats[p] = acc[...]


def pull_kernel(
    batch,
    parts,
    rows,
    sums,
    gain,
    bias,
    place,
    totals,
    w_own,
    w_other,
    expo,
    packed,
    acc,
):
    i = pl.program_id(0)
    half = pl.num_programs(0) // 2
    block, count = expo.shape
    target = hits(place[...], block, count, i * block)
    grad = (expo[...] / totals[0:1] - target.astype(F32)).astype(BF16)
    w_hat = jnp.where(i < half, w_own[...], w_other[...])
    term = lax.dot_general(
        grad, w_hat, (((0,), (0,)), ((), ())), preferred_element_type=F32
    )

    @pl.when(i == 0)
    def _():
        acc[...] = term

    @pl.when(i > 0)
    def _():
        acc[...] += term

    @pl.when(i == pl.num_programs(0) - 1)
    def _():
        total = jnp.sum(sums[...], 0)
        normed, unit_f, scale, _ = head(rows[...], total, gain[...], bias[...], batch)
        pull = acc[...]
        radial = jnp.sum(unit_f * pull, 1, keepdims=True)
        shifts = (pull - unit_f * radial) * scale
        bias_part = jnp.sum(shifts, 0, keepdims=True)
        gain_part = jnp.sum(shifts * normed, 0, keepdims=True)
        tail = pack_ends(bias_part, gain_part).astype(BF16)
        n = pull.shape[0] // parts
        for p in range(parts):
            packed[p, :n] = pull[p * n : (p + 1) * n].astype(BF16)
            packed[p, n:] = tail


def pack_ends(bias_part, gain_part):
    pieces = []
    for value in (bias_part, gain_part):
        for _ in range(3):
            piece = value.astype(BF16).astype(F32)
            value = value - piece
            pieces.append(piece)
    fill = jnp.zeros((PAD - 6, bias_part.shape[1]), F32)
    return jnp.concatenate(pieces + [fill], 0)


def unpack_ends(tail):
    return jnp.concatenate(
        [jnp.sum(tail[0:3], 0, keepdims=True), jnp.sum(tail[3:6], 0, keepdims=True)], 0
    )


def mid_kernel(lines, rows_dev, arrived, packed):
    total = jnp.sum(arrived[...].astype(F32), 0)
    ends = unpack_ends(total[lines * rows_dev :])
    tail = pack_ends(ends[0:1], ends[1:2])[: PAD - rows_dev]
    for p in range(lines):
        piece = total[p * rows_dev : (p + 1) * rows_dev]
        packed[p] = jnp.concatenate([piece, tail], 0).astype(BF16)


def raw_kernel(
    at, place, place_2, totals, unit, unit_2, w_own, after, mine, *sent
):
    i = pl.program_id(0)
    parts = pl.num_programs(0)
    block = w_own.shape[0]
    first = lax.rem(at[0] + i, parts) * block
    raw = None
    for units, places, row in ((unit, place, 0), (unit_2, place_2, 2)):
        cosine = lax.dot_general(
            w_own[...], units[...], (((1,), (1,)), ((), ())), preferred_element_type=F32
        )
        target = hits(places[...], block, units.shape[0], first)
        logits = LOGIT_SCALE * cosine - jnp.where(target, LOGIT_SCALE * MARGIN, 0.0)
        share = jnp.exp(logits) / totals[row : row + 1]
        grad = (share - target.astype(F32)).astype(BF16)
        term = jnp.dot(grad, units[...], preferred_element_type=F32)
        raw = term if raw is None else raw + term

    @pl.when(i == 0)
    def _():
        mine[...] = raw

    for by, out in enumerate(sent):

        @pl.when(i == by + 1)
        def _(out=out):
            out[...] = raw.astype(BF16)


def project_kernel(at, picked, mine, *rest):
    arrived, out = rest[:-1], rest[-1]
    raw = mine[...]
    for piece in arrived:
        raw = raw + piece[...].astype(F32)
    picks = picked[...].astype(F32)
    inv_norm = lax.rsqrt(jnp.sum(picks * picks, 1, keepdims=True) + EPSILON)
    w_unit = picks * inv_norm
    along = jnp.sum(w_unit * raw, 1, keepdims=True)
    out[...] = ((raw - w_unit * along) * inv_norm).astype(BF16)


def order_kernel(at, *refs):
    found, out = refs[:-1], refs[-1]
    parts = len(found)
    source = lax.rem(at[0] - pl.program_id(0) + parts, parts)
    for by, piece in enumerate(found):

        @pl.when(source == by)
        def _(piece=piece):
            out[...] = piece[...]


def fixed(*shape):
    return pl.BlockSpec(shape, lambda i, at: (0,) * len(shape))


def call_at(kernel, grid, ins, outs, shapes, flops, size, exps=0):
    return pl.pallas_call(
        kernel,
        grid_spec=pltpu.PrefetchScalarGridSpec(
            num_scalar_prefetch=1, grid=(grid,), in_specs=ins, out_specs=outs
        ),
        out_shape=shapes,
        compiler_params=pltpu.CompilerParams(vmem_limit_bytes=VMEM),
        cost_estimate=pl.CostEstimate(
            flops=flops, bytes_accessed=size, transcendentals=exps
        ),
    )


def body(embeddings, bn_gain, bn_bias, centres, sample_rows, label_shard, label_slot):
    nx, nz, nc, nr = (lax.axis_size(a) for a in ("x", "z", "core", "rep"))
    ix, iz, ic, ir = (lax.axis_index(a) for a in ("x", "z", "core", "rep"))
    rows_dev, width = embeddings.shape
    slots = sample_rows.shape[1]
    batch = rows_dev * nx * nz * nc * nr
    line_rows = nz * rows_dev
    group = nx * line_rows
    held = nc * slots
    quarter = slots // nr
    at = ir.astype(jnp.int32).reshape(1)
    gain, bias = bn_gain[None], bn_bias[None]

    line = spread(embeddings, "z").reshape(line_rows, width)
    rows = spread(line, "x").reshape(group, width)
    rows_f = rows.astype(F32)
    sums = spread(
        jnp.stack([jnp.sum(rows_f, 0), jnp.sum(rows_f * rows_f, 0)]), ("core", "rep")
    )
    peers = nc * nr

    picked = jnp.take(centres, sample_rows[0], axis=0)
    picks = picked.astype(F32)
    inv_norm = lax.rsqrt(jnp.sum(picks * picks, 1, keepdims=True) + EPSILON)
    w_own = (picks * inv_norm).astype(BF16)
    w_other = shift(w_own, "core", 1)

    def of_core(labels, core):
        lines = labels.reshape(nx * nz, nc, rows_dev)
        return lax.dynamic_index_in_dim(lines, core, 1).reshape(1, group)

    owner, slot = of_core(label_shard, ic), of_core(label_slot, ic)
    chip = (ix * nz + iz) * nc
    place = jnp.where(
        owner == chip + ic, slot, jnp.where(owner == chip + 1 - ic, slot + slots, -1)
    )
    place_2 = jnp.where(
        of_core(label_shard, 1 - ic) == chip + ic, of_core(label_slot, 1 - ic), -1
    )

    block = slots // 2
    near = pl.BlockSpec((block, width), lambda i: (jnp.minimum(i, 1), 0))
    far = pl.BlockSpec((block, width), lambda i: (jnp.maximum(i - 2, 0), 0))
    unit, expo, stats = call(
        lambda *refs: exp_kernel(batch, *refs),
        4,
        [
            whole(group, width),
            whole(peers, 2, width),
            whole(1, width),
            whole(1, width),
            whole(1, group),
            near,
            far,
        ],
        [whole(group, width), rows_of(block, group), whole(nx * nc, 2, group)],
        [
            jax.ShapeDtypeStruct((group, width), BF16),
            jax.ShapeDtypeStruct((held, group), F32),
            jax.ShapeDtypeStruct((nx * nc, 2, group), F32),
        ],
        [pltpu.VMEM((2, group), F32)],
        2 * held * group * width,
        4 * held * group + 2 * held * width,
        held * group,
    )(rows, sums, gain, bias, place, w_own, w_other)
    unit_2 = shift(unit, "core", 1)

    stats = lax.all_to_all(stats, ("x", "core"), 0, 0).reshape(nx, nc, 2, group)
    stats = jnp.sum(stats, 0)
    stats = jnp.where(ic == 0, stats, stats[::-1]).reshape(2 * nc, group)
    stats = jnp.sum(spread(stats, "z"), 0)

    pull = call(
        lambda *refs: pull_kernel(batch, nx, *refs),
        4,
        [
            whole(group, width),
            whole(peers, 2, width),
            whole(1, width),
            whole(1, width),
            whole(1, group),
            whole(2 * nc, group),
            near,
            far,
            rows_of(block, group),
        ],
        whole(nx, line_rows + PAD, width),
        jax.ShapeDtypeStruct((nx, line_rows + PAD, width), BF16),
        [pltpu.VMEM((group, width), F32)],
        2 * held * group * width,
        4 * held * group + 2 * held * width,
    )(rows, sums, gain, bias, place, stats, w_own, w_other, expo)

    piece = jax.ShapeDtypeStruct((quarter, width), BF16)
    mine, *sent = call_at(
        raw_kernel,
        nr,
        [
            fixed(1, group),
            fixed(1, group),
            fixed(2 * nc, group),
            fixed(group, width),
            fixed(group, width),
            pl.BlockSpec((quarter, width), lambda i, at: (lax.rem(at[0] + i, nr), 0)),
            pl.BlockSpec(memory_space=pl.ANY),
        ],
        [fixed(quarter, width)] * nr,
        [jax.ShapeDtypeStruct((quarter, width), F32)] + [piece] * (nr - 1),
        4 * held * group * width,
        2 * held * width,
        held * group,
    )(at, place, place_2, stats, unit, unit_2, w_own, pull)
    came = [shift(sent[by - 1], "rep", by) for by in range(1, nr)]
    grad = call_at(
        project_kernel,
        1,
        [pl.BlockSpec((quarter, width), lambda i, at: (at[0], 0))]
        + [fixed(quarter, width)] * nr,
        fixed(quarter, width),
        piece,
        20 * quarter * width,
        14 * quarter * width,
    )(at, picked, mine, *came)
    found = [grad] + [shift(grad, "rep", by) for by in range(1, nr)]
    centre_grad = call_at(
        order_kernel,
        nr,
        [fixed(quarter, width)] * nr,
        pl.BlockSpec((quarter, width), lambda i, at: (i, 0)),
        jax.ShapeDtypeStruct((slots, width), BF16),
        slots * width,
        4 * slots * width,
    )(at, *found)

    pull = lax.all_to_all(pull, "x", 0, 0)
    pull = call(
        lambda *refs: mid_kernel(nz, rows_dev, *refs),
        1,
        [whole(nx, line_rows + PAD, width)],
        whole(nz, PAD, width),
        jax.ShapeDtypeStruct((nz, PAD, width), BF16),
        [],
        nx * line_rows * width,
        2 * nx * line_rows * width,
    )(pull)
    pull = jnp.sum(lax.all_to_all(pull, "z", 0, 0).astype(F32), 0)
    grad_unit = pull[:rows_dev]
    ends = jnp.sum(spread(unpack_ends(pull[rows_dev:]), ("core", "rep")), 0)

    own_stats = lax.dynamic_slice_in_dim(
        stats, (ix * nz + iz) * rows_dev, rows_dev, 1
    )
    row_loss = jnp.log(own_stats[0]) - own_stats[1]
    normed, unit_f, row_scale, inv_std = head(
        embeddings, jnp.sum(sums, 0), gain, bias, batch
    )
    radial = jnp.sum(unit_f * grad_unit, 1, keepdims=True)
    grad_shift = (grad_unit - unit_f * radial) * row_scale
    bias_grad, gain_grad = ends[0], ends[1]
    emb_grad = inv_std * (
        grad_shift * bn_gain
        - bn_gain * bias_grad / batch
        - normed * (bn_gain * gain_grad / batch)
    )
    return (row_loss, emb_grad, centre_grad, gain_grad, bias_grad)


def solution(mesh):
    shards, replicas = mesh.devices.shape
    split = (4, shards // 8, 2, replicas)
    fine = Mesh(mesh.devices.reshape(split), ("x", "z", "core", "rep"))
    cen = ("x", "z", "core")
    every = cen + ("rep",)
    return jax.shard_map(
        body,
        mesh=fine,
        in_specs=(
            P(every, None),
            P(),
            P(),
            P(cen, None),
            P(cen, None),
            P(None, "rep", None),
            P(None, "rep", None),
        ),
        out_specs=(P(every), P(every, None), P(cen, None), P(), P()),
        check_vma=False,
    )
```

time: 166 us -> 174 us (1.048)
  blocking collectives: 0 us -> 16.1 us
  Pallas kernels: 8.73 us -> 24.6 us
  waiting for transfers between devices: 44.7 us -> 33.1 us
  local copies, waits for them, and re-layouts: 20.3 us -> 11.7 us
  other arithmetic: 15.7 us -> 7.66 us
  starting transfers between devices: 74.7 us -> 78.1 us
    all_to_all x6 -> x4, waiting for transfers between devices: 32.2 us -> 14.7 us  [spread(): return lax.all_to_all(copies, axes, 0, 0)]
    all_to_all x0 -> x1, blocking collectives: none -> 16.1 us  [spread(): return lax.all_to_all(copies, axes, 0, 0)]
    pallas_call x3 -> x5, Pallas kernels: 7.94 us -> 22.8 us  [the longest x1 6.21 us: body(): call(lambda *refs: pull_kernel(batch, nx, *refs), 4, [whole(group, width)...]
    all_to_all x6 -> x4, starting transfers between devices: 44 us -> 33.3 us  [spread(): return lax.all_to_all(copies, axes, 0, 0)]
    unnamed x32 -> x42, local copies, waits for them, and re-layouts: 9.66 us -> 3.04 us
    ppermute x8, starting transfers between devices: 23.7 us -> 30.3 us  [shift(): return lax.ppermute(block, axis, [(i, (i + by) % n) for i in range(n)])]
    all_to_all x0 -> x1, waiting for transfers between devices: none -> 4.74 us  [body(): stats = lax.all_to_all(stats, ('x', 'core'), 0, 0).reshape(nx, nc, 2, group)]
    convert_element_type x3 -> x1, other arithmetic: 5.54 us -> 1.11 us  [body(): w_own = (picks * inv_norm).astype(BF16)]
  transfers between devices with their start and end apart: 16 -> 15, of which waited for: 10 -> 9; matrix products, arithmetic and copies ran while one was open for 14% -> 7% of each run, Pallas kernels for 2% -> 7%
where the time goes in v3:
time: 174 us; the launch traced here: 172 us
  starting transfers between devices  78.1 us (45%)
  waiting for transfers between devices  33.1 us (19%)
  Pallas kernels  24.6 us (14%)
  blocking collectives  16.1 us (9%)
  local copies, waits for them, and re-layouts  11.7 us (7%)
  other arithmetic  7.66 us (4%)
    all_to_all x4, starting transfers between devices, spread(): return lax.all_to_all(copies, axes, 0, 0)  33.3 us
    ppermute x8, starting transfers between devices, shift(): return lax.ppermute(block, axis, [(i, (i + by) % n) for i in range(n)])  30.3 us
    all_to_all x1, blocking collectives, spread(): return lax.all_to_all(copies, axes, 0, 0)  16.1 us
    all_to_all x4, waiting for transfers between devices, spread(): return lax.all_to_all(copies, axes, 0, 0)  14.7 us
    ppermute x8, waiting for transfers between devices, shift(): return lax.ppermute(block, axis, [(i, (i + by) % n) for i in range(n)])  12.8 us
    all_to_all x1, starting transfers between devices, body(): pull = jnp.sum(lax.all_to_all(pull, 'z', 0, 0).astype(F32), 0)  7.24 us
    pallas_call x1, Pallas kernels, body(): call(lambda *refs: pull_kernel(batch, nx, *refs), 4, [whole(group, width)...  6.21 us
    pallas_call x1, Pallas kernels, body(): call_at(raw_kernel, nr, [fixed(1, group), fixed(1, group), fixed(2 * nc,...  5.95 us
  transfers between devices with their start and end apart: 15, of which 9 were waited for; matrix products, arithmetic and copies ran while one was open for 7% of the time, Pallas kernels for 7%

profile of v3, /device:TPU:1, one launch (start us, length us, event | category | flops | bytes accessed | tf_op | source)
XLA Modules:
  0.0 172.3 jit_solution(1971878642486385492)
XLA Ops:
  2.1 15.7 %all-to-all-start = ((bf16[16,8,512]{2,1,0:T(8,128)(2,1)}), bf16[16,8,512]{2,1,0:T(8,128)(2,1)S(1)}, u32[]{:S(2)}, u32[]{:S(2)}) async-start(bf16[16,8,512]{2,1,0:T(8,128)(2,1)} %broadcast_in_dim.67), calls=%async_computation | async-start | bytes 262144 | tf_op jit(solution)/shard_map/all_to_all | solution.py:19
  19.3 3.3 %gather_fusion = bf16[768,512]{1,0:T(8,128)(2,1)} fusion(bf16[2048,512]{1,0:T(8,128)(2,1)S(1)} %copy-done, s32[1024]{0:T(1024)S(1)} %pad_clamp_fusion), kind=kCustom, calls=%fused_computation | custom fusion | bytes 1575936 | tf_op jit(solution)/shard_map/jit(_take)/gather | solution.py:260
  24.3 5.6 %all-to-all-done = bf16[16,8,512]{2,1,0:T(8,128)(2,1)S(1)} async-done(((bf16[16,8,512]{2,1,0:T(8,128)(2,1)}), bf16[16,8,512]{2,1,0:T(8,128)(2,1)S(1)}, u32[]{:S(2)}, u32[]{:S(2)}) %all-to-all-start) | async-done | bytes 131104 | tf_op jit(solution)/shard_map/all_to_all | solution.py:19
  30.7 4.0 %all-to-all-start.1 = ((bf16[4,128,512]{2,1,0:T(8,128)(2,1)}), bf16[4,128,512]{2,1,0:T(8,128)(2,1)S(1)}, u32[]{:S(2)}, u32[]{:S(2)}) async-start(bf16[4,128,512]{2,1,0:T(8,128)(2,1)} %broadcast_in_dim.69), calls=%async_computation.1 | async-start | bytes 1048576 | tf_op jit(solution)/shard_map/all_to_all | solution.py:19
  35.8 5.8 %collective-permute-start = (bf16[768,512]{1,0:T(8,128)(2,1)}, bf16[768,512]{1,0:T(8,128)(2,1)}, u32[]{:S(2)}, u32[]{:S(2)}) collective-permute-start(bf16[768,512]{1,0:T(8,128)(2,1)} %fusion.1.refs_5_.refs_6_.w_own), channel_id=1, source_target_pairs={{0,4},{4,0},{1,5},{5,1},{2,6},{6,2},{3,7},{7,3},{8,12},{12,8},{9,1... | collective-permute-start | bytes 2359304 | tf_op jit(solution)/shard_map/ppermute | solution.py:24
  43.5 8.5 %all-to-all-start.2 = ((f32[8,2,512]{2,1,0:T(2,128)}), f32[8,2,512]{2,1,0:T(2,128)S(1)}, u32[]{:S(2)}, u32[]{:S(2)}) async-start(f32[8,2,512]{2,1,0:T(2,128)} %broadcast_in_dim.70), calls=%async_computation.2 | async-start | bytes 65536 | tf_op jit(solution)/shard_map/all_to_all | solution.py:19
  52.6 4.3 %all-to-all-done.2.refs_1_ = f32[8,2,512]{2,1,0:T(2,128)S(1)} async-done(((f32[8,2,512]{2,1,0:T(2,128)}), f32[8,2,512]{2,1,0:T(2,128)S(1)}, u32[]{:S(2)}, u32[]{:S(2)}) %all-to-all-start.2) | async-done | bytes 32800 | tf_op jit(solution)/shard_map/all_to_all | solution.py:19
  57.5 5.7 %shard_map.110 = (bf16[512,512]{1,0:T(8,128)(2,1)}, f32[1536,512]{1,0:T(8,128)}, f32[8,2,512]{2,1,0:T(2,128)}) custom-call(bf16[512,512]{1,0:T(8,128)(2,1)} %bitcast.20, f32[8,2,512]{2,1,0:T(2,128)} %copy-done.4, f32[1,512]{1,0:T(1,128)} %bitcast.27, f32[1,512]{1,0:T(1,128)} %bitcast.29, s32[1,512]{1,0:T(1,128)} %select_select_fusion.refs_4_.place, ...), custom_call_target="tpu_custom_call" | custom-call | flops 805306368 | bytes 4718592 | tf_op jit(solution)/shard_map/pallas_call | solution.py:282
  63.3 3.6 %all-to-all-start.3 = ((f32[8,2,512]{2,1,0:T(2,128)}), f32[8,2,512]{2,1,0:T(2,128)S(1)}, u32[]{:S(2)}, u32[]{:S(2)}) async-start(f32[8,2,512]{2,1,0:T(2,128)} %get-tuple-element.12), calls=%async_computation.3 | async-start | bytes 65536 | tf_op jit(solution)/shard_map/all_to_all | solution.py:307
  66.9 4.7 %all-to-all-done.3 = f32[8,2,512]{2,1,0:T(2,128)S(1)} async-done(((f32[8,2,512]{2,1,0:T(2,128)}), f32[8,2,512]{2,1,0:T(2,128)S(1)}, u32[]{:S(2)}, u32[]{:S(2)}) %all-to-all-start.3) | async-done | bytes 32800 | tf_op jit(solution)/shard_map/all_to_all | solution.py:307
  71.7 16.1 %all_to_all.40 = f32[16,4,512]{2,1,0:T(4,128)S(1)} all-to-all(f32[16,4,512]{2,1,0:T(4,128)S(1)} %broadcast_in_dim.77), channel_id=1, replica_groups=mesh['x'=4,'z'=16,'core'=2,'rep'=4] {'z'}, dimensions={0} | all-to-all | bytes 262144 | tf_op jit(solution)/shard_map/all_to_all | solution.py:19
  88.5 6.2 %shard_map.111.after = bf16[4,144,512]{2,1,0:T(8,128)(2,1)} custom-call(bf16[512,512]{1,0:T(8,128)(2,1)} %bitcast.21, f32[8,2,512]{2,1,0:T(2,128)} %copy-done.4, f32[1,512]{1,0:T(1,128)} %bitcast.28, f32[1,512]{1,0:T(1,128)} %bitcast.30, s32[1,512]{1,0:T(1,128)} %select_select_fusion.refs_4_.place, f32[4,512]{1,0:T(4,128)} %reduce_sum.112.refs_5_.totals, ...), custom_call_target="tpu_custom_call" | custom-call | flops 805306368 | bytes 4718592 | tf_op jit(solution)/shard_map/pallas_call | solution.py:312
  94.8 3.6 %all-to-all-start.5 = ((bf16[4,144,512]{2,1,0:T(8,128)(2,1)}), bf16[4,144,512]{2,1,0:T(8,128)(2,1)S(1)}, u32[]{:S(2)}, u32[]{:S(2)}) async-start(bf16[4,144,512]{2,1,0:T(8,128)(2,1)} %shard_map.111.after), calls=%async_computation.5 | async-start | bytes 1179648 | tf_op jit(solution)/shard_map/all_to_all | solution.py:374
  98.4 5.7 %collective-permute-start.1 = (bf16[512,512]{1,0:T(8,128)(2,1)S(1)}, bf16[512,512]{1,0:T(8,128)(2,1)}, u32[]{:S(2)}, u32[]{:S(2)}) collective-permute-start(bf16[512,512]{1,0:T(8,128)(2,1)S(1)} %copy-done.19), channel_id=1, source_target_pairs={{0,4},{4,0},{1,5},{5,1},{2,6},{6,2},{3,7},{7,3},{8,12},{12,8},{9,1... | collective-permute-start | bytes 1572872 | tf_op jit(solution)/shard_map/ppermute | solution.py:24
  108.3 7.2 %all-to-all-start.6 = ((bf16[16,16,512]{2,1,0:T(8,128)(2,1)}), bf16[16,16,512]{2,1,0:T(8,128)(2,1)S(1)}, u32[]{:S(2)}, u32[]{:S(2)}) async-start(bf16[16,16,512]{2,1,0:T(8,128)(2,1)} %shard_map.112), calls=%async_computation.6 | async-start | bytes 524288 | tf_op jit(solution)/shard_map/all_to_all | solution.py:385
  115.7 6.0 %shard_map.113 = (f32[192,512]{1,0:T(8,128)}, bf16[192,512]{1,0:T(8,128)(2,1)}, bf16[192,512]{1,0:T(8,128)(2,1)}, bf16[192,512]{1,0:T(8,128)(2,1)}) custom-call(s32[1]{0:T(128)} %bitcast.17.at, s32[1,512]{1,0:T(1,128)} %select_select_fusion.refs_4_.place, s32[1,512]{1,0:T(1,128)} %select_n.72.place_2, f32[4,512]{1,0:T(4,128)} %reduce_sum.112.refs_5_.totals, ...), custom_call_target="tpu_custom_call" | custom-call | flops 1610612736 | bytes 1572864 | tf_op jit(solution)/shard_map/pallas_call | solution.py:334
  124.0 3.7 %collective-permute-start.3 = (bf16[192,512]{1,0:T(8,128)(2,1)}, bf16[192,512]{1,0:T(8,128)(2,1)S(1)}, u32[]{:S(2)}, u32[]{:S(2)}) collective-permute-start(bf16[192,512]{1,0:T(8,128)(2,1)} %get-tuple-element.17), channel_id=1, source_target_pairs={{0,2},{1,3},{2,0},{3,1},{4,6},{5,7},{6,4},{7,5},{8,10},{9,11},{10,... | collective-permute-start | bytes 589832 | tf_op jit(solution)/shard_map/ppermute | solution.py:24
  131.2 3.1 %collective-permute-done.3.rest_1_ = bf16[192,512]{1,0:T(8,128)(2,1)S(1)} collective-permute-done((bf16[192,512]{1,0:T(8,128)(2,1)}, bf16[192,512]{1,0:T(8,128)(2,1)S(1)}, u32[]{:S(2)}, u32[]{:S(2)}) %collective-permute-start.3) | collective-permute-done | bytes 196640 | tf_op jit(solution)/shard_map/ppermute | solution.py:24
  138.3 3.8 %collective-permute-start.7 = (bf16[192,512]{1,0:T(8,128)(2,1)}, bf16[192,512]{1,0:T(8,128)(2,1)S(1)}, u32[]{:S(2)}, u32[]{:S(2)}) collective-permute-start(bf16[192,512]{1,0:T(8,128)(2,1)} %shard_map.114.refs_0_), channel_id=1, source_target_pairs={{0,3},{1,0},{2,1},{3,2},{4,7},{5,4},{6,5},{7,6},{8,11},{9,8},{10,9... | collective-permute-start | bytes 589832 | tf_op jit(solution)/shard_map/ppermute | solution.py:24
  142.2 4.4 %collective-permute-start.6 = (bf16[192,512]{1,0:T(8,128)(2,1)}, bf16[192,512]{1,0:T(8,128)(2,1)S(1)}, u32[]{:S(2)}, u32[]{:S(2)}) collective-permute-start(bf16[192,512]{1,0:T(8,128)(2,1)} %shard_map.114.refs_0_), channel_id=1, source_target_pairs={{0,2},{1,3},{2,0},{3,1},{4,6},{5,7},{6,4},{7,5},{8,10},{9,11},{10,... | collective-permute-start | bytes 589832 | tf_op jit(solution)/shard_map/ppermute | solution.py:24
  150.3 7.2 %collective-permute-done.5.refs_1_ = bf16[192,512]{1,0:T(8,128)(2,1)S(1)} collective-permute-done((bf16[192,512]{1,0:T(8,128)(2,1)}, bf16[192,512]{1,0:T(8,128)(2,1)S(1)}, u32[]{:S(2)}, u32[]{:S(2)}) %collective-permute-start.5) | collective-permute-done | bytes 196640 | tf_op jit(solution)/shard_map/ppermute | solution.py:24
  158.2 2.7 %shard_map.115 = bf16[768,512]{1,0:T(8,128)(2,1)} custom-call(s32[1]{0:T(128)} %bitcast.17.at, bf16[192,512]{1,0:T(8,128)(2,1)} %shard_map.114.refs_0_, bf16[192,512]{1,0:T(8,128)(2,1)} %copy-done.11, bf16[192,512]{1,0:T(8,128)(2,1)} %copy-done.10, bf16[192,512]{1,0:T(8,128)(2,1)} %copy-done.9), custom_call_target="tpu_custom_call" | custom-call | flops 393216 | bytes 1572864 | tf_op jit(solution)/shard_map/pallas_call | solution.py:364
  161.6 5.0 %all-to-all-start.7 = ((f32[8,2,512]{2,1,0:T(2,128)}), f32[8,2,512]{2,1,0:T(2,128)S(1)}, u32[]{:S(2)}, u32[]{:S(2)}) async-start(f32[8,2,512]{2,1,0:T(2,128)} %broadcast_in_dim.80), calls=%async_computation.7 | async-start | bytes 65536 | tf_op jit(solution)/shard_map/all_to_all | solution.py:19
  166.8 4.7 %all-to-all-done.7 = f32[8,2,512]{2,1,0:T(2,128)S(1)} async-done(((f32[8,2,512]{2,1,0:T(2,128)}), f32[8,2,512]{2,1,0:T(2,128)S(1)}, u32[]{:S(2)}, u32[]{:S(2)}) %all-to-all-start.7) | async-done | bytes 32800 | tf_op jit(solution)/shard_map/all_to_all | solution.py:19
  (95 shorter events, 30.3 us)
Async XLA Ops:
  0.6 18.7 %copy-start = (bf16[2048,512]{1,0:T(8,128)(2,1)S(1)}, bf16[2048,512]{1,0:T(8,128)(2,1)}, u32[]{:S(2)}) copy-start(bf16[2048,512]{1,0:T(8,128)(2,1)} %param.10) | copy-start | bytes 6291460
  2.1 27.8 %all-to-all-start = ((bf16[16,8,512]{2,1,0:T(8,128)(2,1)}), bf16[16,8,512]{2,1,0:T(8,128)(2,1)S(1)}, u32[]{:S(2)}, u32[]{:S(2)}) async-start(bf16[16,8,512]{2,1,0:T(8,128)(2,1)} %broadcast_in_dim.67), calls=%async_computation | async-start | bytes 262144 | tf_op jit(solution)/shard_map/all_to_all | solution.py:19
  24.3 11.6 %copy-start.1 = (bf16[768,512]{1,0:T(8,128)(2,1)}, bf16[768,512]{1,0:T(8,128)(2,1)S(1)}, u32[]{:S(2)}) copy-start(bf16[768,512]{1,0:T(8,128)(2,1)S(1)} %get-tuple-element.28.picked) | copy-start | bytes 2359300
  29.9 11.8 %copy-start.17 = (s32[128,1,8]{0,2,1:T(8,128)S(1)}, s32[128,1,8]{0,2,1:T(8,128)}, u32[]{:S(2)}) copy-start(s32[128,1,8]{0,2,1:T(8,128)} %param.12) | copy-start | bytes 12292
  29.9 12.3 %copy-start.18 = (s32[128,1,8]{0,2,1:T(8,128)S(1)}, s32[128,1,8]{0,2,1:T(8,128)}, u32[]{:S(2)}) copy-start(s32[128,1,8]{0,2,1:T(8,128)} %param.13) | copy-start | bytes 12292
  30.7 12.0 %all-to-all-start.1 = ((bf16[4,128,512]{2,1,0:T(8,128)(2,1)}), bf16[4,128,512]{2,1,0:T(8,128)(2,1)S(1)}, u32[]{:S(2)}, u32[]{:S(2)}) async-start(bf16[4,128,512]{2,1,0:T(8,128)(2,1)} %broadcast_in_dim.69), calls=%async_computation.1 | async-start | bytes 1048576 | tf_op jit(solution)/shard_map/all_to_all | solution.py:19
  35.8 16.8 %collective-permute-start = (bf16[768,512]{1,0:T(8,128)(2,1)}, bf16[768,512]{1,0:T(8,128)(2,1)}, u32[]{:S(2)}, u32[]{:S(2)}) collective-permute-start(bf16[768,512]{1,0:T(8,128)(2,1)} %fusion.1.refs_5_.refs_6_.w_own), channel_id=1, source_target_pairs={{0,4},{4,0},{1,5},{5,1},{2,6},{6,2},{3,7},{7,3},{8,12},{12,8},{9,1... | collective-permute-start | bytes 2359304 | tf_op jit(solution)/shard_map/ppermute | solution.py:24
  42.7 14.3 %copy-start.2 = (bf16[4,128,512]{2,1,0:T(8,128)(2,1)}, bf16[4,128,512]{2,1,0:T(8,128)(2,1)S(1)}, u32[]{:S(2)}) copy-start(bf16[4,128,512]{2,1,0:T(8,128)(2,1)S(1)} %all-to-all-done.1) | copy-start | bytes 1572868
  43.5 13.5 %all-to-all-start.2 = ((f32[8,2,512]{2,1,0:T(2,128)}), f32[8,2,512]{2,1,0:T(2,128)S(1)}, u32[]{:S(2)}, u32[]{:S(2)}) async-start(f32[8,2,512]{2,1,0:T(2,128)} %broadcast_in_dim.70), calls=%async_computation.2 | async-start | bytes 65536 | tf_op jit(solution)/shard_map/all_to_all | solution.py:19
  63.3 8.4 %all-to-all-start.3 = ((f32[8,2,512]{2,1,0:T(2,128)}), f32[8,2,512]{2,1,0:T(2,128)S(1)}, u32[]{:S(2)}, u32[]{:S(2)}) async-start(f32[8,2,512]{2,1,0:T(2,128)} %get-tuple-element.12), calls=%async_computation.3 | async-start | bytes 65536 | tf_op jit(solution)/shard_map/all_to_all | solution.py:307
  88.5 16.2 %copy-start.5 = (f32[8,2,512]{2,1,0:T(2,128)S(1)}, f32[8,2,512]{2,1,0:T(2,128)}, u32[]{:S(2)}) copy-start(f32[8,2,512]{2,1,0:T(2,128)} %copy-done.4) | copy-start | bytes 98308
  94.7 20.8 %copy-start.12 = (bf16[8,512]{1,0:T(8,128)(2,1)S(1)}, bf16[8,512]{1,0:T(8,128)(2,1)}, u32[]{:S(2)}) copy-start(bf16[8,512]{1,0:T(8,128)(2,1)} %param.7) | copy-start | bytes 24580
  94.7 20.9 %copy-start.13 = (f32[512]{0:T(512)S(1)}, f32[512]{0:T(512)}, u32[]{:S(2)}) copy-start(f32[512]{0:T(512)} %param.8) | copy-start | bytes 6148
  94.7 20.9 %copy-start.14 = (f32[512]{0:T(512)S(1)}, f32[512]{0:T(512)}, u32[]{:S(2)}) copy-start(f32[512]{0:T(512)} %param.9) | copy-start | bytes 6148
  94.8 10.9 %all-to-all-start.5 = ((bf16[4,144,512]{2,1,0:T(8,128)(2,1)}), bf16[4,144,512]{2,1,0:T(8,128)(2,1)S(1)}, u32[]{:S(2)}, u32[]{:S(2)}) async-start(bf16[4,144,512]{2,1,0:T(8,128)(2,1)} %shard_map.111.after), calls=%async_computation.5 | async-start | bytes 1179648 | tf_op jit(solution)/shard_map/all_to_all | solution.py:374
  98.4 17.3 %collective-permute-start.1 = (bf16[512,512]{1,0:T(8,128)(2,1)S(1)}, bf16[512,512]{1,0:T(8,128)(2,1)}, u32[]{:S(2)}, u32[]{:S(2)}) collective-permute-start(bf16[512,512]{1,0:T(8,128)(2,1)S(1)} %copy-done.19), channel_id=1, source_target_pairs={{0,4},{4,0},{1,5},{5,1},{2,6},{6,2},{3,7},{7,3},{8,12},{12,8},{9,1... | collective-permute-start | bytes 1572872 | tf_op jit(solution)/shard_map/ppermute | solution.py:24
  108.3 52.6 %all-to-all-start.6 = ((bf16[16,16,512]{2,1,0:T(8,128)(2,1)}), bf16[16,16,512]{2,1,0:T(8,128)(2,1)S(1)}, u32[]{:S(2)}, u32[]{:S(2)}) async-start(bf16[16,16,512]{2,1,0:T(8,128)(2,1)} %shard_map.112), calls=%async_computation.6 | async-start | bytes 524288 | tf_op jit(solution)/shard_map/all_to_all | solution.py:385
  121.7 9.5 %collective-permute-start.2 = (bf16[192,512]{1,0:T(8,128)(2,1)}, bf16[192,512]{1,0:T(8,128)(2,1)S(1)}, u32[]{:S(2)}, u32[]{:S(2)}) collective-permute-start(bf16[192,512]{1,0:T(8,128)(2,1)} %get-tuple-element.16), channel_id=1, source_target_pairs={{0,1},{1,2},{2,3},{3,0},{4,5},{5,6},{6,7},{7,4},{8,9},{9,10},{10,1... | collective-permute-start | bytes 589832 | tf_op jit(solution)/shard_map/ppermute | solution.py:24
  124.0 10.3 %collective-permute-start.3 = (bf16[192,512]{1,0:T(8,128)(2,1)}, bf16[192,512]{1,0:T(8,128)(2,1)S(1)}, u32[]{:S(2)}, u32[]{:S(2)}) collective-permute-start(bf16[192,512]{1,0:T(8,128)(2,1)} %get-tuple-element.17), channel_id=1, source_target_pairs={{0,2},{1,3},{2,0},{3,1},{4,6},{5,7},{6,4},{7,5},{8,10},{9,11},{10,... | collective-permute-start | bytes 589832 | tf_op jit(solution)/shard_map/ppermute | solution.py:24
  127.7 7.8 %collective-permute-start.4 = (bf16[192,512]{1,0:T(8,128)(2,1)}, bf16[192,512]{1,0:T(8,128)(2,1)S(1)}, u32[]{:S(2)}, u32[]{:S(2)}) collective-permute-start(bf16[192,512]{1,0:T(8,128)(2,1)} %get-tuple-element.18), channel_id=1, source_target_pairs={{0,3},{1,0},{2,1},{3,2},{4,7},{5,4},{6,5},{7,6},{8,11},{9,8},{10,9... | collective-permute-start | bytes 589832 | tf_op jit(solution)/shard_map/ppermute | solution.py:24
  138.3 10.7 %collective-permute-start.7 = (bf16[192,512]{1,0:T(8,128)(2,1)}, bf16[192,512]{1,0:T(8,128)(2,1)S(1)}, u32[]{:S(2)}, u32[]{:S(2)}) collective-permute-start(bf16[192,512]{1,0:T(8,128)(2,1)} %shard_map.114.refs_0_), channel_id=1, source_target_pairs={{0,3},{1,0},{2,1},{3,2},{4,7},{5,4},{6,5},{7,6},{8,11},{9,8},{10,9... | collective-permute-start | bytes 589832 | tf_op jit(solution)/shard_map/ppermute | solution.py:24
  142.2 8.1 %collective-permute-start.6 = (bf16[192,512]{1,0:T(8,128)(2,1)}, bf16[192,512]{1,0:T(8,128)(2,1)S(1)}, u32[]{:S(2)}, u32[]{:S(2)}) collective-permute-start(bf16[192,512]{1,0:T(8,128)(2,1)} %shard_map.114.refs_0_), channel_id=1, source_target_pairs={{0,2},{1,3},{2,0},{3,1},{4,6},{5,7},{6,4},{7,5},{8,10},{9,11},{10,... | collective-permute-start | bytes 589832 | tf_op jit(solution)/shard_map/ppermute | solution.py:24
  146.6 10.9 %collective-permute-start.5 = (bf16[192,512]{1,0:T(8,128)(2,1)}, bf16[192,512]{1,0:T(8,128)(2,1)S(1)}, u32[]{:S(2)}, u32[]{:S(2)}) collective-permute-start(bf16[192,512]{1,0:T(8,128)(2,1)} %shard_map.114.refs_0_), channel_id=1, source_target_pairs={{0,1},{1,2},{2,3},{3,0},{4,5},{5,6},{6,7},{7,4},{8,9},{9,10},{10,1... | collective-permute-start | bytes 589832 | tf_op jit(solution)/shard_map/ppermute | solution.py:24
  161.6 10.0 %all-to-all-start.7 = ((f32[8,2,512]{2,1,0:T(2,128)}), f32[8,2,512]{2,1,0:T(2,128)S(1)}, u32[]{:S(2)}, u32[]{:S(2)}) async-start(f32[8,2,512]{2,1,0:T(2,128)} %broadcast_in_dim.80), calls=%async_computation.7 | async-start | bytes 65536 | tf_op jit(solution)/shard_map/all_to_all | solution.py:19
  (11 other events, 35.3 us)

commit v4 on v1

v4 whole, which is shorter than its diff:
```python
import jax
import jax.numpy as jnp
from jax import lax
from jax.experimental import pallas as pl
from jax.experimental.pallas import tpu as pltpu
from jax.sharding import Mesh, PartitionSpec as P

LOGIT_SCALE = 64.0
MARGIN = 0.4
EPSILON = 1e-05
F32 = jnp.float32
BF16 = jnp.bfloat16
VMEM = 20 * 1024 * 1024
PAD = 16


def spread(block, axes):
    copies = jnp.broadcast_to(block[None], (lax.axis_size(axes),) + block.shape)
    return lax.all_to_all(copies, axes, 0, 0)


def shift(block, axis, by):
    n = lax.axis_size(axis)
    return lax.ppermute(block, axis, [(i, (i + by) % n) for i in range(n)])


def head(inputs, sums, gain, bias, batch_total):
    mean = sums[0:1] / batch_total
    inv_std = lax.rsqrt(sums[1:2] / batch_total - mean * mean + EPSILON)
    normed = (inputs.astype(F32) - mean) * inv_std
    shifted = normed * gain + bias
    scale = lax.rsqrt(jnp.sum(shifted * shifted, 1, keepdims=True) + EPSILON)
    return normed, shifted * scale, scale, inv_std


def call(kernel, shapes, flops, size, exps=0, scalars=0, skipped=0):
    vmem = pl.BlockSpec(memory_space=pltpu.VMEM)
    smem = pl.BlockSpec(memory_space=pltpu.SMEM)
    left = pl.BlockSpec(memory_space=pl.ANY)

    def run(*args):
        inner = len(args) - scalars - skipped
        return pl.pallas_call(
            kernel,
            in_specs=[smem] * scalars + [vmem] * inner + [left] * skipped,
            out_specs=jax.tree.map(lambda _: vmem, shapes),
            out_shape=shapes,
            compiler_params=pltpu.CompilerParams(vmem_limit_bytes=VMEM),
            cost_estimate=pl.CostEstimate(
                flops=flops, bytes_accessed=size, transcendentals=exps
            ),
        )(*args)

    return run


def hits(place, block, count, first):
    return place == lax.broadcasted_iota(jnp.int32, (block, count), 0) + first


def logits_of(w_hat, unit, place, first):
    cosine = lax.dot_general(
        w_hat, unit, (((1,), (1,)), ((), ())), preferred_element_type=F32
    )
    target = hits(place, w_hat.shape[0], unit.shape[0], first)
    return LOGIT_SCALE * cosine - jnp.where(target, LOGIT_SCALE * MARGIN, 0.0), target


def grad_of(w_hat, unit, place, first, total):
    logits, target = logits_of(w_hat, unit, place, first)
    return (jnp.exp(logits) / total - target.astype(F32)).astype(BF16)


def blocks_of(w_own, w_other):
    block = w_own.shape[0] // 2
    for i in range(4):
        source = w_own if i < 2 else w_other
        yield source[(i % 2) * block : (i % 2 + 1) * block], i * block


def exp_kernel(batch, rows, sums, gain, bias, place, w_own, w_other, unit, stats):
    total = jnp.sum(sums[...], 0)
    units = head(rows[...], total, gain[...], bias[...], batch)[1].astype(BF16)
    unit[...] = units
    exps = hit = None
    for w_hat, first in blocks_of(w_own, w_other):
        logits, target = logits_of(w_hat, units, place[...], first)
        term = jnp.sum(jnp.exp(logits), 0, keepdims=True)
        other = jnp.sum(jnp.where(target, logits, 0.0), 0, keepdims=True)
        exps = term if exps is None else exps + term
        hit = other if hit is None else hit + other
    both = jnp.concatenate([exps, hit], 0)
    for p in range(stats.shape[0]):
        stats[p] = both


def pull_kernel(
    batch, rows, sums, gain, bias, place, totals, unit, w_own, w_other, packed
):
    units = unit[...]
    pull = None
    for w_hat, first in blocks_of(w_own, w_other):
        grad = grad_of(w_hat, units, place[...], first, totals[0:1])
        term = lax.dot_general(
            grad, w_hat, (((0,), (0,)), ((), ())), preferred_element_type=F32
        )
        pull = term if pull is None else pull + term
    total = jnp.sum(sums[...], 0)
    normed, unit_f, scale, _ = head(rows[...], total, gain[...], bias[...], batch)
    radial = jnp.sum(unit_f * pull, 1, keepdims=True)
    shifts = (pull - unit_f * radial) * scale
    bias_part = jnp.sum(shifts, 0, keepdims=True)
    gain_part = jnp.sum(shifts * normed, 0, keepdims=True)
    tail = pack_ends(bias_part, gain_part).astype(BF16)
    parts = packed.shape[0]
    n = pull.shape[0] // parts
    for p in range(parts):
        packed[p, :n] = pull[p * n : (p + 1) * n].astype(BF16)
        packed[p, n:] = tail


def pack_ends(bias_part, gain_part):
    pieces = []
    for value in (bias_part, gain_part):
        for _ in range(3):
            piece = value.astype(BF16).astype(F32)
            value = value - piece
            pieces.append(piece)
    fill = jnp.zeros((PAD - 6, bias_part.shape[1]), F32)
    return jnp.concatenate(pieces + [fill], 0)


def unpack_ends(tail):
    return jnp.concatenate(
        [jnp.sum(tail[0:3], 0, keepdims=True), jnp.sum(tail[3:6], 0, keepdims=True)], 0
    )


def mid_kernel(rows_dev, arrived, packed):
    lines = packed.shape[0]
    total = jnp.sum(arrived[...].astype(F32), 0)
    ends = unpack_ends(total[lines * rows_dev :])
    tail = pack_ends(ends[0:1], ends[1:2])[: PAD - rows_dev]
    for p in range(lines):
        piece = total[p * rows_dev : (p + 1) * rows_dev]
        packed[p] = jnp.concatenate([piece, tail], 0).astype(BF16)


def raw_kernel(
    at, place, place_2, totals, unit, unit_2, w_own, _, mine, *sent
):
    parts = len(sent) + 1
    block = mine.shape[0]
    for i in range(parts):
        first = pl.multiple_of(lax.rem(at[0] + i, parts) * block, 64)
        w_hat = w_own[pl.ds(first, block)]
        raw = None
        for units, places, row in ((unit, place, 0), (unit_2, place_2, 2)):
            grad = grad_of(
                w_hat, units[...], places[...], first, totals[row : row + 1]
            )
            term = jnp.dot(grad, units[...], preferred_element_type=F32)
            raw = term if raw is None else raw + term
        if i == 0:
            mine[...] = raw
        else:
            sent[i - 1][...] = raw.astype(BF16)


def project_kernel(at, picked, mine, *rest):
    arrived, out = rest[:-1], rest[-1]
    block = mine.shape[0]
    raw = mine[...]
    for piece in arrived:
        raw = raw + piece[...].astype(F32)
    picks = picked[pl.ds(pl.multiple_of(at[0] * block, 64), block)].astype(F32)
    inv_norm = lax.rsqrt(jnp.sum(picks * picks, 1, keepdims=True) + EPSILON)
    w_unit = picks * inv_norm
    along = jnp.sum(w_unit * raw, 1, keepdims=True)
    out[...] = ((raw - w_unit * along) * inv_norm).astype(BF16)


def order_kernel(at, *refs):
    found, out = refs[:-1], refs[-1]
    parts = len(found)
    block = found[0].shape[0]
    for by, piece in enumerate(found):
        where = lax.rem(at[0] - by + parts, parts) * block
        out[pl.ds(pl.multiple_of(where, 64), block)] = piece[...]


def body(embeddings, bn_gain, bn_bias, centres, sample_rows, label_shard, label_slot):
    nx, nz, nc, nr = (lax.axis_size(a) for a in ("x", "z", "core", "rep"))
    ix, iz, ic, ir = (lax.axis_index(a) for a in ("x", "z", "core", "rep"))
    rows_dev, width = embeddings.shape
    slots = sample_rows.shape[1]
    batch = rows_dev * nx * nz * nc * nr
    line_rows = nz * rows_dev
    group = nx * line_rows
    held = nc * slots
    quarter = slots // nr
    at = ir.astype(jnp.int32).reshape(1)
    gain, bias = bn_gain[None], bn_bias[None]

    line = spread(embeddings, "z").reshape(line_rows, width)
    rows = spread(line, "x").reshape(group, width)
    rows_f = rows.astype(F32)
    sums = spread(
        jnp.stack([jnp.sum(rows_f, 0), jnp.sum(rows_f * rows_f, 0)]), ("core", "rep")
    )

    picked = jnp.take(centres, sample_rows[0], axis=0)
    picks = picked.astype(F32)
    inv_norm = lax.rsqrt(jnp.sum(picks * picks, 1, keepdims=True) + EPSILON)
    w_own = (picks * inv_norm).astype(BF16)
    w_other = shift(w_own, "core", 1)

    def of_core(labels, core):
        lines = labels.reshape(nx * nz, nc, rows_dev)
        return lax.dynamic_index_in_dim(lines, core, 1).reshape(1, group)

    owner, slot = of_core(label_shard, ic), of_core(label_slot, ic)
    chip = (ix * nz + iz) * nc
    place = jnp.where(
        owner == chip + ic, slot, jnp.where(owner == chip + 1 - ic, slot + slots, -1)
    )
    place_2 = jnp.where(
        of_core(label_shard, 1 - ic) == chip + ic, of_core(label_slot, 1 - ic), -1
    )

    unit, stats = call(
        lambda *refs: exp_kernel(batch, *refs),
        [
            jax.ShapeDtypeStruct((group, width), BF16),
            jax.ShapeDtypeStruct((nx * nc, 2, group), F32),
        ],
        2 * held * group * width,
        2 * held * width,
        held * group,
    )(rows, sums, gain, bias, place, w_own, w_other)
    unit_2 = shift(unit, "core", 1)

    stats = lax.all_to_all(stats, ("x", "core"), 0, 0).reshape(nx, nc, 2, group)
    stats = jnp.sum(stats, 0)
    stats = jnp.where(ic == 0, stats, stats[::-1]).reshape(2 * nc, group)
    stats, unit_2 = lax.optimization_barrier((stats, unit_2))
    stats = jnp.sum(spread(stats, "z"), 0)

    pull = call(
        lambda *refs: pull_kernel(batch, *refs),
        jax.ShapeDtypeStruct((nx, line_rows + PAD, width), BF16),
        4 * held * group * width,
        2 * held * width,
        held * group,
    )(rows, sums, gain, bias, place, stats, unit, w_own, w_other)

    piece = jax.ShapeDtypeStruct((quarter, width), BF16)
    mine, *sent = call(
        raw_kernel,
        [jax.ShapeDtypeStruct((quarter, width), F32)] + [piece] * (nr - 1),
        4 * held * group * width,
        2 * held * width,
        held * group,
        scalars=1,
        skipped=1,
    )(at, place, place_2, stats, unit, unit_2, w_own, pull)
    came = [shift(sent[by - 1], "rep", by) for by in range(1, nr)]
    grad = call(
        project_kernel, piece, 20 * quarter * width, 14 * quarter * width, scalars=1
    )(at, picked, mine, *came)
    found = [grad] + [shift(grad, "rep", by) for by in range(1, nr)]
    centre_grad = call(
        order_kernel,
        jax.ShapeDtypeStruct((slots, width), BF16),
        slots * width,
        4 * slots * width,
        scalars=1,
    )(at, *found)

    pull = lax.all_to_all(pull, "x", 0, 0)
    pull, mine = lax.optimization_barrier((pull, mine))
    pull = call(
        lambda *refs: mid_kernel(rows_dev, *refs),
        jax.ShapeDtypeStruct((nz, PAD, width), BF16),
        nx * line_rows * width,
        2 * nx * line_rows * width,
    )(pull)
    pull = jnp.sum(lax.all_to_all(pull, "z", 0, 0).astype(F32), 0)
    grad_unit = pull[:rows_dev]
    ends = jnp.sum(spread(unpack_ends(pull[rows_dev:]), ("core", "rep")), 0)

    own_stats = lax.dynamic_slice_in_dim(
        stats, (ix * nz + iz) * rows_dev, rows_dev, 1
    )
    row_loss = jnp.log(own_stats[0]) - own_stats[1]
    normed, unit_f, row_scale, inv_std = head(
        embeddings, jnp.sum(sums, 0), gain, bias, batch
    )
    radial = jnp.sum(unit_f * grad_unit, 1, keepdims=True)
    grad_shift = (grad_unit - unit_f * radial) * row_scale
    bias_grad, gain_grad = ends[0], ends[1]
    emb_grad = inv_std * (
        grad_shift * bn_gain
        - bn_gain * bias_grad / batch
        - normed * (bn_gain * gain_grad / batch)
    )
    return (row_loss, emb_grad, centre_grad, gain_grad, bias_grad)


def solution(mesh):
    shards, replicas = mesh.devices.shape
    split = (4, shards // 8, 2, replicas)
    fine = Mesh(mesh.devices.reshape(split), ("x", "z", "core", "rep"))
    cen = ("x", "z", "core")
    every = cen + ("rep",)
    return jax.shard_map(
        body,
        mesh=fine,
        in_specs=(
            P(every, None),
            P(),
            P(),
            P(cen, None),
            P(cen, None),
            P(None, "rep", None),
            P(None, "rep", None),
        ),
        out_specs=(P(every), P(every, None), P(cen, None), P(), P()),
        check_vma=False,
    )
```

time: 219 us -> 161 us (0.74)
  waiting for transfers between devices: 73.1 us -> 33.6 us
  matrix products: 15 us -> 0 us
  Pallas kernels: 0 us -> 14.1 us
  blocking collectives: 29.7 us -> 16.2 us
  starting transfers between devices: 74.7 us -> 70.7 us
  other arithmetic: 12.9 us -> 8.91 us
  local copies, waits for them, and re-layouts: 11.5 us -> 15.3 us
    all_to_all x6 -> x4, waiting for transfers between devices: 42 us -> 15.3 us  [spread(): return lax.all_to_all(copies, axes, 0, 0)]
    all_to_all x5 -> x3, waiting for transfers between devices: 31.2 us -> 4.74 us  [the longest x1 4.74 us: body(): stats = lax.all_to_all(stats, ('x', 'core'), 0, 0).reshape(nx, nc, 2, group)]
    dot_general x4 -> x0, matrix products: 15 us -> none  [the longest x1 4.47 us: body(): cosine = jnp.dot(unit, w_hat.T, preferred_element_type=F32)]
    ppermute x2 -> x8, starting transfers between devices: 12.1 us -> 26.7 us  [shift(): return lax.ppermute(block, axis, [(i, (i + by) % n) for i in range(n)])]
    pallas_call x0 -> x6, Pallas kernels: none -> 14.1 us  [run(): pl.pallas_call(kernel, in_specs=[smem] * scalars + [vmem] * inner + [left...]
    ppermute x2 -> x8, waiting for transfers between devices: 0.01 us -> 13.6 us  [shift(): return lax.ppermute(block, axis, [(i, (i + by) % n) for i in range(n)])]
    all_to_all x6 -> x4, starting transfers between devices: 44.7 us -> 31.2 us  [spread(): return lax.all_to_all(copies, axes, 0, 0)]
    all_to_all x2 -> x1, blocking collectives: 29.7 us -> 16.2 us  [spread(): return lax.all_to_all(copies, axes, 0, 0)]
  transfers between devices with their start and end apart: 13 -> 15, of which waited for: 10 -> 8; matrix products, arithmetic and copies ran while one was open for 12% -> 8% of each run, Pallas kernels for 0% -> 3%
where the time goes in v4:
time: 161 us; the launch traced here: 160 us
  starting transfers between devices  70.7 us (44%)
  waiting for transfers between devices  33.6 us (21%)
  blocking collectives  16.2 us (10%)
  local copies, waits for them, and re-layouts  15.3 us (10%)
  Pallas kernels  14.1 us (9%)
  other arithmetic  8.91 us (6%)
    all_to_all x4, starting transfers between devices, spread(): return lax.all_to_all(copies, axes, 0, 0)  31.2 us
    ppermute x8, starting transfers between devices, shift(): return lax.ppermute(block, axis, [(i, (i + by) % n) for i in range(n)])  26.7 us
    all_to_all x1, blocking collectives, spread(): return lax.all_to_all(copies, axes, 0, 0)  16.2 us
    all_to_all x4, waiting for transfers between devices, spread(): return lax.all_to_all(copies, axes, 0, 0)  15.3 us
    pallas_call x6, Pallas kernels, run(): pl.pallas_call(kernel, in_specs=[smem] * scalars + [vmem] * inner + [left...  14.1 us
    ppermute x8, waiting for transfers between devices, shift(): return lax.ppermute(block, axis, [(i, (i + by) % n) for i in range(n)])  13.6 us
    unnamed x34, local copies, waits for them, and re-layouts  7.15 us
    all_to_all x1, starting transfers between devices, body(): pull = jnp.sum(lax.all_to_all(pull, 'z', 0, 0).astype(F32), 0)  5.91 us
  transfers between devices with their start and end apart: 15, of which 8 were waited for; matrix products, arithmetic and copies ran while one was open for 8% of the time, Pallas kernels for 3%

profile of v4, /device:TPU:1, one launch (start us, length us, event | category | flops | bytes accessed | tf_op | source)
XLA Modules:
  0.0 159.8 jit_solution(10260652900151393855)
XLA Ops:
  2.1 15.7 %all-to-all-start = ((bf16[16,8,512]{2,1,0:T(8,128)(2,1)}), bf16[16,8,512]{2,1,0:T(8,128)(2,1)S(1)}, u32[]{:S(2)}, u32[]{:S(2)}) async-start(bf16[16,8,512]{2,1,0:T(8,128)(2,1)} %broadcast_in_dim.66), calls=%async_computation | async-start | bytes 262144 | tf_op jit(solution)/shard_map/all_to_all | solution.py:19
  19.3 3.3 %gather_fusion = bf16[768,512]{1,0:T(8,128)(2,1)} fusion(bf16[2048,512]{1,0:T(8,128)(2,1)S(1)} %copy-done, s32[1024]{0:T(1024)S(1)} %pad_clamp_fusion), kind=kCustom, calls=%fused_computation | custom fusion | bytes 1575936 | tf_op jit(solution)/shard_map/jit(_take)/gather | solution.py:212
  24.3 5.6 %all-to-all-done = bf16[16,8,512]{2,1,0:T(8,128)(2,1)S(1)} async-done(((bf16[16,8,512]{2,1,0:T(8,128)(2,1)}), bf16[16,8,512]{2,1,0:T(8,128)(2,1)S(1)}, u32[]{:S(2)}, u32[]{:S(2)}) %all-to-all-start) | async-done | bytes 131104 | tf_op jit(solution)/shard_map/all_to_all | solution.py:19
  30.7 4.0 %all-to-all-start.1 = ((bf16[4,128,512]{2,1,0:T(8,128)(2,1)}), bf16[4,128,512]{2,1,0:T(8,128)(2,1)S(1)}, u32[]{:S(2)}, u32[]{:S(2)}) async-start(bf16[4,128,512]{2,1,0:T(8,128)(2,1)} %broadcast_in_dim.68), calls=%async_computation.1 | async-start | bytes 1048576 | tf_op jit(solution)/shard_map/all_to_all | solution.py:19
  35.9 5.8 %collective-permute-start = (bf16[768,512]{1,0:T(8,128)(2,1)}, bf16[768,512]{1,0:T(8,128)(2,1)}, u32[]{:S(2)}, u32[]{:S(2)}) collective-permute-start(bf16[768,512]{1,0:T(8,128)(2,1)} %fusion.1.refs_5_.refs_7_.w_own), channel_id=1, source_target_pairs={{0,4},{4,0},{1,5},{5,1},{2,6},{6,2},{3,7},{7,3},{8,12},{12,8},{9,1... | collective-permute-start | bytes 2359304 | tf_op jit(solution)/shard_map/ppermute | solution.py:24
  45.6 6.4 %all-to-all-start.2 = ((f32[8,2,512]{2,1,0:T(2,128)}), f32[8,2,512]{2,1,0:T(2,128)S(1)}, u32[]{:S(2)}, u32[]{:S(2)}) async-start(f32[8,2,512]{2,1,0:T(2,128)} %broadcast_in_dim.69), calls=%async_computation.2 | async-start | bytes 65536 | tf_op jit(solution)/shard_map/all_to_all | solution.py:19
  52.1 4.9 %all-to-all-done.2.refs_1_ = f32[8,2,512]{2,1,0:T(2,128)S(1)} async-done(((f32[8,2,512]{2,1,0:T(2,128)}), f32[8,2,512]{2,1,0:T(2,128)S(1)}, u32[]{:S(2)}, u32[]{:S(2)}) %all-to-all-start.2) | async-done | bytes 32800 | tf_op jit(solution)/shard_map/all_to_all | solution.py:19
  57.0 3.7 %shard_map.110 = (bf16[512,512]{1,0:T(8,128)(2,1)}, f32[8,2,512]{2,1,0:T(2,128)}) custom-call(bf16[512,512]{1,0:T(8,128)(2,1)S(1)} %bitcast.20, f32[8,2,512]{2,1,0:T(2,128)S(1)} %all-to-all-done.2.refs_1_, f32[1,512]{1,0:T(1,128)S(1)} %bitcast.22, f32[1,512]{1,0:T(1,128)S(1)} %bitcast.24, s32[1,512]{1,0:T(1,128)S(1)} %select_select_fusion.refs_4_.place, ...), custom_call_target="tpu_custom_call" | custom-call | flops 805306368 | bytes 1572864 | tf_op jit(solution)/shard_map/pallas_call | solution.py:43
  60.6 2.3 %collective-permute-start.1 = (bf16[512,512]{1,0:T(8,128)(2,1)}, bf16[512,512]{1,0:T(8,128)(2,1)}, u32[]{:S(2)}, u32[]{:S(2)}) collective-permute-start(bf16[512,512]{1,0:T(8,128)(2,1)} %get-tuple-element.15.refs_6_.unit), channel_id=1, source_target_pairs={{0,4},{4,0},{1,5},{5,1},{2,6},{6,2},{3,7},{7,3},{8,12},{12,8},{9,1... | collective-permute-start | bytes 1572872 | tf_op jit(solution)/shard_map/ppermute | solution.py:24
  62.9 3.4 %all-to-all-start.3 = ((f32[8,2,512]{2,1,0:T(2,128)}), f32[8,2,512]{2,1,0:T(2,128)S(1)}, u32[]{:S(2)}, u32[]{:S(2)}) async-start(f32[8,2,512]{2,1,0:T(2,128)} %get-tuple-element.14), calls=%async_computation.3 | async-start | bytes 65536 | tf_op jit(solution)/shard_map/all_to_all | solution.py:243
  66.3 4.7 %all-to-all-done.3 = f32[8,2,512]{2,1,0:T(2,128)S(1)} async-done(((f32[8,2,512]{2,1,0:T(2,128)}), f32[8,2,512]{2,1,0:T(2,128)S(1)}, u32[]{:S(2)}, u32[]{:S(2)}) %all-to-all-start.3) | async-done | bytes 32800 | tf_op jit(solution)/shard_map/all_to_all | solution.py:243
  71.1 16.2 %all_to_all.40 = f32[16,4,512]{2,1,0:T(4,128)} all-to-all(f32[16,4,512]{2,1,0:T(4,128)S(1)} %broadcast_in_dim.75), channel_id=1, replica_groups=mesh['x'=4,'z'=16,'core'=2,'rep'=4] {'z'}, dimensions={0} | all-to-all | bytes 262144 | tf_op jit(solution)/shard_map/all_to_all | solution.py:19
  88.3 4.8 %shard_map.111._ = bf16[4,144,512]{2,1,0:T(8,128)(2,1)S(1)} custom-call(bf16[512,512]{1,0:T(8,128)(2,1)S(1)} %bitcast.21, f32[8,2,512]{2,1,0:T(2,128)S(1)} %all-to-all-done.2.refs_1_, f32[1,512]{1,0:T(1,128)S(1)} %bitcast.23, f32[1,512]{1,0:T(1,128)S(1)} %bitcast.25, s32[1,512]{1,0:T(1,128)S(1)} %select_select_fusion.refs_4_.place, ...), custom_call_target="tpu_custom_call" | custom-call | flops 1610612736 | bytes 1572864 | tf_op jit(solution)/shard_map/pallas_call | solution.py:43
  93.9 3.5 %all-to-all-start.5 = ((bf16[4,144,512]{2,1,0:T(8,128)(2,1)}), bf16[4,144,512]{2,1,0:T(8,128)(2,1)S(1)}, u32[]{:S(2)}, u32[]{:S(2)}) async-start(bf16[4,144,512]{2,1,0:T(8,128)(2,1)} %copy-done.2), calls=%async_computation.5 | async-start | bytes 1179648 | tf_op jit(solution)/shard_map/all_to_all | solution.py:280
  99.3 4.3 %shard_map.112 = (f32[192,512]{1,0:T(8,128)S(1)}, bf16[192,512]{1,0:T(8,128)(2,1)S(1)}, bf16[192,512]{1,0:T(8,128)(2,1)S(1)}, bf16[192,512]{1,0:T(8,128)(2,1)S(1)}) custom-call(s32[1]{0:T(128)} %bitcast.12.at, s32[1,512]{1,0:T(1,128)S(1)} %select_select_fusion.refs_4_.place, s32[1,512]{1,0:T(1,128)S(1)} %select_n.72.place_2, ...), custom_call_target="tpu_custom_call" | custom-call | flops 1610612736 | bytes 1572864 | tf_op jit(solution)/shard_map/pallas_call | solution.py:43
  107.2 5.9 %all-to-all-start.6 = ((bf16[16,16,512]{2,1,0:T(8,128)(2,1)}), bf16[16,16,512]{2,1,0:T(8,128)(2,1)S(1)}, u32[]{:S(2)}, u32[]{:S(2)}) async-start(bf16[16,16,512]{2,1,0:T(8,128)(2,1)} %copy-done.1), calls=%async_computation.6 | async-start | bytes 524288 | tf_op jit(solution)/shard_map/all_to_all | solution.py:288
  115.6 3.6 %collective-permute-start.3 = (bf16[192,512]{1,0:T(8,128)(2,1)}, bf16[192,512]{1,0:T(8,128)(2,1)S(1)}, u32[]{:S(2)}, u32[]{:S(2)}) collective-permute-start(bf16[192,512]{1,0:T(8,128)(2,1)} %copy-done.9), channel_id=1, source_target_pairs={{0,2},{1,3},{2,0},{3,1},{4,6},{5,7},{6,4},{7,5},{8,10},{9,11},{10,... | collective-permute-start | bytes 589832 | tf_op jit(solution)/shard_map/ppermute | solution.py:24
  119.3 2.8 %collective-permute-start.4 = (bf16[192,512]{1,0:T(8,128)(2,1)}, bf16[192,512]{1,0:T(8,128)(2,1)S(1)}, u32[]{:S(2)}, u32[]{:S(2)}) collective-permute-start(bf16[192,512]{1,0:T(8,128)(2,1)} %copy-done.8), channel_id=1, source_target_pairs={{0,3},{1,0},{2,1},{3,2},{4,7},{5,4},{6,5},{7,6},{8,11},{9,8},{10,9... | collective-permute-start | bytes 589832 | tf_op jit(solution)/shard_map/ppermute | solution.py:24
  122.1 3.9 %collective-permute-done.3.rest_1_ = bf16[192,512]{1,0:T(8,128)(2,1)S(1)} collective-permute-done((bf16[192,512]{1,0:T(8,128)(2,1)}, bf16[192,512]{1,0:T(8,128)(2,1)S(1)}, u32[]{:S(2)}, u32[]{:S(2)}) %collective-permute-start.3) | collective-permute-done | bytes 196640 | tf_op jit(solution)/shard_map/ppermute | solution.py:24
  128.7 4.1 %collective-permute-start.7 = (bf16[192,512]{1,0:T(8,128)(2,1)S(1)}, bf16[192,512]{1,0:T(8,128)(2,1)S(1)}, u32[]{:S(2)}, u32[]{:S(2)}) collective-permute-start(bf16[192,512]{1,0:T(8,128)(2,1)S(1)} %shard_map.114.refs_0_), channel_id=1, source_target_pairs={{0,3},{1,0},{2,1},{3,2},{4,7},{5,4},{6,5},{7,6},{8,11},{9,8},{10,9... | collective-permute-start | bytes 589832 | tf_op jit(solution)/shard_map/ppermute | solution.py:24
  132.8 3.9 %collective-permute-start.6 = (bf16[192,512]{1,0:T(8,128)(2,1)S(1)}, bf16[192,512]{1,0:T(8,128)(2,1)S(1)}, u32[]{:S(2)}, u32[]{:S(2)}) collective-permute-start(bf16[192,512]{1,0:T(8,128)(2,1)S(1)} %shard_map.114.refs_0_), channel_id=1, source_target_pairs={{0,2},{1,3},{2,0},{3,1},{4,6},{5,7},{6,4},{7,5},{8,10},{9,11},{10,... | collective-permute-start | bytes 589832 | tf_op jit(solution)/shard_map/ppermute | solution.py:24
  140.7 6.7 %collective-permute-done.5.refs_1_ = bf16[192,512]{1,0:T(8,128)(2,1)S(1)} collective-permute-done((bf16[192,512]{1,0:T(8,128)(2,1)S(1)}, bf16[192,512]{1,0:T(8,128)(2,1)S(1)}, u32[]{:S(2)}, u32[]{:S(2)}) %collective-permute-start.5) | collective-permute-done | bytes 196640 | tf_op jit(solution)/shard_map/ppermute | solution.py:24
  149.1 5.0 %all-to-all-start.7 = ((f32[8,2,512]{2,1,0:T(2,128)}), f32[8,2,512]{2,1,0:T(2,128)S(1)}, u32[]{:S(2)}, u32[]{:S(2)}) async-start(f32[8,2,512]{2,1,0:T(2,128)} %broadcast_in_dim.79), calls=%async_computation.7 | async-start | bytes 65536 | tf_op jit(solution)/shard_map/all_to_all | solution.py:19
  154.3 4.7 %all-to-all-done.7 = f32[8,2,512]{2,1,0:T(2,128)S(1)} async-done(((f32[8,2,512]{2,1,0:T(2,128)}), f32[8,2,512]{2,1,0:T(2,128)S(1)}, u32[]{:S(2)}, u32[]{:S(2)}) %all-to-all-start.7) | async-done | bytes 32800 | tf_op jit(solution)/shard_map/all_to_all | solution.py:19
  (87 shorter events, 29.3 us)
Async XLA Ops:
  0.6 18.7 %copy-start = (bf16[2048,512]{1,0:T(8,128)(2,1)S(1)}, bf16[2048,512]{1,0:T(8,128)(2,1)}, u32[]{:S(2)}) copy-start(bf16[2048,512]{1,0:T(8,128)(2,1)} %param.10) | copy-start | bytes 6291460
  2.1 27.8 %all-to-all-start = ((bf16[16,8,512]{2,1,0:T(8,128)(2,1)}), bf16[16,8,512]{2,1,0:T(8,128)(2,1)S(1)}, u32[]{:S(2)}, u32[]{:S(2)}) async-start(bf16[16,8,512]{2,1,0:T(8,128)(2,1)} %broadcast_in_dim.66), calls=%async_computation | async-start | bytes 262144 | tf_op jit(solution)/shard_map/all_to_all | solution.py:19
  29.9 11.8 %copy-start.14 = (s32[128,1,8]{0,2,1:T(8,128)S(1)}, s32[128,1,8]{0,2,1:T(8,128)}, u32[]{:S(2)}) copy-start(s32[128,1,8]{0,2,1:T(8,128)} %param.12) | copy-start | bytes 12292
  29.9 12.4 %copy-start.15 = (s32[128,1,8]{0,2,1:T(8,128)S(1)}, s32[128,1,8]{0,2,1:T(8,128)}, u32[]{:S(2)}) copy-start(s32[128,1,8]{0,2,1:T(8,128)} %param.13) | copy-start | bytes 12292
  30.7 14.1 %all-to-all-start.1 = ((bf16[4,128,512]{2,1,0:T(8,128)(2,1)}), bf16[4,128,512]{2,1,0:T(8,128)(2,1)S(1)}, u32[]{:S(2)}, u32[]{:S(2)}) async-start(bf16[4,128,512]{2,1,0:T(8,128)(2,1)} %broadcast_in_dim.68), calls=%async_computation.1 | async-start | bytes 1048576 | tf_op jit(solution)/shard_map/all_to_all | solution.py:19
  34.7 22.2 %copy-start.6 = (f32[512]{0:T(512)S(1)}, f32[512]{0:T(512)}, u32[]{:S(2)}) copy-start(f32[512]{0:T(512)} %param.8) | copy-start | bytes 6148
  34.7 22.2 %copy-start.7 = (f32[512]{0:T(512)S(1)}, f32[512]{0:T(512)}, u32[]{:S(2)}) copy-start(f32[512]{0:T(512)} %param.9) | copy-start | bytes 6148
  35.9 16.2 %collective-permute-start = (bf16[768,512]{1,0:T(8,128)(2,1)}, bf16[768,512]{1,0:T(8,128)(2,1)}, u32[]{:S(2)}, u32[]{:S(2)}) collective-permute-start(bf16[768,512]{1,0:T(8,128)(2,1)} %fusion.1.refs_5_.refs_7_.w_own), channel_id=1, source_target_pairs={{0,4},{4,0},{1,5},{5,1},{2,6},{6,2},{3,7},{7,3},{8,12},{12,8},{9,1... | collective-permute-start | bytes 2359304 | tf_op jit(solution)/shard_map/ppermute | solution.py:24
  45.6 11.3 %all-to-all-start.2 = ((f32[8,2,512]{2,1,0:T(2,128)}), f32[8,2,512]{2,1,0:T(2,128)S(1)}, u32[]{:S(2)}, u32[]{:S(2)}) async-start(f32[8,2,512]{2,1,0:T(2,128)} %broadcast_in_dim.69), calls=%async_computation.2 | async-start | bytes 65536 | tf_op jit(solution)/shard_map/all_to_all | solution.py:19
  60.6 10.5 %collective-permute-start.1 = (bf16[512,512]{1,0:T(8,128)(2,1)}, bf16[512,512]{1,0:T(8,128)(2,1)}, u32[]{:S(2)}, u32[]{:S(2)}) collective-permute-start(bf16[512,512]{1,0:T(8,128)(2,1)} %get-tuple-element.15.refs_6_.unit), channel_id=1, source_target_pairs={{0,4},{4,0},{1,5},{5,1},{2,6},{6,2},{3,7},{7,3},{8,12},{12,8},{9,1... | collective-permute-start | bytes 1572872 | tf_op jit(solution)/shard_map/ppermute | solution.py:24
  62.9 8.1 %all-to-all-start.3 = ((f32[8,2,512]{2,1,0:T(2,128)}), f32[8,2,512]{2,1,0:T(2,128)S(1)}, u32[]{:S(2)}, u32[]{:S(2)}) async-start(f32[8,2,512]{2,1,0:T(2,128)} %get-tuple-element.14), calls=%async_computation.3 | async-start | bytes 65536 | tf_op jit(solution)/shard_map/all_to_all | solution.py:243
  93.1 0.8 copy-start.2
  93.9 12.5 %all-to-all-start.5 = ((bf16[4,144,512]{2,1,0:T(8,128)(2,1)}), bf16[4,144,512]{2,1,0:T(8,128)(2,1)S(1)}, u32[]{:S(2)}, u32[]{:S(2)}) async-start(bf16[4,144,512]{2,1,0:T(8,128)(2,1)} %copy-done.2), calls=%async_computation.5 | async-start | bytes 1179648 | tf_op jit(solution)/shard_map/all_to_all | solution.py:280
  98.3 1.1 copy-start.3
  99.3 13.9 %copy-start.11 = (bf16[8,512]{1,0:T(8,128)(2,1)S(1)}, bf16[8,512]{1,0:T(8,128)(2,1)}, u32[]{:S(2)}) copy-start(bf16[8,512]{1,0:T(8,128)(2,1)} %param.7) | copy-start | bytes 24580
  107.2 41.1 %all-to-all-start.6 = ((bf16[16,16,512]{2,1,0:T(8,128)(2,1)}), bf16[16,16,512]{2,1,0:T(8,128)(2,1)S(1)}, u32[]{:S(2)}, u32[]{:S(2)}) async-start(bf16[16,16,512]{2,1,0:T(8,128)(2,1)} %copy-done.1), calls=%async_computation.6 | async-start | bytes 524288 | tf_op jit(solution)/shard_map/all_to_all | solution.py:288
  113.3 8.8 %collective-permute-start.2 = (bf16[192,512]{1,0:T(8,128)(2,1)}, bf16[192,512]{1,0:T(8,128)(2,1)S(1)}, u32[]{:S(2)}, u32[]{:S(2)}) collective-permute-start(bf16[192,512]{1,0:T(8,128)(2,1)} %copy-done.10), channel_id=1, source_target_pairs={{0,1},{1,2},{2,3},{3,0},{4,5},{5,6},{6,7},{7,4},{8,9},{9,10},{10,1... | collective-permute-start | bytes 589832 | tf_op jit(solution)/shard_map/ppermute | solution.py:24
  115.6 10.4 %collective-permute-start.3 = (bf16[192,512]{1,0:T(8,128)(2,1)}, bf16[192,512]{1,0:T(8,128)(2,1)S(1)}, u32[]{:S(2)}, u32[]{:S(2)}) collective-permute-start(bf16[192,512]{1,0:T(8,128)(2,1)} %copy-done.9), channel_id=1, source_target_pairs={{0,2},{1,3},{2,0},{3,1},{4,6},{5,7},{6,4},{7,5},{8,10},{9,11},{10,... | collective-permute-start | bytes 589832 | tf_op jit(solution)/shard_map/ppermute | solution.py:24
  119.3 8.2 %collective-permute-start.4 = (bf16[192,512]{1,0:T(8,128)(2,1)}, bf16[192,512]{1,0:T(8,128)(2,1)S(1)}, u32[]{:S(2)}, u32[]{:S(2)}) collective-permute-start(bf16[192,512]{1,0:T(8,128)(2,1)} %copy-done.8), channel_id=1, source_target_pairs={{0,3},{1,0},{2,1},{3,2},{4,7},{5,4},{6,5},{7,6},{8,11},{9,8},{10,9... | collective-permute-start | bytes 589832 | tf_op jit(solution)/shard_map/ppermute | solution.py:24
  127.5 1.0 copy-start.5
  128.7 10.4 %collective-permute-start.7 = (bf16[192,512]{1,0:T(8,128)(2,1)S(1)}, bf16[192,512]{1,0:T(8,128)(2,1)S(1)}, u32[]{:S(2)}, u32[]{:S(2)}) collective-permute-start(bf16[192,512]{1,0:T(8,128)(2,1)S(1)} %shard_map.114.refs_0_), channel_id=1, source_target_pairs={{0,3},{1,0},{2,1},{3,2},{4,7},{5,4},{6,5},{7,6},{8,11},{9,8},{10,9... | collective-permute-start | bytes 589832 | tf_op jit(solution)/shard_map/ppermute | solution.py:24
  132.8 7.9 %collective-permute-start.6 = (bf16[192,512]{1,0:T(8,128)(2,1)S(1)}, bf16[192,512]{1,0:T(8,128)(2,1)S(1)}, u32[]{:S(2)}, u32[]{:S(2)}) collective-permute-start(bf16[192,512]{1,0:T(8,128)(2,1)S(1)} %shard_map.114.refs_0_), channel_id=1, source_target_pairs={{0,2},{1,3},{2,0},{3,1},{4,6},{5,7},{6,4},{7,5},{8,10},{9,11},{10,... | collective-permute-start | bytes 589832 | tf_op jit(solution)/shard_map/ppermute | solution.py:24
  136.7 10.7 %collective-permute-start.5 = (bf16[192,512]{1,0:T(8,128)(2,1)S(1)}, bf16[192,512]{1,0:T(8,128)(2,1)S(1)}, u32[]{:S(2)}, u32[]{:S(2)}) collective-permute-start(bf16[192,512]{1,0:T(8,128)(2,1)S(1)} %shard_map.114.refs_0_), channel_id=1, source_target_pairs={{0,1},{1,2},{2,3},{3,0},{4,5},{5,6},{6,7},{7,4},{8,9},{9,10},{10,1... | collective-permute-start | bytes 589832 | tf_op jit(solution)/shard_map/ppermute | solution.py:24
  149.1 10.0 %all-to-all-start.7 = ((f32[8,2,512]{2,1,0:T(2,128)}), f32[8,2,512]{2,1,0:T(2,128)S(1)}, u32[]{:S(2)}, u32[]{:S(2)}) async-start(f32[8,2,512]{2,1,0:T(2,128)} %broadcast_in_dim.79), calls=%async_computation.7 | async-start | bytes 65536 | tf_op jit(solution)/shard_map/all_to_all | solution.py:19
  (7 other events, 4.9 us)

commit v5 on v4

--- a/solution.py
+++ b/solution.py
@@ -33,25 +33,23 @@
     return normed, shifted * scale, scale, inv_std
 
 
-def call(kernel, shapes, flops, size, exps=0, scalars=0, skipped=0):
-    vmem = pl.BlockSpec(memory_space=pltpu.VMEM)
-    smem = pl.BlockSpec(memory_space=pltpu.SMEM)
-    left = pl.BlockSpec(memory_space=pl.ANY)
-
-    def run(*args):
-        inner = len(args) - scalars - skipped
-        return pl.pallas_call(
-            kernel,
-            in_specs=[smem] * scalars + [vmem] * inner + [left] * skipped,
-            out_specs=jax.tree.map(lambda _: vmem, shapes),
-            out_shape=shapes,
-            compiler_params=pltpu.CompilerParams(vmem_limit_bytes=VMEM),
-            cost_estimate=pl.CostEstimate(
-                flops=flops, bytes_accessed=size, transcendentals=exps
-            ),
-        )(*args)
-
-    return run
+VM = pl.BlockSpec(memory_space=pltpu.VMEM)
+SM = pl.BlockSpec(memory_space=pltpu.SMEM)
+HB = pl.BlockSpec(memory_space=pl.ANY)
+
+
+def call(kernel, ins, outs, shapes, flops, size, exps=0, scratch=()):
+    return pl.pallas_call(
+        kernel,
+        in_specs=ins,
+        out_specs=outs,
+        out_shape=shapes,
+        scratch_shapes=list(scratch),
+        compiler_params=pltpu.CompilerParams(vmem_limit_bytes=VMEM),
+        cost_estimate=pl.CostEstimate(
+            flops=flops, bytes_accessed=size, transcendentals=exps
+        ),
+    )
 
 
 def hits(place, block, count, first):
@@ -78,10 +76,20 @@
         yield source[(i % 2) * block : (i % 2 + 1) * block], i * block
 
 
-def exp_kernel(batch, rows, sums, gain, bias, place, w_own, w_other, unit, stats):
+def place_of(at, by, parts, block):
+    return pl.multiple_of(lax.rem(at[0] - by + parts, parts) * block, block)
+
+
+def exp_kernel(
+    batch, lines, at, sums, gain, bias, place, w_own, w_other, *refs
+):
+    found, (unit, stats) = refs[:lines], refs[lines:]
+    n = found[0].shape[0]
     total = jnp.sum(sums[...], 0)
-    units = head(rows[...], total, gain[...], bias[...], batch)[1].astype(BF16)
-    unit[...] = units
+    for by, piece in enumerate(found):
+        part = head(piece[...], total, gain[...], bias[...], batch)[1].astype(BF16)
+        unit[pl.ds(place_of(at, by, lines, n), n)] = part
+    units = unit[...]
     exps = hit = None
     for w_hat, first in blocks_of(w_own, w_other):
         logits, target = logits_of(w_hat, units, place[...], first)
@@ -95,8 +103,10 @@
 
 
 def pull_kernel(
-    batch, rows, sums, gain, bias, place, totals, unit, w_own, w_other, packed
+    batch, lines, at, sums, gain, bias, place, totals, unit, w_own, w_other, *refs
 ):
+    found, (packed, acc) = refs[:lines], refs[lines:]
+    n = found[0].shape[0]
     units = unit[...]
     pull = None
     for w_hat, first in blocks_of(w_own, w_other):
@@ -105,17 +115,20 @@
             grad, w_hat, (((0,), (0,)), ((), ())), preferred_element_type=F32
         )
         pull = term if pull is None else pull + term
+    acc[...] = pull
     total = jnp.sum(sums[...], 0)
-    normed, unit_f, scale, _ = head(rows[...], total, gain[...], bias[...], batch)
-    radial = jnp.sum(unit_f * pull, 1, keepdims=True)
-    shifts = (pull - unit_f * radial) * scale
-    bias_part = jnp.sum(shifts, 0, keepdims=True)
-    gain_part = jnp.sum(shifts * normed, 0, keepdims=True)
+    bias_part = gain_part = 0.0
+    for by, piece in enumerate(found):
+        where = place_of(at, by, lines, n)
+        part = acc[pl.ds(where, n)]
+        normed, unit_f, scale, _ = head(piece[...], total, gain[...], bias[...], batch)
+        radial = jnp.sum(unit_f * part, 1, keepdims=True)
+        shifts = (part - unit_f * radial) * scale
+        bias_part = bias_part + jnp.sum(shifts, 0, keepdims=True)
+        gain_part = gain_part + jnp.sum(shifts * normed, 0, keepdims=True)
     tail = pack_ends(bias_part, gain_part).astype(BF16)
-    parts = packed.shape[0]
-    n = pull.shape[0] // parts
-    for p in range(parts):
-        packed[p, :n] = pull[p * n : (p + 1) * n].astype(BF16)
+    for p in range(lines):
+        packed[p, :n] = acc[p * n : (p + 1) * n].astype(BF16)
         packed[p, n:] = tail
 
 
@@ -146,11 +159,10 @@
         packed[p] = jnp.concatenate([piece, tail], 0).astype(BF16)
 
 
-def raw_kernel(
-    at, place, place_2, totals, unit, unit_2, w_own, _, mine, *sent
-):
-    parts = len(sent) + 1
+def raw_kernel(parts, at, place, place_2, totals, unit, unit_2, w_own, _, *refs):
+    outs, (mine, sent, sems) = refs[:parts], refs[parts:]
     block = mine.shape[0]
+    copies = []
     for i in range(parts):
         first = pl.multiple_of(lax.rem(at[0] + i, parts) * block, 64)
         w_hat = w_own[pl.ds(first, block)]
@@ -163,30 +175,45 @@
             raw = term if raw is None else raw + term
         if i == 0:
             mine[...] = raw
+            source = mine
         else:
-            sent[i - 1][...] = raw.astype(BF16)
-
-
-def project_kernel(at, picked, mine, *rest):
-    arrived, out = rest[:-1], rest[-1]
-    block = mine.shape[0]
-    raw = mine[...]
-    for piece in arrived:
+            sent[i - 1] = raw.astype(BF16)
+            source = sent.at[i - 1]
+        copies.append(pltpu.make_async_copy(source, outs[i], sems.at[i]))
+        copies[-1].start()
+    for copy in copies:
+        copy.wait()
+
+
+def project_kernel(parts, at, picked, *refs):
+    found, (out, picks_ref, sem) = refs[:parts], refs[parts:]
+    block = out.shape[0]
+    rows = pl.ds(pl.multiple_of(at[0] * block, 64), block)
+    copy = pltpu.make_async_copy(picked.at[rows], picks_ref, sem)
+    copy.start()
+    raw = found[0][...]
+    for piece in found[1:]:
         raw = raw + piece[...].astype(F32)
-    picks = picked[pl.ds(pl.multiple_of(at[0] * block, 64), block)].astype(F32)
+    copy.wait()
+    picks = picks_ref[...].astype(F32)
     inv_norm = lax.rsqrt(jnp.sum(picks * picks, 1, keepdims=True) + EPSILON)
     w_unit = picks * inv_norm
     along = jnp.sum(w_unit * raw, 1, keepdims=True)
     out[...] = ((raw - w_unit * along) * inv_norm).astype(BF16)
 
 
-def order_kernel(at, *refs):
-    found, out = refs[:-1], refs[-1]
-    parts = len(found)
+def order_kernel(parts, at, *refs):
+    found, (out, sems) = refs[:parts], refs[parts:]
     block = found[0].shape[0]
+    copies = []
     for by, piece in enumerate(found):
-        where = lax.rem(at[0] - by + parts, parts) * block
-        out[pl.ds(pl.multiple_of(where, 64), block)] = piece[...]
+        where = pl.multiple_of(lax.rem(at[0] - by + parts, parts) * block, 64)
+        copies.append(
+            pltpu.make_async_copy(piece, out.at[pl.ds(where, block)], sems.at[by])
+        )
+        copies[-1].start()
+    for copy in copies:
+        copy.wait()
 
 
 def body(embeddings, bn_gain, bn_bias, centres, sample_rows, label_shard, label_slot):
@@ -200,14 +227,16 @@
     held = nc * slots
     quarter = slots // nr
     at = ir.astype(jnp.int32).reshape(1)
+    at_x = ix.astype(jnp.int32).reshape(1)
     gain, bias = bn_gain[None], bn_bias[None]
 
     line = spread(embeddings, "z").reshape(line_rows, width)
-    rows = spread(line, "x").reshape(group, width)
-    rows_f = rows.astype(F32)
+    line_f = line.astype(F32)
     sums = spread(
-        jnp.stack([jnp.sum(rows_f, 0), jnp.sum(rows_f * rows_f, 0)]), ("core", "rep")
-    )
+        jnp.stack([jnp.sum(line_f, 0), jnp.sum(line_f * line_f, 0)]),
+        ("x", "core", "rep"),
+    )
+    lines = [line] + [shift(line, "x", by) for by in range(1, nx)]
 
     picked = jnp.take(centres, sample_rows[0], axis=0)
     picks = picked.astype(F32)
@@ -229,7 +258,9 @@
     )
 
     unit, stats = call(
-        lambda *refs: exp_kernel(batch, *refs),
+        lambda *refs: exp_kernel(batch, nx, *refs),
+        [SM] + [VM] * (6 + nx),
+        [VM] * 2,
         [
             jax.ShapeDtypeStruct((group, width), BF16),
             jax.ShapeDtypeStruct((nx * nc, 2, group), F32),
@@ -237,7 +268,7 @@
         2 * held * group * width,
         2 * held * width,
         held * group,
-    )(rows, sums, gain, bias, place, w_own, w_other)
+    )(at_x, sums, gain, bias, place, w_own, w_other, *lines)
     unit_2 = shift(unit, "core", 1)
 
     stats = lax.all_to_all(stats, ("x", "core"), 0, 0).reshape(nx, nc, 2, group)
@@ -247,47 +278,70 @@
     stats = jnp.sum(spread(stats, "z"), 0)
 
     pull = call(
-        lambda *refs: pull_kernel(batch, *refs),
+        lambda *refs: pull_kernel(batch, nx, *refs),
+        [SM] + [VM] * (8 + nx),
+        VM,
         jax.ShapeDtypeStruct((nx, line_rows + PAD, width), BF16),
         4 * held * group * width,
         2 * held * width,
         held * group,
-    )(rows, sums, gain, bias, place, stats, unit, w_own, w_other)
+        [pltpu.VMEM((group, width), F32)],
+    )(at_x, sums, gain, bias, place, stats, unit, w_own, w_other, *lines)
 
     piece = jax.ShapeDtypeStruct((quarter, width), BF16)
     mine, *sent = call(
-        raw_kernel,
+        lambda *refs: raw_kernel(nr, *refs),
+        [SM] + [VM] * 6 + [HB],
+        [HB] * nr,
         [jax.ShapeDtypeStruct((quarter, width), F32)] + [piece] * (nr - 1),
         4 * held * group * width,
         2 * held * width,
         held * group,
-        scalars=1,
-        skipped=1,
+        [
+            pltpu.VMEM((quarter, width), F32),
+            pltpu.VMEM((nr - 1, quarter, width), BF16),
+            pltpu.SemaphoreType.DMA((nr,)),
+        ],
     )(at, place, place_2, stats, unit, unit_2, w_own, pull)
     came = [shift(sent[by - 1], "rep", by) for by in range(1, nr)]
     grad = call(
-        project_kernel, piece, 20 * quarter * width, 14 * quarter * width, scalars=1
+        lambda *refs: project_kernel(nr, *refs),
+        [SM, HB] + [VM] * nr,
+        VM,
+        piece,
+        20 * quarter * width,
+        14 * quarter * width,
+        0,
+        [pltpu.VMEM((quarter, width), BF16), pltpu.SemaphoreType.DMA],
     )(at, picked, mine, *came)
-    found = [grad] + [shift(grad, "rep", by) for by in range(1, nr)]
-    centre_grad = call(
-        order_kernel,
-        jax.ShapeDtypeStruct((slots, width), BF16),
-        slots * width,
-        4 * slots * width,
-        scalars=1,
-    )(at, *found)
 
     pull = lax.all_to_all(pull, "x", 0, 0)
     pull, mine = lax.optimization_barrier((pull, mine))
     pull = call(
         lambda *refs: mid_kernel(rows_dev, *refs),
+        [VM],
+        VM,
         jax.ShapeDtypeStruct((nz, PAD, width), BF16),
         nx * line_rows * width,
         2 * nx * line_rows * width,
     )(pull)
     pull = jnp.sum(lax.all_to_all(pull, "z", 0, 0).astype(F32), 0)
     grad_unit = pull[:rows_dev]
-    ends = jnp.sum(spread(unpack_ends(pull[rows_dev:]), ("core", "rep")), 0)
+    ends = unpack_ends(pull[rows_dev:])
+    ends = jnp.broadcast_to(ends[None], (nc * nr,) + ends.shape)
+    ends, grad = lax.optimization_barrier((ends, grad))
+    ends = jnp.sum(lax.all_to_all(ends, ("core", "rep"), 0, 0), 0)
+    found = [grad] + [shift(grad, "rep", by) for by in range(1, nr)]
+    centre_grad = call(
+        lambda *refs: order_kernel(nr, *refs),
+        [SM] + [HB] * nr,
+        HB,
+        jax.ShapeDtypeStruct((slots, width), BF16),
+        slots * width,
+        4 * slots * width,
+        0,
+        [pltpu.SemaphoreType.DMA((nr,))],
+    )(at, *found)
 
     own_stats = lax.dynamic_slice_in_dim(
         stats, (ix * nz + iz) * rows_dev, rows_dev, 1

time: 161 us -> 161 us (level)
  waiting for transfers between devices: 33.6 us -> 23.3 us
  starting transfers between devices: 70.7 us -> 78.4 us
  blocking collectives: 16.2 us -> 19.4 us
  local copies, waits for them, and re-layouts: 15.3 us -> 13.2 us
  Pallas kernels: 14.1 us -> 16.1 us
    ppermute x8 -> x11, waiting for transfers between devices: 13.6 us -> 5.72 us  [shift(): return lax.ppermute(block, axis, [(i, (i + by) % n) for i in range(n)])]
    all_to_all x4 -> x2, waiting for transfers between devices: 15.3 us -> 8.17 us  [spread(): return lax.all_to_all(copies, axes, 0, 0)]
    all_to_all x0 -> x1, starting transfers between devices: none -> 6.58 us  [body(): ends = jnp.sum(lax.all_to_all(ends, ('core', 'rep'), 0, 0), 0)]
    ppermute x8 -> x11, starting transfers between devices: 26.7 us -> 32.5 us  [shift(): return lax.ppermute(block, axis, [(i, (i + by) % n) for i in range(n)])]
    all_to_all x0 -> x1, waiting for transfers between devices: none -> 4.74 us  [body(): ends = jnp.sum(lax.all_to_all(ends, ('core', 'rep'), 0, 0), 0)]
    all_to_all x4 -> x2, starting transfers between devices: 31.2 us -> 26.7 us  [spread(): return lax.all_to_all(copies, axes, 0, 0)]
    all_to_all x1, blocking collectives: 16.2 us -> 19.4 us  [spread(): return lax.all_to_all(copies, axes, 0, 0)]
    pallas_call x6, Pallas kernels: 14.1 us -> 16.1 us  [the longest x1 5.85 us: body(): call(lambda *refs: raw_kernel(nr, *refs), [SM] + [VM] * 6 + [HB], [HB] *...]
  transfers between devices with their start and end apart: 15 -> 17, of which waited for: 8 -> 6; matrix products, arithmetic and copies ran while one was open for 8% -> 7% of each run, Pallas kernels for 3% -> 4%
where the time goes in v5:
time: 161 us; the launch traced here: 160 us
  starting transfers between devices  78.4 us (49%)
  waiting for transfers between devices  23.3 us (14%)
  blocking collectives  19.4 us (12%)
  Pallas kernels  16.1 us (10%)
  local copies, waits for them, and re-layouts  13.2 us (8%)
  other arithmetic  8.24 us (5%)
    ppermute x11, starting transfers between devices, shift(): return lax.ppermute(block, axis, [(i, (i + by) % n) for i in range(n)])  32.5 us
    all_to_all x2, starting transfers between devices, spread(): return lax.all_to_all(copies, axes, 0, 0)  26.7 us
    all_to_all x1, blocking collectives, spread(): return lax.all_to_all(copies, axes, 0, 0)  19.4 us
    all_to_all x2, waiting for transfers between devices, spread(): return lax.all_to_all(copies, axes, 0, 0)  8.17 us
    all_to_all x1, starting transfers between devices, body(): ends = jnp.sum(lax.all_to_all(ends, ('core', 'rep'), 0, 0), 0)  6.58 us
    unnamed x36, local copies, waits for them, and re-layouts  6.55 us
    all_to_all x1, starting transfers between devices, body(): pull = jnp.sum(lax.all_to_all(pull, 'z', 0, 0).astype(F32), 0)  5.91 us
    pallas_call x1, Pallas kernels, body(): call(lambda *refs: raw_kernel(nr, *refs), [SM] + [VM] * 6 + [HB], [HB] *...  5.85 us
  transfers between devices with their start and end apart: 17, of which 6 were waited for; matrix products, arithmetic and copies ran while one was open for 7% of the time, Pallas kernels for 4%

profile of v5, /device:TPU:1, one launch (start us, length us, event | category | flops | bytes accessed | tf_op | source)
XLA Modules:
  0.0 159.8 jit_solution(18085435258958134721)
XLA Ops:
  2.2 15.7 %all-to-all-start = ((bf16[16,8,512]{2,1,0:T(8,128)(2,1)}), bf16[16,8,512]{2,1,0:T(8,128)(2,1)S(1)}, u32[]{:S(2)}, u32[]{:S(2)}) async-start(bf16[16,8,512]{2,1,0:T(8,128)(2,1)} %broadcast_in_dim.33), calls=%async_computation | async-start | bytes 262144 | tf_op jit(solution)/shard_map/all_to_all | solution.py:19
  19.3 3.3 %gather_fusion = bf16[768,512]{1,0:T(8,128)(2,1)} fusion(bf16[2048,512]{1,0:T(8,128)(2,1)S(1)} %copy-done, s32[1024]{0:T(1024)S(1)} %pad_clamp_fusion), kind=kCustom, calls=%fused_computation | custom fusion | bytes 1575936 | tf_op jit(solution)/shard_map/jit(_take)/gather | solution.py:241
  25.4 2.9 %collective-permute-start = (bf16[768,512]{1,0:T(8,128)(2,1)}, bf16[768,512]{1,0:T(8,128)(2,1)}, u32[]{:S(2)}, u32[]{:S(2)}) collective-permute-start(bf16[768,512]{1,0:T(8,128)(2,1)} %fusion.1.refs_5_.refs_7_.refs_6_), channel_id=1, source_target_pairs={{0,4},{4,0},{1,5},{5,1},{2,6},{6,2},{3,7},{7,3},{8,12},{12,8},{9,1... | collective-permute-start | bytes 2359304 | tf_op jit(solution)/shard_map/ppermute | solution.py:24
  29.9 4.4 %collective-permute-start.3 = (bf16[128,512]{1,0:T(8,128)(2,1)S(1)}, bf16[128,512]{1,0:T(8,128)(2,1)S(1)}, u32[]{:S(2)}, u32[]{:S(2)}) collective-permute-start(bf16[128,512]{1,0:T(8,128)(2,1)S(1)} %bitcast.20), channel_id=1, source_target_pairs={{0,384},{128,0},{256,128},{384,256},{1,385},{129,1},{257,129},{385... | collective-permute-start | bytes 393224 | tf_op jit(solution)/shard_map/ppermute | solution.py:24
  34.3 2.4 %collective-permute-start.2 = (bf16[128,512]{1,0:T(8,128)(2,1)S(1)}, bf16[128,512]{1,0:T(8,128)(2,1)S(1)}, u32[]{:S(2)}, u32[]{:S(2)}) collective-permute-start(bf16[128,512]{1,0:T(8,128)(2,1)S(1)} %bitcast.21), channel_id=1, source_target_pairs={{0,256},{128,384},{256,0},{384,128},{1,257},{129,385},{257,1},{385... | collective-permute-start | bytes 393224 | tf_op jit(solution)/shard_map/ppermute | solution.py:24
  36.7 2.5 %collective-permute-start.1 = (bf16[128,512]{1,0:T(8,128)(2,1)S(1)}, bf16[128,512]{1,0:T(8,128)(2,1)}, u32[]{:S(2)}, u32[]{:S(2)}) collective-permute-start(bf16[128,512]{1,0:T(8,128)(2,1)S(1)} %bitcast.22), channel_id=1, source_target_pairs={{0,128},{128,256},{256,384},{384,0},{1,129},{129,257},{257,385},{3... | collective-permute-start | bytes 393224 | tf_op jit(solution)/shard_map/ppermute | solution.py:24
  40.0 10.9 %all-to-all-start.1 = ((f32[32,2,512]{2,1,0:T(2,128)}), f32[32,2,512]{2,1,0:T(2,128)S(1)}, u32[]{:S(2)}, u32[]{:S(2)}) async-start(f32[32,2,512]{2,1,0:T(2,128)} %broadcast_in_dim.60), calls=%async_computation.1 | async-start | bytes 262144 | tf_op jit(solution)/shard_map/all_to_all | solution.py:19
  50.9 7.6 %all-to-all-done.1.refs_1_ = f32[32,2,512]{2,1,0:T(2,128)S(1)} async-done(((f32[32,2,512]{2,1,0:T(2,128)}), f32[32,2,512]{2,1,0:T(2,128)S(1)}, u32[]{:S(2)}, u32[]{:S(2)}) %all-to-all-start.1) | async-done | bytes 131104 | tf_op jit(solution)/shard_map/all_to_all | solution.py:19
  58.5 3.7 %shard_map.110 = (bf16[512,512]{1,0:T(8,128)(2,1)}, f32[8,2,512]{2,1,0:T(2,128)}) custom-call(s32[1]{0:T(128)} %bitcast.refs_0_, f32[32,2,512]{2,1,0:T(2,128)S(1)} %all-to-all-done.1.refs_1_, f32[1,512]{1,0:T(1,128)S(1)} %bitcast.25, f32[1,512]{1,0:T(1,128)S(1)} %bitcast.27, s32[1,512]{1,0:T(1,128)S(1)} %select_select_fusion.refs_4_.refs_1_, ...), custom_call_target="tpu_custom_call" | custom-call | flops 805306368 | bytes 1572864 | tf_op jit(solution)/shard_map/pallas_call | solution.py:260
  62.3 2.4 %collective-permute-start.4 = (bf16[512,512]{1,0:T(8,128)(2,1)}, bf16[512,512]{1,0:T(8,128)(2,1)}, u32[]{:S(2)}, u32[]{:S(2)}) collective-permute-start(bf16[512,512]{1,0:T(8,128)(2,1)} %get-tuple-element.17.refs_6_.refs_4_), channel_id=1, source_target_pairs={{0,4},{4,0},{1,5},{5,1},{2,6},{6,2},{3,7},{7,3},{8,12},{12,8},{9,1... | collective-permute-start | bytes 1572872 | tf_op jit(solution)/shard_map/ppermute | solution.py:24
  64.7 3.3 %all-to-all-start.2 = ((f32[8,2,512]{2,1,0:T(2,128)}), f32[8,2,512]{2,1,0:T(2,128)S(1)}, u32[]{:S(2)}, u32[]{:S(2)}) async-start(f32[8,2,512]{2,1,0:T(2,128)} %get-tuple-element.16), calls=%async_computation.2 | async-start | bytes 65536 | tf_op jit(solution)/shard_map/all_to_all | solution.py:274
  68.0 4.7 %all-to-all-done.2 = f32[8,2,512]{2,1,0:T(2,128)S(1)} async-done(((f32[8,2,512]{2,1,0:T(2,128)}), f32[8,2,512]{2,1,0:T(2,128)S(1)}, u32[]{:S(2)}, u32[]{:S(2)}) %all-to-all-start.2) | async-done | bytes 32800 | tf_op jit(solution)/shard_map/all_to_all | solution.py:274
  72.8 19.4 %all_to_all.35 = f32[16,4,512]{2,1,0:T(4,128)} all-to-all(f32[16,4,512]{2,1,0:T(4,128)S(1)} %broadcast_in_dim.66), channel_id=1, replica_groups=mesh['x'=4,'z'=16,'core'=2,'rep'=4] {'z'}, dimensions={0} | all-to-all | bytes 262144 | tf_op jit(solution)/shard_map/all_to_all | solution.py:19
  93.1 5.0 %shard_map.111.refs_7_ = bf16[4,144,512]{2,1,0:T(8,128)(2,1)S(1)} custom-call(s32[1]{0:T(128)} %bitcast.refs_0_, f32[32,2,512]{2,1,0:T(2,128)S(1)} %all-to-all-done.1.refs_1_, f32[1,512]{1,0:T(1,128)S(1)} %bitcast.26, f32[1,512]{1,0:T(1,128)S(1)} %bitcast.28, s32[1,512]{1,0:T(1,128)S(1)} %select_select_fusion.refs_4_.refs_1_, ...), custom_call_target="tpu_custom_call" | custom-call | flops 1610612736 | bytes 1572864 | tf_op jit(solution)/shard_map/pallas_call | solution.py:280
  98.9 3.5 %all-to-all-start.4 = ((bf16[4,144,512]{2,1,0:T(8,128)(2,1)}), bf16[4,144,512]{2,1,0:T(8,128)(2,1)S(1)}, u32[]{:S(2)}, u32[]{:S(2)}) async-start(bf16[4,144,512]{2,1,0:T(8,128)(2,1)} %copy-done.2), calls=%async_computation.4 | async-start | bytes 1179648 | tf_op jit(solution)/shard_map/all_to_all | solution.py:318
  103.6 5.8 %shard_map.112 = (f32[192,512]{1,0:T(8,128)S(1)}, bf16[192,512]{1,0:T(8,128)(2,1)S(1)}, bf16[192,512]{1,0:T(8,128)(2,1)S(1)}, bf16[192,512]{1,0:T(8,128)(2,1)S(1)}) custom-call(s32[1]{0:T(128)} %bitcast.12.refs_0_, s32[1,512]{1,0:T(1,128)S(1)} %select_select_fusion.refs_4_.refs_1_, s32[1,512]{1,0:T(1,128)S(1)} %select_n.72.refs_2_, ...), custom_call_target="tpu_custom_call" | custom-call | flops 1610612736 | bytes 1572864 | tf_op jit(solution)/shard_map/pallas_call | solution.py:292
  113.0 5.9 %all-to-all-start.5 = ((bf16[16,16,512]{2,1,0:T(8,128)(2,1)}), bf16[16,16,512]{2,1,0:T(8,128)(2,1)S(1)}, u32[]{:S(2)}, u32[]{:S(2)}) async-start(bf16[16,16,512]{2,1,0:T(8,128)(2,1)} %copy-done.1), calls=%async_computation.5 | async-start | bytes 524288 | tf_op jit(solution)/shard_map/all_to_all | solution.py:328
  122.3 3.8 %collective-permute-start.6 = (bf16[192,512]{1,0:T(8,128)(2,1)}, bf16[192,512]{1,0:T(8,128)(2,1)S(1)}, u32[]{:S(2)}, u32[]{:S(2)}) collective-permute-start(bf16[192,512]{1,0:T(8,128)(2,1)} %copy-done.10), channel_id=1, source_target_pairs={{0,2},{1,3},{2,0},{3,1},{4,6},{5,7},{6,4},{7,5},{8,10},{9,11},{10,... | collective-permute-start | bytes 589832 | tf_op jit(solution)/shard_map/ppermute | solution.py:24
  126.1 2.7 %collective-permute-start.7 = (bf16[192,512]{1,0:T(8,128)(2,1)}, bf16[192,512]{1,0:T(8,128)(2,1)S(1)}, u32[]{:S(2)}, u32[]{:S(2)}) collective-permute-start(bf16[192,512]{1,0:T(8,128)(2,1)} %copy-done.9), channel_id=1, source_target_pairs={{0,3},{1,0},{2,1},{3,2},{4,7},{5,4},{6,5},{7,6},{8,11},{9,8},{10,9... | collective-permute-start | bytes 589832 | tf_op jit(solution)/shard_map/ppermute | solution.py:24
  129.4 3.4 %collective-permute-done.6.refs_4_ = bf16[192,512]{1,0:T(8,128)(2,1)S(1)} collective-permute-done((bf16[192,512]{1,0:T(8,128)(2,1)}, bf16[192,512]{1,0:T(8,128)(2,1)S(1)}, u32[]{:S(2)}, u32[]{:S(2)}) %collective-permute-start.6) | collective-permute-done | bytes 196640 | tf_op jit(solution)/shard_map/ppermute | solution.py:24
  132.8 2.3 %collective-permute-done.7.refs_5_ = bf16[192,512]{1,0:T(8,128)(2,1)S(1)} collective-permute-done((bf16[192,512]{1,0:T(8,128)(2,1)}, bf16[192,512]{1,0:T(8,128)(2,1)S(1)}, u32[]{:S(2)}, u32[]{:S(2)}) %collective-permute-start.7) | collective-permute-done | bytes 196640 | tf_op jit(solution)/shard_map/ppermute | solution.py:24
  137.4 4.7 %collective-permute-start.10 = (bf16[192,512]{1,0:T(8,128)(2,1)S(1)}, bf16[192,512]{1,0:T(8,128)(2,1)S(1)}, u32[]{:S(2)}, u32[]{:S(2)}) collective-permute-start(bf16[192,512]{1,0:T(8,128)(2,1)S(1)} %shard_map.114.refs_1_), channel_id=1, source_target_pairs={{0,3},{1,0},{2,1},{3,2},{4,7},{5,4},{6,5},{7,6},{8,11},{9,8},{10,9... | collective-permute-start | bytes 589832 | tf_op jit(solution)/shard_map/ppermute | solution.py:24
  146.6 6.6 %all-to-all-start.6 = ((f32[8,2,512]{2,1,0:T(2,128)}), f32[8,2,512]{2,1,0:T(2,128)S(1)}, u32[]{:S(2)}, u32[]{:S(2)}) async-start(f32[8,2,512]{2,1,0:T(2,128)} %broadcast_in_dim.70), calls=%async_computation.6 | async-start | bytes 65536 | tf_op jit(solution)/shard_map/all_to_all | solution.py:333
  153.3 4.7 %all-to-all-done.6 = f32[8,2,512]{2,1,0:T(2,128)S(1)} async-done(((f32[8,2,512]{2,1,0:T(2,128)}), f32[8,2,512]{2,1,0:T(2,128)S(1)}, u32[]{:S(2)}, u32[]{:S(2)}) %all-to-all-start.6) | async-done | bytes 32800 | tf_op jit(solution)/shard_map/all_to_all | solution.py:333
  (92 shorter events, 27.0 us)
Async XLA Ops:
  0.6 18.7 %copy-start = (bf16[2048,512]{1,0:T(8,128)(2,1)S(1)}, bf16[2048,512]{1,0:T(8,128)(2,1)}, u32[]{:S(2)}) copy-start(bf16[2048,512]{1,0:T(8,128)(2,1)} %param.10) | copy-start | bytes 6291460
  2.2 27.8 %all-to-all-start = ((bf16[16,8,512]{2,1,0:T(8,128)(2,1)}), bf16[16,8,512]{2,1,0:T(8,128)(2,1)S(1)}, u32[]{:S(2)}, u32[]{:S(2)}) async-start(bf16[16,8,512]{2,1,0:T(8,128)(2,1)} %broadcast_in_dim.33), calls=%async_computation | async-start | bytes 262144 | tf_op jit(solution)/shard_map/all_to_all | solution.py:19
  22.7 5.7 %copy-start.15 = (s32[128,1,8]{0,2,1:T(8,128)S(1)}, s32[128,1,8]{0,2,1:T(8,128)}, u32[]{:S(2)}) copy-start(s32[128,1,8]{0,2,1:T(8,128)} %param.12) | copy-start | bytes 12292
  22.7 6.2 %copy-start.16 = (s32[128,1,8]{0,2,1:T(8,128)S(1)}, s32[128,1,8]{0,2,1:T(8,128)}, u32[]{:S(2)}) copy-start(s32[128,1,8]{0,2,1:T(8,128)} %param.13) | copy-start | bytes 12292
  24.3 34.2 %copy-start.7 = (f32[512]{0:T(512)S(1)}, f32[512]{0:T(512)}, u32[]{:S(2)}) copy-start(f32[512]{0:T(512)} %param.8) | copy-start | bytes 6148
  24.3 34.2 %copy-start.8 = (f32[512]{0:T(512)S(1)}, f32[512]{0:T(512)}, u32[]{:S(2)}) copy-start(f32[512]{0:T(512)} %param.9) | copy-start | bytes 6148
  25.4 33.1 %collective-permute-start = (bf16[768,512]{1,0:T(8,128)(2,1)}, bf16[768,512]{1,0:T(8,128)(2,1)}, u32[]{:S(2)}, u32[]{:S(2)}) collective-permute-start(bf16[768,512]{1,0:T(8,128)(2,1)} %fusion.1.refs_5_.refs_7_.refs_6_), channel_id=1, source_target_pairs={{0,4},{4,0},{1,5},{5,1},{2,6},{6,2},{3,7},{7,3},{8,12},{12,8},{9,1... | collective-permute-start | bytes 2359304 | tf_op jit(solution)/shard_map/ppermute | solution.py:24
  29.9 28.6 %collective-permute-start.3 = (bf16[128,512]{1,0:T(8,128)(2,1)S(1)}, bf16[128,512]{1,0:T(8,128)(2,1)S(1)}, u32[]{:S(2)}, u32[]{:S(2)}) collective-permute-start(bf16[128,512]{1,0:T(8,128)(2,1)S(1)} %bitcast.20), channel_id=1, source_target_pairs={{0,384},{128,0},{256,128},{384,256},{1,385},{129,1},{257,129},{385... | collective-permute-start | bytes 393224 | tf_op jit(solution)/shard_map/ppermute | solution.py:24
  34.3 24.2 %collective-permute-start.2 = (bf16[128,512]{1,0:T(8,128)(2,1)S(1)}, bf16[128,512]{1,0:T(8,128)(2,1)S(1)}, u32[]{:S(2)}, u32[]{:S(2)}) collective-permute-start(bf16[128,512]{1,0:T(8,128)(2,1)S(1)} %bitcast.21), channel_id=1, source_target_pairs={{0,256},{128,384},{256,0},{384,128},{1,257},{129,385},{257,1},{385... | collective-permute-start | bytes 393224 | tf_op jit(solution)/shard_map/ppermute | solution.py:24
  36.7 21.8 %collective-permute-start.1 = (bf16[128,512]{1,0:T(8,128)(2,1)S(1)}, bf16[128,512]{1,0:T(8,128)(2,1)}, u32[]{:S(2)}, u32[]{:S(2)}) collective-permute-start(bf16[128,512]{1,0:T(8,128)(2,1)S(1)} %bitcast.22), channel_id=1, source_target_pairs={{0,128},{128,256},{256,384},{384,0},{1,129},{129,257},{257,385},{3... | collective-permute-start | bytes 393224 | tf_op jit(solution)/shard_map/ppermute | solution.py:24
  40.0 18.5 %all-to-all-start.1 = ((f32[32,2,512]{2,1,0:T(2,128)}), f32[32,2,512]{2,1,0:T(2,128)S(1)}, u32[]{:S(2)}, u32[]{:S(2)}) async-start(f32[32,2,512]{2,1,0:T(2,128)} %broadcast_in_dim.60), calls=%async_computation.1 | async-start | bytes 262144 | tf_op jit(solution)/shard_map/all_to_all | solution.py:19
  58.5 34.6 %copy-start.4 = (f32[32,2,512]{2,1,0:T(2,128)}, f32[32,2,512]{2,1,0:T(2,128)S(1)}, u32[]{:S(2)}) copy-start(f32[32,2,512]{2,1,0:T(2,128)S(1)} %all-to-all-done.1.refs_1_) | copy-start | bytes 393220
  62.3 10.5 %collective-permute-start.4 = (bf16[512,512]{1,0:T(8,128)(2,1)}, bf16[512,512]{1,0:T(8,128)(2,1)}, u32[]{:S(2)}, u32[]{:S(2)}) collective-permute-start(bf16[512,512]{1,0:T(8,128)(2,1)} %get-tuple-element.17.refs_6_.refs_4_), channel_id=1, source_target_pairs={{0,4},{4,0},{1,5},{5,1},{2,6},{6,2},{3,7},{7,3},{8,12},{12,8},{9,1... | collective-permute-start | bytes 1572872 | tf_op jit(solution)/shard_map/ppermute | solution.py:24
  64.7 8.0 %all-to-all-start.2 = ((f32[8,2,512]{2,1,0:T(2,128)}), f32[8,2,512]{2,1,0:T(2,128)S(1)}, u32[]{:S(2)}, u32[]{:S(2)}) async-start(f32[8,2,512]{2,1,0:T(2,128)} %get-tuple-element.16), calls=%async_computation.2 | async-start | bytes 65536 | tf_op jit(solution)/shard_map/all_to_all | solution.py:274
  98.9 13.3 %all-to-all-start.4 = ((bf16[4,144,512]{2,1,0:T(8,128)(2,1)}), bf16[4,144,512]{2,1,0:T(8,128)(2,1)S(1)}, u32[]{:S(2)}, u32[]{:S(2)}) async-start(bf16[4,144,512]{2,1,0:T(8,128)(2,1)} %copy-done.2), calls=%async_computation.4 | async-start | bytes 1179648 | tf_op jit(solution)/shard_map/all_to_all | solution.py:318
  103.6 16.3 %copy-start.12 = (bf16[8,512]{1,0:T(8,128)(2,1)S(1)}, bf16[8,512]{1,0:T(8,128)(2,1)}, u32[]{:S(2)}) copy-start(bf16[8,512]{1,0:T(8,128)(2,1)} %param.7) | copy-start | bytes 24580
  113.0 23.7 %all-to-all-start.5 = ((bf16[16,16,512]{2,1,0:T(8,128)(2,1)}), bf16[16,16,512]{2,1,0:T(8,128)(2,1)S(1)}, u32[]{:S(2)}, u32[]{:S(2)}) async-start(bf16[16,16,512]{2,1,0:T(8,128)(2,1)} %copy-done.1), calls=%async_computation.5 | async-start | bytes 524288 | tf_op jit(solution)/shard_map/all_to_all | solution.py:328
  120.0 9.4 %collective-permute-start.5 = (bf16[192,512]{1,0:T(8,128)(2,1)}, bf16[192,512]{1,0:T(8,128)(2,1)S(1)}, u32[]{:S(2)}, u32[]{:S(2)}) collective-permute-start(bf16[192,512]{1,0:T(8,128)(2,1)} %copy-done.11), channel_id=1, source_target_pairs={{0,1},{1,2},{2,3},{3,0},{4,5},{5,6},{6,7},{7,4},{8,9},{9,10},{10,1... | collective-permute-start | bytes 589832 | tf_op jit(solution)/shard_map/ppermute | solution.py:24
  122.3 10.5 %collective-permute-start.6 = (bf16[192,512]{1,0:T(8,128)(2,1)}, bf16[192,512]{1,0:T(8,128)(2,1)S(1)}, u32[]{:S(2)}, u32[]{:S(2)}) collective-permute-start(bf16[192,512]{1,0:T(8,128)(2,1)} %copy-done.10), channel_id=1, source_target_pairs={{0,2},{1,3},{2,0},{3,1},{4,6},{5,7},{6,4},{7,5},{8,10},{9,11},{10,... | collective-permute-start | bytes 589832 | tf_op jit(solution)/shard_map/ppermute | solution.py:24
  126.1 9.0 %collective-permute-start.7 = (bf16[192,512]{1,0:T(8,128)(2,1)}, bf16[192,512]{1,0:T(8,128)(2,1)S(1)}, u32[]{:S(2)}, u32[]{:S(2)}) collective-permute-start(bf16[192,512]{1,0:T(8,128)(2,1)} %copy-done.9), channel_id=1, source_target_pairs={{0,3},{1,0},{2,1},{3,2},{4,7},{5,4},{6,5},{7,6},{8,11},{9,8},{10,9... | collective-permute-start | bytes 589832 | tf_op jit(solution)/shard_map/ppermute | solution.py:24
  137.4 21.4 %collective-permute-start.10 = (bf16[192,512]{1,0:T(8,128)(2,1)S(1)}, bf16[192,512]{1,0:T(8,128)(2,1)S(1)}, u32[]{:S(2)}, u32[]{:S(2)}) collective-permute-start(bf16[192,512]{1,0:T(8,128)(2,1)S(1)} %shard_map.114.refs_1_), channel_id=1, source_target_pairs={{0,3},{1,0},{2,1},{3,2},{4,7},{5,4},{6,5},{7,6},{8,11},{9,8},{10,9... | collective-permute-start | bytes 589832 | tf_op jit(solution)/shard_map/ppermute | solution.py:24
  142.2 16.7 %collective-permute-start.9 = (bf16[192,512]{1,0:T(8,128)(2,1)S(1)}, bf16[192,512]{1,0:T(8,128)(2,1)S(1)}, u32[]{:S(2)}, u32[]{:S(2)}) collective-permute-start(bf16[192,512]{1,0:T(8,128)(2,1)S(1)} %shard_map.114.refs_1_), channel_id=1, source_target_pairs={{0,2},{1,3},{2,0},{3,1},{4,6},{5,7},{6,4},{7,5},{8,10},{9,11},{10,... | collective-permute-start | bytes 589832 | tf_op jit(solution)/shard_map/ppermute | solution.py:24
  144.4 14.5 %collective-permute-start.8 = (bf16[192,512]{1,0:T(8,128)(2,1)S(1)}, bf16[192,512]{1,0:T(8,128)(2,1)S(1)}, u32[]{:S(2)}, u32[]{:S(2)}) collective-permute-start(bf16[192,512]{1,0:T(8,128)(2,1)S(1)} %shard_map.114.refs_1_), channel_id=1, source_target_pairs={{0,1},{1,2},{2,3},{3,0},{4,5},{5,6},{6,7},{7,4},{8,9},{9,10},{10,1... | collective-permute-start | bytes 589832 | tf_op jit(solution)/shard_map/ppermute | solution.py:24
  146.6 11.5 %all-to-all-start.6 = ((f32[8,2,512]{2,1,0:T(2,128)}), f32[8,2,512]{2,1,0:T(2,128)S(1)}, u32[]{:S(2)}, u32[]{:S(2)}) async-start(f32[8,2,512]{2,1,0:T(2,128)} %broadcast_in_dim.70), calls=%async_computation.6 | async-start | bytes 65536 | tf_op jit(solution)/shard_map/all_to_all | solution.py:333
  (10 other events, 9.7 us)

commit v6 on v5

v6 whole, which is shorter than its diff:
```python
import jax
import jax.numpy as jnp
from jax import lax
from jax.experimental import pallas as pl
from jax.experimental.pallas import tpu as pltpu
from jax.sharding import Mesh, PartitionSpec as P

LOGIT_SCALE = 64.0
MARGIN = 0.4
EPSILON = 1e-05
F32 = jnp.float32
BF16 = jnp.bfloat16
LARGE = 60 * 1024 * 1024
SMALL = 20 * 1024 * 1024
PAD = 16


def spread(block, axes):
    copies = jnp.broadcast_to(block[None], (lax.axis_size(axes),) + block.shape)
    return lax.all_to_all(copies, axes, 0, 0)


def shift(block, axis, by):
    n = lax.axis_size(axis)
    return lax.ppermute(block, axis, [(i, (i + by) % n) for i in range(n)])


def head(inputs, sums, gain, bias, batch_total):
    mean = sums[0:1] / batch_total
    inv_std = lax.rsqrt(sums[1:2] / batch_total - mean * mean + EPSILON)
    normed = (inputs.astype(F32) - mean) * inv_std
    shifted = normed * gain + bias
    scale = lax.rsqrt(jnp.sum(shifted * shifted, 1, keepdims=True) + EPSILON)
    return normed, shifted * scale, scale, inv_std


VM = pl.BlockSpec(memory_space=pltpu.VMEM)
SM = pl.BlockSpec(memory_space=pltpu.SMEM)
HB = pl.BlockSpec(memory_space=pl.ANY)
HO = pl.BlockSpec(memory_space=pltpu.HBM)


def call(kernel, ins, outs, shapes, flops, size, exps=0, scratch=(), grant=LARGE):
    return pl.pallas_call(
        kernel,
        in_specs=ins,
        out_specs=outs,
        out_shape=shapes,
        scratch_shapes=list(scratch),
        compiler_params=pltpu.CompilerParams(vmem_limit_bytes=grant),
        cost_estimate=pl.CostEstimate(
            flops=flops, bytes_accessed=size, transcendentals=exps
        ),
    )


def hits(place, block, count, first):
    return place == lax.broadcasted_iota(jnp.int32, (block, count), 0) + first


def logits_of(w_hat, unit, place, first):
    cosine = lax.dot_general(
        w_hat, unit, (((1,), (1,)), ((), ())), preferred_element_type=F32
    )
    target = hits(place, w_hat.shape[0], unit.shape[0], first)
    return LOGIT_SCALE * cosine - jnp.where(target, LOGIT_SCALE * MARGIN, 0.0), target


def grad_of(w_hat, unit, place, first, total):
    logits, target = logits_of(w_hat, unit, place, first)
    return (jnp.exp(logits) / total - target.astype(F32)).astype(BF16)


def blocks_of(w_own, w_other):
    block = w_own.shape[0] // 2
    for i in range(4):
        source = w_own if i < 2 else w_other
        yield source[(i % 2) * block : (i % 2 + 1) * block], i * block


def exp_kernel(batch, rows, sums, gain, bias, place, w_own, w_other, unit, stats):
    total = jnp.sum(sums[...], 0)
    units = head(rows[...], total, gain[...], bias[...], batch)[1].astype(BF16)
    unit[...] = units
    exps = hit = None
    for w_hat, first in blocks_of(w_own, w_other):
        logits, target = logits_of(w_hat, units, place[...], first)
        term = jnp.sum(jnp.exp(logits), 0, keepdims=True)
        other = jnp.sum(jnp.where(target, logits, 0.0), 0, keepdims=True)
        exps = term if exps is None else exps + term
        hit = other if hit is None else hit + other
    both = jnp.concatenate([exps, hit], 0)
    for p in range(stats.shape[0]):
        stats[p] = both


def pull_kernel(
    batch, rows, sums, gain, bias, place, totals, unit, w_own, w_other, packed
):
    units = unit[...]
    row_total = jnp.sum(totals[...], 0)[0:1, : units.shape[0]]
    pull = None
    for w_hat, first in blocks_of(w_own, w_other):
        grad = grad_of(w_hat, units, place[...], first, row_total)
        term = lax.dot_general(
            grad, w_hat, (((0,), (0,)), ((), ())), preferred_element_type=F32
        )
        pull = term if pull is None else pull + term
    total = jnp.sum(sums[...], 0)
    normed, unit_f, scale, _ = head(rows[...], total, gain[...], bias[...], batch)
    radial = jnp.sum(unit_f * pull, 1, keepdims=True)
    shifts = (pull - unit_f * radial) * scale
    bias_part = jnp.sum(shifts, 0, keepdims=True)
    gain_part = jnp.sum(shifts * normed, 0, keepdims=True)
    tail = tail_of(bias_part, gain_part)
    parts = packed.shape[0]
    n = pull.shape[0] // parts
    for p in range(parts):
        packed[p, :n] = pull[p * n : (p + 1) * n].astype(BF16)
        packed[p, n:] = tail


def tail_of(bias_part, gain_part):
    pieces = split(bias_part, 3) + split(gain_part, 3)
    fill = jnp.zeros((PAD - 6, bias_part.shape[1]), F32)
    return jnp.concatenate(pieces + [fill], 0).astype(BF16)


def sums_of(tail):
    return jnp.concatenate(
        [jnp.sum(tail[k : k + 3], 0, keepdims=True) for k in (0, 3)], 0
    )


def split(value, count):
    pieces = []
    for _ in range(count):
        piece = value.astype(BF16).astype(F32)
        value = value - piece
        pieces.append(piece)
    return pieces


def total_kernel(lines, at, arrived, out):
    group = arrived.shape[2]
    n = group // lines
    place = at[0] * n if n % 128 else pl.multiple_of(at[0] * n, 128)
    own = other = hit = 0.0
    for x in range(lines):
        own = own + arrived[2 * x + at[1], 0:1]
        other = other + arrived[2 * x + 1 - at[1], 0:1]
        hit = hit + arrived[2 * x + at[1], 1:2, pl.ds(place, n)]
    both = jnp.concatenate(
        [
            jnp.concatenate([own, hit], 1),
            jnp.concatenate([other, jnp.zeros_like(hit)], 1),
        ],
        0,
    )
    for p in range(out.shape[0]):
        out[p] = both


def mid_kernel(rows_dev, arrived, packed):
    lines, _, lane = packed.shape
    total = jnp.sum(arrived[...].astype(F32), 0)
    width = total.shape[1]
    cuts = [slice(k, k + lane) for k in range(0, width, lane)]
    ends = sums_of(total[lines * rows_dev :])
    rows = split(ends[0:1], 2) + split(ends[1:2], 2)
    tail = [row[:, cut] for row in rows for cut in cuts]
    for p in range(lines):
        piece = total[p * rows_dev : (p + 1) * rows_dev]
        packed[p] = jnp.concatenate([piece[:, c] for c in cuts] + tail, 0).astype(BF16)


def home_kernel(rows_dev, arrived, grad, ends):
    total = jnp.sum(arrived[...].astype(F32), 0)
    lane = total.shape[1]
    n = grad.shape[1] // lane
    grad[...] = jnp.concatenate(
        [total[k * rows_dev : (k + 1) * rows_dev] for k in range(n)], 1
    )
    tail = total[n * rows_dev :]
    rows = []
    for v in range(2):
        both = tail[2 * v * n : (2 * v + 1) * n] + tail[(2 * v + 1) * n : (2 * v + 2) * n]
        rows.append(jnp.concatenate([both[k : k + 1] for k in range(n)], 1))
    ends[...] = jnp.concatenate(rows, 0)


def raw_kernel(parts, at, place, place_2, totals, unit, unit_2, w_own, _, *refs):
    outs, (mine, sent, sems) = refs[:parts], refs[parts:]
    block = mine.shape[0]
    copies = []
    group = unit.shape[0]
    total = jnp.sum(totals[...], 0)
    for i in range(parts):
        first = pl.multiple_of(lax.rem(at[0] + i, parts) * block, 64)
        w_hat = w_own[pl.ds(first, block)]
        raw = None
        for units, places, row in ((unit, place, 0), (unit_2, place_2, 1)):
            grad = grad_of(
                w_hat, units[...], places[...], first, total[row : row + 1, :group]
            )
            term = jnp.dot(grad, units[...], preferred_element_type=F32)
            raw = term if raw is None else raw + term
        if i == 0:
            mine[...] = raw
            source = mine
        else:
            sent[i - 1] = raw.astype(BF16)
            source = sent.at[i - 1]
        copies.append(pltpu.make_async_copy(source, outs[i], sems.at[i]))
        copies[-1].start()
    for copy in copies:
        copy.wait()


def project_kernel(parts, at, picked, ends, ends_2, *refs):
    found, (packed, picks_ref, sem) = refs[:parts], refs[parts:]
    block = picks_ref.shape[0]
    rows = pl.ds(pl.multiple_of(at[0] * block, 64), block)
    copy = pltpu.make_async_copy(picked.at[rows], picks_ref, sem)
    copy.start()
    raw = found[0][...]
    for piece in found[1:]:
        raw = raw + piece[...].astype(F32)
    both = ends[...] + ends_2[...]
    tail = tail_of(both[0:1], both[1:2])
    copy.wait()
    picks = picks_ref[...].astype(F32)
    inv_norm = lax.rsqrt(jnp.sum(picks * picks, 1, keepdims=True) + EPSILON)
    w_unit = picks * inv_norm
    along = jnp.sum(w_unit * raw, 1, keepdims=True)
    grad = ((raw - w_unit * along) * inv_norm).astype(BF16)
    for p in range(parts):
        packed[p, :block] = grad
        packed[p, block:] = tail


def final_kernel(
    batch, at, arrived, inputs, sums, gain, bias, grad_unit, totals, loss, emb, grad, ends
):
    parts, tall, _ = arrived.shape
    block = tall - PAD
    tail = 0.0
    for p in range(parts):
        grad[p * block : (p + 1) * block] = arrived[p, :block]
        tail = tail + arrived[p, block:].astype(F32)
    both = sums_of(tail)
    ends[...] = both
    bias_grad, gain_grad = both[0:1], both[1:2]
    total = jnp.sum(sums[...], 0)
    normed, unit_f, scale, inv_std = head(
        inputs[...], total, gain[...], bias[...], batch
    )
    pull = grad_unit[...]
    radial = jnp.sum(unit_f * pull, 1, keepdims=True)
    shifts = (pull - unit_f * radial) * scale
    emb[...] = inv_std * (
        shifts * gain[...]
        - gain[...] * bias_grad / batch
        - normed * (gain[...] * gain_grad / batch)
    )
    own = jnp.sum(totals[...], 0)[0:1]
    n = inputs.shape[0]
    shape = (n, own.shape[1])
    ahead = lax.broadcasted_iota(jnp.int32, shape, 1) - lax.broadcasted_iota(
        jnp.int32, shape, 0
    )
    found = [
        jnp.sum(jnp.where(ahead == at[k], own, 0.0), 1, keepdims=True) for k in (0, 1)
    ]
    values = jnp.log(found[0]) - found[1]
    square = (n, n)
    same = lax.broadcasted_iota(jnp.int32, square, 0) == lax.broadcasted_iota(
        jnp.int32, square, 1
    )
    loss[...] = jnp.sum(jnp.where(same, values, 0.0), 0, keepdims=True)


def body(embeddings, bn_gain, bn_bias, centres, sample_rows, label_shard, label_slot):
    nx, nz, nc, nr = (lax.axis_size(a) for a in ("x", "z", "core", "rep"))
    ix, iz, ic, ir = (lax.axis_index(a) for a in ("x", "z", "core", "rep"))
    rows_dev, width = embeddings.shape
    slots = sample_rows.shape[1]
    batch = rows_dev * nx * nz * nc * nr
    line_rows = nz * rows_dev
    group = nx * line_rows
    held = nc * slots
    quarter = slots // nr
    at = ir.astype(jnp.int32).reshape(1)
    gain, bias = bn_gain[None], bn_bias[None]

    line = spread(embeddings, "z").reshape(line_rows, width)
    rows = spread(line, "x").reshape(group, width)
    rows_f = rows.astype(F32)
    sums = spread(
        jnp.stack([jnp.sum(rows_f, 0), jnp.sum(rows_f * rows_f, 0)]), ("core", "rep")
    )

    picked = centres.at[sample_rows[0]].get(mode="promise_in_bounds")
    picks = picked.astype(F32)
    inv_norm = lax.rsqrt(jnp.sum(picks * picks, 1, keepdims=True) + EPSILON)
    w_own = (picks * inv_norm).astype(BF16)
    w_other = shift(w_own, "core", 1)

    def of_core(labels, core):
        lines = labels.reshape(nx * nz, nc, rows_dev)
        return lax.dynamic_index_in_dim(lines, core, 1).reshape(1, group)

    owner, slot = of_core(label_shard, ic), of_core(label_slot, ic)
    chip = (ix * nz + iz) * nc
    place = jnp.where(
        owner == chip + ic, slot, jnp.where(owner == chip + 1 - ic, slot + slots, -1)
    )
    place_2 = jnp.where(
        of_core(label_shard, 1 - ic) == chip + ic, of_core(label_slot, 1 - ic), -1
    )

    unit, stats = call(
        lambda *refs: exp_kernel(batch, *refs),
        [VM] * 7,
        [VM] * 2,
        [
            jax.ShapeDtypeStruct((group, width), BF16),
            jax.ShapeDtypeStruct((nx * nc, 2, group), F32),
        ],
        2 * held * group * width,
        2 * held * width,
        held * group,
    )(rows, sums, gain, bias, place, w_own, w_other)
    unit_2 = shift(unit, "core", 1)

    stats = lax.all_to_all(stats, ("x", "core"), 0, 0)
    totals = call(
        lambda *refs: total_kernel(nx, *refs),
        [SM, VM],
        VM,
        jax.ShapeDtypeStruct((nz, nc, group + line_rows), F32),
        16 * group,
        64 * group,
        grant=SMALL,
    )(jnp.stack([ix, ic]).astype(jnp.int32), stats)
    totals, unit_2, place_2 = lax.optimization_barrier((totals, unit_2, place_2))
    totals = lax.all_to_all(totals, "z", 0, 0)

    pull = call(
        lambda *refs: pull_kernel(batch, *refs),
        [VM] * 9,
        VM,
        jax.ShapeDtypeStruct((nx, line_rows + PAD, width), BF16),
        4 * held * group * width,
        2 * held * width,
        held * group,
    )(rows, sums, gain, bias, place, totals, unit, w_own, w_other)

    piece = jax.ShapeDtypeStruct((quarter, width), BF16)
    mine, *sent = call(
        lambda *refs: raw_kernel(nr, *refs),
        [SM] + [VM] * 6 + [HB],
        [HO] * nr,
        [jax.ShapeDtypeStruct((quarter, width), F32)] + [piece] * (nr - 1),
        4 * held * group * width,
        2 * held * width,
        held * group,
        [
            pltpu.VMEM((quarter, width), F32),
            pltpu.VMEM((nr - 1, quarter, width), BF16),
            pltpu.SemaphoreType.DMA((nr,)),
        ],
    )(at, place, place_2, totals, unit, unit_2, w_own, pull)
    came = [shift(sent[by - 1], "rep", by) for by in range(1, nr)]
    pull = lax.all_to_all(pull, "x", 0, 0)
    pull, mine = lax.optimization_barrier((pull, mine))
    lanes = min(width, 128)
    tall = (rows_dev + 4) * (width // lanes)
    pull = call(
        lambda *refs: mid_kernel(rows_dev, *refs),
        [VM],
        VM,
        jax.ShapeDtypeStruct((nz, tall, lanes), BF16),
        nx * line_rows * width,
        2 * nx * line_rows * width,
        grant=SMALL,
    )(pull)
    pull = lax.all_to_all(pull, "z", 0, 0)
    grad_unit, ends = call(
        lambda *refs: home_kernel(rows_dev, *refs),
        [VM],
        [VM] * 2,
        [
            jax.ShapeDtypeStruct((rows_dev, width), F32),
            jax.ShapeDtypeStruct((2, width), F32),
        ],
        nz * tall * lanes,
        2 * nz * tall * lanes,
        grant=SMALL,
    )(pull)
    last = call(
        lambda *refs: project_kernel(nr, *refs),
        [SM, HB] + [VM] * (2 + nr),
        VM,
        jax.ShapeDtypeStruct((nr, quarter + PAD, width), BF16),
        20 * quarter * width,
        14 * quarter * width,
        0,
        [pltpu.VMEM((quarter, width), BF16), pltpu.SemaphoreType.DMA],
        grant=SMALL,
    )(at, picked, ends, shift(ends, "core", 1), mine, *came)
    last = lax.all_to_all(last, "rep", 0, 0)

    own = jnp.stack([(ix * nz + iz) * rows_dev, group + iz * rows_dev])
    row_loss, emb_grad, centre_grad, ends = call(
        lambda *refs: final_kernel(batch, *refs),
        [SM] + [VM] * 7,
        [VM] * 4,
        [
            jax.ShapeDtypeStruct((1, rows_dev), F32),
            jax.ShapeDtypeStruct((rows_dev, width), F32),
            jax.ShapeDtypeStruct((slots, width), BF16),
            jax.ShapeDtypeStruct((2, width), F32),
        ],
        slots * width,
        4 * slots * width,
        grant=SMALL,
    )(own.astype(jnp.int32), last, embeddings, sums, gain, bias, grad_unit, totals)
    return (row_loss[0], emb_grad, centre_grad, ends[1], ends[0])


def solution(mesh):
    shards, replicas = mesh.devices.shape
    split = (4, shards // 8, 2, replicas)
    fine = Mesh(mesh.devices.reshape(split), ("x", "z", "core", "rep"))
    cen = ("x", "z", "core")
    every = cen + ("rep",)
    return jax.shard_map(
        body,
        mesh=fine,
        in_specs=(
            P(every, None),
            P(),
            P(),
            P(cen, None),
            P(cen, None),
            P(None, "rep", None),
            P(None, "rep", None),
        ),
        out_specs=(P(every), P(every, None), P(cen, None), P(), P()),
        check_vma=False,
    )
```

time: 161 us -> 159 us (0.988)
  waiting for transfers between devices: 23.3 us -> 36.2 us
  starting transfers between devices: 78.4 us -> 66.7 us
  other arithmetic: 8.24 us -> 4.34 us
  blocking collectives: 19.4 us -> 16 us
  Pallas kernels: 16.1 us -> 18.8 us
    all_to_all x3, waiting for transfers between devices: 9.44 us -> 20.3 us  [the longest x1 12.7 us: body(): last = lax.all_to_all(last, 'rep', 0, 0)]
    ppermute x11 -> x6, starting transfers between devices: 32.5 us -> 24.2 us  [shift(): return lax.ppermute(block, axis, [(i, (i + by) % n) for i in range(n)])]
    ppermute x11 -> x6, waiting for transfers between devices: 5.72 us -> 0.78 us  [shift(): return lax.ppermute(block, axis, [(i, (i + by) % n) for i in range(n)])]
    all_to_all x2 -> x3, waiting for transfers between devices: 8.17 us -> 12.7 us  [spread(): return lax.all_to_all(copies, axes, 0, 0)]
    all_to_all x3, starting transfers between devices: 15.8 us -> 12.3 us  [the longest x1 5.41 us: body(): pull = lax.all_to_all(pull, 'z', 0, 0)]
    all_to_all x1, blocking collectives: 19.4 us -> 16 us  [body(): totals = lax.all_to_all(totals, 'z', 0, 0)]
    pallas_call x5 -> x7, Pallas kernels: 16 us -> 18.7 us  [the longest x1 5.89 us: body(): call(lambda *refs: pull_kernel(batch, *refs), [VM] * 9, VM, jax.ShapeDtyp...]
    all_to_all x1, waiting for transfers between devices: 0.01 us -> 2.45 us  [body(): pull = lax.all_to_all(pull, 'x', 0, 0)]
  transfers between devices with their start and end apart: 17 -> 13, of which waited for: 6 -> 7; matrix products, arithmetic and copies ran while one was open for 7% -> 6% of each run, Pallas kernels for 4% -> 4%
where the time goes in v6:
time: 159 us; the launch traced here: 158 us
  starting transfers between devices  66.7 us (42%)
  waiting for transfers between devices  36.2 us (23%)
  Pallas kernels  18.8 us (12%)
  blocking collectives  16 us (10%)
  local copies, waits for them, and re-layouts  14.6 us (9%)
  other arithmetic  4.34 us (3%)
    all_to_all x3, starting transfers between devices, spread(): return lax.all_to_all(copies, axes, 0, 0)  26.8 us
    ppermute x6, starting transfers between devices, shift(): return lax.ppermute(block, axis, [(i, (i + by) % n) for i in range(n)])  24.2 us
    all_to_all x1, blocking collectives, body(): totals = lax.all_to_all(totals, 'z', 0, 0)  16 us
    all_to_all x3, waiting for transfers between devices, spread(): return lax.all_to_all(copies, axes, 0, 0)  12.7 us
    all_to_all x1, waiting for transfers between devices, body(): last = lax.all_to_all(last, 'rep', 0, 0)  12.7 us
    unnamed x34, local copies, waits for them, and re-layouts  7.43 us
    pallas_call x1, Pallas kernels, body(): call(lambda *refs: pull_kernel(batch, *refs), [VM] * 9, VM, jax.ShapeDtyp...  5.89 us
    all_to_all x1, starting transfers between devices, body(): pull = lax.all_to_all(pull, 'z', 0, 0)  5.41 us
  transfers between devices with their start and end apart: 13, of which 7 were waited for; matrix products, arithmetic and copies ran while one was open for 6% of the time, Pallas kernels for 4%

profile of v6, /device:TPU:1, one launch (start us, length us, event | category | flops | bytes accessed | tf_op | source)
XLA Modules:
  0.0 157.7 jit_solution(6205008772460748491)
XLA Ops:
  2.2 15.7 %all-to-all-start = ((bf16[16,8,512]{2,1,0:T(8,128)(2,1)}), bf16[16,8,512]{2,1,0:T(8,128)(2,1)S(1)}, u32[]{:S(2)}, u32[]{:S(2)}) async-start(bf16[16,8,512]{2,1,0:T(8,128)(2,1)} %broadcast_in_dim.34), calls=%async_computation | async-start | bytes 262144 | tf_op jit(solution)/shard_map/all_to_all | solution.py:20
  18.6 2.7 %gather_fusion = bf16[768,512]{1,0:T(8,128)(2,1)S(1)} fusion(bf16[2048,512]{1,0:T(8,128)(2,1)S(1)} %copy-done, s32[1024]{0:T(1024)S(1)} %pad_clamp_fusion), kind=kCustom, calls=%fused_computation | custom fusion | bytes 1575936 | tf_op jit(solution)/shard_map/gather | solution.py:303
  21.6 8.3 %all-to-all-done = bf16[16,8,512]{2,1,0:T(8,128)(2,1)S(1)} async-done(((bf16[16,8,512]{2,1,0:T(8,128)(2,1)}), bf16[16,8,512]{2,1,0:T(8,128)(2,1)S(1)}, u32[]{:S(2)}, u32[]{:S(2)}) %all-to-all-start) | async-done | bytes 131104 | tf_op jit(solution)/shard_map/all_to_all | solution.py:20
  30.8 4.0 %all-to-all-start.1 = ((bf16[4,128,512]{2,1,0:T(8,128)(2,1)}), bf16[4,128,512]{2,1,0:T(8,128)(2,1)S(1)}, u32[]{:S(2)}, u32[]{:S(2)}) async-start(bf16[4,128,512]{2,1,0:T(8,128)(2,1)} %broadcast_in_dim.36), calls=%async_computation.1 | async-start | bytes 1048576 | tf_op jit(solution)/shard_map/all_to_all | solution.py:20
  35.9 5.8 %collective-permute-start = (bf16[768,512]{1,0:T(8,128)(2,1)}, bf16[768,512]{1,0:T(8,128)(2,1)}, u32[]{:S(2)}, u32[]{:S(2)}) collective-permute-start(bf16[768,512]{1,0:T(8,128)(2,1)} %fusion.1.refs_5_.refs_7_.refs_6_), channel_id=1, source_target_pairs={{0,4},{4,0},{1,5},{5,1},{2,6},{6,2},{3,7},{7,3},{8,12},{12,8},{9,1... | collective-permute-start | bytes 2359304 | tf_op jit(solution)/shard_map/ppermute | solution.py:25
  45.1 7.0 %all-to-all-start.2 = ((f32[8,2,512]{2,1,0:T(2,128)}), f32[8,2,512]{2,1,0:T(2,128)S(1)}, u32[]{:S(2)}, u32[]{:S(2)}) async-start(f32[8,2,512]{2,1,0:T(2,128)} %broadcast_in_dim.37), calls=%async_computation.2 | async-start | bytes 65536 | tf_op jit(solution)/shard_map/all_to_all | solution.py:20
  52.7 4.3 %all-to-all-done.2.refs_1_.refs_3_ = f32[8,2,512]{2,1,0:T(2,128)S(1)} async-done(((f32[8,2,512]{2,1,0:T(2,128)}), f32[8,2,512]{2,1,0:T(2,128)S(1)}, u32[]{:S(2)}, u32[]{:S(2)}) %all-to-all-start.2) | async-done | bytes 32800 | tf_op jit(solution)/shard_map/all_to_all | solution.py:20
  57.6 3.9 %shard_map.110 = (bf16[512,512]{1,0:T(8,128)(2,1)}, f32[8,2,512]{2,1,0:T(2,128)}) custom-call(bf16[512,512]{1,0:T(8,128)(2,1)} %bitcast.24, f32[8,2,512]{2,1,0:T(2,128)} %copy-done.5, f32[1,512]{1,0:T(1,128)} %bitcast.18, f32[1,512]{1,0:T(1,128)} %bitcast.21, s32[1,512]{1,0:T(1,128)} %select_select_fusion.refs_4_.refs_1_, ...), custom_call_target="tpu_custom_call" | custom-call | flops 805306368 | bytes 1572864 | tf_op jit(solution)/shard_map/pallas_call | solution.py:322
  61.5 2.3 %collective-permute-start.1 = (bf16[512,512]{1,0:T(8,128)(2,1)}, bf16[512,512]{1,0:T(8,128)(2,1)S(1)}, u32[]{:S(2)}, u32[]{:S(2)}) collective-permute-start(bf16[512,512]{1,0:T(8,128)(2,1)} %get-tuple-element.23.refs_6_.refs_4_), channel_id=1, source_target_pairs={{0,4},{4,0},{1,5},{5,1},{2,6},{6,2},{3,7},{7,3},{8,12},{12,8},{9,1... | collective-permute-start | bytes 1572872 | tf_op jit(solution)/shard_map/ppermute | solution.py:25
  63.8 3.4 %all-to-all-start.3 = ((f32[8,2,512]{2,1,0:T(2,128)}), f32[8,2,512]{2,1,0:T(2,128)S(1)}, u32[]{:S(2)}, u32[]{:S(2)}) async-start(f32[8,2,512]{2,1,0:T(2,128)} %get-tuple-element.22), calls=%async_computation.3 | async-start | bytes 65536 | tf_op jit(solution)/shard_map/all_to_all | solution.py:336
  67.9 4.0 %all-to-all-done.3.refs_1_ = f32[8,2,512]{2,1,0:T(2,128)S(1)} async-done(((f32[8,2,512]{2,1,0:T(2,128)}), f32[8,2,512]{2,1,0:T(2,128)S(1)}, u32[]{:S(2)}, u32[]{:S(2)}) %all-to-all-start.3) | async-done | bytes 32800 | tf_op jit(solution)/shard_map/all_to_all | solution.py:336
  72.5 16.0 %all_to_all.40.refs_5_.refs_3_.refs_7_ = f32[16,2,640]{2,1,0:T(2,128)} all-to-all(f32[16,2,640]{2,1,0:T(2,128)S(1)} %shard_map.111), channel_id=1, replica_groups=mesh['x'=4,'z'=16,'core'=2,'rep'=4] {'z'}, dimensions={0} | all-to-all | bytes 163840 | tf_op jit(solution)/shard_map/all_to_all | solution.py:347
  88.6 5.9 %shard_map.112.refs_7_ = bf16[4,144,512]{2,1,0:T(8,128)(2,1)} custom-call(bf16[512,512]{1,0:T(8,128)(2,1)} %bitcast.25, f32[8,2,512]{2,1,0:T(2,128)} %copy-done.5, f32[1,512]{1,0:T(1,128)} %bitcast.19, f32[1,512]{1,0:T(1,128)} %bitcast.22, s32[1,512]{1,0:T(1,128)} %select_select_fusion.refs_4_.refs_1_, f32[16,2,640]{2,1,0:T(2,128)} %all_to_all.40.refs_5_.refs_3_.refs_7_, ...), custom_call_target="tpu_custom_call" | custom-call | flops 1610612736 | bytes 1572864 | tf_op jit(solution)/shard_map/pallas_call | solution.py:349
  94.4 3.5 %all-to-all-start.5 = ((bf16[4,144,512]{2,1,0:T(8,128)(2,1)}), bf16[4,144,512]{2,1,0:T(8,128)(2,1)S(1)}, u32[]{:S(2)}, u32[]{:S(2)}) async-start(bf16[4,144,512]{2,1,0:T(8,128)(2,1)} %shard_map.112.refs_7_), calls=%async_computation.5 | async-start | bytes 1179648 | tf_op jit(solution)/shard_map/all_to_all | solution.py:375
  97.9 5.1 %shard_map.113 = (f32[192,512]{1,0:T(8,128)}, bf16[192,512]{1,0:T(8,128)(2,1)}, bf16[192,512]{1,0:T(8,128)(2,1)}, bf16[192,512]{1,0:T(8,128)(2,1)}) custom-call(s32[1]{0:T(128)} %bitcast.2.refs_0_, s32[1,512]{1,0:T(1,128)} %select_select_fusion.refs_4_.refs_1_, s32[1,512]{1,0:T(1,128)} %select_n.55.refs_2_, ...), custom_call_target="tpu_custom_call" | custom-call | flops 1610612736 | bytes 1572864 | tf_op jit(solution)/shard_map/pallas_call | solution.py:360
  103.1 2.4 %all-to-all-done.5.refs_0_ = bf16[4,144,512]{2,1,0:T(8,128)(2,1)S(1)} async-done(((bf16[4,144,512]{2,1,0:T(8,128)(2,1)}), bf16[4,144,512]{2,1,0:T(8,128)(2,1)S(1)}, u32[]{:S(2)}, u32[]{:S(2)}) %all-to-all-start.5) | async-done | bytes 589856 | tf_op jit(solution)/shard_map/all_to_all | solution.py:375
  106.3 5.4 %all-to-all-start.6 = ((bf16[16,48,128]{2,1,0:T(8,128)(2,1)}), bf16[16,48,128]{2,1,0:T(8,128)(2,1)S(1)}, u32[]{:S(2)}, u32[]{:S(2)}) async-start(bf16[16,48,128]{2,1,0:T(8,128)(2,1)} %copy-done.2), calls=%async_computation.6 | async-start | bytes 393216 | tf_op jit(solution)/shard_map/all_to_all | solution.py:388
  111.7 2.3 %collective-permute-start.3 = (bf16[192,512]{1,0:T(8,128)(2,1)}, bf16[192,512]{1,0:T(8,128)(2,1)S(1)}, u32[]{:S(2)}, u32[]{:S(2)}) collective-permute-start(bf16[192,512]{1,0:T(8,128)(2,1)} %get-tuple-element.31), channel_id=1, source_target_pairs={{0,1},{1,2},{2,3},{3,0},{4,5},{5,6},{6,7},{7,4},{8,9},{9,10},{10,1... | collective-permute-start | bytes 589832 | tf_op jit(solution)/shard_map/ppermute | solution.py:25
  114.0 3.6 %collective-permute-start.4 = (bf16[192,512]{1,0:T(8,128)(2,1)}, bf16[192,512]{1,0:T(8,128)(2,1)S(1)}, u32[]{:S(2)}, u32[]{:S(2)}) collective-permute-start(bf16[192,512]{1,0:T(8,128)(2,1)} %get-tuple-element.32), channel_id=1, source_target_pairs={{0,2},{1,3},{2,0},{3,1},{4,6},{5,7},{6,4},{7,5},{8,10},{9,11},{10,... | collective-permute-start | bytes 589832 | tf_op jit(solution)/shard_map/ppermute | solution.py:25
  117.6 2.7 %collective-permute-start.5 = (bf16[192,512]{1,0:T(8,128)(2,1)}, bf16[192,512]{1,0:T(8,128)(2,1)}, u32[]{:S(2)}, u32[]{:S(2)}) collective-permute-start(bf16[192,512]{1,0:T(8,128)(2,1)} %get-tuple-element.33), channel_id=1, source_target_pairs={{0,3},{1,0},{2,1},{3,2},{4,7},{5,4},{6,5},{7,6},{8,11},{9,8},{10,9... | collective-permute-start | bytes 589832 | tf_op jit(solution)/shard_map/ppermute | solution.py:25
  120.4 3.7 %all-to-all-done.6.refs_0_ = bf16[16,48,128]{2,1,0:T(8,128)(2,1)S(1)} async-done(((bf16[16,48,128]{2,1,0:T(8,128)(2,1)}), bf16[16,48,128]{2,1,0:T(8,128)(2,1)S(1)}, u32[]{:S(2)}, u32[]{:S(2)}) %all-to-all-start.6) | async-done | bytes 196640 | tf_op jit(solution)/shard_map/all_to_all | solution.py:388
  124.7 7.5 %collective-permute-start.2 = (f32[2,512]{1,0:T(2,128)S(1)}, f32[2,512]{1,0:T(2,128)S(1)}, u32[]{:S(2)}, u32[]{:S(2)}) collective-permute-start(f32[2,512]{1,0:T(2,128)S(1)} %get-tuple-element.29.refs_2_), channel_id=1, source_target_pairs={{0,4},{4,0},{1,5},{5,1},{2,6},{6,2},{3,7},{7,3},{8,12},{12,8},{9,1... | collective-permute-start | bytes 12296 | tf_op jit(solution)/shard_map/ppermute | solution.py:25
  136.4 3.5 %all-to-all-start.7 = ((bf16[4,208,512]{2,1,0:T(8,128)(2,1)}), bf16[4,208,512]{2,1,0:T(8,128)(2,1)S(1)}, u32[]{:S(2)}, u32[]{:S(2)}) async-start(bf16[4,208,512]{2,1,0:T(8,128)(2,1)} %copy-done.1), calls=%async_computation.7 | async-start | bytes 1703936 | tf_op jit(solution)/shard_map/all_to_all | solution.py:412
  140.0 12.7 %all-to-all-done.7.refs_1_ = bf16[4,208,512]{2,1,0:T(8,128)(2,1)S(1)} async-done(((bf16[4,208,512]{2,1,0:T(8,128)(2,1)}), bf16[4,208,512]{2,1,0:T(8,128)(2,1)S(1)}, u32[]{:S(2)}, u32[]{:S(2)}) %all-to-all-start.7) | async-done | bytes 852000 | tf_op jit(solution)/shard_map/all_to_all | solution.py:412
  (66 shorter events, 20.9 us)
Async XLA Ops:
  0.6 18.0 %copy-start = (bf16[2048,512]{1,0:T(8,128)(2,1)S(1)}, bf16[2048,512]{1,0:T(8,128)(2,1)}, u32[]{:S(2)}) copy-start(bf16[2048,512]{1,0:T(8,128)(2,1)} %param.10) | copy-start | bytes 6291460
  2.2 27.8 %all-to-all-start = ((bf16[16,8,512]{2,1,0:T(8,128)(2,1)}), bf16[16,8,512]{2,1,0:T(8,128)(2,1)S(1)}, u32[]{:S(2)}, u32[]{:S(2)}) async-start(bf16[16,8,512]{2,1,0:T(8,128)(2,1)} %broadcast_in_dim.34), calls=%async_computation | async-start | bytes 262144 | tf_op jit(solution)/shard_map/all_to_all | solution.py:20
  29.9 11.8 %copy-start.13 = (s32[128,1,8]{0,2,1:T(8,128)S(1)}, s32[128,1,8]{0,2,1:T(8,128)}, u32[]{:S(2)}) copy-start(s32[128,1,8]{0,2,1:T(8,128)} %param.12) | copy-start | bytes 12292
  29.9 12.4 %copy-start.14 = (s32[128,1,8]{0,2,1:T(8,128)S(1)}, s32[128,1,8]{0,2,1:T(8,128)}, u32[]{:S(2)}) copy-start(s32[128,1,8]{0,2,1:T(8,128)} %param.13) | copy-start | bytes 12292
  30.8 13.5 %all-to-all-start.1 = ((bf16[4,128,512]{2,1,0:T(8,128)(2,1)}), bf16[4,128,512]{2,1,0:T(8,128)(2,1)S(1)}, u32[]{:S(2)}, u32[]{:S(2)}) async-start(bf16[4,128,512]{2,1,0:T(8,128)(2,1)} %broadcast_in_dim.36), calls=%async_computation.1 | async-start | bytes 1048576 | tf_op jit(solution)/shard_map/all_to_all | solution.py:20
  35.9 16.8 %collective-permute-start = (bf16[768,512]{1,0:T(8,128)(2,1)}, bf16[768,512]{1,0:T(8,128)(2,1)}, u32[]{:S(2)}, u32[]{:S(2)}) collective-permute-start(bf16[768,512]{1,0:T(8,128)(2,1)} %fusion.1.refs_5_.refs_7_.refs_6_), channel_id=1, source_target_pairs={{0,4},{4,0},{1,5},{5,1},{2,6},{6,2},{3,7},{7,3},{8,12},{12,8},{9,1... | collective-permute-start | bytes 2359304 | tf_op jit(solution)/shard_map/ppermute | solution.py:25
  44.3 12.7 %copy-start.12 = (bf16[4,128,512]{2,1,0:T(8,128)(2,1)}, bf16[4,128,512]{2,1,0:T(8,128)(2,1)S(1)}, u32[]{:S(2)}) copy-start(bf16[4,128,512]{2,1,0:T(8,128)(2,1)S(1)} %all-to-all-done.1) | copy-start | bytes 1572868
  45.1 11.9 %all-to-all-start.2 = ((f32[8,2,512]{2,1,0:T(2,128)}), f32[8,2,512]{2,1,0:T(2,128)S(1)}, u32[]{:S(2)}, u32[]{:S(2)}) async-start(f32[8,2,512]{2,1,0:T(2,128)} %broadcast_in_dim.37), calls=%async_computation.2 | async-start | bytes 65536 | tf_op jit(solution)/shard_map/all_to_all | solution.py:20
  61.5 11.0 %collective-permute-start.1 = (bf16[512,512]{1,0:T(8,128)(2,1)}, bf16[512,512]{1,0:T(8,128)(2,1)S(1)}, u32[]{:S(2)}, u32[]{:S(2)}) collective-permute-start(bf16[512,512]{1,0:T(8,128)(2,1)} %get-tuple-element.23.refs_6_.refs_4_), channel_id=1, source_target_pairs={{0,4},{4,0},{1,5},{5,1},{2,6},{6,2},{3,7},{7,3},{8,12},{12,8},{9,1... | collective-permute-start | bytes 1572872 | tf_op jit(solution)/shard_map/ppermute | solution.py:25
  63.8 8.1 %all-to-all-start.3 = ((f32[8,2,512]{2,1,0:T(2,128)}), f32[8,2,512]{2,1,0:T(2,128)S(1)}, u32[]{:S(2)}, u32[]{:S(2)}) async-start(f32[8,2,512]{2,1,0:T(2,128)} %get-tuple-element.22), calls=%async_computation.3 | async-start | bytes 65536 | tf_op jit(solution)/shard_map/all_to_all | solution.py:336
  72.5 21.9 %copy-start.15 = (bf16[512,512]{1,0:T(8,128)(2,1)}, bf16[512,512]{1,0:T(8,128)(2,1)S(1)}, u32[]{:S(2)}) copy-start(bf16[512,512]{1,0:T(8,128)(2,1)S(1)} %collective-permute-done.1.refs_5_) | copy-start | bytes 1572868
  94.4 11.1 %all-to-all-start.5 = ((bf16[4,144,512]{2,1,0:T(8,128)(2,1)}), bf16[4,144,512]{2,1,0:T(8,128)(2,1)S(1)}, u32[]{:S(2)}, u32[]{:S(2)}) async-start(bf16[4,144,512]{2,1,0:T(8,128)(2,1)} %shard_map.112.refs_7_), calls=%async_computation.5 | async-start | bytes 1179648 | tf_op jit(solution)/shard_map/all_to_all | solution.py:375
  106.3 17.8 %all-to-all-start.6 = ((bf16[16,48,128]{2,1,0:T(8,128)(2,1)}), bf16[16,48,128]{2,1,0:T(8,128)(2,1)S(1)}, u32[]{:S(2)}, u32[]{:S(2)}) async-start(bf16[16,48,128]{2,1,0:T(8,128)(2,1)} %copy-done.2), calls=%async_computation.6 | async-start | bytes 393216 | tf_op jit(solution)/shard_map/all_to_all | solution.py:388
  111.7 20.5 %collective-permute-start.3 = (bf16[192,512]{1,0:T(8,128)(2,1)}, bf16[192,512]{1,0:T(8,128)(2,1)S(1)}, u32[]{:S(2)}, u32[]{:S(2)}) collective-permute-start(bf16[192,512]{1,0:T(8,128)(2,1)} %get-tuple-element.31), channel_id=1, source_target_pairs={{0,1},{1,2},{2,3},{3,0},{4,5},{5,6},{6,7},{7,4},{8,9},{9,10},{10,1... | collective-permute-start | bytes 589832 | tf_op jit(solution)/shard_map/ppermute | solution.py:25
  114.0 18.2 %collective-permute-start.4 = (bf16[192,512]{1,0:T(8,128)(2,1)}, bf16[192,512]{1,0:T(8,128)(2,1)S(1)}, u32[]{:S(2)}, u32[]{:S(2)}) collective-permute-start(bf16[192,512]{1,0:T(8,128)(2,1)} %get-tuple-element.32), channel_id=1, source_target_pairs={{0,2},{1,3},{2,0},{3,1},{4,6},{5,7},{6,4},{7,5},{8,10},{9,11},{10,... | collective-permute-start | bytes 589832 | tf_op jit(solution)/shard_map/ppermute | solution.py:25
  117.6 14.6 %collective-permute-start.5 = (bf16[192,512]{1,0:T(8,128)(2,1)}, bf16[192,512]{1,0:T(8,128)(2,1)}, u32[]{:S(2)}, u32[]{:S(2)}) collective-permute-start(bf16[192,512]{1,0:T(8,128)(2,1)} %get-tuple-element.33), channel_id=1, source_target_pairs={{0,3},{1,0},{2,1},{3,2},{4,7},{5,4},{6,5},{7,6},{8,11},{9,8},{10,9... | collective-permute-start | bytes 589832 | tf_op jit(solution)/shard_map/ppermute | solution.py:25
  124.1 28.6 %copy-start.4 = (f32[16,2,640]{2,1,0:T(2,128)S(1)}, f32[16,2,640]{2,1,0:T(2,128)}, u32[]{:S(2)}) copy-start(f32[16,2,640]{2,1,0:T(2,128)} %all_to_all.40.refs_5_.refs_3_.refs_7_) | copy-start | bytes 245764
  124.7 8.3 %collective-permute-start.2 = (f32[2,512]{1,0:T(2,128)S(1)}, f32[2,512]{1,0:T(2,128)S(1)}, u32[]{:S(2)}, u32[]{:S(2)}) collective-permute-start(f32[2,512]{1,0:T(2,128)S(1)} %get-tuple-element.29.refs_2_), channel_id=1, source_target_pairs={{0,4},{4,0},{1,5},{5,1},{2,6},{6,2},{3,7},{7,3},{8,12},{12,8},{9,1... | collective-permute-start | bytes 12296 | tf_op jit(solution)/shard_map/ppermute | solution.py:25
  133.0 1.0 copy-start.3
  134.0 18.7 %copy-start.9 = (f32[8,512]{1,0:T(8,128)S(1)}, f32[8,512]{1,0:T(8,128)}, u32[]{:S(2)}) copy-start(f32[8,512]{1,0:T(8,128)} %copy-done.8) | copy-start | bytes 49156
  135.5 0.9 copy-start.1
  136.4 16.2 %all-to-all-start.7 = ((bf16[4,208,512]{2,1,0:T(8,128)(2,1)}), bf16[4,208,512]{2,1,0:T(8,128)(2,1)S(1)}, u32[]{:S(2)}, u32[]{:S(2)}) async-start(bf16[4,208,512]{2,1,0:T(8,128)(2,1)} %copy-done.1), calls=%async_computation.7 | async-start | bytes 1703936 | tf_op jit(solution)/shard_map/all_to_all | solution.py:412
  152.7 0.8 copy-start.6
  153.4 0.7 copy-start.7
  (5 other events, 3.3 us)

commit v7 on v6

--- a/solution.py
+++ b/solution.py
@@ -186,7 +186,9 @@
     for v in range(2):
         both = tail[2 * v * n : (2 * v + 1) * n] + tail[(2 * v + 1) * n : (2 * v + 2) * n]
         rows.append(jnp.concatenate([both[k : k + 1] for k in range(n)], 1))
-    ends[...] = jnp.concatenate(rows, 0)
+    both = jnp.concatenate(rows, 0)
+    for p in range(ends.shape[0]):
+        ends[p] = both
 
 
 def raw_kernel(parts, at, place, place_2, totals, unit, unit_2, w_own, _, *refs):
@@ -217,40 +219,25 @@
         copy.wait()
 
 
-def project_kernel(parts, at, picked, ends, ends_2, *refs):
-    found, (packed, picks_ref, sem) = refs[:parts], refs[parts:]
-    block = picks_ref.shape[0]
+def project_kernel(parts, at, picked, *refs):
+    found, (out, picks_ref, sem) = refs[:parts], refs[parts:]
+    block = out.shape[0]
     rows = pl.ds(pl.multiple_of(at[0] * block, 64), block)
     copy = pltpu.make_async_copy(picked.at[rows], picks_ref, sem)
     copy.start()
     raw = found[0][...]
     for piece in found[1:]:
         raw = raw + piece[...].astype(F32)
-    both = ends[...] + ends_2[...]
-    tail = tail_of(both[0:1], both[1:2])
     copy.wait()
     picks = picks_ref[...].astype(F32)
     inv_norm = lax.rsqrt(jnp.sum(picks * picks, 1, keepdims=True) + EPSILON)
     w_unit = picks * inv_norm
     along = jnp.sum(w_unit * raw, 1, keepdims=True)
-    grad = ((raw - w_unit * along) * inv_norm).astype(BF16)
-    for p in range(parts):
-        packed[p, :block] = grad
-        packed[p, block:] = tail
-
-
-def final_kernel(
-    batch, at, arrived, inputs, sums, gain, bias, grad_unit, totals, loss, emb, grad, ends
-):
-    parts, tall, _ = arrived.shape
-    block = tall - PAD
-    tail = 0.0
-    for p in range(parts):
-        grad[p * block : (p + 1) * block] = arrived[p, :block]
-        tail = tail + arrived[p, block:].astype(F32)
-    both = sums_of(tail)
-    ends[...] = both
-    bias_grad, gain_grad = both[0:1], both[1:2]
+    out[...] = ((raw - w_unit * along) * inv_norm).astype(BF16)
+
+
+def own_kernel(batch, at, inputs, sums, gain, bias, grad_unit, totals, terms, loss):
+    n = inputs.shape[0]
     total = jnp.sum(sums[...], 0)
     normed, unit_f, scale, inv_std = head(
         inputs[...], total, gain[...], bias[...], batch
@@ -258,13 +245,11 @@
     pull = grad_unit[...]
     radial = jnp.sum(unit_f * pull, 1, keepdims=True)
     shifts = (pull - unit_f * radial) * scale
-    emb[...] = inv_std * (
-        shifts * gain[...]
-        - gain[...] * bias_grad / batch
-        - normed * (gain[...] * gain_grad / batch)
-    )
+    share = inv_std * gain[...]
+    terms[0:n] = shifts * share
+    terms[n : 2 * n] = normed * (share / batch)
+    terms[2 * n : 3 * n] = jnp.broadcast_to(share / batch, (n, share.shape[1]))
     own = jnp.sum(totals[...], 0)[0:1]
-    n = inputs.shape[0]
     shape = (n, own.shape[1])
     ahead = lax.broadcasted_iota(jnp.int32, shape, 1) - lax.broadcasted_iota(
         jnp.int32, shape, 0
@@ -278,6 +263,21 @@
         jnp.int32, square, 1
     )
     loss[...] = jnp.sum(jnp.where(same, values, 0.0), 0, keepdims=True)
+
+
+def final_kernel(parts, at, terms, ends, *refs):
+    found, (emb, grad, gain_grad, bias_grad) = refs[:parts], refs[parts:]
+    block = found[0].shape[0]
+    n = emb.shape[0]
+    both = jnp.sum(ends[...], 0)
+    bias_grad[...] = both[0:1]
+    gain_grad[...] = both[1:2]
+    emb[...] = (
+        terms[0:n] - terms[2 * n : 3 * n] * both[0:1] - terms[n : 2 * n] * both[1:2]
+    )
+    for by, piece in enumerate(found):
+        where = lax.rem(at[0] - by + parts, parts) * block
+        grad[pl.ds(pl.multiple_of(where, 64), block)] = piece[...]
 
 
 def body(embeddings, bn_gain, bn_bias, centres, sample_rows, label_shard, label_slot):
@@ -293,17 +293,18 @@
     at = ir.astype(jnp.int32).reshape(1)
     gain, bias = bn_gain[None], bn_bias[None]
 
+    picked = centres.at[sample_rows[0]].get(mode="promise_in_bounds")
+    picks = picked.astype(F32)
+    inv_norm = lax.rsqrt(jnp.sum(picks * picks, 1, keepdims=True) + EPSILON)
+    w_own = (picks * inv_norm).astype(BF16)
+
     line = spread(embeddings, "z").reshape(line_rows, width)
+    line, w_own = lax.optimization_barrier((line, w_own))
     rows = spread(line, "x").reshape(group, width)
     rows_f = rows.astype(F32)
     sums = spread(
         jnp.stack([jnp.sum(rows_f, 0), jnp.sum(rows_f * rows_f, 0)]), ("core", "rep")
     )
-
-    picked = centres.at[sample_rows[0]].get(mode="promise_in_bounds")
-    picks = picked.astype(F32)
-    inv_norm = lax.rsqrt(jnp.sum(picks * picks, 1, keepdims=True) + EPSILON)
-    w_own = (picks * inv_norm).astype(BF16)
     w_other = shift(w_own, "core", 1)
 
     def of_core(labels, core):
@@ -372,6 +373,17 @@
         ],
     )(at, place, place_2, totals, unit, unit_2, w_own, pull)
     came = [shift(sent[by - 1], "rep", by) for by in range(1, nr)]
+    grad = call(
+        lambda *refs: project_kernel(nr, *refs),
+        [SM, HB] + [VM] * nr,
+        VM,
+        piece,
+        20 * quarter * width,
+        14 * quarter * width,
+        0,
+        [pltpu.VMEM((quarter, width), BF16), pltpu.SemaphoreType.DMA],
+        grant=SMALL,
+    )(at, picked, mine, *came)
     pull = lax.all_to_all(pull, "x", 0, 0)
     pull, mine = lax.optimization_barrier((pull, mine))
     lanes = min(width, 128)
@@ -392,41 +404,42 @@
         [VM] * 2,
         [
             jax.ShapeDtypeStruct((rows_dev, width), F32),
-            jax.ShapeDtypeStruct((2, width), F32),
+            jax.ShapeDtypeStruct((nc * nr, 2, width), F32),
         ],
         nz * tall * lanes,
         2 * nz * tall * lanes,
         grant=SMALL,
     )(pull)
-    last = call(
-        lambda *refs: project_kernel(nr, *refs),
-        [SM, HB] + [VM] * (2 + nr),
-        VM,
-        jax.ShapeDtypeStruct((nr, quarter + PAD, width), BF16),
-        20 * quarter * width,
-        14 * quarter * width,
-        0,
-        [pltpu.VMEM((quarter, width), BF16), pltpu.SemaphoreType.DMA],
-        grant=SMALL,
-    )(at, picked, ends, shift(ends, "core", 1), mine, *came)
-    last = lax.all_to_all(last, "rep", 0, 0)
+    ends = lax.all_to_all(ends, ("core", "rep"), 0, 0)
 
     own = jnp.stack([(ix * nz + iz) * rows_dev, group + iz * rows_dev])
-    row_loss, emb_grad, centre_grad, ends = call(
-        lambda *refs: final_kernel(batch, *refs),
-        [SM] + [VM] * 7,
+    terms, row_loss = call(
+        lambda *refs: own_kernel(batch, *refs),
+        [SM] + [VM] * 6,
+        [VM] * 2,
+        [
+            jax.ShapeDtypeStruct((3 * rows_dev, width), F32),
+            jax.ShapeDtypeStruct((1, rows_dev), F32),
+        ],
+        40 * rows_dev * width,
+        40 * rows_dev * width,
+        grant=SMALL,
+    )(own.astype(jnp.int32), embeddings, sums, gain, bias, grad_unit, totals)
+    emb_grad, centre_grad, gain_grad, bias_grad = call(
+        lambda *refs: final_kernel(nr, *refs),
+        [SM] + [VM] * (2 + nr),
         [VM] * 4,
         [
-            jax.ShapeDtypeStruct((1, rows_dev), F32),
             jax.ShapeDtypeStruct((rows_dev, width), F32),
             jax.ShapeDtypeStruct((slots, width), BF16),
-            jax.ShapeDtypeStruct((2, width), F32),
+            jax.ShapeDtypeStruct((1, width), F32),
+            jax.ShapeDtypeStruct((1, width), F32),
         ],
         slots * width,
         4 * slots * width,
         grant=SMALL,
-    )(own.astype(jnp.int32), last, embeddings, sums, gain, bias, grad_unit, totals)
-    return (row_loss[0], emb_grad, centre_grad, ends[1], ends[0])
+    )(at, terms, ends, grad, *[shift(grad, "rep", by) for by in range(1, nr)])
+    return (row_loss[0], emb_grad, centre_grad, gain_grad[0], bias_grad[0])
 
 
 def solution(mesh):

time: 159 us -> 153 us (0.962)
  waiting for transfers between devices: 36.2 us -> 23.2 us
  starting transfers between devices: 66.7 us -> 74.6 us
    all_to_all x1, waiting for transfers between devices: 12.7 us -> 0.13 us  [body(): ends = lax.all_to_all(ends, ('core', 'rep'), 0, 0)]
    ppermute x6 -> x8, waiting for transfers between devices: 0.78 us -> 5.12 us  [shift(): return lax.ppermute(block, axis, [(i, (i + by) % n) for i in range(n)])]
    all_to_all x1, waiting for transfers between devices: 3.68 us -> 0.01 us  [body(): pull = lax.all_to_all(pull, 'z', 0, 0)]
    all_to_all x1, starting transfers between devices: 3.5 us -> 7.16 us  [body(): ends = lax.all_to_all(ends, ('core', 'rep'), 0, 0)]
    ppermute x6 -> x8, starting transfers between devices: 24.2 us -> 27 us  [shift(): return lax.ppermute(block, axis, [(i, (i + by) % n) for i in range(n)])]
    unnamed x34 -> x32, local copies, waits for them, and re-layouts: 7.43 us -> 6.91 us
  transfers between devices with their start and end apart: 13 -> 15, of which waited for: 7 -> 7; matrix products, arithmetic and copies ran while one was open for 6% -> 6% of each run, Pallas kernels for 4% -> 5%
where the time goes in v7:
time: 153 us; the launch traced here: 152 us
  starting transfers between devices  74.6 us (49%)
  waiting for transfers between devices  23.2 us (15%)
  Pallas kernels  18.9 us (12%)
  blocking collectives  16 us (10%)
  local copies, waits for them, and re-layouts  14.3 us (9%)
  other arithmetic  4.02 us (3%)
    all_to_all x3, starting transfers between devices, spread(): return lax.all_to_all(copies, axes, 0, 0)  28.2 us
    ppermute x8, starting transfers between devices, shift(): return lax.ppermute(block, axis, [(i, (i + by) % n) for i in range(n)])  27 us
    all_to_all x1, blocking collectives, body(): totals = lax.all_to_all(totals, 'z', 0, 0)  16 us
    all_to_all x3, waiting for transfers between devices, spread(): return lax.all_to_all(copies, axes, 0, 0)  11.6 us
    all_to_all x1, starting transfers between devices, body(): ends = lax.all_to_all(ends, ('core', 'rep'), 0, 0)  7.16 us
    unnamed x32, local copies, waits for them, and re-layouts  6.91 us
    pallas_call x1, Pallas kernels, body(): call(lambda *refs: pull_kernel(batch, *refs), [VM] * 9, VM, jax.ShapeDtyp...  5.91 us
    all_to_all x1, starting transfers between devices, body(): pull = lax.all_to_all(pull, 'z', 0, 0)  5.41 us
  transfers between devices with their start and end apart: 15, of which 7 were waited for; matrix products, arithmetic and copies ran while one was open for 6% of the time, Pallas kernels for 5%

profile of v7, /device:TPU:1, one launch (start us, length us, event | category | flops | bytes accessed | tf_op | source)
XLA Modules:
  0.0 152.0 jit_solution(2001353008516335277)
XLA Ops:
  2.1 15.7 %all-to-all-start = ((bf16[16,8,512]{2,1,0:T(8,128)(2,1)}), bf16[16,8,512]{2,1,0:T(8,128)(2,1)S(1)}, u32[]{:S(2)}, u32[]{:S(2)}) async-start(bf16[16,8,512]{2,1,0:T(8,128)(2,1)} %broadcast_in_dim.16), calls=%async_computation | async-start | bytes 262144 | tf_op jit(solution)/shard_map/all_to_all | solution.py:20
  18.6 2.7 %gather_fusion = bf16[768,512]{1,0:T(8,128)(2,1)S(1)} fusion(bf16[2048,512]{1,0:T(8,128)(2,1)S(1)} %copy-done, s32[1024]{0:T(1024)S(1)} %pad_clamp_fusion), kind=kCustom, calls=%fused_computation | custom fusion | bytes 1575936 | tf_op jit(solution)/shard_map/gather | solution.py:296
  22.7 7.2 %all-to-all-done = bf16[16,8,512]{2,1,0:T(8,128)(2,1)S(1)} async-done(((bf16[16,8,512]{2,1,0:T(8,128)(2,1)}), bf16[16,8,512]{2,1,0:T(8,128)(2,1)S(1)}, u32[]{:S(2)}, u32[]{:S(2)}) %all-to-all-start) | async-done | bytes 131104 | tf_op jit(solution)/shard_map/all_to_all | solution.py:20
  30.7 4.0 %all-to-all-start.1 = ((bf16[4,128,512]{2,1,0:T(8,128)(2,1)}), bf16[4,128,512]{2,1,0:T(8,128)(2,1)S(1)}, u32[]{:S(2)}, u32[]{:S(2)}) async-start(bf16[4,128,512]{2,1,0:T(8,128)(2,1)} %broadcast_in_dim.34), calls=%async_computation.1 | async-start | bytes 1048576 | tf_op jit(solution)/shard_map/all_to_all | solution.py:20
  34.8 5.8 %collective-permute-start = (bf16[768,512]{1,0:T(8,128)(2,1)}, bf16[768,512]{1,0:T(8,128)(2,1)}, u32[]{:S(2)}, u32[]{:S(2)}) collective-permute-start(bf16[768,512]{1,0:T(8,128)(2,1)} %fusion.1.refs_5_.refs_7_.refs_6_), channel_id=1, source_target_pairs={{0,4},{4,0},{1,5},{5,1},{2,6},{6,2},{3,7},{7,3},{8,12},{12,8},{9,1... | collective-permute-start | bytes 2359304 | tf_op jit(solution)/shard_map/ppermute | solution.py:25
  43.8 8.4 %all-to-all-start.2 = ((f32[8,2,512]{2,1,0:T(2,128)}), f32[8,2,512]{2,1,0:T(2,128)S(1)}, u32[]{:S(2)}, u32[]{:S(2)}) async-start(f32[8,2,512]{2,1,0:T(2,128)} %broadcast_in_dim.35), calls=%async_computation.2 | async-start | bytes 65536 | tf_op jit(solution)/shard_map/all_to_all | solution.py:20
  52.8 4.3 %all-to-all-done.2.refs_1_.refs_2_ = f32[8,2,512]{2,1,0:T(2,128)S(1)} async-done(((f32[8,2,512]{2,1,0:T(2,128)}), f32[8,2,512]{2,1,0:T(2,128)S(1)}, u32[]{:S(2)}, u32[]{:S(2)}) %all-to-all-start.2) | async-done | bytes 32800 | tf_op jit(solution)/shard_map/all_to_all | solution.py:20
  57.7 3.9 %shard_map.110 = (bf16[512,512]{1,0:T(8,128)(2,1)}, f32[8,2,512]{2,1,0:T(2,128)}) custom-call(bf16[512,512]{1,0:T(8,128)(2,1)} %bitcast.24, f32[8,2,512]{2,1,0:T(2,128)} %copy-done.6, f32[1,512]{1,0:T(1,128)} %bitcast.18, f32[1,512]{1,0:T(1,128)} %bitcast.21, s32[1,512]{1,0:T(1,128)} %select_select_fusion.refs_4_.refs_1_, ...), custom_call_target="tpu_custom_call" | custom-call | flops 805306368 | bytes 1572864 | tf_op jit(solution)/shard_map/pallas_call | solution.py:323
  61.6 2.3 %collective-permute-start.1 = (bf16[512,512]{1,0:T(8,128)(2,1)}, bf16[512,512]{1,0:T(8,128)(2,1)}, u32[]{:S(2)}, u32[]{:S(2)}) collective-permute-start(bf16[512,512]{1,0:T(8,128)(2,1)} %get-tuple-element.28.refs_6_.refs_4_), channel_id=1, source_target_pairs={{0,4},{4,0},{1,5},{5,1},{2,6},{6,2},{3,7},{7,3},{8,12},{12,8},{9,1... | collective-permute-start | bytes 1572872 | tf_op jit(solution)/shard_map/ppermute | solution.py:25
  64.0 3.3 %all-to-all-start.3 = ((f32[8,2,512]{2,1,0:T(2,128)}), f32[8,2,512]{2,1,0:T(2,128)S(1)}, u32[]{:S(2)}, u32[]{:S(2)}) async-start(f32[8,2,512]{2,1,0:T(2,128)} %get-tuple-element.27), calls=%async_computation.3 | async-start | bytes 65536 | tf_op jit(solution)/shard_map/all_to_all | solution.py:337
  68.0 4.0 %all-to-all-done.3.refs_1_ = f32[8,2,512]{2,1,0:T(2,128)S(1)} async-done(((f32[8,2,512]{2,1,0:T(2,128)}), f32[8,2,512]{2,1,0:T(2,128)S(1)}, u32[]{:S(2)}, u32[]{:S(2)}) %all-to-all-start.3) | async-done | bytes 32800 | tf_op jit(solution)/shard_map/all_to_all | solution.py:337
  72.6 16.0 %all_to_all.40.refs_5_.refs_3_.refs_6_ = f32[16,2,640]{2,1,0:T(2,128)} all-to-all(f32[16,2,640]{2,1,0:T(2,128)S(1)} %shard_map.111), channel_id=1, replica_groups=mesh['x'=4,'z'=16,'core'=2,'rep'=4] {'z'}, dimensions={0} | all-to-all | bytes 163840 | tf_op jit(solution)/shard_map/all_to_all | solution.py:348
  88.6 5.9 %shard_map.112.refs_7_ = bf16[4,144,512]{2,1,0:T(8,128)(2,1)} custom-call(bf16[512,512]{1,0:T(8,128)(2,1)} %bitcast.25, f32[8,2,512]{2,1,0:T(2,128)} %copy-done.6, f32[1,512]{1,0:T(1,128)} %bitcast.19, f32[1,512]{1,0:T(1,128)} %bitcast.22, s32[1,512]{1,0:T(1,128)} %select_select_fusion.refs_4_.refs_1_, f32[16,2,640]{2,1,0:T(2,128)} %all_to_all.40.refs_5_.refs_3_.refs_6_, ...), custom_call_target="tpu_custom_call" | custom-call | flops 1610612736 | bytes 1572864 | tf_op jit(solution)/shard_map/pallas_call | solution.py:350
  94.6 3.5 %all-to-all-start.5 = ((bf16[4,144,512]{2,1,0:T(8,128)(2,1)}), bf16[4,144,512]{2,1,0:T(8,128)(2,1)S(1)}, u32[]{:S(2)}, u32[]{:S(2)}) async-start(bf16[4,144,512]{2,1,0:T(8,128)(2,1)} %shard_map.112.refs_7_), calls=%async_computation.5 | async-start | bytes 1179648 | tf_op jit(solution)/shard_map/all_to_all | solution.py:387
  98.0 5.1 %shard_map.113 = (f32[192,512]{1,0:T(8,128)}, bf16[192,512]{1,0:T(8,128)(2,1)}, bf16[192,512]{1,0:T(8,128)(2,1)}, bf16[192,512]{1,0:T(8,128)(2,1)}) custom-call(s32[1]{0:T(128)} %bitcast.13.refs_0_, s32[1,512]{1,0:T(1,128)} %select_select_fusion.refs_4_.refs_1_, s32[1,512]{1,0:T(1,128)} %select_n.55.refs_2_, ...), custom_call_target="tpu_custom_call" | custom-call | flops 1610612736 | bytes 1572864 | tf_op jit(solution)/shard_map/pallas_call | solution.py:361
  103.2 2.4 %all-to-all-done.5.refs_0_ = bf16[4,144,512]{2,1,0:T(8,128)(2,1)S(1)} async-done(((bf16[4,144,512]{2,1,0:T(8,128)(2,1)}), bf16[4,144,512]{2,1,0:T(8,128)(2,1)S(1)}, u32[]{:S(2)}, u32[]{:S(2)}) %all-to-all-start.5) | async-done | bytes 589856 | tf_op jit(solution)/shard_map/all_to_all | solution.py:387
  106.4 5.4 %all-to-all-start.6 = ((bf16[16,48,128]{2,1,0:T(8,128)(2,1)}), bf16[16,48,128]{2,1,0:T(8,128)(2,1)S(1)}, u32[]{:S(2)}, u32[]{:S(2)}) async-start(bf16[16,48,128]{2,1,0:T(8,128)(2,1)} %copy-done.1), calls=%async_computation.6 | async-start | bytes 393216 | tf_op jit(solution)/shard_map/all_to_all | solution.py:400
  111.8 2.3 %collective-permute-start.2 = (bf16[192,512]{1,0:T(8,128)(2,1)}, bf16[192,512]{1,0:T(8,128)(2,1)S(1)}, u32[]{:S(2)}, u32[]{:S(2)}) collective-permute-start(bf16[192,512]{1,0:T(8,128)(2,1)} %get-tuple-element.38), channel_id=1, source_target_pairs={{0,1},{1,2},{2,3},{3,0},{4,5},{5,6},{6,7},{7,4},{8,9},{9,10},{10,1... | collective-permute-start | bytes 589832 | tf_op jit(solution)/shard_map/ppermute | solution.py:25
  114.1 3.6 %collective-permute-start.3 = (bf16[192,512]{1,0:T(8,128)(2,1)}, bf16[192,512]{1,0:T(8,128)(2,1)S(1)}, u32[]{:S(2)}, u32[]{:S(2)}) collective-permute-start(bf16[192,512]{1,0:T(8,128)(2,1)} %get-tuple-element.39), channel_id=1, source_target_pairs={{0,2},{1,3},{2,0},{3,1},{4,6},{5,7},{6,4},{7,5},{8,10},{9,11},{10,... | collective-permute-start | bytes 589832 | tf_op jit(solution)/shard_map/ppermute | solution.py:25
  117.7 2.8 %collective-permute-start.4 = (bf16[192,512]{1,0:T(8,128)(2,1)}, bf16[192,512]{1,0:T(8,128)(2,1)S(1)}, u32[]{:S(2)}, u32[]{:S(2)}) collective-permute-start(bf16[192,512]{1,0:T(8,128)(2,1)} %get-tuple-element.40), channel_id=1, source_target_pairs={{0,3},{1,0},{2,1},{3,2},{4,7},{5,4},{6,5},{7,6},{8,11},{9,8},{10,9... | collective-permute-start | bytes 589832 | tf_op jit(solution)/shard_map/ppermute | solution.py:25
  120.5 4.1 %collective-permute-done.3.refs_4_ = bf16[192,512]{1,0:T(8,128)(2,1)S(1)} collective-permute-done((bf16[192,512]{1,0:T(8,128)(2,1)}, bf16[192,512]{1,0:T(8,128)(2,1)S(1)}, u32[]{:S(2)}, u32[]{:S(2)}) %collective-permute-start.3) | collective-permute-done | bytes 196640 | tf_op jit(solution)/shard_map/ppermute | solution.py:25
  127.2 4.0 %collective-permute-start.7 = (bf16[192,512]{1,0:T(8,128)(2,1)S(1)}, bf16[192,512]{1,0:T(8,128)(2,1)S(1)}, u32[]{:S(2)}, u32[]{:S(2)}) collective-permute-start(bf16[192,512]{1,0:T(8,128)(2,1)S(1)} %shard_map.117.refs_3_), channel_id=1, source_target_pairs={{0,3},{1,0},{2,1},{3,2},{4,7},{5,4},{6,5},{7,6},{8,11},{9,8},{10,9... | collective-permute-start | bytes 589832 | tf_op jit(solution)/shard_map/ppermute | solution.py:25
  131.3 4.2 %collective-permute-start.6 = (bf16[192,512]{1,0:T(8,128)(2,1)S(1)}, bf16[192,512]{1,0:T(8,128)(2,1)S(1)}, u32[]{:S(2)}, u32[]{:S(2)}) collective-permute-start(bf16[192,512]{1,0:T(8,128)(2,1)S(1)} %shard_map.117.refs_3_), channel_id=1, source_target_pairs={{0,2},{1,3},{2,0},{3,1},{4,6},{5,7},{6,4},{7,5},{8,10},{9,11},{10,... | collective-permute-start | bytes 589832 | tf_op jit(solution)/shard_map/ppermute | solution.py:25
  138.1 7.2 %all-to-all-start.7 = ((f32[8,2,512]{2,1,0:T(2,128)}), f32[8,2,512]{2,1,0:T(2,128)S(1)}, u32[]{:S(2)}, u32[]{:S(2)}) async-start(f32[8,2,512]{2,1,0:T(2,128)} %get-tuple-element.37), calls=%async_computation.7 | async-start | bytes 65536 | tf_op jit(solution)/shard_map/all_to_all | solution.py:413
  (68 shorter events, 22.7 us)
Async XLA Ops:
  0.6 18.0 %copy-start = (bf16[2048,512]{1,0:T(8,128)(2,1)S(1)}, bf16[2048,512]{1,0:T(8,128)(2,1)}, u32[]{:S(2)}) copy-start(bf16[2048,512]{1,0:T(8,128)(2,1)} %param.10) | copy-start | bytes 6291460
  2.1 27.8 %all-to-all-start = ((bf16[16,8,512]{2,1,0:T(8,128)(2,1)}), bf16[16,8,512]{2,1,0:T(8,128)(2,1)S(1)}, u32[]{:S(2)}, u32[]{:S(2)}) async-start(bf16[16,8,512]{2,1,0:T(8,128)(2,1)} %broadcast_in_dim.16), calls=%async_computation | async-start | bytes 262144 | tf_op jit(solution)/shard_map/all_to_all | solution.py:20
  21.5 19.1 %copy-start.13 = (s32[128,1,8]{0,2,1:T(8,128)S(1)}, s32[128,1,8]{0,2,1:T(8,128)}, u32[]{:S(2)}) copy-start(s32[128,1,8]{0,2,1:T(8,128)} %param.12) | copy-start | bytes 12292
  21.6 19.6 %copy-start.14 = (s32[128,1,8]{0,2,1:T(8,128)S(1)}, s32[128,1,8]{0,2,1:T(8,128)}, u32[]{:S(2)}) copy-start(s32[128,1,8]{0,2,1:T(8,128)} %param.13) | copy-start | bytes 12292
  30.7 12.2 %all-to-all-start.1 = ((bf16[4,128,512]{2,1,0:T(8,128)(2,1)}), bf16[4,128,512]{2,1,0:T(8,128)(2,1)S(1)}, u32[]{:S(2)}, u32[]{:S(2)}) async-start(bf16[4,128,512]{2,1,0:T(8,128)(2,1)} %broadcast_in_dim.34), calls=%async_computation.1 | async-start | bytes 1048576 | tf_op jit(solution)/shard_map/all_to_all | solution.py:20
  34.8 22.4 %collective-permute-start = (bf16[768,512]{1,0:T(8,128)(2,1)}, bf16[768,512]{1,0:T(8,128)(2,1)}, u32[]{:S(2)}, u32[]{:S(2)}) collective-permute-start(bf16[768,512]{1,0:T(8,128)(2,1)} %fusion.1.refs_5_.refs_7_.refs_6_), channel_id=1, source_target_pairs={{0,4},{4,0},{1,5},{5,1},{2,6},{6,2},{3,7},{7,3},{8,12},{12,8},{9,1... | collective-permute-start | bytes 2359304 | tf_op jit(solution)/shard_map/ppermute | solution.py:25
  42.9 14.2 %copy-start.11 = (bf16[4,128,512]{2,1,0:T(8,128)(2,1)}, bf16[4,128,512]{2,1,0:T(8,128)(2,1)S(1)}, u32[]{:S(2)}) copy-start(bf16[4,128,512]{2,1,0:T(8,128)(2,1)S(1)} %all-to-all-done.1) | copy-start | bytes 1572868
  43.8 23.6 %copy-start.12 = (s32[64,8]{1,0:T(8,128)S(1)}, s32[64,8]{1,0:T(8,128)}, u32[]{:S(2)}) copy-start(s32[64,8]{1,0:T(8,128)} %get-tuple-element.47) | copy-start | bytes 6148
  43.8 13.4 %all-to-all-start.2 = ((f32[8,2,512]{2,1,0:T(2,128)}), f32[8,2,512]{2,1,0:T(2,128)S(1)}, u32[]{:S(2)}, u32[]{:S(2)}) async-start(f32[8,2,512]{2,1,0:T(2,128)} %broadcast_in_dim.35), calls=%async_computation.2 | async-start | bytes 65536 | tf_op jit(solution)/shard_map/all_to_all | solution.py:20
  61.6 11.0 %collective-permute-start.1 = (bf16[512,512]{1,0:T(8,128)(2,1)}, bf16[512,512]{1,0:T(8,128)(2,1)}, u32[]{:S(2)}, u32[]{:S(2)}) collective-permute-start(bf16[512,512]{1,0:T(8,128)(2,1)} %get-tuple-element.28.refs_6_.refs_4_), channel_id=1, source_target_pairs={{0,4},{4,0},{1,5},{5,1},{2,6},{6,2},{3,7},{7,3},{8,12},{12,8},{9,1... | collective-permute-start | bytes 1572872 | tf_op jit(solution)/shard_map/ppermute | solution.py:25
  64.0 8.1 %all-to-all-start.3 = ((f32[8,2,512]{2,1,0:T(2,128)}), f32[8,2,512]{2,1,0:T(2,128)S(1)}, u32[]{:S(2)}, u32[]{:S(2)}) async-start(f32[8,2,512]{2,1,0:T(2,128)} %get-tuple-element.27), calls=%async_computation.3 | async-start | bytes 65536 | tf_op jit(solution)/shard_map/all_to_all | solution.py:337
  94.6 11.1 %all-to-all-start.5 = ((bf16[4,144,512]{2,1,0:T(8,128)(2,1)}), bf16[4,144,512]{2,1,0:T(8,128)(2,1)S(1)}, u32[]{:S(2)}, u32[]{:S(2)}) async-start(bf16[4,144,512]{2,1,0:T(8,128)(2,1)} %shard_map.112.refs_7_), calls=%async_computation.5 | async-start | bytes 1179648 | tf_op jit(solution)/shard_map/all_to_all | solution.py:387
  105.6 39.7 %copy-start.3 = (f32[16,2,640]{2,1,0:T(2,128)S(1)}, f32[16,2,640]{2,1,0:T(2,128)}, u32[]{:S(2)}) copy-start(f32[16,2,640]{2,1,0:T(2,128)} %all_to_all.40.refs_5_.refs_3_.refs_6_) | copy-start | bytes 245764
  106.4 31.1 %all-to-all-start.6 = ((bf16[16,48,128]{2,1,0:T(8,128)(2,1)}), bf16[16,48,128]{2,1,0:T(8,128)(2,1)S(1)}, u32[]{:S(2)}, u32[]{:S(2)}) async-start(bf16[16,48,128]{2,1,0:T(8,128)(2,1)} %copy-done.1), calls=%async_computation.6 | async-start | bytes 393216 | tf_op jit(solution)/shard_map/all_to_all | solution.py:400
  111.8 8.7 %collective-permute-start.2 = (bf16[192,512]{1,0:T(8,128)(2,1)}, bf16[192,512]{1,0:T(8,128)(2,1)S(1)}, u32[]{:S(2)}, u32[]{:S(2)}) collective-permute-start(bf16[192,512]{1,0:T(8,128)(2,1)} %get-tuple-element.38), channel_id=1, source_target_pairs={{0,1},{1,2},{2,3},{3,0},{4,5},{5,6},{6,7},{7,4},{8,9},{9,10},{10,1... | collective-permute-start | bytes 589832 | tf_op jit(solution)/shard_map/ppermute | solution.py:25
  114.1 10.5 %collective-permute-start.3 = (bf16[192,512]{1,0:T(8,128)(2,1)}, bf16[192,512]{1,0:T(8,128)(2,1)S(1)}, u32[]{:S(2)}, u32[]{:S(2)}) collective-permute-start(bf16[192,512]{1,0:T(8,128)(2,1)} %get-tuple-element.39), channel_id=1, source_target_pairs={{0,2},{1,3},{2,0},{3,1},{4,6},{5,7},{6,4},{7,5},{8,10},{9,11},{10,... | collective-permute-start | bytes 589832 | tf_op jit(solution)/shard_map/ppermute | solution.py:25
  117.7 7.9 %collective-permute-start.4 = (bf16[192,512]{1,0:T(8,128)(2,1)}, bf16[192,512]{1,0:T(8,128)(2,1)S(1)}, u32[]{:S(2)}, u32[]{:S(2)}) collective-permute-start(bf16[192,512]{1,0:T(8,128)(2,1)} %get-tuple-element.40), channel_id=1, source_target_pairs={{0,3},{1,0},{2,1},{3,2},{4,7},{5,4},{6,5},{7,6},{8,11},{9,8},{10,9... | collective-permute-start | bytes 589832 | tf_op jit(solution)/shard_map/ppermute | solution.py:25
  125.6 1.0 copy-start.2
  127.2 22.1 %collective-permute-start.7 = (bf16[192,512]{1,0:T(8,128)(2,1)S(1)}, bf16[192,512]{1,0:T(8,128)(2,1)S(1)}, u32[]{:S(2)}, u32[]{:S(2)}) collective-permute-start(bf16[192,512]{1,0:T(8,128)(2,1)S(1)} %shard_map.117.refs_3_), channel_id=1, source_target_pairs={{0,3},{1,0},{2,1},{3,2},{4,7},{5,4},{6,5},{7,6},{8,11},{9,8},{10,9... | collective-permute-start | bytes 589832 | tf_op jit(solution)/shard_map/ppermute | solution.py:25
  131.3 18.1 %collective-permute-start.6 = (bf16[192,512]{1,0:T(8,128)(2,1)S(1)}, bf16[192,512]{1,0:T(8,128)(2,1)S(1)}, u32[]{:S(2)}, u32[]{:S(2)}) collective-permute-start(bf16[192,512]{1,0:T(8,128)(2,1)S(1)} %shard_map.117.refs_3_), channel_id=1, source_target_pairs={{0,2},{1,3},{2,0},{3,1},{4,6},{5,7},{6,4},{7,5},{8,10},{9,11},{10,... | collective-permute-start | bytes 589832 | tf_op jit(solution)/shard_map/ppermute | solution.py:25
  135.5 13.9 %collective-permute-start.5 = (bf16[192,512]{1,0:T(8,128)(2,1)S(1)}, bf16[192,512]{1,0:T(8,128)(2,1)S(1)}, u32[]{:S(2)}, u32[]{:S(2)}) collective-permute-start(bf16[192,512]{1,0:T(8,128)(2,1)S(1)} %shard_map.117.refs_3_), channel_id=1, source_target_pairs={{0,1},{1,2},{2,3},{3,0},{4,5},{5,6},{6,7},{7,4},{8,9},{9,10},{10,1... | collective-permute-start | bytes 589832 | tf_op jit(solution)/shard_map/ppermute | solution.py:25
  138.1 12.1 %all-to-all-start.7 = ((f32[8,2,512]{2,1,0:T(2,128)}), f32[8,2,512]{2,1,0:T(2,128)S(1)}, u32[]{:S(2)}, u32[]{:S(2)}) async-start(f32[8,2,512]{2,1,0:T(2,128)} %get-tuple-element.37), calls=%async_computation.7 | async-start | bytes 65536 | tf_op jit(solution)/shard_map/all_to_all | solution.py:413
  145.3 0.8 copy-start.7
  150.2 0.9 copy-start.5
  (6 other events, 4.0 us)

commit v8 on v7

--- a/solution.py
+++ b/solution.py
@@ -266,18 +266,24 @@
 
 
 def final_kernel(parts, at, terms, ends, *refs):
-    found, (emb, grad, gain_grad, bias_grad) = refs[:parts], refs[parts:]
+    found, (emb, grad, gain_grad, bias_grad, sems) = refs[:parts], refs[parts:]
     block = found[0].shape[0]
     n = emb.shape[0]
+    copies = []
+    for by, piece in enumerate(found):
+        where = pl.multiple_of(lax.rem(at[0] - by + parts, parts) * block, 64)
+        copies.append(
+            pltpu.make_async_copy(piece, grad.at[pl.ds(where, block)], sems.at[by])
+        )
+        copies[-1].start()
     both = jnp.sum(ends[...], 0)
     bias_grad[...] = both[0:1]
     gain_grad[...] = both[1:2]
     emb[...] = (
         terms[0:n] - terms[2 * n : 3 * n] * both[0:1] - terms[n : 2 * n] * both[1:2]
     )
-    for by, piece in enumerate(found):
-        where = lax.rem(at[0] - by + parts, parts) * block
-        grad[pl.ds(pl.multiple_of(where, 64), block)] = piece[...]
+    for copy in copies:
+        copy.wait()
 
 
 def body(embeddings, bn_gain, bn_bias, centres, sample_rows, label_shard, label_slot):
@@ -298,6 +304,19 @@
     inv_norm = lax.rsqrt(jnp.sum(picks * picks, 1, keepdims=True) + EPSILON)
     w_own = (picks * inv_norm).astype(BF16)
 
+    def of_core(labels, core):
+        lines = labels.reshape(nx * nz, nc, rows_dev)
+        return lax.dynamic_index_in_dim(lines, core, 1).reshape(1, group)
+
+    owner, slot = of_core(label_shard, ic), of_core(label_slot, ic)
+    chip = (ix * nz + iz) * nc
+    place = jnp.where(
+        owner == chip + ic, slot, jnp.where(owner == chip + 1 - ic, slot + slots, -1)
+    )
+    place_2 = jnp.where(
+        of_core(label_shard, 1 - ic) == chip + ic, of_core(label_slot, 1 - ic), -1
+    )
+
     line = spread(embeddings, "z").reshape(line_rows, width)
     line, w_own = lax.optimization_barrier((line, w_own))
     rows = spread(line, "x").reshape(group, width)
@@ -306,19 +325,6 @@
         jnp.stack([jnp.sum(rows_f, 0), jnp.sum(rows_f * rows_f, 0)]), ("core", "rep")
     )
     w_other = shift(w_own, "core", 1)
-
-    def of_core(labels, core):
-        lines = labels.reshape(nx * nz, nc, rows_dev)
-        return lax.dynamic_index_in_dim(lines, core, 1).reshape(1, group)
-
-    owner, slot = of_core(label_shard, ic), of_core(label_slot, ic)
-    chip = (ix * nz + iz) * nc
-    place = jnp.where(
-        owner == chip + ic, slot, jnp.where(owner == chip + 1 - ic, slot + slots, -1)
-    )
-    place_2 = jnp.where(
-        of_core(label_shard, 1 - ic) == chip + ic, of_core(label_slot, 1 - ic), -1
-    )
 
     unit, stats = call(
         lambda *refs: exp_kernel(batch, *refs),
@@ -373,6 +379,9 @@
         ],
     )(at, place, place_2, totals, unit, unit_2, w_own, pull)
     came = [shift(sent[by - 1], "rep", by) for by in range(1, nr)]
+
+    pull = lax.all_to_all(pull, "x", 0, 0)
+    pull, came = lax.optimization_barrier((pull, came))
     grad = call(
         lambda *refs: project_kernel(nr, *refs),
         [SM, HB] + [VM] * nr,
@@ -384,8 +393,6 @@
         [pltpu.VMEM((quarter, width), BF16), pltpu.SemaphoreType.DMA],
         grant=SMALL,
     )(at, picked, mine, *came)
-    pull = lax.all_to_all(pull, "x", 0, 0)
-    pull, mine = lax.optimization_barrier((pull, mine))
     lanes = min(width, 128)
     tall = (rows_dev + 4) * (width // lanes)
     pull = call(
@@ -427,7 +434,7 @@
     )(own.astype(jnp.int32), embeddings, sums, gain, bias, grad_unit, totals)
     emb_grad, centre_grad, gain_grad, bias_grad = call(
         lambda *refs: final_kernel(nr, *refs),
-        [SM] + [VM] * (2 + nr),
+        [SM] + [VM] * 2 + [HB] * nr,
         [VM] * 4,
         [
             jax.ShapeDtypeStruct((rows_dev, width), F32),
@@ -437,6 +444,8 @@
         ],
         slots * width,
         4 * slots * width,
+        0,
+        [pltpu.SemaphoreType.DMA((nr,))],
         grant=SMALL,
     )(at, terms, ends, grad, *[shift(grad, "rep", by) for by in range(1, nr)])
     return (row_loss[0], emb_grad, centre_grad, gain_grad[0], bias_grad[0])

time: 153 us -> 156 us (1.020)
  local copies, waits for them, and re-layouts: 14.3 us -> 19.1 us
  waiting for transfers between devices: 23.2 us -> 20 us
    unnamed x32 -> x44, local copies, waits for them, and re-layouts: 6.91 us -> 11.7 us
    all_to_all x1, waiting for transfers between devices: 2.43 us -> 0.01 us  [body(): pull = lax.all_to_all(pull, 'x', 0, 0)]
  transfers between devices with their start and end apart: 15 -> 15, of which waited for: 7 -> 6; matrix products, arithmetic and copies ran while one was open for 6% -> 6% of each run, Pallas kernels for 5% -> 5%
where the time goes in v8:
time: 156 us; the launch traced here: 155 us
  starting transfers between devices  74.8 us (48%)
  waiting for transfers between devices  20 us (13%)
  Pallas kernels  20 us (13%)
  local copies, waits for them, and re-layouts  19.1 us (12%)
  blocking collectives  16 us (10%)
  other arithmetic  4.02 us (3%)
    all_to_all x3, starting transfers between devices, spread(): return lax.all_to_all(copies, axes, 0, 0)  28.2 us
    ppermute x8, starting transfers between devices, shift(): return lax.ppermute(block, axis, [(i, (i + by) % n) for i in range(n)])  26.5 us
    all_to_all x1, blocking collectives, body(): totals = lax.all_to_all(totals, 'z', 0, 0)  16 us
    unnamed x44, local copies, waits for them, and re-layouts  11.7 us
    all_to_all x3, waiting for transfers between devices, spread(): return lax.all_to_all(copies, axes, 0, 0)  11.6 us
    all_to_all x1, starting transfers between devices, body(): ends = lax.all_to_all(ends, ('core', 'rep'), 0, 0)  8.42 us
    pallas_call x1, Pallas kernels, body(): call(lambda *refs: pull_kernel(batch, *refs), [VM] * 9, VM, jax.ShapeDtyp...  5.92 us
    pallas_call x1, Pallas kernels, body(): call(lambda *refs: raw_kernel(nr, *refs), [SM] + [VM] * 6 + [HB], [HO] *...  5.13 us
  transfers between devices with their start and end apart: 15, of which 6 were waited for; matrix products, arithmetic and copies ran while one was open for 6% of the time, Pallas kernels for 5%

profile of v8, /device:TPU:1, one launch (start us, length us, event | category | flops | bytes accessed | tf_op | source)
XLA Modules:
  0.0 154.8 jit_solution(4207430719729140035)
XLA Ops:
  2.1 15.7 %all-to-all-start = ((bf16[16,8,512]{2,1,0:T(8,128)(2,1)}), bf16[16,8,512]{2,1,0:T(8,128)(2,1)S(1)}, u32[]{:S(2)}, u32[]{:S(2)}) async-start(bf16[16,8,512]{2,1,0:T(8,128)(2,1)} %broadcast_in_dim.17), calls=%async_computation | async-start | bytes 262144 | tf_op jit(solution)/shard_map/all_to_all | solution.py:20
  18.6 2.7 %gather_fusion = bf16[768,512]{1,0:T(8,128)(2,1)S(1)} fusion(bf16[2048,512]{1,0:T(8,128)(2,1)S(1)} %copy-done, s32[1024]{0:T(1024)S(1)} %pad_clamp_fusion), kind=kCustom, calls=%fused_computation | custom fusion | bytes 1575936 | tf_op jit(solution)/shard_map/gather | solution.py:302
  22.7 7.2 %all-to-all-done = bf16[16,8,512]{2,1,0:T(8,128)(2,1)S(1)} async-done(((bf16[16,8,512]{2,1,0:T(8,128)(2,1)}), bf16[16,8,512]{2,1,0:T(8,128)(2,1)S(1)}, u32[]{:S(2)}, u32[]{:S(2)}) %all-to-all-start) | async-done | bytes 131104 | tf_op jit(solution)/shard_map/all_to_all | solution.py:20
  30.8 4.0 %all-to-all-start.1 = ((bf16[4,128,512]{2,1,0:T(8,128)(2,1)}), bf16[4,128,512]{2,1,0:T(8,128)(2,1)S(1)}, u32[]{:S(2)}, u32[]{:S(2)}) async-start(bf16[4,128,512]{2,1,0:T(8,128)(2,1)} %broadcast_in_dim.34), calls=%async_computation.1 | async-start | bytes 1048576 | tf_op jit(solution)/shard_map/all_to_all | solution.py:20
  34.8 5.8 %collective-permute-start = (bf16[768,512]{1,0:T(8,128)(2,1)}, bf16[768,512]{1,0:T(8,128)(2,1)}, u32[]{:S(2)}, u32[]{:S(2)}) collective-permute-start(bf16[768,512]{1,0:T(8,128)(2,1)} %fusion.1.refs_5_.refs_7_.refs_6_), channel_id=1, source_target_pairs={{0,4},{4,0},{1,5},{5,1},{2,6},{6,2},{3,7},{7,3},{8,12},{12,8},{9,1... | collective-permute-start | bytes 2359304 | tf_op jit(solution)/shard_map/ppermute | solution.py:25
  43.8 8.4 %all-to-all-start.2 = ((f32[8,2,512]{2,1,0:T(2,128)}), f32[8,2,512]{2,1,0:T(2,128)S(1)}, u32[]{:S(2)}, u32[]{:S(2)}) async-start(f32[8,2,512]{2,1,0:T(2,128)} %broadcast_in_dim.35), calls=%async_computation.2 | async-start | bytes 65536 | tf_op jit(solution)/shard_map/all_to_all | solution.py:20
  52.8 4.3 %all-to-all-done.2.refs_1_.refs_2_ = f32[8,2,512]{2,1,0:T(2,128)S(1)} async-done(((f32[8,2,512]{2,1,0:T(2,128)}), f32[8,2,512]{2,1,0:T(2,128)S(1)}, u32[]{:S(2)}, u32[]{:S(2)}) %all-to-all-start.2) | async-done | bytes 32800 | tf_op jit(solution)/shard_map/all_to_all | solution.py:20
  57.7 3.9 %shard_map.110 = (bf16[512,512]{1,0:T(8,128)(2,1)}, f32[8,2,512]{2,1,0:T(2,128)}) custom-call(bf16[512,512]{1,0:T(8,128)(2,1)} %bitcast.24, f32[8,2,512]{2,1,0:T(2,128)} %copy-done.12, f32[1,512]{1,0:T(1,128)} %bitcast.18, f32[1,512]{1,0:T(1,128)} %bitcast.21, s32[1,512]{1,0:T(1,128)} %select_select_fusion.refs_4_.refs_1_, ...), custom_call_target="tpu_custom_call" | custom-call | flops 805306368 | bytes 1572864 | tf_op jit(solution)/shard_map/pallas_call | solution.py:329
  61.7 2.3 %collective-permute-start.1 = (bf16[512,512]{1,0:T(8,128)(2,1)}, bf16[512,512]{1,0:T(8,128)(2,1)}, u32[]{:S(2)}, u32[]{:S(2)}) collective-permute-start(bf16[512,512]{1,0:T(8,128)(2,1)} %get-tuple-element.31.refs_6_.refs_4_), channel_id=1, source_target_pairs={{0,4},{4,0},{1,5},{5,1},{2,6},{6,2},{3,7},{7,3},{8,12},{12,8},{9,1... | collective-permute-start | bytes 1572872 | tf_op jit(solution)/shard_map/ppermute | solution.py:25
  64.0 3.4 %all-to-all-start.3 = ((f32[8,2,512]{2,1,0:T(2,128)}), f32[8,2,512]{2,1,0:T(2,128)S(1)}, u32[]{:S(2)}, u32[]{:S(2)}) async-start(f32[8,2,512]{2,1,0:T(2,128)} %get-tuple-element.30), calls=%async_computation.3 | async-start | bytes 65536 | tf_op jit(solution)/shard_map/all_to_all | solution.py:343
  68.1 4.0 %all-to-all-done.3.refs_1_ = f32[8,2,512]{2,1,0:T(2,128)S(1)} async-done(((f32[8,2,512]{2,1,0:T(2,128)}), f32[8,2,512]{2,1,0:T(2,128)S(1)}, u32[]{:S(2)}, u32[]{:S(2)}) %all-to-all-start.3) | async-done | bytes 32800 | tf_op jit(solution)/shard_map/all_to_all | solution.py:343
  72.6 16.0 %all_to_all.40.refs_5_.refs_3_.refs_6_ = f32[16,2,640]{2,1,0:T(2,128)} all-to-all(f32[16,2,640]{2,1,0:T(2,128)S(1)} %shard_map.111), channel_id=1, replica_groups=mesh['x'=4,'z'=16,'core'=2,'rep'=4] {'z'}, dimensions={0} | all-to-all | bytes 163840 | tf_op jit(solution)/shard_map/all_to_all | solution.py:354
  88.7 5.9 %shard_map.112.refs_7_ = bf16[4,144,512]{2,1,0:T(8,128)(2,1)} custom-call(bf16[512,512]{1,0:T(8,128)(2,1)} %bitcast.25, f32[8,2,512]{2,1,0:T(2,128)} %copy-done.12, f32[1,512]{1,0:T(1,128)} %bitcast.19, f32[1,512]{1,0:T(1,128)} %bitcast.22, s32[1,512]{1,0:T(1,128)} %select_select_fusion.refs_4_.refs_1_, f32[16,2,640]{2,1,0:T(2,128)} %all_to_all.40.refs_5_.refs_3_.refs_6_, ...), custom_call_target="tpu_custom_call" | custom-call | flops 1610612736 | bytes 1572864 | tf_op jit(solution)/shard_map/pallas_call | solution.py:356
  94.6 3.5 %all-to-all-start.5 = ((bf16[4,144,512]{2,1,0:T(8,128)(2,1)}), bf16[4,144,512]{2,1,0:T(8,128)(2,1)S(1)}, u32[]{:S(2)}, u32[]{:S(2)}) async-start(bf16[4,144,512]{2,1,0:T(8,128)(2,1)} %shard_map.112.refs_7_), calls=%async_computation.5 | async-start | bytes 1179648 | tf_op jit(solution)/shard_map/all_to_all | solution.py:383
  98.1 5.1 %shard_map.113 = (f32[192,512]{1,0:T(8,128)}, bf16[192,512]{1,0:T(8,128)(2,1)}, bf16[192,512]{1,0:T(8,128)(2,1)}, bf16[192,512]{1,0:T(8,128)(2,1)}) custom-call(s32[1]{0:T(128)} %bitcast.13.refs_0_, s32[1,512]{1,0:T(1,128)} %select_select_fusion.refs_4_.refs_1_, s32[1,512]{1,0:T(1,128)} %select_n.55.refs_2_, ...), custom_call_target="tpu_custom_call" | custom-call | flops 1610612736 | bytes 1572864 | tf_op jit(solution)/shard_map/pallas_call | solution.py:367
  103.2 2.3 %collective-permute-start.2 = (bf16[192,512]{1,0:T(8,128)(2,1)}, bf16[192,512]{1,0:T(8,128)(2,1)S(1)}, u32[]{:S(2)}, u32[]{:S(2)}) collective-permute-start(bf16[192,512]{1,0:T(8,128)(2,1)} %get-tuple-element.35), channel_id=1, source_target_pairs={{0,1},{1,2},{2,3},{3,0},{4,5},{5,6},{6,7},{7,4},{8,9},{9,10},{10,1... | collective-permute-start | bytes 589832 | tf_op jit(solution)/shard_map/ppermute | solution.py:25
  105.5 3.6 %collective-permute-start.3 = (bf16[192,512]{1,0:T(8,128)(2,1)}, bf16[192,512]{1,0:T(8,128)(2,1)S(1)}, u32[]{:S(2)}, u32[]{:S(2)}) collective-permute-start(bf16[192,512]{1,0:T(8,128)(2,1)} %get-tuple-element.36), channel_id=1, source_target_pairs={{0,2},{1,3},{2,0},{3,1},{4,6},{5,7},{6,4},{7,5},{8,10},{9,11},{10,... | collective-permute-start | bytes 589832 | tf_op jit(solution)/shard_map/ppermute | solution.py:25
  109.2 2.9 %collective-permute-start.4 = (bf16[192,512]{1,0:T(8,128)(2,1)}, bf16[192,512]{1,0:T(8,128)(2,1)S(1)}, u32[]{:S(2)}, u32[]{:S(2)}) collective-permute-start(bf16[192,512]{1,0:T(8,128)(2,1)} %get-tuple-element.37), channel_id=1, source_target_pairs={{0,3},{1,0},{2,1},{3,2},{4,7},{5,4},{6,5},{7,6},{8,11},{9,8},{10,9... | collective-permute-start | bytes 589832 | tf_op jit(solution)/shard_map/ppermute | solution.py:25
  112.7 3.2 %collective-permute-done.3.refs_4_ = bf16[192,512]{1,0:T(8,128)(2,1)S(1)} collective-permute-done((bf16[192,512]{1,0:T(8,128)(2,1)}, bf16[192,512]{1,0:T(8,128)(2,1)S(1)}, u32[]{:S(2)}, u32[]{:S(2)}) %collective-permute-start.3) | collective-permute-done | bytes 196640 | tf_op jit(solution)/shard_map/ppermute | solution.py:25
  119.2 4.8 %all-to-all-start.6 = ((bf16[16,48,128]{2,1,0:T(8,128)(2,1)}), bf16[16,48,128]{2,1,0:T(8,128)(2,1)S(1)}, u32[]{:S(2)}, u32[]{:S(2)}) async-start(bf16[16,48,128]{2,1,0:T(8,128)(2,1)} %copy-done.1), calls=%async_computation.6 | async-start | bytes 393216 | tf_op jit(solution)/shard_map/all_to_all | solution.py:407
  128.3 5.2 %collective-permute-start.7 = (bf16[192,512]{1,0:T(8,128)(2,1)S(1)}, bf16[192,512]{1,0:T(8,128)(2,1)S(1)}, u32[]{:S(2)}, u32[]{:S(2)}) collective-permute-start(bf16[192,512]{1,0:T(8,128)(2,1)S(1)} %shard_map.117.refs_3_), channel_id=1, source_target_pairs={{0,3},{1,0},{2,1},{3,2},{4,7},{5,4},{6,5},{7,6},{8,11},{9,8},{10,9... | collective-permute-start | bytes 589832 | tf_op jit(solution)/shard_map/ppermute | solution.py:25
  135.5 2.5 %collective-permute-start.5 = (bf16[192,512]{1,0:T(8,128)(2,1)S(1)}, bf16[192,512]{1,0:T(8,128)(2,1)S(1)}, u32[]{:S(2)}, u32[]{:S(2)}) collective-permute-start(bf16[192,512]{1,0:T(8,128)(2,1)S(1)} %shard_map.117.refs_3_), channel_id=1, source_target_pairs={{0,1},{1,2},{2,3},{3,0},{4,5},{5,6},{6,7},{7,4},{8,9},{9,10},{10,1... | collective-permute-start | bytes 589832 | tf_op jit(solution)/shard_map/ppermute | solution.py:25
  138.6 8.4 %all-to-all-start.7 = ((f32[8,2,512]{2,1,0:T(2,128)}), f32[8,2,512]{2,1,0:T(2,128)S(1)}, u32[]{:S(2)}, u32[]{:S(2)}) async-start(f32[8,2,512]{2,1,0:T(2,128)} %get-tuple-element.42), calls=%async_computation.7 | async-start | bytes 65536 | tf_op jit(solution)/shard_map/all_to_all | solution.py:420
  152.9 2.0 %shard_map.118 = (f32[8,512]{1,0:T(8,128)}, bf16[768,512]{1,0:T(8,128)(2,1)}, f32[1,512]{1,0:T(1,128)}, f32[1,512]{1,0:T(1,128)}) custom-call(s32[1]{0:T(128)} %bitcast.13.refs_0_, f32[24,512]{1,0:T(8,128)S(1)} %get-tuple-element.41.refs_1_, f32[8,2,512]{2,1,0:T(2,128)S(1)} %all-to-all-done.7.refs_2_, bf16[192,512]{1,0:T(8,128)(2,1)S(1)} %shard_map.117.refs_3_, ...), custom_call_target="tpu_custom_call" | custom-call | flops 393216 | bytes 1572864 | tf_op jit(solution)/shard_map/pallas_call | solution.py:435
  (80 shorter events, 26.6 us)
Async XLA Ops:
  0.6 18.0 %copy-start = (bf16[2048,512]{1,0:T(8,128)(2,1)S(1)}, bf16[2048,512]{1,0:T(8,128)(2,1)}, u32[]{:S(2)}) copy-start(bf16[2048,512]{1,0:T(8,128)(2,1)} %param.10) | copy-start | bytes 6291460
  2.1 27.8 %all-to-all-start = ((bf16[16,8,512]{2,1,0:T(8,128)(2,1)}), bf16[16,8,512]{2,1,0:T(8,128)(2,1)S(1)}, u32[]{:S(2)}, u32[]{:S(2)}) async-start(bf16[16,8,512]{2,1,0:T(8,128)(2,1)} %broadcast_in_dim.17), calls=%async_computation | async-start | bytes 262144 | tf_op jit(solution)/shard_map/all_to_all | solution.py:20
  21.5 19.1 %copy-start.19 = (s32[128,1,8]{0,2,1:T(8,128)S(1)}, s32[128,1,8]{0,2,1:T(8,128)}, u32[]{:S(2)}) copy-start(s32[128,1,8]{0,2,1:T(8,128)} %param.12) | copy-start | bytes 12292
  21.6 19.6 %copy-start.20 = (s32[128,1,8]{0,2,1:T(8,128)S(1)}, s32[128,1,8]{0,2,1:T(8,128)}, u32[]{:S(2)}) copy-start(s32[128,1,8]{0,2,1:T(8,128)} %param.13) | copy-start | bytes 12292
  30.8 12.2 %all-to-all-start.1 = ((bf16[4,128,512]{2,1,0:T(8,128)(2,1)}), bf16[4,128,512]{2,1,0:T(8,128)(2,1)S(1)}, u32[]{:S(2)}, u32[]{:S(2)}) async-start(bf16[4,128,512]{2,1,0:T(8,128)(2,1)} %broadcast_in_dim.34), calls=%async_computation.1 | async-start | bytes 1048576 | tf_op jit(solution)/shard_map/all_to_all | solution.py:20
  34.8 22.4 %collective-permute-start = (bf16[768,512]{1,0:T(8,128)(2,1)}, bf16[768,512]{1,0:T(8,128)(2,1)}, u32[]{:S(2)}, u32[]{:S(2)}) collective-permute-start(bf16[768,512]{1,0:T(8,128)(2,1)} %fusion.1.refs_5_.refs_7_.refs_6_), channel_id=1, source_target_pairs={{0,4},{4,0},{1,5},{5,1},{2,6},{6,2},{3,7},{7,3},{8,12},{12,8},{9,1... | collective-permute-start | bytes 2359304 | tf_op jit(solution)/shard_map/ppermute | solution.py:25
  43.0 14.2 %copy-start.17 = (bf16[4,128,512]{2,1,0:T(8,128)(2,1)}, bf16[4,128,512]{2,1,0:T(8,128)(2,1)S(1)}, u32[]{:S(2)}) copy-start(bf16[4,128,512]{2,1,0:T(8,128)(2,1)S(1)} %all-to-all-done.1) | copy-start | bytes 1572868
  43.8 23.6 %copy-start.18 = (s32[64,8]{1,0:T(8,128)S(1)}, s32[64,8]{1,0:T(8,128)}, u32[]{:S(2)}) copy-start(s32[64,8]{1,0:T(8,128)} %get-tuple-element.53) | copy-start | bytes 6148
  43.8 13.3 %all-to-all-start.2 = ((f32[8,2,512]{2,1,0:T(2,128)}), f32[8,2,512]{2,1,0:T(2,128)S(1)}, u32[]{:S(2)}, u32[]{:S(2)}) async-start(f32[8,2,512]{2,1,0:T(2,128)} %broadcast_in_dim.35), calls=%async_computation.2 | async-start | bytes 65536 | tf_op jit(solution)/shard_map/all_to_all | solution.py:20
  61.7 11.0 %collective-permute-start.1 = (bf16[512,512]{1,0:T(8,128)(2,1)}, bf16[512,512]{1,0:T(8,128)(2,1)}, u32[]{:S(2)}, u32[]{:S(2)}) collective-permute-start(bf16[512,512]{1,0:T(8,128)(2,1)} %get-tuple-element.31.refs_6_.refs_4_), channel_id=1, source_target_pairs={{0,4},{4,0},{1,5},{5,1},{2,6},{6,2},{3,7},{7,3},{8,12},{12,8},{9,1... | collective-permute-start | bytes 1572872 | tf_op jit(solution)/shard_map/ppermute | solution.py:25
  64.0 8.1 %all-to-all-start.3 = ((f32[8,2,512]{2,1,0:T(2,128)}), f32[8,2,512]{2,1,0:T(2,128)S(1)}, u32[]{:S(2)}, u32[]{:S(2)}) async-start(f32[8,2,512]{2,1,0:T(2,128)} %get-tuple-element.30), calls=%async_computation.3 | async-start | bytes 65536 | tf_op jit(solution)/shard_map/all_to_all | solution.py:343
  94.6 23.8 %all-to-all-start.5 = ((bf16[4,144,512]{2,1,0:T(8,128)(2,1)}), bf16[4,144,512]{2,1,0:T(8,128)(2,1)S(1)}, u32[]{:S(2)}, u32[]{:S(2)}) async-start(bf16[4,144,512]{2,1,0:T(8,128)(2,1)} %shard_map.112.refs_7_), calls=%async_computation.5 | async-start | bytes 1179648 | tf_op jit(solution)/shard_map/all_to_all | solution.py:383
  103.2 8.8 %collective-permute-start.2 = (bf16[192,512]{1,0:T(8,128)(2,1)}, bf16[192,512]{1,0:T(8,128)(2,1)S(1)}, u32[]{:S(2)}, u32[]{:S(2)}) collective-permute-start(bf16[192,512]{1,0:T(8,128)(2,1)} %get-tuple-element.35), channel_id=1, source_target_pairs={{0,1},{1,2},{2,3},{3,0},{4,5},{5,6},{6,7},{7,4},{8,9},{9,10},{10,1... | collective-permute-start | bytes 589832 | tf_op jit(solution)/shard_map/ppermute | solution.py:25
  105.5 10.4 %collective-permute-start.3 = (bf16[192,512]{1,0:T(8,128)(2,1)}, bf16[192,512]{1,0:T(8,128)(2,1)S(1)}, u32[]{:S(2)}, u32[]{:S(2)}) collective-permute-start(bf16[192,512]{1,0:T(8,128)(2,1)} %get-tuple-element.36), channel_id=1, source_target_pairs={{0,2},{1,3},{2,0},{3,1},{4,6},{5,7},{6,4},{7,5},{8,10},{9,11},{10,... | collective-permute-start | bytes 589832 | tf_op jit(solution)/shard_map/ppermute | solution.py:25
  109.2 37.9 %copy-start.3 = (f32[16,2,640]{2,1,0:T(2,128)S(1)}, f32[16,2,640]{2,1,0:T(2,128)}, u32[]{:S(2)}) copy-start(f32[16,2,640]{2,1,0:T(2,128)} %all_to_all.40.refs_5_.refs_3_.refs_6_) | copy-start | bytes 245764
  109.2 8.6 %collective-permute-start.4 = (bf16[192,512]{1,0:T(8,128)(2,1)}, bf16[192,512]{1,0:T(8,128)(2,1)S(1)}, u32[]{:S(2)}, u32[]{:S(2)}) collective-permute-start(bf16[192,512]{1,0:T(8,128)(2,1)} %get-tuple-element.37), channel_id=1, source_target_pairs={{0,3},{1,0},{2,1},{3,2},{4,7},{5,4},{6,5},{7,6},{8,11},{9,8},{10,9... | collective-permute-start | bytes 589832 | tf_op jit(solution)/shard_map/ppermute | solution.py:25
  119.2 18.8 %all-to-all-start.6 = ((bf16[16,48,128]{2,1,0:T(8,128)(2,1)}), bf16[16,48,128]{2,1,0:T(8,128)(2,1)S(1)}, u32[]{:S(2)}, u32[]{:S(2)}) async-start(bf16[16,48,128]{2,1,0:T(8,128)(2,1)} %copy-done.1), calls=%async_computation.6 | async-start | bytes 393216 | tf_op jit(solution)/shard_map/all_to_all | solution.py:407
  124.0 1.0 copy-start.2
  125.9 0.9 copy-start.7
  128.3 22.8 %collective-permute-start.7 = (bf16[192,512]{1,0:T(8,128)(2,1)S(1)}, bf16[192,512]{1,0:T(8,128)(2,1)S(1)}, u32[]{:S(2)}, u32[]{:S(2)}) collective-permute-start(bf16[192,512]{1,0:T(8,128)(2,1)S(1)} %shard_map.117.refs_3_), channel_id=1, source_target_pairs={{0,3},{1,0},{2,1},{3,2},{4,7},{5,4},{6,5},{7,6},{8,11},{9,8},{10,9... | collective-permute-start | bytes 589832 | tf_op jit(solution)/shard_map/ppermute | solution.py:25
  133.5 17.6 %collective-permute-start.6 = (bf16[192,512]{1,0:T(8,128)(2,1)S(1)}, bf16[192,512]{1,0:T(8,128)(2,1)S(1)}, u32[]{:S(2)}, u32[]{:S(2)}) collective-permute-start(bf16[192,512]{1,0:T(8,128)(2,1)S(1)} %shard_map.117.refs_3_), channel_id=1, source_target_pairs={{0,2},{1,3},{2,0},{3,1},{4,6},{5,7},{6,4},{7,5},{8,10},{9,11},{10,... | collective-permute-start | bytes 589832 | tf_op jit(solution)/shard_map/ppermute | solution.py:25
  135.5 15.7 %collective-permute-start.5 = (bf16[192,512]{1,0:T(8,128)(2,1)S(1)}, bf16[192,512]{1,0:T(8,128)(2,1)S(1)}, u32[]{:S(2)}, u32[]{:S(2)}) collective-permute-start(bf16[192,512]{1,0:T(8,128)(2,1)S(1)} %shard_map.117.refs_3_), channel_id=1, source_target_pairs={{0,1},{1,2},{2,3},{3,0},{4,5},{5,6},{6,7},{7,4},{8,9},{9,10},{10,1... | collective-permute-start | bytes 589832 | tf_op jit(solution)/shard_map/ppermute | solution.py:25
  138.6 13.3 %all-to-all-start.7 = ((f32[8,2,512]{2,1,0:T(2,128)}), f32[8,2,512]{2,1,0:T(2,128)S(1)}, u32[]{:S(2)}, u32[]{:S(2)}) async-start(f32[8,2,512]{2,1,0:T(2,128)} %get-tuple-element.42), calls=%async_computation.7 | async-start | bytes 65536 | tf_op jit(solution)/shard_map/all_to_all | solution.py:420
  151.9 0.9 copy-start.11
  (12 other events, 8.7 us)

commit v9 on v7

--- a/solution.py
+++ b/solution.py
@@ -1,3 +1,5 @@
+import math
+
 import jax
 import jax.numpy as jnp
 from jax import lax
@@ -8,6 +10,7 @@
 LOGIT_SCALE = 64.0
 MARGIN = 0.4
 EPSILON = 1e-05
+SHRINK = math.exp(-LOGIT_SCALE * MARGIN)
 F32 = jnp.float32
 BF16 = jnp.bfloat16
 LARGE = 60 * 1024 * 1024
@@ -58,17 +61,17 @@
     return place == lax.broadcasted_iota(jnp.int32, (block, count), 0) + first
 
 
-def logits_of(w_hat, unit, place, first):
+def cosine_of(w_hat, unit, place, first):
     cosine = lax.dot_general(
         w_hat, unit, (((1,), (1,)), ((), ())), preferred_element_type=F32
     )
-    target = hits(place, w_hat.shape[0], unit.shape[0], first)
-    return LOGIT_SCALE * cosine - jnp.where(target, LOGIT_SCALE * MARGIN, 0.0), target
-
-
-def grad_of(w_hat, unit, place, first, total):
-    logits, target = logits_of(w_hat, unit, place, first)
-    return (jnp.exp(logits) / total - target.astype(F32)).astype(BF16)
+    return cosine, hits(place, w_hat.shape[0], unit.shape[0], first)
+
+
+def grad_of(w_hat, unit, place, first, inverse):
+    cosine, target = cosine_of(w_hat, unit, place, first)
+    share = jnp.exp(LOGIT_SCALE * cosine) * inverse
+    return jnp.where(target, share * SHRINK - 1.0, share).astype(BF16)
 
 
 def blocks_of(w_own, w_other):
@@ -84,11 +87,13 @@
     unit[...] = units
     exps = hit = None
     for w_hat, first in blocks_of(w_own, w_other):
-        logits, target = logits_of(w_hat, units, place[...], first)
-        term = jnp.sum(jnp.exp(logits), 0, keepdims=True)
-        other = jnp.sum(jnp.where(target, logits, 0.0), 0, keepdims=True)
+        cosine, target = cosine_of(w_hat, units, place[...], first)
+        term = jnp.exp(LOGIT_SCALE * cosine)
+        term = jnp.sum(jnp.where(target, term * SHRINK, term), 0, keepdims=True)
+        other = jnp.sum(jnp.where(target, cosine, 0.0), 0, keepdims=True)
         exps = term if exps is None else exps + term
         hit = other if hit is None else hit + other
+    hit = jnp.where(place[...] >= 0, LOGIT_SCALE * hit - LOGIT_SCALE * MARGIN, 0.0)
     both = jnp.concatenate([exps, hit], 0)
     for p in range(stats.shape[0]):
         stats[p] = both
@@ -98,10 +103,10 @@
     batch, rows, sums, gain, bias, place, totals, unit, w_own, w_other, packed
 ):
     units = unit[...]
-    row_total = jnp.sum(totals[...], 0)[0:1, : units.shape[0]]
+    inverse = 1.0 / jnp.sum(totals[...], 0)[0:1, : units.shape[0]]
     pull = None
     for w_hat, first in blocks_of(w_own, w_other):
-        grad = grad_of(w_hat, units, place[...], first, row_total)
+        grad = grad_of(w_hat, units, place[...], first, inverse)
         term = lax.dot_general(
             grad, w_hat, (((0,), (0,)), ((), ())), preferred_element_type=F32
         )
@@ -196,14 +201,14 @@
     block = mine.shape[0]
     copies = []
     group = unit.shape[0]
-    total = jnp.sum(totals[...], 0)
+    inverse = 1.0 / jnp.sum(totals[...], 0)[:, :group]
     for i in range(parts):
         first = pl.multiple_of(lax.rem(at[0] + i, parts) * block, 64)
         w_hat = w_own[pl.ds(first, block)]
         raw = None
         for units, places, row in ((unit, place, 0), (unit_2, place_2, 1)):
             grad = grad_of(
-                w_hat, units[...], places[...], first, total[row : row + 1, :group]
+                w_hat, units[...], places[...], first, inverse[row : row + 1]
             )
             term = jnp.dot(grad, units[...], preferred_element_type=F32)
             raw = term if raw is None else raw + term

time: 153 us -> 153 us (level)
  no operation moved by 1% of the time
where the time goes in v9:
time: 153 us; the launch traced here: 152 us
  starting transfers between devices  74.6 us (49%)
  waiting for transfers between devices  23.3 us (15%)
  Pallas kernels  18.8 us (12%)
  blocking collectives  16 us (10%)
  local copies, waits for them, and re-layouts  14.3 us (9%)
  other arithmetic  4.02 us (3%)
    all_to_all x3, starting transfers between devices, spread(): return lax.all_to_all(copies, axes, 0, 0)  28.2 us
    ppermute x8, starting transfers between devices, shift(): return lax.ppermute(block, axis, [(i, (i + by) % n) for i in range(n)])  27 us
    all_to_all x1, blocking collectives, body(): totals = lax.all_to_all(totals, 'z', 0, 0)  16 us
    all_to_all x3, waiting for transfers between devices, spread(): return lax.all_to_all(copies, axes, 0, 0)  11.6 us
    all_to_all x1, starting transfers between devices, body(): ends = lax.all_to_all(ends, ('core', 'rep'), 0, 0)  7.16 us
    unnamed x32, local copies, waits for them, and re-layouts  6.91 us
    pallas_call x1, Pallas kernels, body(): call(lambda *refs: pull_kernel(batch, *refs), [VM] * 9, VM, jax.ShapeDtyp...  5.76 us
    all_to_all x1, starting transfers between devices, body(): pull = lax.all_to_all(pull, 'z', 0, 0)  5.42 us
  transfers between devices with their start and end apart: 15, of which 7 were waited for; matrix products, arithmetic and copies ran while one was open for 6% of the time, Pallas kernels for 5%

profile of v9, /device:TPU:1, one launch (start us, length us, event | category | flops | bytes accessed | tf_op | source)
XLA Modules:
  0.0 151.9 jit_solution(12844635785346873236)
XLA Ops:
  2.1 15.7 %all-to-all-start = ((bf16[16,8,512]{2,1,0:T(8,128)(2,1)}), bf16[16,8,512]{2,1,0:T(8,128)(2,1)S(1)}, u32[]{:S(2)}, u32[]{:S(2)}) async-start(bf16[16,8,512]{2,1,0:T(8,128)(2,1)} %broadcast_in_dim.16), calls=%async_computation | async-start | bytes 262144 | tf_op jit(solution)/shard_map/all_to_all | solution.py:23
  18.6 2.7 %gather_fusion = bf16[768,512]{1,0:T(8,128)(2,1)S(1)} fusion(bf16[2048,512]{1,0:T(8,128)(2,1)S(1)} %copy-done, s32[1024]{0:T(1024)S(1)} %pad_clamp_fusion), kind=kCustom, calls=%fused_computation | custom fusion | bytes 1575936 | tf_op jit(solution)/shard_map/gather | solution.py:301
  22.7 7.2 %all-to-all-done = bf16[16,8,512]{2,1,0:T(8,128)(2,1)S(1)} async-done(((bf16[16,8,512]{2,1,0:T(8,128)(2,1)}), bf16[16,8,512]{2,1,0:T(8,128)(2,1)S(1)}, u32[]{:S(2)}, u32[]{:S(2)}) %all-to-all-start) | async-done | bytes 131104 | tf_op jit(solution)/shard_map/all_to_all | solution.py:23
  30.7 4.0 %all-to-all-start.1 = ((bf16[4,128,512]{2,1,0:T(8,128)(2,1)}), bf16[4,128,512]{2,1,0:T(8,128)(2,1)S(1)}, u32[]{:S(2)}, u32[]{:S(2)}) async-start(bf16[4,128,512]{2,1,0:T(8,128)(2,1)} %broadcast_in_dim.34), calls=%async_computation.1 | async-start | bytes 1048576 | tf_op jit(solution)/shard_map/all_to_all | solution.py:23
  34.8 5.8 %collective-permute-start = (bf16[768,512]{1,0:T(8,128)(2,1)}, bf16[768,512]{1,0:T(8,128)(2,1)}, u32[]{:S(2)}, u32[]{:S(2)}) collective-permute-start(bf16[768,512]{1,0:T(8,128)(2,1)} %fusion.1.refs_5_.refs_7_.refs_6_), channel_id=1, source_target_pairs={{0,4},{4,0},{1,5},{5,1},{2,6},{6,2},{3,7},{7,3},{8,12},{12,8},{9,1... | collective-permute-start | bytes 2359304 | tf_op jit(solution)/shard_map/ppermute | solution.py:28
  43.8 8.4 %all-to-all-start.2 = ((f32[8,2,512]{2,1,0:T(2,128)}), f32[8,2,512]{2,1,0:T(2,128)S(1)}, u32[]{:S(2)}, u32[]{:S(2)}) async-start(f32[8,2,512]{2,1,0:T(2,128)} %broadcast_in_dim.35), calls=%async_computation.2 | async-start | bytes 65536 | tf_op jit(solution)/shard_map/all_to_all | solution.py:23
  52.8 4.3 %all-to-all-done.2.refs_1_.refs_2_ = f32[8,2,512]{2,1,0:T(2,128)S(1)} async-done(((f32[8,2,512]{2,1,0:T(2,128)}), f32[8,2,512]{2,1,0:T(2,128)S(1)}, u32[]{:S(2)}, u32[]{:S(2)}) %all-to-all-start.2) | async-done | bytes 32800 | tf_op jit(solution)/shard_map/all_to_all | solution.py:23
  57.7 3.9 %shard_map.110 = (bf16[512,512]{1,0:T(8,128)(2,1)}, f32[8,2,512]{2,1,0:T(2,128)}) custom-call(bf16[512,512]{1,0:T(8,128)(2,1)} %bitcast.24, f32[8,2,512]{2,1,0:T(2,128)} %copy-done.6, f32[1,512]{1,0:T(1,128)} %bitcast.18, f32[1,512]{1,0:T(1,128)} %bitcast.21, s32[1,512]{1,0:T(1,128)} %select_select_fusion.refs_4_.refs_1_, ...), custom_call_target="tpu_custom_call" | custom-call | flops 805306368 | bytes 1572864 | tf_op jit(solution)/shard_map/pallas_call | solution.py:328
  61.6 2.3 %collective-permute-start.1 = (bf16[512,512]{1,0:T(8,128)(2,1)}, bf16[512,512]{1,0:T(8,128)(2,1)}, u32[]{:S(2)}, u32[]{:S(2)}) collective-permute-start(bf16[512,512]{1,0:T(8,128)(2,1)} %get-tuple-element.28.refs_6_.refs_4_), channel_id=1, source_target_pairs={{0,4},{4,0},{1,5},{5,1},{2,6},{6,2},{3,7},{7,3},{8,12},{12,8},{9,1... | collective-permute-start | bytes 1572872 | tf_op jit(solution)/shard_map/ppermute | solution.py:28
  63.9 3.4 %all-to-all-start.3 = ((f32[8,2,512]{2,1,0:T(2,128)}), f32[8,2,512]{2,1,0:T(2,128)S(1)}, u32[]{:S(2)}, u32[]{:S(2)}) async-start(f32[8,2,512]{2,1,0:T(2,128)} %get-tuple-element.27), calls=%async_computation.3 | async-start | bytes 65536 | tf_op jit(solution)/shard_map/all_to_all | solution.py:342
  68.0 4.0 %all-to-all-done.3.refs_1_ = f32[8,2,512]{2,1,0:T(2,128)S(1)} async-done(((f32[8,2,512]{2,1,0:T(2,128)}), f32[8,2,512]{2,1,0:T(2,128)S(1)}, u32[]{:S(2)}, u32[]{:S(2)}) %all-to-all-start.3) | async-done | bytes 32800 | tf_op jit(solution)/shard_map/all_to_all | solution.py:342
  72.6 16.0 %all_to_all.40.refs_5_.refs_3_.refs_6_ = f32[16,2,640]{2,1,0:T(2,128)} all-to-all(f32[16,2,640]{2,1,0:T(2,128)S(1)} %shard_map.111), channel_id=1, replica_groups=mesh['x'=4,'z'=16,'core'=2,'rep'=4] {'z'}, dimensions={0} | all-to-all | bytes 163840 | tf_op jit(solution)/shard_map/all_to_all | solution.py:353
  88.6 5.8 %shard_map.112.refs_7_ = bf16[4,144,512]{2,1,0:T(8,128)(2,1)} custom-call(bf16[512,512]{1,0:T(8,128)(2,1)} %bitcast.25, f32[8,2,512]{2,1,0:T(2,128)} %copy-done.6, f32[1,512]{1,0:T(1,128)} %bitcast.19, f32[1,512]{1,0:T(1,128)} %bitcast.22, s32[1,512]{1,0:T(1,128)} %select_select_fusion.refs_4_.refs_1_, f32[16,2,640]{2,1,0:T(2,128)} %all_to_all.40.refs_5_.refs_3_.refs_6_, ...), custom_call_target="tpu_custom_call" | custom-call | flops 1610612736 | bytes 1572864 | tf_op jit(solution)/shard_map/pallas_call | solution.py:355
  94.4 3.5 %all-to-all-start.5 = ((bf16[4,144,512]{2,1,0:T(8,128)(2,1)}), bf16[4,144,512]{2,1,0:T(8,128)(2,1)S(1)}, u32[]{:S(2)}, u32[]{:S(2)}) async-start(bf16[4,144,512]{2,1,0:T(8,128)(2,1)} %shard_map.112.refs_7_), calls=%async_computation.5 | async-start | bytes 1179648 | tf_op jit(solution)/shard_map/all_to_all | solution.py:392
  97.9 5.1 %shard_map.113 = (f32[192,512]{1,0:T(8,128)}, bf16[192,512]{1,0:T(8,128)(2,1)}, bf16[192,512]{1,0:T(8,128)(2,1)}, bf16[192,512]{1,0:T(8,128)(2,1)}) custom-call(s32[1]{0:T(128)} %bitcast.13.refs_0_, s32[1,512]{1,0:T(1,128)} %select_select_fusion.refs_4_.refs_1_, s32[1,512]{1,0:T(1,128)} %select_n.55.refs_2_, ...), custom_call_target="tpu_custom_call" | custom-call | flops 1610612736 | bytes 1572864 | tf_op jit(solution)/shard_map/pallas_call | solution.py:366
  103.0 2.4 %all-to-all-done.5.refs_0_ = bf16[4,144,512]{2,1,0:T(8,128)(2,1)S(1)} async-done(((bf16[4,144,512]{2,1,0:T(8,128)(2,1)}), bf16[4,144,512]{2,1,0:T(8,128)(2,1)S(1)}, u32[]{:S(2)}, u32[]{:S(2)}) %all-to-all-start.5) | async-done | bytes 589856 | tf_op jit(solution)/shard_map/all_to_all | solution.py:392
  106.2 5.4 %all-to-all-start.6 = ((bf16[16,48,128]{2,1,0:T(8,128)(2,1)}), bf16[16,48,128]{2,1,0:T(8,128)(2,1)S(1)}, u32[]{:S(2)}, u32[]{:S(2)}) async-start(bf16[16,48,128]{2,1,0:T(8,128)(2,1)} %copy-done.1), calls=%async_computation.6 | async-start | bytes 393216 | tf_op jit(solution)/shard_map/all_to_all | solution.py:405
  111.6 2.3 %collective-permute-start.2 = (bf16[192,512]{1,0:T(8,128)(2,1)}, bf16[192,512]{1,0:T(8,128)(2,1)S(1)}, u32[]{:S(2)}, u32[]{:S(2)}) collective-permute-start(bf16[192,512]{1,0:T(8,128)(2,1)} %get-tuple-element.38), channel_id=1, source_target_pairs={{0,1},{1,2},{2,3},{3,0},{4,5},{5,6},{6,7},{7,4},{8,9},{9,10},{10,1... | collective-permute-start | bytes 589832 | tf_op jit(solution)/shard_map/ppermute | solution.py:28
  113.9 3.6 %collective-permute-start.3 = (bf16[192,512]{1,0:T(8,128)(2,1)}, bf16[192,512]{1,0:T(8,128)(2,1)S(1)}, u32[]{:S(2)}, u32[]{:S(2)}) collective-permute-start(bf16[192,512]{1,0:T(8,128)(2,1)} %get-tuple-element.39), channel_id=1, source_target_pairs={{0,2},{1,3},{2,0},{3,1},{4,6},{5,7},{6,4},{7,5},{8,10},{9,11},{10,... | collective-permute-start | bytes 589832 | tf_op jit(solution)/shard_map/ppermute | solution.py:28
  117.6 2.8 %collective-permute-start.4 = (bf16[192,512]{1,0:T(8,128)(2,1)}, bf16[192,512]{1,0:T(8,128)(2,1)S(1)}, u32[]{:S(2)}, u32[]{:S(2)}) collective-permute-start(bf16[192,512]{1,0:T(8,128)(2,1)} %get-tuple-element.40), channel_id=1, source_target_pairs={{0,3},{1,0},{2,1},{3,2},{4,7},{5,4},{6,5},{7,6},{8,11},{9,8},{10,9... | collective-permute-start | bytes 589832 | tf_op jit(solution)/shard_map/ppermute | solution.py:28
  120.3 4.1 %collective-permute-done.3.refs_4_ = bf16[192,512]{1,0:T(8,128)(2,1)S(1)} collective-permute-done((bf16[192,512]{1,0:T(8,128)(2,1)}, bf16[192,512]{1,0:T(8,128)(2,1)S(1)}, u32[]{:S(2)}, u32[]{:S(2)}) %collective-permute-start.3) | collective-permute-done | bytes 196640 | tf_op jit(solution)/shard_map/ppermute | solution.py:28
  127.0 4.1 %collective-permute-start.7 = (bf16[192,512]{1,0:T(8,128)(2,1)S(1)}, bf16[192,512]{1,0:T(8,128)(2,1)S(1)}, u32[]{:S(2)}, u32[]{:S(2)}) collective-permute-start(bf16[192,512]{1,0:T(8,128)(2,1)S(1)} %shard_map.117.refs_3_), channel_id=1, source_target_pairs={{0,3},{1,0},{2,1},{3,2},{4,7},{5,4},{6,5},{7,6},{8,11},{9,8},{10,9... | collective-permute-start | bytes 589832 | tf_op jit(solution)/shard_map/ppermute | solution.py:28
  131.1 4.2 %collective-permute-start.6 = (bf16[192,512]{1,0:T(8,128)(2,1)S(1)}, bf16[192,512]{1,0:T(8,128)(2,1)S(1)}, u32[]{:S(2)}, u32[]{:S(2)}) collective-permute-start(bf16[192,512]{1,0:T(8,128)(2,1)S(1)} %shard_map.117.refs_3_), channel_id=1, source_target_pairs={{0,2},{1,3},{2,0},{3,1},{4,6},{5,7},{6,4},{7,5},{8,10},{9,11},{10,... | collective-permute-start | bytes 589832 | tf_op jit(solution)/shard_map/ppermute | solution.py:28
  137.9 7.2 %all-to-all-start.7 = ((f32[8,2,512]{2,1,0:T(2,128)}), f32[8,2,512]{2,1,0:T(2,128)S(1)}, u32[]{:S(2)}, u32[]{:S(2)}) async-start(f32[8,2,512]{2,1,0:T(2,128)} %get-tuple-element.37), calls=%async_computation.7 | async-start | bytes 65536 | tf_op jit(solution)/shard_map/all_to_all | solution.py:418
  (68 shorter events, 22.7 us)
Async XLA Ops:
  0.6 18.0 %copy-start = (bf16[2048,512]{1,0:T(8,128)(2,1)S(1)}, bf16[2048,512]{1,0:T(8,128)(2,1)}, u32[]{:S(2)}) copy-start(bf16[2048,512]{1,0:T(8,128)(2,1)} %param.10) | copy-start | bytes 6291460
  2.1 27.8 %all-to-all-start = ((bf16[16,8,512]{2,1,0:T(8,128)(2,1)}), bf16[16,8,512]{2,1,0:T(8,128)(2,1)S(1)}, u32[]{:S(2)}, u32[]{:S(2)}) async-start(bf16[16,8,512]{2,1,0:T(8,128)(2,1)} %broadcast_in_dim.16), calls=%async_computation | async-start | bytes 262144 | tf_op jit(solution)/shard_map/all_to_all | solution.py:23
  21.5 19.1 %copy-start.13 = (s32[128,1,8]{0,2,1:T(8,128)S(1)}, s32[128,1,8]{0,2,1:T(8,128)}, u32[]{:S(2)}) copy-start(s32[128,1,8]{0,2,1:T(8,128)} %param.12) | copy-start | bytes 12292
  21.6 19.6 %copy-start.14 = (s32[128,1,8]{0,2,1:T(8,128)S(1)}, s32[128,1,8]{0,2,1:T(8,128)}, u32[]{:S(2)}) copy-start(s32[128,1,8]{0,2,1:T(8,128)} %param.13) | copy-start | bytes 12292
  30.7 12.2 %all-to-all-start.1 = ((bf16[4,128,512]{2,1,0:T(8,128)(2,1)}), bf16[4,128,512]{2,1,0:T(8,128)(2,1)S(1)}, u32[]{:S(2)}, u32[]{:S(2)}) async-start(bf16[4,128,512]{2,1,0:T(8,128)(2,1)} %broadcast_in_dim.34), calls=%async_computation.1 | async-start | bytes 1048576 | tf_op jit(solution)/shard_map/all_to_all | solution.py:23
  34.8 22.4 %collective-permute-start = (bf16[768,512]{1,0:T(8,128)(2,1)}, bf16[768,512]{1,0:T(8,128)(2,1)}, u32[]{:S(2)}, u32[]{:S(2)}) collective-permute-start(bf16[768,512]{1,0:T(8,128)(2,1)} %fusion.1.refs_5_.refs_7_.refs_6_), channel_id=1, source_target_pairs={{0,4},{4,0},{1,5},{5,1},{2,6},{6,2},{3,7},{7,3},{8,12},{12,8},{9,1... | collective-permute-start | bytes 2359304 | tf_op jit(solution)/shard_map/ppermute | solution.py:28
  42.9 14.2 %copy-start.11 = (bf16[4,128,512]{2,1,0:T(8,128)(2,1)}, bf16[4,128,512]{2,1,0:T(8,128)(2,1)S(1)}, u32[]{:S(2)}) copy-start(bf16[4,128,512]{2,1,0:T(8,128)(2,1)S(1)} %all-to-all-done.1) | copy-start | bytes 1572868
  43.8 23.6 %copy-start.12 = (s32[64,8]{1,0:T(8,128)S(1)}, s32[64,8]{1,0:T(8,128)}, u32[]{:S(2)}) copy-start(s32[64,8]{1,0:T(8,128)} %get-tuple-element.47) | copy-start | bytes 6148
  43.8 13.4 %all-to-all-start.2 = ((f32[8,2,512]{2,1,0:T(2,128)}), f32[8,2,512]{2,1,0:T(2,128)S(1)}, u32[]{:S(2)}, u32[]{:S(2)}) async-start(f32[8,2,512]{2,1,0:T(2,128)} %broadcast_in_dim.35), calls=%async_computation.2 | async-start | bytes 65536 | tf_op jit(solution)/shard_map/all_to_all | solution.py:23
  61.6 11.0 %collective-permute-start.1 = (bf16[512,512]{1,0:T(8,128)(2,1)}, bf16[512,512]{1,0:T(8,128)(2,1)}, u32[]{:S(2)}, u32[]{:S(2)}) collective-permute-start(bf16[512,512]{1,0:T(8,128)(2,1)} %get-tuple-element.28.refs_6_.refs_4_), channel_id=1, source_target_pairs={{0,4},{4,0},{1,5},{5,1},{2,6},{6,2},{3,7},{7,3},{8,12},{12,8},{9,1... | collective-permute-start | bytes 1572872 | tf_op jit(solution)/shard_map/ppermute | solution.py:28
  63.9 8.1 %all-to-all-start.3 = ((f32[8,2,512]{2,1,0:T(2,128)}), f32[8,2,512]{2,1,0:T(2,128)S(1)}, u32[]{:S(2)}, u32[]{:S(2)}) async-start(f32[8,2,512]{2,1,0:T(2,128)} %get-tuple-element.27), calls=%async_computation.3 | async-start | bytes 65536 | tf_op jit(solution)/shard_map/all_to_all | solution.py:342
  94.4 11.1 %all-to-all-start.5 = ((bf16[4,144,512]{2,1,0:T(8,128)(2,1)}), bf16[4,144,512]{2,1,0:T(8,128)(2,1)S(1)}, u32[]{:S(2)}, u32[]{:S(2)}) async-start(bf16[4,144,512]{2,1,0:T(8,128)(2,1)} %shard_map.112.refs_7_), calls=%async_computation.5 | async-start | bytes 1179648 | tf_op jit(solution)/shard_map/all_to_all | solution.py:392
  105.4 39.7 %copy-start.3 = (f32[16,2,640]{2,1,0:T(2,128)S(1)}, f32[16,2,640]{2,1,0:T(2,128)}, u32[]{:S(2)}) copy-start(f32[16,2,640]{2,1,0:T(2,128)} %all_to_all.40.refs_5_.refs_3_.refs_6_) | copy-start | bytes 245764
  106.2 31.1 %all-to-all-start.6 = ((bf16[16,48,128]{2,1,0:T(8,128)(2,1)}), bf16[16,48,128]{2,1,0:T(8,128)(2,1)S(1)}, u32[]{:S(2)}, u32[]{:S(2)}) async-start(bf16[16,48,128]{2,1,0:T(8,128)(2,1)} %copy-done.1), calls=%async_computation.6 | async-start | bytes 393216 | tf_op jit(solution)/shard_map/all_to_all | solution.py:405
  111.6 8.7 %collective-permute-start.2 = (bf16[192,512]{1,0:T(8,128)(2,1)}, bf16[192,512]{1,0:T(8,128)(2,1)S(1)}, u32[]{:S(2)}, u32[]{:S(2)}) collective-permute-start(bf16[192,512]{1,0:T(8,128)(2,1)} %get-tuple-element.38), channel_id=1, source_target_pairs={{0,1},{1,2},{2,3},{3,0},{4,5},{5,6},{6,7},{7,4},{8,9},{9,10},{10,1... | collective-permute-start | bytes 589832 | tf_op jit(solution)/shard_map/ppermute | solution.py:28
  113.9 10.5 %collective-permute-start.3 = (bf16[192,512]{1,0:T(8,128)(2,1)}, bf16[192,512]{1,0:T(8,128)(2,1)S(1)}, u32[]{:S(2)}, u32[]{:S(2)}) collective-permute-start(bf16[192,512]{1,0:T(8,128)(2,1)} %get-tuple-element.39), channel_id=1, source_target_pairs={{0,2},{1,3},{2,0},{3,1},{4,6},{5,7},{6,4},{7,5},{8,10},{9,11},{10,... | collective-permute-start | bytes 589832 | tf_op jit(solution)/shard_map/ppermute | solution.py:28
  117.6 7.9 %collective-permute-start.4 = (bf16[192,512]{1,0:T(8,128)(2,1)}, bf16[192,512]{1,0:T(8,128)(2,1)S(1)}, u32[]{:S(2)}, u32[]{:S(2)}) collective-permute-start(bf16[192,512]{1,0:T(8,128)(2,1)} %get-tuple-element.40), channel_id=1, source_target_pairs={{0,3},{1,0},{2,1},{3,2},{4,7},{5,4},{6,5},{7,6},{8,11},{9,8},{10,9... | collective-permute-start | bytes 589832 | tf_op jit(solution)/shard_map/ppermute | solution.py:28
  125.5 1.0 copy-start.2
  127.0 22.1 %collective-permute-start.7 = (bf16[192,512]{1,0:T(8,128)(2,1)S(1)}, bf16[192,512]{1,0:T(8,128)(2,1)S(1)}, u32[]{:S(2)}, u32[]{:S(2)}) collective-permute-start(bf16[192,512]{1,0:T(8,128)(2,1)S(1)} %shard_map.117.refs_3_), channel_id=1, source_target_pairs={{0,3},{1,0},{2,1},{3,2},{4,7},{5,4},{6,5},{7,6},{8,11},{9,8},{10,9... | collective-permute-start | bytes 589832 | tf_op jit(solution)/shard_map/ppermute | solution.py:28
  131.1 18.1 %collective-permute-start.6 = (bf16[192,512]{1,0:T(8,128)(2,1)S(1)}, bf16[192,512]{1,0:T(8,128)(2,1)S(1)}, u32[]{:S(2)}, u32[]{:S(2)}) collective-permute-start(bf16[192,512]{1,0:T(8,128)(2,1)S(1)} %shard_map.117.refs_3_), channel_id=1, source_target_pairs={{0,2},{1,3},{2,0},{3,1},{4,6},{5,7},{6,4},{7,5},{8,10},{9,11},{10,... | collective-permute-start | bytes 589832 | tf_op jit(solution)/shard_map/ppermute | solution.py:28
  135.3 13.9 %collective-permute-start.5 = (bf16[192,512]{1,0:T(8,128)(2,1)S(1)}, bf16[192,512]{1,0:T(8,128)(2,1)S(1)}, u32[]{:S(2)}, u32[]{:S(2)}) collective-permute-start(bf16[192,512]{1,0:T(8,128)(2,1)S(1)} %shard_map.117.refs_3_), channel_id=1, source_target_pairs={{0,1},{1,2},{2,3},{3,0},{4,5},{5,6},{6,7},{7,4},{8,9},{9,10},{10,1... | collective-permute-start | bytes 589832 | tf_op jit(solution)/shard_map/ppermute | solution.py:28
  137.9 12.1 %all-to-all-start.7 = ((f32[8,2,512]{2,1,0:T(2,128)}), f32[8,2,512]{2,1,0:T(2,128)S(1)}, u32[]{:S(2)}, u32[]{:S(2)}) async-start(f32[8,2,512]{2,1,0:T(2,128)} %get-tuple-element.37), calls=%async_computation.7 | async-start | bytes 65536 | tf_op jit(solution)/shard_map/all_to_all | solution.py:418
  145.1 0.8 copy-start.7
  150.0 0.9 copy-start.5
  (6 other events, 4.0 us)

commit v10 on v9

--- a/solution.py
+++ b/solution.py
@@ -270,9 +270,7 @@
     loss[...] = jnp.sum(jnp.where(same, values, 0.0), 0, keepdims=True)
 
 
-def final_kernel(parts, at, terms, ends, *refs):
-    found, (emb, grad, gain_grad, bias_grad) = refs[:parts], refs[parts:]
-    block = found[0].shape[0]
+def final_kernel(terms, ends, emb, gain_grad, bias_grad):
     n = emb.shape[0]
     both = jnp.sum(ends[...], 0)
     bias_grad[...] = both[0:1]
@@ -280,9 +278,6 @@
     emb[...] = (
         terms[0:n] - terms[2 * n : 3 * n] * both[0:1] - terms[n : 2 * n] * both[1:2]
     )
-    for by, piece in enumerate(found):
-        where = lax.rem(at[0] - by + parts, parts) * block
-        grad[pl.ds(pl.multiple_of(where, 64), block)] = piece[...]
 
 
 def body(embeddings, bn_gain, bn_bias, centres, sample_rows, label_shard, label_slot):
@@ -430,20 +425,20 @@
         40 * rows_dev * width,
         grant=SMALL,
     )(own.astype(jnp.int32), embeddings, sums, gain, bias, grad_unit, totals)
-    emb_grad, centre_grad, gain_grad, bias_grad = call(
-        lambda *refs: final_kernel(nr, *refs),
-        [SM] + [VM] * (2 + nr),
-        [VM] * 4,
+    emb_grad, gain_grad, bias_grad = call(
+        final_kernel,
+        [VM] * 2,
+        [VM] * 3,
         [
             jax.ShapeDtypeStruct((rows_dev, width), F32),
-            jax.ShapeDtypeStruct((slots, width), BF16),
             jax.ShapeDtypeStruct((1, width), F32),
             jax.ShapeDtypeStruct((1, width), F32),
         ],
-        slots * width,
-        4 * slots * width,
-        grant=SMALL,
-    )(at, terms, ends, grad, *[shift(grad, "rep", by) for by in range(1, nr)])
+        8 * rows_dev * width,
+        16 * rows_dev * width,
+        grant=SMALL,
+    )(terms, ends)
+    centre_grad = lax.all_gather(grad, "rep", axis=0, tiled=True)
     return (row_loss[0], emb_grad, centre_grad, gain_grad[0], bias_grad[0])
 
 

time: 153 us -> 158 us (1.033)
  blocking collectives: 16 us -> 28.1 us
  starting transfers between devices: 74.6 us -> 64.9 us
    all_gather x0 -> x1, blocking collectives: none -> 12.1 us  [body(): centre_grad = lax.all_gather(grad, 'rep', axis=0, tiled=True)]
    ppermute x8 -> x5, starting transfers between devices: 27 us -> 16.8 us  [shift(): return lax.ppermute(block, axis, [(i, (i + by) % n) for i in range(n)])]
    unnamed x32 -> x35, local copies, waits for them, and re-layouts: 6.91 us -> 8.46 us
    ppermute x8 -> x5, waiting for transfers between devices: 5.14 us -> 3.87 us  [shift(): return lax.ppermute(block, axis, [(i, (i + by) % n) for i in range(n)])]
  transfers between devices with their start and end apart: 15 -> 12, of which waited for: 7 -> 6; matrix products, arithmetic and copies ran while one was open for 6% -> 6% of each run, Pallas kernels for 5% -> 5%
where the time goes in v10:
time: 158 us; the launch traced here: 156 us
  starting transfers between devices  64.9 us (41%)
  blocking collectives  28.1 us (18%)
  waiting for transfers between devices  21.9 us (14%)
  Pallas kernels  19.4 us (12%)
  local copies, waits for them, and re-layouts  15.8 us (10%)
  other arithmetic  4.53 us (3%)
    all_to_all x3, starting transfers between devices, spread(): return lax.all_to_all(copies, axes, 0, 0)  28.2 us
    ppermute x5, starting transfers between devices, shift(): return lax.ppermute(block, axis, [(i, (i + by) % n) for i in range(n)])  16.8 us
    all_to_all x1, blocking collectives, body(): totals = lax.all_to_all(totals, 'z', 0, 0)  16.1 us
    all_gather x1, blocking collectives, body(): centre_grad = lax.all_gather(grad, 'rep', axis=0, tiled=True)  12.1 us
    all_to_all x3, waiting for transfers between devices, spread(): return lax.all_to_all(copies, axes, 0, 0)  11.6 us
    unnamed x35, local copies, waits for them, and re-layouts  8.46 us
    all_to_all x1, starting transfers between devices, body(): ends = lax.all_to_all(ends, ('core', 'rep'), 0, 0)  7.68 us
    pallas_call x1, Pallas kernels, body(): call(lambda *refs: pull_kernel(batch, *refs), [VM] * 9, VM, jax.ShapeDtyp...  5.74 us
  transfers between devices with their start and end apart: 12, of which 6 were waited for; matrix products, arithmetic and copies ran while one was open for 6% of the time, Pallas kernels for 5%

profile of v10, /device:TPU:1, one launch (start us, length us, event | category | flops | bytes accessed | tf_op | source)
XLA Modules:
  0.0 155.6 jit_solution(1744786471906345252)
XLA Ops:
  2.2 15.7 %all-to-all-start = ((bf16[16,8,512]{2,1,0:T(8,128)(2,1)}), bf16[16,8,512]{2,1,0:T(8,128)(2,1)S(1)}, u32[]{:S(2)}, u32[]{:S(2)}) async-start(bf16[16,8,512]{2,1,0:T(8,128)(2,1)} %broadcast_in_dim.16), calls=%async_computation | async-start | bytes 262144 | tf_op jit(solution)/shard_map/all_to_all | solution.py:23
  18.6 2.7 %gather_fusion = bf16[768,512]{1,0:T(8,128)(2,1)S(1)} fusion(bf16[2048,512]{1,0:T(8,128)(2,1)S(1)} %copy-done, s32[1024]{0:T(1024)S(1)} %pad_clamp_fusion), kind=kCustom, calls=%fused_computation | custom fusion | bytes 1575936 | tf_op jit(solution)/shard_map/gather | solution.py:296
  22.7 7.2 %all-to-all-done = bf16[16,8,512]{2,1,0:T(8,128)(2,1)S(1)} async-done(((bf16[16,8,512]{2,1,0:T(8,128)(2,1)}), bf16[16,8,512]{2,1,0:T(8,128)(2,1)S(1)}, u32[]{:S(2)}, u32[]{:S(2)}) %all-to-all-start) | async-done | bytes 131104 | tf_op jit(solution)/shard_map/all_to_all | solution.py:23
  30.8 4.0 %all-to-all-start.1 = ((bf16[4,128,512]{2,1,0:T(8,128)(2,1)}), bf16[4,128,512]{2,1,0:T(8,128)(2,1)S(1)}, u32[]{:S(2)}, u32[]{:S(2)}) async-start(bf16[4,128,512]{2,1,0:T(8,128)(2,1)} %broadcast_in_dim.34), calls=%async_computation.1 | async-start | bytes 1048576 | tf_op jit(solution)/shard_map/all_to_all | solution.py:23
  34.8 5.8 %collective-permute-start = (bf16[768,512]{1,0:T(8,128)(2,1)}, bf16[768,512]{1,0:T(8,128)(2,1)}, u32[]{:S(2)}, u32[]{:S(2)}) collective-permute-start(bf16[768,512]{1,0:T(8,128)(2,1)} %fusion.1.refs_5_.refs_7_.refs_6_), channel_id=1, source_target_pairs={{0,4},{4,0},{1,5},{5,1},{2,6},{6,2},{3,7},{7,3},{8,12},{12,8},{9,1... | collective-permute-start | bytes 2359304 | tf_op jit(solution)/shard_map/ppermute | solution.py:28
  43.8 8.4 %all-to-all-start.2 = ((f32[8,2,512]{2,1,0:T(2,128)}), f32[8,2,512]{2,1,0:T(2,128)S(1)}, u32[]{:S(2)}, u32[]{:S(2)}) async-start(f32[8,2,512]{2,1,0:T(2,128)} %broadcast_in_dim.35), calls=%async_computation.2 | async-start | bytes 65536 | tf_op jit(solution)/shard_map/all_to_all | solution.py:23
  52.8 4.3 %all-to-all-done.2.refs_1_.refs_2_ = f32[8,2,512]{2,1,0:T(2,128)S(1)} async-done(((f32[8,2,512]{2,1,0:T(2,128)}), f32[8,2,512]{2,1,0:T(2,128)S(1)}, u32[]{:S(2)}, u32[]{:S(2)}) %all-to-all-start.2) | async-done | bytes 32800 | tf_op jit(solution)/shard_map/all_to_all | solution.py:23
  57.7 3.9 %shard_map.110 = (bf16[512,512]{1,0:T(8,128)(2,1)}, f32[8,2,512]{2,1,0:T(2,128)}) custom-call(bf16[512,512]{1,0:T(8,128)(2,1)} %bitcast.24, f32[8,2,512]{2,1,0:T(2,128)} %copy-done.6, f32[1,512]{1,0:T(1,128)} %bitcast.18, f32[1,512]{1,0:T(1,128)} %bitcast.21, s32[1,512]{1,0:T(1,128)} %select_select_fusion.refs_4_.refs_1_, ...), custom_call_target="tpu_custom_call" | custom-call | flops 805306368 | bytes 1572864 | tf_op jit(solution)/shard_map/pallas_call | solution.py:323
  61.6 2.3 %collective-permute-start.1 = (bf16[512,512]{1,0:T(8,128)(2,1)}, bf16[512,512]{1,0:T(8,128)(2,1)}, u32[]{:S(2)}, u32[]{:S(2)}) collective-permute-start(bf16[512,512]{1,0:T(8,128)(2,1)} %get-tuple-element.27.refs_6_.refs_4_), channel_id=1, source_target_pairs={{0,4},{4,0},{1,5},{5,1},{2,6},{6,2},{3,7},{7,3},{8,12},{12,8},{9,1... | collective-permute-start | bytes 1572872 | tf_op jit(solution)/shard_map/ppermute | solution.py:28
  63.9 3.4 %all-to-all-start.3 = ((f32[8,2,512]{2,1,0:T(2,128)}), f32[8,2,512]{2,1,0:T(2,128)S(1)}, u32[]{:S(2)}, u32[]{:S(2)}) async-start(f32[8,2,512]{2,1,0:T(2,128)} %get-tuple-element.26), calls=%async_computation.3 | async-start | bytes 65536 | tf_op jit(solution)/shard_map/all_to_all | solution.py:337
  68.0 4.0 %all-to-all-done.3.refs_1_ = f32[8,2,512]{2,1,0:T(2,128)S(1)} async-done(((f32[8,2,512]{2,1,0:T(2,128)}), f32[8,2,512]{2,1,0:T(2,128)S(1)}, u32[]{:S(2)}, u32[]{:S(2)}) %all-to-all-start.3) | async-done | bytes 32800 | tf_op jit(solution)/shard_map/all_to_all | solution.py:337
  72.6 16.1 %all_to_all.40.refs_5_.refs_3_.refs_6_ = f32[16,2,640]{2,1,0:T(2,128)} all-to-all(f32[16,2,640]{2,1,0:T(2,128)S(1)} %shard_map.111), channel_id=1, replica_groups=mesh['x'=4,'z'=16,'core'=2,'rep'=4] {'z'}, dimensions={0} | all-to-all | bytes 163840 | tf_op jit(solution)/shard_map/all_to_all | solution.py:348
  88.6 5.7 %shard_map.112.refs_7_ = bf16[4,144,512]{2,1,0:T(8,128)(2,1)} custom-call(bf16[512,512]{1,0:T(8,128)(2,1)} %bitcast.25, f32[8,2,512]{2,1,0:T(2,128)} %copy-done.6, f32[1,512]{1,0:T(1,128)} %bitcast.19, f32[1,512]{1,0:T(1,128)} %bitcast.22, s32[1,512]{1,0:T(1,128)} %select_select_fusion.refs_4_.refs_1_, f32[16,2,640]{2,1,0:T(2,128)} %all_to_all.40.refs_5_.refs_3_.refs_6_, ...), custom_call_target="tpu_custom_call" | custom-call | flops 1610612736 | bytes 1572864 | tf_op jit(solution)/shard_map/pallas_call | solution.py:350
  94.4 3.5 %all-to-all-start.5 = ((bf16[4,144,512]{2,1,0:T(8,128)(2,1)}), bf16[4,144,512]{2,1,0:T(8,128)(2,1)S(1)}, u32[]{:S(2)}, u32[]{:S(2)}) async-start(bf16[4,144,512]{2,1,0:T(8,128)(2,1)} %shard_map.112.refs_7_), calls=%async_computation.5 | async-start | bytes 1179648 | tf_op jit(solution)/shard_map/all_to_all | solution.py:387
  97.9 5.1 %shard_map.113 = (f32[192,512]{1,0:T(8,128)}, bf16[192,512]{1,0:T(8,128)(2,1)}, bf16[192,512]{1,0:T(8,128)(2,1)}, bf16[192,512]{1,0:T(8,128)(2,1)}) custom-call(s32[1]{0:T(128)} %bitcast.13.refs_0_, s32[1,512]{1,0:T(1,128)} %select_select_fusion.refs_4_.refs_1_, s32[1,512]{1,0:T(1,128)} %select_n.55.refs_2_, ...), custom_call_target="tpu_custom_call" | custom-call | flops 1610612736 | bytes 1572864 | tf_op jit(solution)/shard_map/pallas_call | solution.py:361
  103.0 2.4 %all-to-all-done.5.refs_0_ = bf16[4,144,512]{2,1,0:T(8,128)(2,1)S(1)} async-done(((bf16[4,144,512]{2,1,0:T(8,128)(2,1)}), bf16[4,144,512]{2,1,0:T(8,128)(2,1)S(1)}, u32[]{:S(2)}, u32[]{:S(2)}) %all-to-all-start.5) | async-done | bytes 589856 | tf_op jit(solution)/shard_map/all_to_all | solution.py:387
  106.2 5.4 %all-to-all-start.6 = ((bf16[16,48,128]{2,1,0:T(8,128)(2,1)}), bf16[16,48,128]{2,1,0:T(8,128)(2,1)S(1)}, u32[]{:S(2)}, u32[]{:S(2)}) async-start(bf16[16,48,128]{2,1,0:T(8,128)(2,1)} %copy-done.1), calls=%async_computation.6 | async-start | bytes 393216 | tf_op jit(solution)/shard_map/all_to_all | solution.py:400
  111.6 2.3 %collective-permute-start.2 = (bf16[192,512]{1,0:T(8,128)(2,1)}, bf16[192,512]{1,0:T(8,128)(2,1)S(1)}, u32[]{:S(2)}, u32[]{:S(2)}) collective-permute-start(bf16[192,512]{1,0:T(8,128)(2,1)} %get-tuple-element.38), channel_id=1, source_target_pairs={{0,1},{1,2},{2,3},{3,0},{4,5},{5,6},{6,7},{7,4},{8,9},{9,10},{10,1... | collective-permute-start | bytes 589832 | tf_op jit(solution)/shard_map/ppermute | solution.py:28
  113.9 3.6 %collective-permute-start.3 = (bf16[192,512]{1,0:T(8,128)(2,1)}, bf16[192,512]{1,0:T(8,128)(2,1)S(1)}, u32[]{:S(2)}, u32[]{:S(2)}) collective-permute-start(bf16[192,512]{1,0:T(8,128)(2,1)} %get-tuple-element.39), channel_id=1, source_target_pairs={{0,2},{1,3},{2,0},{3,1},{4,6},{5,7},{6,4},{7,5},{8,10},{9,11},{10,... | collective-permute-start | bytes 589832 | tf_op jit(solution)/shard_map/ppermute | solution.py:28
  117.6 2.8 %collective-permute-start.4 = (bf16[192,512]{1,0:T(8,128)(2,1)}, bf16[192,512]{1,0:T(8,128)(2,1)}, u32[]{:S(2)}, u32[]{:S(2)}) collective-permute-start(bf16[192,512]{1,0:T(8,128)(2,1)} %get-tuple-element.40), channel_id=1, source_target_pairs={{0,3},{1,0},{2,1},{3,2},{4,7},{5,4},{6,5},{7,6},{8,11},{9,8},{10,9... | collective-permute-start | bytes 589832 | tf_op jit(solution)/shard_map/ppermute | solution.py:28
  120.9 3.5 %collective-permute-done.3.refs_4_ = bf16[192,512]{1,0:T(8,128)(2,1)S(1)} collective-permute-done((bf16[192,512]{1,0:T(8,128)(2,1)}, bf16[192,512]{1,0:T(8,128)(2,1)S(1)}, u32[]{:S(2)}, u32[]{:S(2)}) %collective-permute-start.3) | collective-permute-done | bytes 196640 | tf_op jit(solution)/shard_map/ppermute | solution.py:28
  127.4 1.5 shard_map.118
  129.6 7.7 %all-to-all-start.7 = ((f32[8,2,512]{2,1,0:T(2,128)}), f32[8,2,512]{2,1,0:T(2,128)S(1)}, u32[]{:S(2)}, u32[]{:S(2)}) async-start(f32[8,2,512]{2,1,0:T(2,128)} %get-tuple-element.36), calls=%async_computation.7 | async-start | bytes 65536 | tf_op jit(solution)/shard_map/all_to_all | solution.py:413
  137.3 12.1 %all_gather.3 = bf16[768,512]{1,0:T(8,128)(2,1)S(1)} all-gather(bf16[192,512]{1,0:T(8,128)(2,1)S(1)} %shard_map.118), channel_id=1, replica_groups=mesh['x'=4,'z'=16,'core'=2,'rep'=4] {'rep'}, dimensions={0}, use_global_device_ids=true | all-gather | bytes 983040 | tf_op jit(solution)/shard_map/all_gather | solution.py:441
  (66 shorter events, 21.2 us)
Async XLA Ops:
  0.6 18.0 %copy-start = (bf16[2048,512]{1,0:T(8,128)(2,1)S(1)}, bf16[2048,512]{1,0:T(8,128)(2,1)}, u32[]{:S(2)}) copy-start(bf16[2048,512]{1,0:T(8,128)(2,1)} %param.10) | copy-start | bytes 6291460
  2.2 27.8 %all-to-all-start = ((bf16[16,8,512]{2,1,0:T(8,128)(2,1)}), bf16[16,8,512]{2,1,0:T(8,128)(2,1)S(1)}, u32[]{:S(2)}, u32[]{:S(2)}) async-start(bf16[16,8,512]{2,1,0:T(8,128)(2,1)} %broadcast_in_dim.16), calls=%async_computation | async-start | bytes 262144 | tf_op jit(solution)/shard_map/all_to_all | solution.py:23
  21.6 19.1 %copy-start.14 = (s32[128,1,8]{0,2,1:T(8,128)S(1)}, s32[128,1,8]{0,2,1:T(8,128)}, u32[]{:S(2)}) copy-start(s32[128,1,8]{0,2,1:T(8,128)} %param.12) | copy-start | bytes 12292
  21.6 19.6 %copy-start.15 = (s32[128,1,8]{0,2,1:T(8,128)S(1)}, s32[128,1,8]{0,2,1:T(8,128)}, u32[]{:S(2)}) copy-start(s32[128,1,8]{0,2,1:T(8,128)} %param.13) | copy-start | bytes 12292
  30.8 12.2 %all-to-all-start.1 = ((bf16[4,128,512]{2,1,0:T(8,128)(2,1)}), bf16[4,128,512]{2,1,0:T(8,128)(2,1)S(1)}, u32[]{:S(2)}, u32[]{:S(2)}) async-start(bf16[4,128,512]{2,1,0:T(8,128)(2,1)} %broadcast_in_dim.34), calls=%async_computation.1 | async-start | bytes 1048576 | tf_op jit(solution)/shard_map/all_to_all | solution.py:23
  34.8 22.4 %collective-permute-start = (bf16[768,512]{1,0:T(8,128)(2,1)}, bf16[768,512]{1,0:T(8,128)(2,1)}, u32[]{:S(2)}, u32[]{:S(2)}) collective-permute-start(bf16[768,512]{1,0:T(8,128)(2,1)} %fusion.1.refs_5_.refs_7_.refs_6_), channel_id=1, source_target_pairs={{0,4},{4,0},{1,5},{5,1},{2,6},{6,2},{3,7},{7,3},{8,12},{12,8},{9,1... | collective-permute-start | bytes 2359304 | tf_op jit(solution)/shard_map/ppermute | solution.py:28
  43.0 14.2 %copy-start.12 = (bf16[4,128,512]{2,1,0:T(8,128)(2,1)}, bf16[4,128,512]{2,1,0:T(8,128)(2,1)S(1)}, u32[]{:S(2)}) copy-start(bf16[4,128,512]{2,1,0:T(8,128)(2,1)S(1)} %all-to-all-done.1) | copy-start | bytes 1572868
  43.8 23.6 %copy-start.13 = (s32[64,8]{1,0:T(8,128)S(1)}, s32[64,8]{1,0:T(8,128)}, u32[]{:S(2)}) copy-start(s32[64,8]{1,0:T(8,128)} %get-tuple-element.45) | copy-start | bytes 6148
  43.8 13.3 %all-to-all-start.2 = ((f32[8,2,512]{2,1,0:T(2,128)}), f32[8,2,512]{2,1,0:T(2,128)S(1)}, u32[]{:S(2)}, u32[]{:S(2)}) async-start(f32[8,2,512]{2,1,0:T(2,128)} %broadcast_in_dim.35), calls=%async_computation.2 | async-start | bytes 65536 | tf_op jit(solution)/shard_map/all_to_all | solution.py:23
  61.6 11.0 %collective-permute-start.1 = (bf16[512,512]{1,0:T(8,128)(2,1)}, bf16[512,512]{1,0:T(8,128)(2,1)}, u32[]{:S(2)}, u32[]{:S(2)}) collective-permute-start(bf16[512,512]{1,0:T(8,128)(2,1)} %get-tuple-element.27.refs_6_.refs_4_), channel_id=1, source_target_pairs={{0,4},{4,0},{1,5},{5,1},{2,6},{6,2},{3,7},{7,3},{8,12},{12,8},{9,1... | collective-permute-start | bytes 1572872 | tf_op jit(solution)/shard_map/ppermute | solution.py:28
  63.9 8.1 %all-to-all-start.3 = ((f32[8,2,512]{2,1,0:T(2,128)}), f32[8,2,512]{2,1,0:T(2,128)S(1)}, u32[]{:S(2)}, u32[]{:S(2)}) async-start(f32[8,2,512]{2,1,0:T(2,128)} %get-tuple-element.26), calls=%async_computation.3 | async-start | bytes 65536 | tf_op jit(solution)/shard_map/all_to_all | solution.py:337
  94.4 11.1 %all-to-all-start.5 = ((bf16[4,144,512]{2,1,0:T(8,128)(2,1)}), bf16[4,144,512]{2,1,0:T(8,128)(2,1)S(1)}, u32[]{:S(2)}, u32[]{:S(2)}) async-start(bf16[4,144,512]{2,1,0:T(8,128)(2,1)} %shard_map.112.refs_7_), calls=%async_computation.5 | async-start | bytes 1179648 | tf_op jit(solution)/shard_map/all_to_all | solution.py:387
  106.2 22.7 %all-to-all-start.6 = ((bf16[16,48,128]{2,1,0:T(8,128)(2,1)}), bf16[16,48,128]{2,1,0:T(8,128)(2,1)S(1)}, u32[]{:S(2)}, u32[]{:S(2)}) async-start(bf16[16,48,128]{2,1,0:T(8,128)(2,1)} %copy-done.1), calls=%async_computation.6 | async-start | bytes 393216 | tf_op jit(solution)/shard_map/all_to_all | solution.py:400
  111.6 9.3 %collective-permute-start.2 = (bf16[192,512]{1,0:T(8,128)(2,1)}, bf16[192,512]{1,0:T(8,128)(2,1)S(1)}, u32[]{:S(2)}, u32[]{:S(2)}) collective-permute-start(bf16[192,512]{1,0:T(8,128)(2,1)} %get-tuple-element.38), channel_id=1, source_target_pairs={{0,1},{1,2},{2,3},{3,0},{4,5},{5,6},{6,7},{7,4},{8,9},{9,10},{10,1... | collective-permute-start | bytes 589832 | tf_op jit(solution)/shard_map/ppermute | solution.py:28
  113.9 10.5 %collective-permute-start.3 = (bf16[192,512]{1,0:T(8,128)(2,1)}, bf16[192,512]{1,0:T(8,128)(2,1)S(1)}, u32[]{:S(2)}, u32[]{:S(2)}) collective-permute-start(bf16[192,512]{1,0:T(8,128)(2,1)} %get-tuple-element.39), channel_id=1, source_target_pairs={{0,2},{1,3},{2,0},{3,1},{4,6},{5,7},{6,4},{7,5},{8,10},{9,11},{10,... | collective-permute-start | bytes 589832 | tf_op jit(solution)/shard_map/ppermute | solution.py:28
  117.6 7.9 %collective-permute-start.4 = (bf16[192,512]{1,0:T(8,128)(2,1)}, bf16[192,512]{1,0:T(8,128)(2,1)}, u32[]{:S(2)}, u32[]{:S(2)}) collective-permute-start(bf16[192,512]{1,0:T(8,128)(2,1)} %get-tuple-element.40), channel_id=1, source_target_pairs={{0,3},{1,0},{2,1},{3,2},{4,7},{5,4},{6,5},{7,6},{8,11},{9,8},{10,9... | collective-permute-start | bytes 589832 | tf_op jit(solution)/shard_map/ppermute | solution.py:28
  125.5 1.0 copy-start.2
  126.5 0.9 copy-start.5
  127.4 22.0 %copy-start.3 = (f32[16,2,640]{2,1,0:T(2,128)S(1)}, f32[16,2,640]{2,1,0:T(2,128)}, u32[]{:S(2)}) copy-start(f32[16,2,640]{2,1,0:T(2,128)} %all_to_all.40.refs_5_.refs_3_.refs_6_) | copy-start | bytes 245764
  129.6 24.5 %all-to-all-start.7 = ((f32[8,2,512]{2,1,0:T(2,128)}), f32[8,2,512]{2,1,0:T(2,128)S(1)}, u32[]{:S(2)}, u32[]{:S(2)}) async-start(f32[8,2,512]{2,1,0:T(2,128)} %get-tuple-element.36), calls=%async_computation.7 | async-start | bytes 65536 | tf_op jit(solution)/shard_map/all_to_all | solution.py:413
  149.3 0.8 copy-start.7
  150.1 0.7 copy-start.8
  150.8 0.7 copy-start.9
  151.5 0.7 copy-start.10
  (4 other events, 2.6 us)

commit v11 on v9

--- a/solution.py
+++ b/solution.py
@@ -225,14 +225,18 @@
 
 
 def project_kernel(parts, at, picked, *refs):
-    found, (out, picks_ref, sem) = refs[:parts], refs[parts:]
+    found, (out, picks_ref, raw_ref, sems) = refs[:parts], refs[parts:]
     block = out.shape[0]
     rows = pl.ds(pl.multiple_of(at[0] * block, 64), block)
-    copy = pltpu.make_async_copy(picked.at[rows], picks_ref, sem)
+    copy = pltpu.make_async_copy(picked.at[rows], picks_ref, sems.at[0])
     copy.start()
-    raw = found[0][...]
-    for piece in found[1:]:
+    copy_2 = pltpu.make_async_copy(found[0], raw_ref, sems.at[1])
+    copy_2.start()
+    raw = found[1][...].astype(F32)
+    for piece in found[2:]:
         raw = raw + piece[...].astype(F32)
+    copy_2.wait()
+    raw = raw_ref[...] + raw
     copy.wait()
     picks = picks_ref[...].astype(F32)
     inv_norm = lax.rsqrt(jnp.sum(picks * picks, 1, keepdims=True) + EPSILON)
@@ -380,13 +384,17 @@
     came = [shift(sent[by - 1], "rep", by) for by in range(1, nr)]
     grad = call(
         lambda *refs: project_kernel(nr, *refs),
-        [SM, HB] + [VM] * nr,
+        [SM, HB, HB] + [VM] * (nr - 1),
         VM,
         piece,
         20 * quarter * width,
         14 * quarter * width,
         0,
-        [pltpu.VMEM((quarter, width), BF16), pltpu.SemaphoreType.DMA],
+        [
+            pltpu.VMEM((quarter, width), BF16),
+            pltpu.VMEM((quarter, width), F32),
+            pltpu.SemaphoreType.DMA((2,)),
+        ],
         grant=SMALL,
     )(at, picked, mine, *came)
     pull = lax.all_to_all(pull, "x", 0, 0)

time: 153 us -> 153 us (level)
  no operation moved by 1% of the time
where the time goes in v11:
time: 153 us; the launch traced here: 152 us
  starting transfers between devices  74.6 us (49%)
  waiting for transfers between devices  23.3 us (15%)
  Pallas kernels  19 us (12%)
  blocking collectives  16 us (10%)
  local copies, waits for them, and re-layouts  14.3 us (9%)
  other arithmetic  4.02 us (3%)
    all_to_all x3, starting transfers between devices, spread(): return lax.all_to_all(copies, axes, 0, 0)  28.2 us
    ppermute x8, starting transfers between devices, shift(): return lax.ppermute(block, axis, [(i, (i + by) % n) for i in range(n)])  27 us
    all_to_all x1, blocking collectives, body(): totals = lax.all_to_all(totals, 'z', 0, 0)  16 us
    all_to_all x3, waiting for transfers between devices, spread(): return lax.all_to_all(copies, axes, 0, 0)  11.6 us
    all_to_all x1, starting transfers between devices, body(): ends = lax.all_to_all(ends, ('core', 'rep'), 0, 0)  7.16 us
    unnamed x32, local copies, waits for them, and re-layouts  6.91 us
    pallas_call x1, Pallas kernels, body(): call(lambda *refs: pull_kernel(batch, *refs), [VM] * 9, VM, jax.ShapeDtyp...  5.76 us
    all_to_all x1, starting transfers between devices, body(): pull = lax.all_to_all(pull, 'z', 0, 0)  5.42 us
  transfers between devices with their start and end apart: 15, of which 7 were waited for; matrix products, arithmetic and copies ran while one was open for 6% of the time, Pallas kernels for 5%

profile of v11, /device:TPU:1, one launch (start us, length us, event | category | flops | bytes accessed | tf_op | source)
XLA Modules:
  0.0 152.1 jit_solution(16093068892168683193)
XLA Ops:
  2.1 15.7 %all-to-all-start = ((bf16[16,8,512]{2,1,0:T(8,128)(2,1)}), bf16[16,8,512]{2,1,0:T(8,128)(2,1)S(1)}, u32[]{:S(2)}, u32[]{:S(2)}) async-start(bf16[16,8,512]{2,1,0:T(8,128)(2,1)} %broadcast_in_dim.16), calls=%async_computation | async-start | bytes 262144 | tf_op jit(solution)/shard_map/all_to_all | solution.py:23
  18.6 2.7 %gather_fusion = bf16[768,512]{1,0:T(8,128)(2,1)S(1)} fusion(bf16[2048,512]{1,0:T(8,128)(2,1)S(1)} %copy-done, s32[1024]{0:T(1024)S(1)} %pad_clamp_fusion), kind=kCustom, calls=%fused_computation | custom fusion | bytes 1575936 | tf_op jit(solution)/shard_map/gather | solution.py:305
  22.7 7.2 %all-to-all-done = bf16[16,8,512]{2,1,0:T(8,128)(2,1)S(1)} async-done(((bf16[16,8,512]{2,1,0:T(8,128)(2,1)}), bf16[16,8,512]{2,1,0:T(8,128)(2,1)S(1)}, u32[]{:S(2)}, u32[]{:S(2)}) %all-to-all-start) | async-done | bytes 131104 | tf_op jit(solution)/shard_map/all_to_all | solution.py:23
  30.7 4.0 %all-to-all-start.1 = ((bf16[4,128,512]{2,1,0:T(8,128)(2,1)}), bf16[4,128,512]{2,1,0:T(8,128)(2,1)S(1)}, u32[]{:S(2)}, u32[]{:S(2)}) async-start(bf16[4,128,512]{2,1,0:T(8,128)(2,1)} %broadcast_in_dim.34), calls=%async_computation.1 | async-start | bytes 1048576 | tf_op jit(solution)/shard_map/all_to_all | solution.py:23
  34.8 5.8 %collective-permute-start = (bf16[768,512]{1,0:T(8,128)(2,1)}, bf16[768,512]{1,0:T(8,128)(2,1)}, u32[]{:S(2)}, u32[]{:S(2)}) collective-permute-start(bf16[768,512]{1,0:T(8,128)(2,1)} %fusion.1.refs_5_.refs_7_.refs_6_), channel_id=1, source_target_pairs={{0,4},{4,0},{1,5},{5,1},{2,6},{6,2},{3,7},{7,3},{8,12},{12,8},{9,1... | collective-permute-start | bytes 2359304 | tf_op jit(solution)/shard_map/ppermute | solution.py:28
  43.8 8.4 %all-to-all-start.2 = ((f32[8,2,512]{2,1,0:T(2,128)}), f32[8,2,512]{2,1,0:T(2,128)S(1)}, u32[]{:S(2)}, u32[]{:S(2)}) async-start(f32[8,2,512]{2,1,0:T(2,128)} %broadcast_in_dim.35), calls=%async_computation.2 | async-start | bytes 65536 | tf_op jit(solution)/shard_map/all_to_all | solution.py:23
  52.8 4.3 %all-to-all-done.2.refs_1_.refs_2_ = f32[8,2,512]{2,1,0:T(2,128)S(1)} async-done(((f32[8,2,512]{2,1,0:T(2,128)}), f32[8,2,512]{2,1,0:T(2,128)S(1)}, u32[]{:S(2)}, u32[]{:S(2)}) %all-to-all-start.2) | async-done | bytes 32800 | tf_op jit(solution)/shard_map/all_to_all | solution.py:23
  57.7 3.9 %shard_map.110 = (bf16[512,512]{1,0:T(8,128)(2,1)}, f32[8,2,512]{2,1,0:T(2,128)}) custom-call(bf16[512,512]{1,0:T(8,128)(2,1)} %bitcast.24, f32[8,2,512]{2,1,0:T(2,128)} %copy-done.6, f32[1,512]{1,0:T(1,128)} %bitcast.18, f32[1,512]{1,0:T(1,128)} %bitcast.21, s32[1,512]{1,0:T(1,128)} %select_select_fusion.refs_4_.refs_1_, ...), custom_call_target="tpu_custom_call" | custom-call | flops 805306368 | bytes 1572864 | tf_op jit(solution)/shard_map/pallas_call | solution.py:332
  61.6 2.3 %collective-permute-start.1 = (bf16[512,512]{1,0:T(8,128)(2,1)}, bf16[512,512]{1,0:T(8,128)(2,1)}, u32[]{:S(2)}, u32[]{:S(2)}) collective-permute-start(bf16[512,512]{1,0:T(8,128)(2,1)} %get-tuple-element.28.refs_6_.refs_4_), channel_id=1, source_target_pairs={{0,4},{4,0},{1,5},{5,1},{2,6},{6,2},{3,7},{7,3},{8,12},{12,8},{9,1... | collective-permute-start | bytes 1572872 | tf_op jit(solution)/shard_map/ppermute | solution.py:28
  63.9 3.4 %all-to-all-start.3 = ((f32[8,2,512]{2,1,0:T(2,128)}), f32[8,2,512]{2,1,0:T(2,128)S(1)}, u32[]{:S(2)}, u32[]{:S(2)}) async-start(f32[8,2,512]{2,1,0:T(2,128)} %get-tuple-element.27), calls=%async_computation.3 | async-start | bytes 65536 | tf_op jit(solution)/shard_map/all_to_all | solution.py:346
  68.0 4.0 %all-to-all-done.3.refs_1_ = f32[8,2,512]{2,1,0:T(2,128)S(1)} async-done(((f32[8,2,512]{2,1,0:T(2,128)}), f32[8,2,512]{2,1,0:T(2,128)S(1)}, u32[]{:S(2)}, u32[]{:S(2)}) %all-to-all-start.3) | async-done | bytes 32800 | tf_op jit(solution)/shard_map/all_to_all | solution.py:346
  72.6 16.0 %all_to_all.40.refs_5_.refs_3_.refs_6_ = f32[16,2,640]{2,1,0:T(2,128)} all-to-all(f32[16,2,640]{2,1,0:T(2,128)S(1)} %shard_map.111), channel_id=1, replica_groups=mesh['x'=4,'z'=16,'core'=2,'rep'=4] {'z'}, dimensions={0} | all-to-all | bytes 163840 | tf_op jit(solution)/shard_map/all_to_all | solution.py:357
  88.6 5.8 %shard_map.112.refs_7_ = bf16[4,144,512]{2,1,0:T(8,128)(2,1)} custom-call(bf16[512,512]{1,0:T(8,128)(2,1)} %bitcast.25, f32[8,2,512]{2,1,0:T(2,128)} %copy-done.6, f32[1,512]{1,0:T(1,128)} %bitcast.19, f32[1,512]{1,0:T(1,128)} %bitcast.22, s32[1,512]{1,0:T(1,128)} %select_select_fusion.refs_4_.refs_1_, f32[16,2,640]{2,1,0:T(2,128)} %all_to_all.40.refs_5_.refs_3_.refs_6_, ...), custom_call_target="tpu_custom_call" | custom-call | flops 1610612736 | bytes 1572864 | tf_op jit(solution)/shard_map/pallas_call | solution.py:359
  94.4 3.5 %all-to-all-start.5 = ((bf16[4,144,512]{2,1,0:T(8,128)(2,1)}), bf16[4,144,512]{2,1,0:T(8,128)(2,1)S(1)}, u32[]{:S(2)}, u32[]{:S(2)}) async-start(bf16[4,144,512]{2,1,0:T(8,128)(2,1)} %shard_map.112.refs_7_), calls=%async_computation.5 | async-start | bytes 1179648 | tf_op jit(solution)/shard_map/all_to_all | solution.py:400
  97.9 5.1 %shard_map.113 = (f32[192,512]{1,0:T(8,128)}, bf16[192,512]{1,0:T(8,128)(2,1)}, bf16[192,512]{1,0:T(8,128)(2,1)}, bf16[192,512]{1,0:T(8,128)(2,1)}) custom-call(s32[1]{0:T(128)} %bitcast.13.refs_0_, s32[1,512]{1,0:T(1,128)} %select_select_fusion.refs_4_.refs_1_, s32[1,512]{1,0:T(1,128)} %select_n.55.refs_2_, ...), custom_call_target="tpu_custom_call" | custom-call | flops 1610612736 | bytes 1572864 | tf_op jit(solution)/shard_map/pallas_call | solution.py:370
  103.0 2.4 %all-to-all-done.5.refs_0_ = bf16[4,144,512]{2,1,0:T(8,128)(2,1)S(1)} async-done(((bf16[4,144,512]{2,1,0:T(8,128)(2,1)}), bf16[4,144,512]{2,1,0:T(8,128)(2,1)S(1)}, u32[]{:S(2)}, u32[]{:S(2)}) %all-to-all-start.5) | async-done | bytes 589856 | tf_op jit(solution)/shard_map/all_to_all | solution.py:400
  106.2 5.4 %all-to-all-start.6 = ((bf16[16,48,128]{2,1,0:T(8,128)(2,1)}), bf16[16,48,128]{2,1,0:T(8,128)(2,1)S(1)}, u32[]{:S(2)}, u32[]{:S(2)}) async-start(bf16[16,48,128]{2,1,0:T(8,128)(2,1)} %copy-done.1), calls=%async_computation.6 | async-start | bytes 393216 | tf_op jit(solution)/shard_map/all_to_all | solution.py:413
  111.6 2.3 %collective-permute-start.2 = (bf16[192,512]{1,0:T(8,128)(2,1)}, bf16[192,512]{1,0:T(8,128)(2,1)S(1)}, u32[]{:S(2)}, u32[]{:S(2)}) collective-permute-start(bf16[192,512]{1,0:T(8,128)(2,1)} %get-tuple-element.38), channel_id=1, source_target_pairs={{0,1},{1,2},{2,3},{3,0},{4,5},{5,6},{6,7},{7,4},{8,9},{9,10},{10,1... | collective-permute-start | bytes 589832 | tf_op jit(solution)/shard_map/ppermute | solution.py:28
  113.9 3.6 %collective-permute-start.3 = (bf16[192,512]{1,0:T(8,128)(2,1)}, bf16[192,512]{1,0:T(8,128)(2,1)S(1)}, u32[]{:S(2)}, u32[]{:S(2)}) collective-permute-start(bf16[192,512]{1,0:T(8,128)(2,1)} %get-tuple-element.39), channel_id=1, source_target_pairs={{0,2},{1,3},{2,0},{3,1},{4,6},{5,7},{6,4},{7,5},{8,10},{9,11},{10,... | collective-permute-start | bytes 589832 | tf_op jit(solution)/shard_map/ppermute | solution.py:28
  117.6 2.8 %collective-permute-start.4 = (bf16[192,512]{1,0:T(8,128)(2,1)}, bf16[192,512]{1,0:T(8,128)(2,1)S(1)}, u32[]{:S(2)}, u32[]{:S(2)}) collective-permute-start(bf16[192,512]{1,0:T(8,128)(2,1)} %get-tuple-element.40), channel_id=1, source_target_pairs={{0,3},{1,0},{2,1},{3,2},{4,7},{5,4},{6,5},{7,6},{8,11},{9,8},{10,9... | collective-permute-start | bytes 589832 | tf_op jit(solution)/shard_map/ppermute | solution.py:28
  120.3 4.1 %collective-permute-done.3.refs_4_ = bf16[192,512]{1,0:T(8,128)(2,1)S(1)} collective-permute-done((bf16[192,512]{1,0:T(8,128)(2,1)}, bf16[192,512]{1,0:T(8,128)(2,1)S(1)}, u32[]{:S(2)}, u32[]{:S(2)}) %collective-permute-start.3) | collective-permute-done | bytes 196640 | tf_op jit(solution)/shard_map/ppermute | solution.py:28
  127.2 4.1 %collective-permute-start.7 = (bf16[192,512]{1,0:T(8,128)(2,1)S(1)}, bf16[192,512]{1,0:T(8,128)(2,1)S(1)}, u32[]{:S(2)}, u32[]{:S(2)}) collective-permute-start(bf16[192,512]{1,0:T(8,128)(2,1)S(1)} %shard_map.117.refs_3_), channel_id=1, source_target_pairs={{0,3},{1,0},{2,1},{3,2},{4,7},{5,4},{6,5},{7,6},{8,11},{9,8},{10,9... | collective-permute-start | bytes 589832 | tf_op jit(solution)/shard_map/ppermute | solution.py:28
  131.3 4.2 %collective-permute-start.6 = (bf16[192,512]{1,0:T(8,128)(2,1)S(1)}, bf16[192,512]{1,0:T(8,128)(2,1)S(1)}, u32[]{:S(2)}, u32[]{:S(2)}) collective-permute-start(bf16[192,512]{1,0:T(8,128)(2,1)S(1)} %shard_map.117.refs_3_), channel_id=1, source_target_pairs={{0,2},{1,3},{2,0},{3,1},{4,6},{5,7},{6,4},{7,5},{8,10},{9,11},{10,... | collective-permute-start | bytes 589832 | tf_op jit(solution)/shard_map/ppermute | solution.py:28
  138.1 7.2 %all-to-all-start.7 = ((f32[8,2,512]{2,1,0:T(2,128)}), f32[8,2,512]{2,1,0:T(2,128)S(1)}, u32[]{:S(2)}, u32[]{:S(2)}) async-start(f32[8,2,512]{2,1,0:T(2,128)} %get-tuple-element.37), calls=%async_computation.7 | async-start | bytes 65536 | tf_op jit(solution)/shard_map/all_to_all | solution.py:426
  (68 shorter events, 22.9 us)
Async XLA Ops:
  0.6 18.0 %copy-start = (bf16[2048,512]{1,0:T(8,128)(2,1)S(1)}, bf16[2048,512]{1,0:T(8,128)(2,1)}, u32[]{:S(2)}) copy-start(bf16[2048,512]{1,0:T(8,128)(2,1)} %param.10) | copy-start | bytes 6291460
  2.1 27.8 %all-to-all-start = ((bf16[16,8,512]{2,1,0:T(8,128)(2,1)}), bf16[16,8,512]{2,1,0:T(8,128)(2,1)S(1)}, u32[]{:S(2)}, u32[]{:S(2)}) async-start(bf16[16,8,512]{2,1,0:T(8,128)(2,1)} %broadcast_in_dim.16), calls=%async_computation | async-start | bytes 262144 | tf_op jit(solution)/shard_map/all_to_all | solution.py:23
  21.5 19.1 %copy-start.13 = (s32[128,1,8]{0,2,1:T(8,128)S(1)}, s32[128,1,8]{0,2,1:T(8,128)}, u32[]{:S(2)}) copy-start(s32[128,1,8]{0,2,1:T(8,128)} %param.12) | copy-start | bytes 12292
  21.6 19.6 %copy-start.14 = (s32[128,1,8]{0,2,1:T(8,128)S(1)}, s32[128,1,8]{0,2,1:T(8,128)}, u32[]{:S(2)}) copy-start(s32[128,1,8]{0,2,1:T(8,128)} %param.13) | copy-start | bytes 12292
  30.7 12.2 %all-to-all-start.1 = ((bf16[4,128,512]{2,1,0:T(8,128)(2,1)}), bf16[4,128,512]{2,1,0:T(8,128)(2,1)S(1)}, u32[]{:S(2)}, u32[]{:S(2)}) async-start(bf16[4,128,512]{2,1,0:T(8,128)(2,1)} %broadcast_in_dim.34), calls=%async_computation.1 | async-start | bytes 1048576 | tf_op jit(solution)/shard_map/all_to_all | solution.py:23
  34.8 22.4 %collective-permute-start = (bf16[768,512]{1,0:T(8,128)(2,1)}, bf16[768,512]{1,0:T(8,128)(2,1)}, u32[]{:S(2)}, u32[]{:S(2)}) collective-permute-start(bf16[768,512]{1,0:T(8,128)(2,1)} %fusion.1.refs_5_.refs_7_.refs_6_), channel_id=1, source_target_pairs={{0,4},{4,0},{1,5},{5,1},{2,6},{6,2},{3,7},{7,3},{8,12},{12,8},{9,1... | collective-permute-start | bytes 2359304 | tf_op jit(solution)/shard_map/ppermute | solution.py:28
  42.9 14.2 %copy-start.11 = (bf16[4,128,512]{2,1,0:T(8,128)(2,1)}, bf16[4,128,512]{2,1,0:T(8,128)(2,1)S(1)}, u32[]{:S(2)}) copy-start(bf16[4,128,512]{2,1,0:T(8,128)(2,1)S(1)} %all-to-all-done.1) | copy-start | bytes 1572868
  43.8 23.6 %copy-start.12 = (s32[64,8]{1,0:T(8,128)S(1)}, s32[64,8]{1,0:T(8,128)}, u32[]{:S(2)}) copy-start(s32[64,8]{1,0:T(8,128)} %get-tuple-element.47) | copy-start | bytes 6148
  43.8 13.4 %all-to-all-start.2 = ((f32[8,2,512]{2,1,0:T(2,128)}), f32[8,2,512]{2,1,0:T(2,128)S(1)}, u32[]{:S(2)}, u32[]{:S(2)}) async-start(f32[8,2,512]{2,1,0:T(2,128)} %broadcast_in_dim.35), calls=%async_computation.2 | async-start | bytes 65536 | tf_op jit(solution)/shard_map/all_to_all | solution.py:23
  61.6 11.0 %collective-permute-start.1 = (bf16[512,512]{1,0:T(8,128)(2,1)}, bf16[512,512]{1,0:T(8,128)(2,1)}, u32[]{:S(2)}, u32[]{:S(2)}) collective-permute-start(bf16[512,512]{1,0:T(8,128)(2,1)} %get-tuple-element.28.refs_6_.refs_4_), channel_id=1, source_target_pairs={{0,4},{4,0},{1,5},{5,1},{2,6},{6,2},{3,7},{7,3},{8,12},{12,8},{9,1... | collective-permute-start | bytes 1572872 | tf_op jit(solution)/shard_map/ppermute | solution.py:28
  63.9 8.1 %all-to-all-start.3 = ((f32[8,2,512]{2,1,0:T(2,128)}), f32[8,2,512]{2,1,0:T(2,128)S(1)}, u32[]{:S(2)}, u32[]{:S(2)}) async-start(f32[8,2,512]{2,1,0:T(2,128)} %get-tuple-element.27), calls=%async_computation.3 | async-start | bytes 65536 | tf_op jit(solution)/shard_map/all_to_all | solution.py:346
  94.4 11.1 %all-to-all-start.5 = ((bf16[4,144,512]{2,1,0:T(8,128)(2,1)}), bf16[4,144,512]{2,1,0:T(8,128)(2,1)S(1)}, u32[]{:S(2)}, u32[]{:S(2)}) async-start(bf16[4,144,512]{2,1,0:T(8,128)(2,1)} %shard_map.112.refs_7_), calls=%async_computation.5 | async-start | bytes 1179648 | tf_op jit(solution)/shard_map/all_to_all | solution.py:400
  105.4 39.9 %copy-start.3 = (f32[16,2,640]{2,1,0:T(2,128)S(1)}, f32[16,2,640]{2,1,0:T(2,128)}, u32[]{:S(2)}) copy-start(f32[16,2,640]{2,1,0:T(2,128)} %all_to_all.40.refs_5_.refs_3_.refs_6_) | copy-start | bytes 245764
  106.2 31.3 %all-to-all-start.6 = ((bf16[16,48,128]{2,1,0:T(8,128)(2,1)}), bf16[16,48,128]{2,1,0:T(8,128)(2,1)S(1)}, u32[]{:S(2)}, u32[]{:S(2)}) async-start(bf16[16,48,128]{2,1,0:T(8,128)(2,1)} %copy-done.1), calls=%async_computation.6 | async-start | bytes 393216 | tf_op jit(solution)/shard_map/all_to_all | solution.py:413
  111.6 8.7 %collective-permute-start.2 = (bf16[192,512]{1,0:T(8,128)(2,1)}, bf16[192,512]{1,0:T(8,128)(2,1)S(1)}, u32[]{:S(2)}, u32[]{:S(2)}) collective-permute-start(bf16[192,512]{1,0:T(8,128)(2,1)} %get-tuple-element.38), channel_id=1, source_target_pairs={{0,1},{1,2},{2,3},{3,0},{4,5},{5,6},{6,7},{7,4},{8,9},{9,10},{10,1... | collective-permute-start | bytes 589832 | tf_op jit(solution)/shard_map/ppermute | solution.py:28
  113.9 10.5 %collective-permute-start.3 = (bf16[192,512]{1,0:T(8,128)(2,1)}, bf16[192,512]{1,0:T(8,128)(2,1)S(1)}, u32[]{:S(2)}, u32[]{:S(2)}) collective-permute-start(bf16[192,512]{1,0:T(8,128)(2,1)} %get-tuple-element.39), channel_id=1, source_target_pairs={{0,2},{1,3},{2,0},{3,1},{4,6},{5,7},{6,4},{7,5},{8,10},{9,11},{10,... | collective-permute-start | bytes 589832 | tf_op jit(solution)/shard_map/ppermute | solution.py:28
  117.6 7.9 %collective-permute-start.4 = (bf16[192,512]{1,0:T(8,128)(2,1)}, bf16[192,512]{1,0:T(8,128)(2,1)S(1)}, u32[]{:S(2)}, u32[]{:S(2)}) collective-permute-start(bf16[192,512]{1,0:T(8,128)(2,1)} %get-tuple-element.40), channel_id=1, source_target_pairs={{0,3},{1,0},{2,1},{3,2},{4,7},{5,4},{6,5},{7,6},{8,11},{9,8},{10,9... | collective-permute-start | bytes 589832 | tf_op jit(solution)/shard_map/ppermute | solution.py:28
  125.5 1.0 copy-start.2
  127.2 22.1 %collective-permute-start.7 = (bf16[192,512]{1,0:T(8,128)(2,1)S(1)}, bf16[192,512]{1,0:T(8,128)(2,1)S(1)}, u32[]{:S(2)}, u32[]{:S(2)}) collective-permute-start(bf16[192,512]{1,0:T(8,128)(2,1)S(1)} %shard_map.117.refs_3_), channel_id=1, source_target_pairs={{0,3},{1,0},{2,1},{3,2},{4,7},{5,4},{6,5},{7,6},{8,11},{9,8},{10,9... | collective-permute-start | bytes 589832 | tf_op jit(solution)/shard_map/ppermute | solution.py:28
  131.3 18.1 %collective-permute-start.6 = (bf16[192,512]{1,0:T(8,128)(2,1)S(1)}, bf16[192,512]{1,0:T(8,128)(2,1)S(1)}, u32[]{:S(2)}, u32[]{:S(2)}) collective-permute-start(bf16[192,512]{1,0:T(8,128)(2,1)S(1)} %shard_map.117.refs_3_), channel_id=1, source_target_pairs={{0,2},{1,3},{2,0},{3,1},{4,6},{5,7},{6,4},{7,5},{8,10},{9,11},{10,... | collective-permute-start | bytes 589832 | tf_op jit(solution)/shard_map/ppermute | solution.py:28
  135.5 13.9 %collective-permute-start.5 = (bf16[192,512]{1,0:T(8,128)(2,1)S(1)}, bf16[192,512]{1,0:T(8,128)(2,1)S(1)}, u32[]{:S(2)}, u32[]{:S(2)}) collective-permute-start(bf16[192,512]{1,0:T(8,128)(2,1)S(1)} %shard_map.117.refs_3_), channel_id=1, source_target_pairs={{0,1},{1,2},{2,3},{3,0},{4,5},{5,6},{6,7},{7,4},{8,9},{9,10},{10,1... | collective-permute-start | bytes 589832 | tf_op jit(solution)/shard_map/ppermute | solution.py:28
  138.1 12.1 %all-to-all-start.7 = ((f32[8,2,512]{2,1,0:T(2,128)}), f32[8,2,512]{2,1,0:T(2,128)S(1)}, u32[]{:S(2)}, u32[]{:S(2)}) async-start(f32[8,2,512]{2,1,0:T(2,128)} %get-tuple-element.37), calls=%async_computation.7 | async-start | bytes 65536 | tf_op jit(solution)/shard_map/all_to_all | solution.py:426
  145.4 0.8 copy-start.7
  150.2 0.9 copy-start.5
  (6 other events, 4.0 us)

commit v12 on v9

--- a/solution.py
+++ b/solution.py
@@ -377,7 +377,8 @@
             pltpu.SemaphoreType.DMA((nr,)),
         ],
     )(at, place, place_2, totals, unit, unit_2, w_own, pull)
-    came = [shift(sent[by - 1], "rep", by) for by in range(1, nr)]
+    far_first = sorted(range(1, nr), key=lambda by: -min(by, nr - by))
+    came = [shift(sent[by - 1], "rep", by) for by in far_first]
     grad = call(
         lambda *refs: project_kernel(nr, *refs),
         [SM, HB] + [VM] * nr,

time: 153 us -> 152 us (level)
  waiting for transfers between devices: 23.3 us -> 21.5 us
    ppermute x8, waiting for transfers between devices: 5.14 us -> 3.35 us  [shift(): return lax.ppermute(block, axis, [(i, (i + by) % n) for i in range(n)])]
  transfers between devices with their start and end apart: 15 -> 15, of which waited for: 7 -> 6; matrix products, arithmetic and copies ran while one was open for 6% -> 6% of each run, Pallas kernels for 5% -> 5%
where the time goes in v12:
time: 152 us; the launch traced here: 151 us
  starting transfers between devices  75.5 us (50%)
  waiting for transfers between devices  21.5 us (14%)
  Pallas kernels  18.8 us (12%)
  blocking collectives  16 us (11%)
  local copies, waits for them, and re-layouts  14.3 us (9%)
  other arithmetic  4.02 us (3%)
    all_to_all x3, starting transfers between devices, spread(): return lax.all_to_all(copies, axes, 0, 0)  28.2 us
    ppermute x8, starting transfers between devices, shift(): return lax.ppermute(block, axis, [(i, (i + by) % n) for i in range(n)])  26.6 us
    all_to_all x1, blocking collectives, body(): totals = lax.all_to_all(totals, 'z', 0, 0)  16 us
    all_to_all x3, waiting for transfers between devices, spread(): return lax.all_to_all(copies, axes, 0, 0)  11.6 us
    all_to_all x1, starting transfers between devices, body(): ends = lax.all_to_all(ends, ('core', 'rep'), 0, 0)  8.52 us
    unnamed x32, local copies, waits for them, and re-layouts  6.91 us
    pallas_call x1, Pallas kernels, body(): call(lambda *refs: pull_kernel(batch, *refs), [VM] * 9, VM, jax.ShapeDtyp...  5.76 us
    all_to_all x1, starting transfers between devices, body(): pull = lax.all_to_all(pull, 'z', 0, 0)  5.42 us
  transfers between devices with their start and end apart: 15, of which 6 were waited for; matrix products, arithmetic and copies ran while one was open for 6% of the time, Pallas kernels for 5%

profile of v12, /device:TPU:1, one launch (start us, length us, event | category | flops | bytes accessed | tf_op | source)
XLA Modules:
  0.0 151.0 jit_solution(16090299569939348414)
XLA Ops:
  2.1 15.7 %all-to-all-start = ((bf16[16,8,512]{2,1,0:T(8,128)(2,1)}), bf16[16,8,512]{2,1,0:T(8,128)(2,1)S(1)}, u32[]{:S(2)}, u32[]{:S(2)}) async-start(bf16[16,8,512]{2,1,0:T(8,128)(2,1)} %broadcast_in_dim.16), calls=%async_computation | async-start | bytes 262144 | tf_op jit(solution)/shard_map/all_to_all | solution.py:23
  18.6 2.7 %gather_fusion = bf16[768,512]{1,0:T(8,128)(2,1)S(1)} fusion(bf16[2048,512]{1,0:T(8,128)(2,1)S(1)} %copy-done, s32[1024]{0:T(1024)S(1)} %pad_clamp_fusion), kind=kCustom, calls=%fused_computation | custom fusion | bytes 1575936 | tf_op jit(solution)/shard_map/gather | solution.py:301
  22.7 7.2 %all-to-all-done = bf16[16,8,512]{2,1,0:T(8,128)(2,1)S(1)} async-done(((bf16[16,8,512]{2,1,0:T(8,128)(2,1)}), bf16[16,8,512]{2,1,0:T(8,128)(2,1)S(1)}, u32[]{:S(2)}, u32[]{:S(2)}) %all-to-all-start) | async-done | bytes 131104 | tf_op jit(solution)/shard_map/all_to_all | solution.py:23
  30.7 4.0 %all-to-all-start.1 = ((bf16[4,128,512]{2,1,0:T(8,128)(2,1)}), bf16[4,128,512]{2,1,0:T(8,128)(2,1)S(1)}, u32[]{:S(2)}, u32[]{:S(2)}) async-start(bf16[4,128,512]{2,1,0:T(8,128)(2,1)} %broadcast_in_dim.34), calls=%async_computation.1 | async-start | bytes 1048576 | tf_op jit(solution)/shard_map/all_to_all | solution.py:23
  34.8 5.8 %collective-permute-start = (bf16[768,512]{1,0:T(8,128)(2,1)}, bf16[768,512]{1,0:T(8,128)(2,1)}, u32[]{:S(2)}, u32[]{:S(2)}) collective-permute-start(bf16[768,512]{1,0:T(8,128)(2,1)} %fusion.1.refs_5_.refs_7_.refs_6_), channel_id=1, source_target_pairs={{0,4},{4,0},{1,5},{5,1},{2,6},{6,2},{3,7},{7,3},{8,12},{12,8},{9,1... | collective-permute-start | bytes 2359304 | tf_op jit(solution)/shard_map/ppermute | solution.py:28
  43.8 8.4 %all-to-all-start.2 = ((f32[8,2,512]{2,1,0:T(2,128)}), f32[8,2,512]{2,1,0:T(2,128)S(1)}, u32[]{:S(2)}, u32[]{:S(2)}) async-start(f32[8,2,512]{2,1,0:T(2,128)} %broadcast_in_dim.35), calls=%async_computation.2 | async-start | bytes 65536 | tf_op jit(solution)/shard_map/all_to_all | solution.py:23
  52.8 4.3 %all-to-all-done.2.refs_1_.refs_2_ = f32[8,2,512]{2,1,0:T(2,128)S(1)} async-done(((f32[8,2,512]{2,1,0:T(2,128)}), f32[8,2,512]{2,1,0:T(2,128)S(1)}, u32[]{:S(2)}, u32[]{:S(2)}) %all-to-all-start.2) | async-done | bytes 32800 | tf_op jit(solution)/shard_map/all_to_all | solution.py:23
  57.7 3.9 %shard_map.110 = (bf16[512,512]{1,0:T(8,128)(2,1)}, f32[8,2,512]{2,1,0:T(2,128)}) custom-call(bf16[512,512]{1,0:T(8,128)(2,1)} %bitcast.24, f32[8,2,512]{2,1,0:T(2,128)} %copy-done.6, f32[1,512]{1,0:T(1,128)} %bitcast.18, f32[1,512]{1,0:T(1,128)} %bitcast.21, s32[1,512]{1,0:T(1,128)} %select_select_fusion.refs_4_.refs_1_, ...), custom_call_target="tpu_custom_call" | custom-call | flops 805306368 | bytes 1572864 | tf_op jit(solution)/shard_map/pallas_call | solution.py:328
  61.6 2.3 %collective-permute-start.1 = (bf16[512,512]{1,0:T(8,128)(2,1)}, bf16[512,512]{1,0:T(8,128)(2,1)}, u32[]{:S(2)}, u32[]{:S(2)}) collective-permute-start(bf16[512,512]{1,0:T(8,128)(2,1)} %get-tuple-element.28.refs_6_.refs_4_), channel_id=1, source_target_pairs={{0,4},{4,0},{1,5},{5,1},{2,6},{6,2},{3,7},{7,3},{8,12},{12,8},{9,1... | collective-permute-start | bytes 1572872 | tf_op jit(solution)/shard_map/ppermute | solution.py:28
  63.9 3.4 %all-to-all-start.3 = ((f32[8,2,512]{2,1,0:T(2,128)}), f32[8,2,512]{2,1,0:T(2,128)S(1)}, u32[]{:S(2)}, u32[]{:S(2)}) async-start(f32[8,2,512]{2,1,0:T(2,128)} %get-tuple-element.27), calls=%async_computation.3 | async-start | bytes 65536 | tf_op jit(solution)/shard_map/all_to_all | solution.py:342
  68.0 4.0 %all-to-all-done.3.refs_1_ = f32[8,2,512]{2,1,0:T(2,128)S(1)} async-done(((f32[8,2,512]{2,1,0:T(2,128)}), f32[8,2,512]{2,1,0:T(2,128)S(1)}, u32[]{:S(2)}, u32[]{:S(2)}) %all-to-all-start.3) | async-done | bytes 32800 | tf_op jit(solution)/shard_map/all_to_all | solution.py:342
  72.6 16.0 %all_to_all.40.refs_5_.refs_3_.refs_6_ = f32[16,2,640]{2,1,0:T(2,128)} all-to-all(f32[16,2,640]{2,1,0:T(2,128)S(1)} %shard_map.111), channel_id=1, replica_groups=mesh['x'=4,'z'=16,'core'=2,'rep'=4] {'z'}, dimensions={0} | all-to-all | bytes 163840 | tf_op jit(solution)/shard_map/all_to_all | solution.py:353
  88.6 5.8 %shard_map.112.refs_7_ = bf16[4,144,512]{2,1,0:T(8,128)(2,1)} custom-call(bf16[512,512]{1,0:T(8,128)(2,1)} %bitcast.25, f32[8,2,512]{2,1,0:T(2,128)} %copy-done.6, f32[1,512]{1,0:T(1,128)} %bitcast.19, f32[1,512]{1,0:T(1,128)} %bitcast.22, s32[1,512]{1,0:T(1,128)} %select_select_fusion.refs_4_.refs_1_, f32[16,2,640]{2,1,0:T(2,128)} %all_to_all.40.refs_5_.refs_3_.refs_6_, ...), custom_call_target="tpu_custom_call" | custom-call | flops 1610612736 | bytes 1572864 | tf_op jit(solution)/shard_map/pallas_call | solution.py:355
  94.4 3.5 %all-to-all-start.5 = ((bf16[4,144,512]{2,1,0:T(8,128)(2,1)}), bf16[4,144,512]{2,1,0:T(8,128)(2,1)S(1)}, u32[]{:S(2)}, u32[]{:S(2)}) async-start(bf16[4,144,512]{2,1,0:T(8,128)(2,1)} %shard_map.112.refs_7_), calls=%async_computation.5 | async-start | bytes 1179648 | tf_op jit(solution)/shard_map/all_to_all | solution.py:393
  97.9 5.1 %shard_map.113 = (f32[192,512]{1,0:T(8,128)}, bf16[192,512]{1,0:T(8,128)(2,1)}, bf16[192,512]{1,0:T(8,128)(2,1)}, bf16[192,512]{1,0:T(8,128)(2,1)}) custom-call(s32[1]{0:T(128)} %bitcast.13.refs_0_, s32[1,512]{1,0:T(1,128)} %select_select_fusion.refs_4_.refs_1_, s32[1,512]{1,0:T(1,128)} %select_n.55.refs_2_, ...), custom_call_target="tpu_custom_call" | custom-call | flops 1610612736 | bytes 1572864 | tf_op jit(solution)/shard_map/pallas_call | solution.py:366
  103.0 2.4 %all-to-all-done.5.refs_0_ = bf16[4,144,512]{2,1,0:T(8,128)(2,1)S(1)} async-done(((bf16[4,144,512]{2,1,0:T(8,128)(2,1)}), bf16[4,144,512]{2,1,0:T(8,128)(2,1)S(1)}, u32[]{:S(2)}, u32[]{:S(2)}) %all-to-all-start.5) | async-done | bytes 589856 | tf_op jit(solution)/shard_map/all_to_all | solution.py:393
  106.2 5.4 %all-to-all-start.6 = ((bf16[16,48,128]{2,1,0:T(8,128)(2,1)}), bf16[16,48,128]{2,1,0:T(8,128)(2,1)S(1)}, u32[]{:S(2)}, u32[]{:S(2)}) async-start(bf16[16,48,128]{2,1,0:T(8,128)(2,1)} %copy-done.1), calls=%async_computation.6 | async-start | bytes 393216 | tf_op jit(solution)/shard_map/all_to_all | solution.py:406
  111.6 2.8 %collective-permute-start.2 = (bf16[192,512]{1,0:T(8,128)(2,1)}, bf16[192,512]{1,0:T(8,128)(2,1)S(1)}, u32[]{:S(2)}, u32[]{:S(2)}) collective-permute-start(bf16[192,512]{1,0:T(8,128)(2,1)} %get-tuple-element.38), channel_id=1, source_target_pairs={{0,2},{1,3},{2,0},{3,1},{4,6},{5,7},{6,4},{7,5},{8,10},{9,11},{10,... | collective-permute-start | bytes 589832 | tf_op jit(solution)/shard_map/ppermute | solution.py:28
  114.4 2.5 %collective-permute-start.3 = (bf16[192,512]{1,0:T(8,128)(2,1)}, bf16[192,512]{1,0:T(8,128)(2,1)S(1)}, u32[]{:S(2)}, u32[]{:S(2)}) collective-permute-start(bf16[192,512]{1,0:T(8,128)(2,1)} %get-tuple-element.39), channel_id=1, source_target_pairs={{0,1},{1,2},{2,3},{3,0},{4,5},{5,6},{6,7},{7,4},{8,9},{9,10},{10,1... | collective-permute-start | bytes 589832 | tf_op jit(solution)/shard_map/ppermute | solution.py:28
  117.0 4.0 %collective-permute-start.4 = (bf16[192,512]{1,0:T(8,128)(2,1)}, bf16[192,512]{1,0:T(8,128)(2,1)S(1)}, u32[]{:S(2)}, u32[]{:S(2)}) collective-permute-start(bf16[192,512]{1,0:T(8,128)(2,1)} %get-tuple-element.40), channel_id=1, source_target_pairs={{0,3},{1,0},{2,1},{3,2},{4,7},{5,4},{6,5},{7,6},{8,11},{9,8},{10,9... | collective-permute-start | bytes 589832 | tf_op jit(solution)/shard_map/ppermute | solution.py:28
  120.9 3.3 %collective-permute-done.3.refs_4_ = bf16[192,512]{1,0:T(8,128)(2,1)S(1)} collective-permute-done((bf16[192,512]{1,0:T(8,128)(2,1)}, bf16[192,512]{1,0:T(8,128)(2,1)S(1)}, u32[]{:S(2)}, u32[]{:S(2)}) %collective-permute-start.3) | collective-permute-done | bytes 196640 | tf_op jit(solution)/shard_map/ppermute | solution.py:28
  125.8 4.8 %collective-permute-start.7 = (bf16[192,512]{1,0:T(8,128)(2,1)S(1)}, bf16[192,512]{1,0:T(8,128)(2,1)S(1)}, u32[]{:S(2)}, u32[]{:S(2)}) collective-permute-start(bf16[192,512]{1,0:T(8,128)(2,1)S(1)} %shard_map.117.refs_3_), channel_id=1, source_target_pairs={{0,3},{1,0},{2,1},{3,2},{4,7},{5,4},{6,5},{7,6},{8,11},{9,8},{10,9... | collective-permute-start | bytes 589832 | tf_op jit(solution)/shard_map/ppermute | solution.py:28
  132.8 2.3 %collective-permute-start.5 = (bf16[192,512]{1,0:T(8,128)(2,1)S(1)}, bf16[192,512]{1,0:T(8,128)(2,1)S(1)}, u32[]{:S(2)}, u32[]{:S(2)}) collective-permute-start(bf16[192,512]{1,0:T(8,128)(2,1)S(1)} %shard_map.117.refs_3_), channel_id=1, source_target_pairs={{0,1},{1,2},{2,3},{3,0},{4,5},{5,6},{6,7},{7,4},{8,9},{9,10},{10,1... | collective-permute-start | bytes 589832 | tf_op jit(solution)/shard_map/ppermute | solution.py:28
  135.7 8.5 %all-to-all-start.7 = ((f32[8,2,512]{2,1,0:T(2,128)}), f32[8,2,512]{2,1,0:T(2,128)S(1)}, u32[]{:S(2)}, u32[]{:S(2)}) async-start(f32[8,2,512]{2,1,0:T(2,128)} %get-tuple-element.37), calls=%async_computation.7 | async-start | bytes 65536 | tf_op jit(solution)/shard_map/all_to_all | solution.py:419
  (68 shorter events, 21.9 us)
Async XLA Ops:
  0.6 18.0 %copy-start = (bf16[2048,512]{1,0:T(8,128)(2,1)S(1)}, bf16[2048,512]{1,0:T(8,128)(2,1)}, u32[]{:S(2)}) copy-start(bf16[2048,512]{1,0:T(8,128)(2,1)} %param.10) | copy-start | bytes 6291460
  2.1 27.8 %all-to-all-start = ((bf16[16,8,512]{2,1,0:T(8,128)(2,1)}), bf16[16,8,512]{2,1,0:T(8,128)(2,1)S(1)}, u32[]{:S(2)}, u32[]{:S(2)}) async-start(bf16[16,8,512]{2,1,0:T(8,128)(2,1)} %broadcast_in_dim.16), calls=%async_computation | async-start | bytes 262144 | tf_op jit(solution)/shard_map/all_to_all | solution.py:23
  21.5 19.1 %copy-start.13 = (s32[128,1,8]{0,2,1:T(8,128)S(1)}, s32[128,1,8]{0,2,1:T(8,128)}, u32[]{:S(2)}) copy-start(s32[128,1,8]{0,2,1:T(8,128)} %param.12) | copy-start | bytes 12292
  21.6 19.6 %copy-start.14 = (s32[128,1,8]{0,2,1:T(8,128)S(1)}, s32[128,1,8]{0,2,1:T(8,128)}, u32[]{:S(2)}) copy-start(s32[128,1,8]{0,2,1:T(8,128)} %param.13) | copy-start | bytes 12292
  30.7 12.2 %all-to-all-start.1 = ((bf16[4,128,512]{2,1,0:T(8,128)(2,1)}), bf16[4,128,512]{2,1,0:T(8,128)(2,1)S(1)}, u32[]{:S(2)}, u32[]{:S(2)}) async-start(bf16[4,128,512]{2,1,0:T(8,128)(2,1)} %broadcast_in_dim.34), calls=%async_computation.1 | async-start | bytes 1048576 | tf_op jit(solution)/shard_map/all_to_all | solution.py:23
  34.8 22.4 %collective-permute-start = (bf16[768,512]{1,0:T(8,128)(2,1)}, bf16[768,512]{1,0:T(8,128)(2,1)}, u32[]{:S(2)}, u32[]{:S(2)}) collective-permute-start(bf16[768,512]{1,0:T(8,128)(2,1)} %fusion.1.refs_5_.refs_7_.refs_6_), channel_id=1, source_target_pairs={{0,4},{4,0},{1,5},{5,1},{2,6},{6,2},{3,7},{7,3},{8,12},{12,8},{9,1... | collective-permute-start | bytes 2359304 | tf_op jit(solution)/shard_map/ppermute | solution.py:28
  42.9 14.2 %copy-start.11 = (bf16[4,128,512]{2,1,0:T(8,128)(2,1)}, bf16[4,128,512]{2,1,0:T(8,128)(2,1)S(1)}, u32[]{:S(2)}) copy-start(bf16[4,128,512]{2,1,0:T(8,128)(2,1)S(1)} %all-to-all-done.1) | copy-start | bytes 1572868
  43.8 23.6 %copy-start.12 = (s32[64,8]{1,0:T(8,128)S(1)}, s32[64,8]{1,0:T(8,128)}, u32[]{:S(2)}) copy-start(s32[64,8]{1,0:T(8,128)} %get-tuple-element.47) | copy-start | bytes 6148
  43.8 13.4 %all-to-all-start.2 = ((f32[8,2,512]{2,1,0:T(2,128)}), f32[8,2,512]{2,1,0:T(2,128)S(1)}, u32[]{:S(2)}, u32[]{:S(2)}) async-start(f32[8,2,512]{2,1,0:T(2,128)} %broadcast_in_dim.35), calls=%async_computation.2 | async-start | bytes 65536 | tf_op jit(solution)/shard_map/all_to_all | solution.py:23
  61.6 11.0 %collective-permute-start.1 = (bf16[512,512]{1,0:T(8,128)(2,1)}, bf16[512,512]{1,0:T(8,128)(2,1)}, u32[]{:S(2)}, u32[]{:S(2)}) collective-permute-start(bf16[512,512]{1,0:T(8,128)(2,1)} %get-tuple-element.28.refs_6_.refs_4_), channel_id=1, source_target_pairs={{0,4},{4,0},{1,5},{5,1},{2,6},{6,2},{3,7},{7,3},{8,12},{12,8},{9,1... | collective-permute-start | bytes 1572872 | tf_op jit(solution)/shard_map/ppermute | solution.py:28
  63.9 8.1 %all-to-all-start.3 = ((f32[8,2,512]{2,1,0:T(2,128)}), f32[8,2,512]{2,1,0:T(2,128)S(1)}, u32[]{:S(2)}, u32[]{:S(2)}) async-start(f32[8,2,512]{2,1,0:T(2,128)} %get-tuple-element.27), calls=%async_computation.3 | async-start | bytes 65536 | tf_op jit(solution)/shard_map/all_to_all | solution.py:342
  94.4 11.1 %all-to-all-start.5 = ((bf16[4,144,512]{2,1,0:T(8,128)(2,1)}), bf16[4,144,512]{2,1,0:T(8,128)(2,1)S(1)}, u32[]{:S(2)}, u32[]{:S(2)}) async-start(bf16[4,144,512]{2,1,0:T(8,128)(2,1)} %shard_map.112.refs_7_), calls=%async_computation.5 | async-start | bytes 1179648 | tf_op jit(solution)/shard_map/all_to_all | solution.py:393
  105.4 38.9 %copy-start.3 = (f32[16,2,640]{2,1,0:T(2,128)S(1)}, f32[16,2,640]{2,1,0:T(2,128)}, u32[]{:S(2)}) copy-start(f32[16,2,640]{2,1,0:T(2,128)} %all_to_all.40.refs_5_.refs_3_.refs_6_) | copy-start | bytes 245764
  106.2 28.8 %all-to-all-start.6 = ((bf16[16,48,128]{2,1,0:T(8,128)(2,1)}), bf16[16,48,128]{2,1,0:T(8,128)(2,1)S(1)}, u32[]{:S(2)}, u32[]{:S(2)}) async-start(bf16[16,48,128]{2,1,0:T(8,128)(2,1)} %copy-done.1), calls=%async_computation.6 | async-start | bytes 393216 | tf_op jit(solution)/shard_map/all_to_all | solution.py:406
  111.6 9.3 %collective-permute-start.2 = (bf16[192,512]{1,0:T(8,128)(2,1)}, bf16[192,512]{1,0:T(8,128)(2,1)S(1)}, u32[]{:S(2)}, u32[]{:S(2)}) collective-permute-start(bf16[192,512]{1,0:T(8,128)(2,1)} %get-tuple-element.38), channel_id=1, source_target_pairs={{0,2},{1,3},{2,0},{3,1},{4,6},{5,7},{6,4},{7,5},{8,10},{9,11},{10,... | collective-permute-start | bytes 589832 | tf_op jit(solution)/shard_map/ppermute | solution.py:28
  114.4 9.8 %collective-permute-start.3 = (bf16[192,512]{1,0:T(8,128)(2,1)}, bf16[192,512]{1,0:T(8,128)(2,1)S(1)}, u32[]{:S(2)}, u32[]{:S(2)}) collective-permute-start(bf16[192,512]{1,0:T(8,128)(2,1)} %get-tuple-element.39), channel_id=1, source_target_pairs={{0,1},{1,2},{2,3},{3,0},{4,5},{5,6},{6,7},{7,4},{8,9},{9,10},{10,1... | collective-permute-start | bytes 589832 | tf_op jit(solution)/shard_map/ppermute | solution.py:28
  117.0 7.3 %collective-permute-start.4 = (bf16[192,512]{1,0:T(8,128)(2,1)}, bf16[192,512]{1,0:T(8,128)(2,1)S(1)}, u32[]{:S(2)}, u32[]{:S(2)}) collective-permute-start(bf16[192,512]{1,0:T(8,128)(2,1)} %get-tuple-element.40), channel_id=1, source_target_pairs={{0,3},{1,0},{2,1},{3,2},{4,7},{5,4},{6,5},{7,6},{8,11},{9,8},{10,9... | collective-permute-start | bytes 589832 | tf_op jit(solution)/shard_map/ppermute | solution.py:28
  124.3 1.0 copy-start.2
  125.8 22.5 %collective-permute-start.7 = (bf16[192,512]{1,0:T(8,128)(2,1)S(1)}, bf16[192,512]{1,0:T(8,128)(2,1)S(1)}, u32[]{:S(2)}, u32[]{:S(2)}) collective-permute-start(bf16[192,512]{1,0:T(8,128)(2,1)S(1)} %shard_map.117.refs_3_), channel_id=1, source_target_pairs={{0,3},{1,0},{2,1},{3,2},{4,7},{5,4},{6,5},{7,6},{8,11},{9,8},{10,9... | collective-permute-start | bytes 589832 | tf_op jit(solution)/shard_map/ppermute | solution.py:28
  130.6 17.7 %collective-permute-start.6 = (bf16[192,512]{1,0:T(8,128)(2,1)S(1)}, bf16[192,512]{1,0:T(8,128)(2,1)S(1)}, u32[]{:S(2)}, u32[]{:S(2)}) collective-permute-start(bf16[192,512]{1,0:T(8,128)(2,1)S(1)} %shard_map.117.refs_3_), channel_id=1, source_target_pairs={{0,2},{1,3},{2,0},{3,1},{4,6},{5,7},{6,4},{7,5},{8,10},{9,11},{10,... | collective-permute-start | bytes 589832 | tf_op jit(solution)/shard_map/ppermute | solution.py:28
  132.8 15.6 %collective-permute-start.5 = (bf16[192,512]{1,0:T(8,128)(2,1)S(1)}, bf16[192,512]{1,0:T(8,128)(2,1)S(1)}, u32[]{:S(2)}, u32[]{:S(2)}) collective-permute-start(bf16[192,512]{1,0:T(8,128)(2,1)S(1)} %shard_map.117.refs_3_), channel_id=1, source_target_pairs={{0,1},{1,2},{2,3},{3,0},{4,5},{5,6},{6,7},{7,4},{8,9},{9,10},{10,1... | collective-permute-start | bytes 589832 | tf_op jit(solution)/shard_map/ppermute | solution.py:28
  135.7 13.4 %all-to-all-start.7 = ((f32[8,2,512]{2,1,0:T(2,128)}), f32[8,2,512]{2,1,0:T(2,128)S(1)}, u32[]{:S(2)}, u32[]{:S(2)}) async-start(f32[8,2,512]{2,1,0:T(2,128)} %get-tuple-element.37), calls=%async_computation.7 | async-start | bytes 65536 | tf_op jit(solution)/shard_map/all_to_all | solution.py:419
  144.3 0.8 copy-start.7
  149.1 0.9 copy-start.5
  (6 other events, 4.0 us)

commit v13 on v12

--- a/solution.py
+++ b/solution.py
@@ -431,6 +431,7 @@
         40 * rows_dev * width,
         grant=SMALL,
     )(own.astype(jnp.int32), embeddings, sums, gain, bias, grad_unit, totals)
+    moved = {by: shift(grad, "rep", by) for by in reversed(far_first)}
     emb_grad, centre_grad, gain_grad, bias_grad = call(
         lambda *refs: final_kernel(nr, *refs),
         [SM] + [VM] * (2 + nr),
@@ -444,7 +445,7 @@
         slots * width,
         4 * slots * width,
         grant=SMALL,
-    )(at, terms, ends, grad, *[shift(grad, "rep", by) for by in range(1, nr)])
+    )(at, terms, ends, grad, *[moved[by] for by in range(1, nr)])
     return (row_loss[0], emb_grad, centre_grad, gain_grad[0], bias_grad[0])
 
 

time: 152 us -> 152 us (level)
  no operation moved by 1% of the time
where the time goes in v13:
time: 152 us; the launch traced here: 151 us
  starting transfers between devices  75.5 us (50%)
  waiting for transfers between devices  21.5 us (14%)
  Pallas kernels  18.8 us (12%)
  blocking collectives  16 us (11%)
  local copies, waits for them, and re-layouts  14.3 us (9%)
  other arithmetic  4.02 us (3%)
    all_to_all x3, starting transfers between devices, spread(): return lax.all_to_all(copies, axes, 0, 0)  28.2 us
    ppermute x8, starting transfers between devices, shift(): return lax.ppermute(block, axis, [(i, (i + by) % n) for i in range(n)])  26.6 us
    all_to_all x1, blocking collectives, body(): totals = lax.all_to_all(totals, 'z', 0, 0)  16 us
    all_to_all x3, waiting for transfers between devices, spread(): return lax.all_to_all(copies, axes, 0, 0)  11.6 us
    all_to_all x1, starting transfers between devices, body(): ends = lax.all_to_all(ends, ('core', 'rep'), 0, 0)  8.52 us
    unnamed x32, local copies, waits for them, and re-layouts  6.91 us
    pallas_call x1, Pallas kernels, body(): call(lambda *refs: pull_kernel(batch, *refs), [VM] * 9, VM, jax.ShapeDtyp...  5.76 us
    all_to_all x1, starting transfers between devices, body(): pull = lax.all_to_all(pull, 'z', 0, 0)  5.42 us
  transfers between devices with their start and end apart: 15, of which 6 were waited for; matrix products, arithmetic and copies ran while one was open for 6% of the time, Pallas kernels for 5%

profile of v13, /device:TPU:1, one launch (start us, length us, event | category | flops | bytes accessed | tf_op | source)
XLA Modules:
  0.0 151.0 jit_solution(16090299569939348414)
XLA Ops:
  2.1 15.7 %all-to-all-start = ((bf16[16,8,512]{2,1,0:T(8,128)(2,1)}), bf16[16,8,512]{2,1,0:T(8,128)(2,1)S(1)}, u32[]{:S(2)}, u32[]{:S(2)}) async-start(bf16[16,8,512]{2,1,0:T(8,128)(2,1)} %broadcast_in_dim.16), calls=%async_computation | async-start | bytes 262144 | tf_op jit(solution)/shard_map/all_to_all | solution.py:23
  18.6 2.7 %gather_fusion = bf16[768,512]{1,0:T(8,128)(2,1)S(1)} fusion(bf16[2048,512]{1,0:T(8,128)(2,1)S(1)} %copy-done, s32[1024]{0:T(1024)S(1)} %pad_clamp_fusion), kind=kCustom, calls=%fused_computation | custom fusion | bytes 1575936 | tf_op jit(solution)/shard_map/gather | solution.py:301
  22.7 7.2 %all-to-all-done = bf16[16,8,512]{2,1,0:T(8,128)(2,1)S(1)} async-done(((bf16[16,8,512]{2,1,0:T(8,128)(2,1)}), bf16[16,8,512]{2,1,0:T(8,128)(2,1)S(1)}, u32[]{:S(2)}, u32[]{:S(2)}) %all-to-all-start) | async-done | bytes 131104 | tf_op jit(solution)/shard_map/all_to_all | solution.py:23
  30.7 4.0 %all-to-all-start.1 = ((bf16[4,128,512]{2,1,0:T(8,128)(2,1)}), bf16[4,128,512]{2,1,0:T(8,128)(2,1)S(1)}, u32[]{:S(2)}, u32[]{:S(2)}) async-start(bf16[4,128,512]{2,1,0:T(8,128)(2,1)} %broadcast_in_dim.34), calls=%async_computation.1 | async-start | bytes 1048576 | tf_op jit(solution)/shard_map/all_to_all | solution.py:23
  34.8 5.8 %collective-permute-start = (bf16[768,512]{1,0:T(8,128)(2,1)}, bf16[768,512]{1,0:T(8,128)(2,1)}, u32[]{:S(2)}, u32[]{:S(2)}) collective-permute-start(bf16[768,512]{1,0:T(8,128)(2,1)} %fusion.1.refs_5_.refs_7_.refs_6_), channel_id=1, source_target_pairs={{0,4},{4,0},{1,5},{5,1},{2,6},{6,2},{3,7},{7,3},{8,12},{12,8},{9,1... | collective-permute-start | bytes 2359304 | tf_op jit(solution)/shard_map/ppermute | solution.py:28
  43.8 8.4 %all-to-all-start.2 = ((f32[8,2,512]{2,1,0:T(2,128)}), f32[8,2,512]{2,1,0:T(2,128)S(1)}, u32[]{:S(2)}, u32[]{:S(2)}) async-start(f32[8,2,512]{2,1,0:T(2,128)} %broadcast_in_dim.35), calls=%async_computation.2 | async-start | bytes 65536 | tf_op jit(solution)/shard_map/all_to_all | solution.py:23
  52.8 4.3 %all-to-all-done.2.refs_1_.refs_2_ = f32[8,2,512]{2,1,0:T(2,128)S(1)} async-done(((f32[8,2,512]{2,1,0:T(2,128)}), f32[8,2,512]{2,1,0:T(2,128)S(1)}, u32[]{:S(2)}, u32[]{:S(2)}) %all-to-all-start.2) | async-done | bytes 32800 | tf_op jit(solution)/shard_map/all_to_all | solution.py:23
  57.7 3.9 %shard_map.110 = (bf16[512,512]{1,0:T(8,128)(2,1)}, f32[8,2,512]{2,1,0:T(2,128)}) custom-call(bf16[512,512]{1,0:T(8,128)(2,1)} %bitcast.24, f32[8,2,512]{2,1,0:T(2,128)} %copy-done.6, f32[1,512]{1,0:T(1,128)} %bitcast.18, f32[1,512]{1,0:T(1,128)} %bitcast.21, s32[1,512]{1,0:T(1,128)} %select_select_fusion.refs_4_.refs_1_, ...), custom_call_target="tpu_custom_call" | custom-call | flops 805306368 | bytes 1572864 | tf_op jit(solution)/shard_map/pallas_call | solution.py:328
  61.6 2.3 %collective-permute-start.1 = (bf16[512,512]{1,0:T(8,128)(2,1)}, bf16[512,512]{1,0:T(8,128)(2,1)}, u32[]{:S(2)}, u32[]{:S(2)}) collective-permute-start(bf16[512,512]{1,0:T(8,128)(2,1)} %get-tuple-element.28.refs_6_.refs_4_), channel_id=1, source_target_pairs={{0,4},{4,0},{1,5},{5,1},{2,6},{6,2},{3,7},{7,3},{8,12},{12,8},{9,1... | collective-permute-start | bytes 1572872 | tf_op jit(solution)/shard_map/ppermute | solution.py:28
  63.9 3.4 %all-to-all-start.3 = ((f32[8,2,512]{2,1,0:T(2,128)}), f32[8,2,512]{2,1,0:T(2,128)S(1)}, u32[]{:S(2)}, u32[]{:S(2)}) async-start(f32[8,2,512]{2,1,0:T(2,128)} %get-tuple-element.27), calls=%async_computation.3 | async-start | bytes 65536 | tf_op jit(solution)/shard_map/all_to_all | solution.py:342
  68.0 4.0 %all-to-all-done.3.refs_1_ = f32[8,2,512]{2,1,0:T(2,128)S(1)} async-done(((f32[8,2,512]{2,1,0:T(2,128)}), f32[8,2,512]{2,1,0:T(2,128)S(1)}, u32[]{:S(2)}, u32[]{:S(2)}) %all-to-all-start.3) | async-done | bytes 32800 | tf_op jit(solution)/shard_map/all_to_all | solution.py:342
  72.6 16.0 %all_to_all.40.refs_5_.refs_3_.refs_6_ = f32[16,2,640]{2,1,0:T(2,128)} all-to-all(f32[16,2,640]{2,1,0:T(2,128)S(1)} %shard_map.111), channel_id=1, replica_groups=mesh['x'=4,'z'=16,'core'=2,'rep'=4] {'z'}, dimensions={0} | all-to-all | bytes 163840 | tf_op jit(solution)/shard_map/all_to_all | solution.py:353
  88.6 5.8 %shard_map.112.refs_7_ = bf16[4,144,512]{2,1,0:T(8,128)(2,1)} custom-call(bf16[512,512]{1,0:T(8,128)(2,1)} %bitcast.25, f32[8,2,512]{2,1,0:T(2,128)} %copy-done.6, f32[1,512]{1,0:T(1,128)} %bitcast.19, f32[1,512]{1,0:T(1,128)} %bitcast.22, s32[1,512]{1,0:T(1,128)} %select_select_fusion.refs_4_.refs_1_, f32[16,2,640]{2,1,0:T(2,128)} %all_to_all.40.refs_5_.refs_3_.refs_6_, ...), custom_call_target="tpu_custom_call" | custom-call | flops 1610612736 | bytes 1572864 | tf_op jit(solution)/shard_map/pallas_call | solution.py:355
  94.4 3.5 %all-to-all-start.5 = ((bf16[4,144,512]{2,1,0:T(8,128)(2,1)}), bf16[4,144,512]{2,1,0:T(8,128)(2,1)S(1)}, u32[]{:S(2)}, u32[]{:S(2)}) async-start(bf16[4,144,512]{2,1,0:T(8,128)(2,1)} %shard_map.112.refs_7_), calls=%async_computation.5 | async-start | bytes 1179648 | tf_op jit(solution)/shard_map/all_to_all | solution.py:393
  97.9 5.1 %shard_map.113 = (f32[192,512]{1,0:T(8,128)}, bf16[192,512]{1,0:T(8,128)(2,1)}, bf16[192,512]{1,0:T(8,128)(2,1)}, bf16[192,512]{1,0:T(8,128)(2,1)}) custom-call(s32[1]{0:T(128)} %bitcast.13.refs_0_, s32[1,512]{1,0:T(1,128)} %select_select_fusion.refs_4_.refs_1_, s32[1,512]{1,0:T(1,128)} %select_n.55.refs_2_, ...), custom_call_target="tpu_custom_call" | custom-call | flops 1610612736 | bytes 1572864 | tf_op jit(solution)/shard_map/pallas_call | solution.py:366
  103.0 2.4 %all-to-all-done.5.refs_0_ = bf16[4,144,512]{2,1,0:T(8,128)(2,1)S(1)} async-done(((bf16[4,144,512]{2,1,0:T(8,128)(2,1)}), bf16[4,144,512]{2,1,0:T(8,128)(2,1)S(1)}, u32[]{:S(2)}, u32[]{:S(2)}) %all-to-all-start.5) | async-done | bytes 589856 | tf_op jit(solution)/shard_map/all_to_all | solution.py:393
  106.2 5.4 %all-to-all-start.6 = ((bf16[16,48,128]{2,1,0:T(8,128)(2,1)}), bf16[16,48,128]{2,1,0:T(8,128)(2,1)S(1)}, u32[]{:S(2)}, u32[]{:S(2)}) async-start(bf16[16,48,128]{2,1,0:T(8,128)(2,1)} %copy-done.1), calls=%async_computation.6 | async-start | bytes 393216 | tf_op jit(solution)/shard_map/all_to_all | solution.py:406
  111.6 2.8 %collective-permute-start.2 = (bf16[192,512]{1,0:T(8,128)(2,1)}, bf16[192,512]{1,0:T(8,128)(2,1)S(1)}, u32[]{:S(2)}, u32[]{:S(2)}) collective-permute-start(bf16[192,512]{1,0:T(8,128)(2,1)} %get-tuple-element.38), channel_id=1, source_target_pairs={{0,2},{1,3},{2,0},{3,1},{4,6},{5,7},{6,4},{7,5},{8,10},{9,11},{10,... | collective-permute-start | bytes 589832 | tf_op jit(solution)/shard_map/ppermute | solution.py:28
  114.4 2.5 %collective-permute-start.3 = (bf16[192,512]{1,0:T(8,128)(2,1)}, bf16[192,512]{1,0:T(8,128)(2,1)S(1)}, u32[]{:S(2)}, u32[]{:S(2)}) collective-permute-start(bf16[192,512]{1,0:T(8,128)(2,1)} %get-tuple-element.39), channel_id=1, source_target_pairs={{0,1},{1,2},{2,3},{3,0},{4,5},{5,6},{6,7},{7,4},{8,9},{9,10},{10,1... | collective-permute-start | bytes 589832 | tf_op jit(solution)/shard_map/ppermute | solution.py:28
  117.0 4.0 %collective-permute-start.4 = (bf16[192,512]{1,0:T(8,128)(2,1)}, bf16[192,512]{1,0:T(8,128)(2,1)S(1)}, u32[]{:S(2)}, u32[]{:S(2)}) collective-permute-start(bf16[192,512]{1,0:T(8,128)(2,1)} %get-tuple-element.40), channel_id=1, source_target_pairs={{0,3},{1,0},{2,1},{3,2},{4,7},{5,4},{6,5},{7,6},{8,11},{9,8},{10,9... | collective-permute-start | bytes 589832 | tf_op jit(solution)/shard_map/ppermute | solution.py:28
  120.9 3.3 %collective-permute-done.3.refs_4_ = bf16[192,512]{1,0:T(8,128)(2,1)S(1)} collective-permute-done((bf16[192,512]{1,0:T(8,128)(2,1)}, bf16[192,512]{1,0:T(8,128)(2,1)S(1)}, u32[]{:S(2)}, u32[]{:S(2)}) %collective-permute-start.3) | collective-permute-done | bytes 196640 | tf_op jit(solution)/shard_map/ppermute | solution.py:28
  125.8 4.8 %collective-permute-start.7 = (bf16[192,512]{1,0:T(8,128)(2,1)S(1)}, bf16[192,512]{1,0:T(8,128)(2,1)S(1)}, u32[]{:S(2)}, u32[]{:S(2)}) collective-permute-start(bf16[192,512]{1,0:T(8,128)(2,1)S(1)} %shard_map.117.refs_3_), channel_id=1, source_target_pairs={{0,3},{1,0},{2,1},{3,2},{4,7},{5,4},{6,5},{7,6},{8,11},{9,8},{10,9... | collective-permute-start | bytes 589832 | tf_op jit(solution)/shard_map/ppermute | solution.py:28
  132.8 2.3 %collective-permute-start.5 = (bf16[192,512]{1,0:T(8,128)(2,1)S(1)}, bf16[192,512]{1,0:T(8,128)(2,1)S(1)}, u32[]{:S(2)}, u32[]{:S(2)}) collective-permute-start(bf16[192,512]{1,0:T(8,128)(2,1)S(1)} %shard_map.117.refs_3_), channel_id=1, source_target_pairs={{0,1},{1,2},{2,3},{3,0},{4,5},{5,6},{6,7},{7,4},{8,9},{9,10},{10,1... | collective-permute-start | bytes 589832 | tf_op jit(solution)/shard_map/ppermute | solution.py:28
  135.7 8.5 %all-to-all-start.7 = ((f32[8,2,512]{2,1,0:T(2,128)}), f32[8,2,512]{2,1,0:T(2,128)S(1)}, u32[]{:S(2)}, u32[]{:S(2)}) async-start(f32[8,2,512]{2,1,0:T(2,128)} %get-tuple-element.37), calls=%async_computation.7 | async-start | bytes 65536 | tf_op jit(solution)/shard_map/all_to_all | solution.py:419
  (68 shorter events, 21.9 us)
Async XLA Ops:
  0.6 18.0 %copy-start = (bf16[2048,512]{1,0:T(8,128)(2,1)S(1)}, bf16[2048,512]{1,0:T(8,128)(2,1)}, u32[]{:S(2)}) copy-start(bf16[2048,512]{1,0:T(8,128)(2,1)} %param.10) | copy-start | bytes 6291460
  2.1 27.8 %all-to-all-start = ((bf16[16,8,512]{2,1,0:T(8,128)(2,1)}), bf16[16,8,512]{2,1,0:T(8,128)(2,1)S(1)}, u32[]{:S(2)}, u32[]{:S(2)}) async-start(bf16[16,8,512]{2,1,0:T(8,128)(2,1)} %broadcast_in_dim.16), calls=%async_computation | async-start | bytes 262144 | tf_op jit(solution)/shard_map/all_to_all | solution.py:23
  21.5 19.1 %copy-start.13 = (s32[128,1,8]{0,2,1:T(8,128)S(1)}, s32[128,1,8]{0,2,1:T(8,128)}, u32[]{:S(2)}) copy-start(s32[128,1,8]{0,2,1:T(8,128)} %param.12) | copy-start | bytes 12292
  21.6 19.6 %copy-start.14 = (s32[128,1,8]{0,2,1:T(8,128)S(1)}, s32[128,1,8]{0,2,1:T(8,128)}, u32[]{:S(2)}) copy-start(s32[128,1,8]{0,2,1:T(8,128)} %param.13) | copy-start | bytes 12292
  30.7 12.2 %all-to-all-start.1 = ((bf16[4,128,512]{2,1,0:T(8,128)(2,1)}), bf16[4,128,512]{2,1,0:T(8,128)(2,1)S(1)}, u32[]{:S(2)}, u32[]{:S(2)}) async-start(bf16[4,128,512]{2,1,0:T(8,128)(2,1)} %broadcast_in_dim.34), calls=%async_computation.1 | async-start | bytes 1048576 | tf_op jit(solution)/shard_map/all_to_all | solution.py:23
  34.8 22.4 %collective-permute-start = (bf16[768,512]{1,0:T(8,128)(2,1)}, bf16[768,512]{1,0:T(8,128)(2,1)}, u32[]{:S(2)}, u32[]{:S(2)}) collective-permute-start(bf16[768,512]{1,0:T(8,128)(2,1)} %fusion.1.refs_5_.refs_7_.refs_6_), channel_id=1, source_target_pairs={{0,4},{4,0},{1,5},{5,1},{2,6},{6,2},{3,7},{7,3},{8,12},{12,8},{9,1... | collective-permute-start | bytes 2359304 | tf_op jit(solution)/shard_map/ppermute | solution.py:28
  42.9 14.2 %copy-start.11 = (bf16[4,128,512]{2,1,0:T(8,128)(2,1)}, bf16[4,128,512]{2,1,0:T(8,128)(2,1)S(1)}, u32[]{:S(2)}) copy-start(bf16[4,128,512]{2,1,0:T(8,128)(2,1)S(1)} %all-to-all-done.1) | copy-start | bytes 1572868
  43.8 23.6 %copy-start.12 = (s32[64,8]{1,0:T(8,128)S(1)}, s32[64,8]{1,0:T(8,128)}, u32[]{:S(2)}) copy-start(s32[64,8]{1,0:T(8,128)} %get-tuple-element.47) | copy-start | bytes 6148
  43.8 13.4 %all-to-all-start.2 = ((f32[8,2,512]{2,1,0:T(2,128)}), f32[8,2,512]{2,1,0:T(2,128)S(1)}, u32[]{:S(2)}, u32[]{:S(2)}) async-start(f32[8,2,512]{2,1,0:T(2,128)} %broadcast_in_dim.35), calls=%async_computation.2 | async-start | bytes 65536 | tf_op jit(solution)/shard_map/all_to_all | solution.py:23
  61.6 11.0 %collective-permute-start.1 = (bf16[512,512]{1,0:T(8,128)(2,1)}, bf16[512,512]{1,0:T(8,128)(2,1)}, u32[]{:S(2)}, u32[]{:S(2)}) collective-permute-start(bf16[512,512]{1,0:T(8,128)(2,1)} %get-tuple-element.28.refs_6_.refs_4_), channel_id=1, source_target_pairs={{0,4},{4,0},{1,5},{5,1},{2,6},{6,2},{3,7},{7,3},{8,12},{12,8},{9,1... | collective-permute-start | bytes 1572872 | tf_op jit(solution)/shard_map/ppermute | solution.py:28
  63.9 8.1 %all-to-all-start.3 = ((f32[8,2,512]{2,1,0:T(2,128)}), f32[8,2,512]{2,1,0:T(2,128)S(1)}, u32[]{:S(2)}, u32[]{:S(2)}) async-start(f32[8,2,512]{2,1,0:T(2,128)} %get-tuple-element.27), calls=%async_computation.3 | async-start | bytes 65536 | tf_op jit(solution)/shard_map/all_to_all | solution.py:342
  94.4 11.1 %all-to-all-start.5 = ((bf16[4,144,512]{2,1,0:T(8,128)(2,1)}), bf16[4,144,512]{2,1,0:T(8,128)(2,1)S(1)}, u32[]{:S(2)}, u32[]{:S(2)}) async-start(bf16[4,144,512]{2,1,0:T(8,128)(2,1)} %shard_map.112.refs_7_), calls=%async_computation.5 | async-start | bytes 1179648 | tf_op jit(solution)/shard_map/all_to_all | solution.py:393
  105.4 38.9 %copy-start.3 = (f32[16,2,640]{2,1,0:T(2,128)S(1)}, f32[16,2,640]{2,1,0:T(2,128)}, u32[]{:S(2)}) copy-start(f32[16,2,640]{2,1,0:T(2,128)} %all_to_all.40.refs_5_.refs_3_.refs_6_) | copy-start | bytes 245764
  106.2 28.8 %all-to-all-start.6 = ((bf16[16,48,128]{2,1,0:T(8,128)(2,1)}), bf16[16,48,128]{2,1,0:T(8,128)(2,1)S(1)}, u32[]{:S(2)}, u32[]{:S(2)}) async-start(bf16[16,48,128]{2,1,0:T(8,128)(2,1)} %copy-done.1), calls=%async_computation.6 | async-start | bytes 393216 | tf_op jit(solution)/shard_map/all_to_all | solution.py:406
  111.6 9.3 %collective-permute-start.2 = (bf16[192,512]{1,0:T(8,128)(2,1)}, bf16[192,512]{1,0:T(8,128)(2,1)S(1)}, u32[]{:S(2)}, u32[]{:S(2)}) collective-permute-start(bf16[192,512]{1,0:T(8,128)(2,1)} %get-tuple-element.38), channel_id=1, source_target_pairs={{0,2},{1,3},{2,0},{3,1},{4,6},{5,7},{6,4},{7,5},{8,10},{9,11},{10,... | collective-permute-start | bytes 589832 | tf_op jit(solution)/shard_map/ppermute | solution.py:28
  114.4 9.8 %collective-permute-start.3 = (bf16[192,512]{1,0:T(8,128)(2,1)}, bf16[192,512]{1,0:T(8,128)(2,1)S(1)}, u32[]{:S(2)}, u32[]{:S(2)}) collective-permute-start(bf16[192,512]{1,0:T(8,128)(2,1)} %get-tuple-element.39), channel_id=1, source_target_pairs={{0,1},{1,2},{2,3},{3,0},{4,5},{5,6},{6,7},{7,4},{8,9},{9,10},{10,1... | collective-permute-start | bytes 589832 | tf_op jit(solution)/shard_map/ppermute | solution.py:28
  117.0 7.3 %collective-permute-start.4 = (bf16[192,512]{1,0:T(8,128)(2,1)}, bf16[192,512]{1,0:T(8,128)(2,1)S(1)}, u32[]{:S(2)}, u32[]{:S(2)}) collective-permute-start(bf16[192,512]{1,0:T(8,128)(2,1)} %get-tuple-element.40), channel_id=1, source_target_pairs={{0,3},{1,0},{2,1},{3,2},{4,7},{5,4},{6,5},{7,6},{8,11},{9,8},{10,9... | collective-permute-start | bytes 589832 | tf_op jit(solution)/shard_map/ppermute | solution.py:28
  124.3 1.0 copy-start.2
  125.8 22.5 %collective-permute-start.7 = (bf16[192,512]{1,0:T(8,128)(2,1)S(1)}, bf16[192,512]{1,0:T(8,128)(2,1)S(1)}, u32[]{:S(2)}, u32[]{:S(2)}) collective-permute-start(bf16[192,512]{1,0:T(8,128)(2,1)S(1)} %shard_map.117.refs_3_), channel_id=1, source_target_pairs={{0,3},{1,0},{2,1},{3,2},{4,7},{5,4},{6,5},{7,6},{8,11},{9,8},{10,9... | collective-permute-start | bytes 589832 | tf_op jit(solution)/shard_map/ppermute | solution.py:28
  130.6 17.7 %collective-permute-start.6 = (bf16[192,512]{1,0:T(8,128)(2,1)S(1)}, bf16[192,512]{1,0:T(8,128)(2,1)S(1)}, u32[]{:S(2)}, u32[]{:S(2)}) collective-permute-start(bf16[192,512]{1,0:T(8,128)(2,1)S(1)} %shard_map.117.refs_3_), channel_id=1, source_target_pairs={{0,2},{1,3},{2,0},{3,1},{4,6},{5,7},{6,4},{7,5},{8,10},{9,11},{10,... | collective-permute-start | bytes 589832 | tf_op jit(solution)/shard_map/ppermute | solution.py:28
  132.8 15.6 %collective-permute-start.5 = (bf16[192,512]{1,0:T(8,128)(2,1)S(1)}, bf16[192,512]{1,0:T(8,128)(2,1)S(1)}, u32[]{:S(2)}, u32[]{:S(2)}) collective-permute-start(bf16[192,512]{1,0:T(8,128)(2,1)S(1)} %shard_map.117.refs_3_), channel_id=1, source_target_pairs={{0,1},{1,2},{2,3},{3,0},{4,5},{5,6},{6,7},{7,4},{8,9},{9,10},{10,1... | collective-permute-start | bytes 589832 | tf_op jit(solution)/shard_map/ppermute | solution.py:28
  135.7 13.4 %all-to-all-start.7 = ((f32[8,2,512]{2,1,0:T(2,128)}), f32[8,2,512]{2,1,0:T(2,128)S(1)}, u32[]{:S(2)}, u32[]{:S(2)}) async-start(f32[8,2,512]{2,1,0:T(2,128)} %get-tuple-element.37), calls=%async_computation.7 | async-start | bytes 65536 | tf_op jit(solution)/shard_map/all_to_all | solution.py:419
  144.3 0.8 copy-start.7
  149.1 0.9 copy-start.5
  (6 other events, 4.0 us)
